TPU v7x, 32 devices: a whole 2x2x4 slice. The times are simulated.
32 devices in a mesh: curve: 8 (over z, y), cross: 4 (over x, core).
Axes of the slice: x: 2, y: 2, z: 4, core: 2. Of those that a mesh axis runs over, the one named last changes fastest.
Arguments:
- populations: float32 [96, 19, 4096], P(('curve', 'cross')), may hold values from 0 to 3, as said below
- site_flags: int32 [96, 5832], P(('curve', 'cross')), may hold values from 0 to 1, as said below
- neighbours: int32 [96, 18], P(('curve', 'cross')), may hold values from -1 to 95, as said below
- migrations: int32 [32, 3], replicated, may hold values from -1 to 31, as said below
- counts: int32 [32], P(('curve', 'cross')), may hold values from 1 to 3, as said below
Outputs:
- advanced: float32 [96, 19, 4096], P(('curve', 'cross'))
Inputs may be any that keep to these rules, and one draw needn't show every extreme that they name: Weighted populations of a flow of density near one and small velocity; every entry is positive. `site_flags`: the padding sites carry the flags of the neighbouring block's sites there, 0 where no block lies; corner padding sites and all sites of empty slots are 0. `neighbours`: A block named in direction c_j lies on the device whose curve index exceeds the block's own by the first component of c_j and whose cross index exceeds it by the second; a block in direction c_j names the first block in direction -c_j. Empty slots name none. `migrations`: at most one block leaves a device, to the device one step lower or higher along curve with the same cross index; -1 in all three columns where none leaves. Destination slots lie below the receiver's count and no two moves share one. `counts`: the live blocks of a device fill its slots 0 to count - 1; in every draw some device holds 3.
All inputs are finite; a program needn't handle non-finite values.
Results may differ from a plain program's by a relative error of at most 0.0003.
Values sent between devices are 32-bit elements; how exact they have to be, the bound alone decides.
No kernel may reach another device: no remote copies, remote signals or barrier semaphores. Data moves between devices by JAX's collectives and lax.ppermute only.
A program may use at most 128 MiB of HBM per device.

v0:
```python
import functools

import jax
import jax.numpy as jnp
import numpy as np
from jax import lax
from jax.experimental import pallas as pl
from jax.experimental.pallas import tpu as pltpu
from jax.sharding import PartitionSpec as P

EDGE = 16
STEPS = 3
SLOTS = 3
POPS = 19
PLANES = SLOTS * POPS + SLOTS
FLAG0 = SLOTS * POPS
GROUP = 24
PLANE = 4 * GROUP
SLOT = POPS * PLANE
STRIP = 6 * PLANES
HALF = POPS * EDGE
PAIRS = PLANES // 2
LIMIT = 48 * 1024 * 1024

VELOCITY = [
    (0, 0, 0),
    (1, 0, 0),
    (-1, 0, 0),
    (0, 1, 0),
    (0, -1, 0),
    (0, 0, 1),
    (0, 0, -1),
    (1, 1, 0),
    (-1, -1, 0),
    (1, -1, 0),
    (-1, 1, 0),
    (1, 0, 1),
    (-1, 0, -1),
    (1, 0, -1),
    (-1, 0, 1),
    (0, 1, 1),
    (0, -1, -1),
    (0, 1, -1),
    (0, -1, 1),
]
OPPOSITE = [0, 2, 1, 4, 3, 6, 5, 8, 7, 10, 9, 12, 11, 14, 13, 16, 15, 18, 17]


def lanes_iota():
    return lax.broadcasted_iota(jnp.int32, (8, 128), 1)


def rows_iota():
    return lax.broadcasted_iota(jnp.int32, (8, 128), 0)


def aligned(start, size=8):
    return pl.ds(pl.multiple_of(start, 8), size)


def move_slots(moves, where, curve_size, cross_size):
    curve, cross = where[0], where[1]

    def landed(source, target):
        inside = (source >= 0) & (source < curve_size) & (target >= 0) & (target < curve_size)
        row = jnp.clip(source, 0, curve_size - 1) * cross_size + cross
        rank = target * cross_size + cross
        hit = inside & (moves[row * 3] >= 0) & (moves[row * 3 + 1] == rank)
        return jnp.where(hit, moves[row * 3 + 2], -1)

    here = curve * cross_size + cross
    return (
        landed(curve - 1, curve),
        landed(curve + 1, curve),
        landed(curve - 2, curve - 1),
        landed(curve, curve - 1),
        landed(curve + 2, curve + 1),
        landed(curve, curve + 1),
        jnp.maximum(moves[here * 3], 0),
    )


def pack_kernel(
    curve_size,
    cross_size,
    moves,
    where,
    counts,
    pops,
    flags,
    cells,
    up_msg,
    down_msg,
    up2_msg,
    down2_msg,
    inner_msg,
    wide_flags,
    plane_flags,
    site_flags,
):
    wide_flags[...] = jnp.zeros_like(wide_flags)
    wide_flags[0:SLOTS, 0 : flags.shape[1]] = flags[...].astype(jnp.float32)
    span = EDGE + 2
    for x in range(EDGE):
        start = (x + 1) * span * span
        base = start // 128 * 128
        window = wide_flags[:, base : base + 512]
        window = pltpu.roll(window, (512 - (start - base)) % 512, axis=1)
        plane_flags[8 * x : 8 * x + 8, :] = window[:, :384].astype(jnp.bfloat16)
    lane_in = lax.broadcasted_iota(jnp.int32, (384, 256), 0)
    site = lax.broadcasted_iota(jnp.int32, (384, 256), 1)
    chosen = lane_in == (site // EDGE + 1) * span + site % EDGE + 1
    product = jnp.dot(
        plane_flags[...],
        jnp.where(chosen, 1.0, 0.0).astype(jnp.bfloat16),
        preferred_element_type=jnp.float32,
    )
    site_flags[0:128, :] = product[:, :128]
    site_flags[128:256, :] = product[:, 128:]
    for s in range(SLOTS):
        live = s < counts[0]
        for y in range(2):
            piece = site_flags[pl.ds(128 * y + s, EDGE, stride=8), :]
            is_fluid = (piece == 1.0) & live
            row = (FLAG0 + s) * 32 + y * EDGE
            cells[row : row + EDGE, :] = jnp.where(is_fluid, 1.0, 0.0)

    for s in range(SLOTS):
        for x in range(EDGE):
            for y in range(2):
                tile = 2 * x + y
                for p, size in ((0, 8), (8, 8), (16, 3)):
                    row = (s * POPS + p) * 32 + y * EDGE + x
                    cells[pl.ds(row, size, stride=32), :] = pops[
                        s, p : p + size, 128 * tile : 128 * tile + 128
                    ]

    for y in range(2):
        for k in range(3):
            out = (y * 3 + k) * PLANES
            up_msg[out : out + PLANES, :] = cells[pl.ds(y * EDGE + 13 + k, PLANES, stride=32), :]
            down_msg[out : out + PLANES, :] = cells[pl.ds(y * EDGE + k, PLANES, stride=32), :]

    curve, cross = where[0], where[1]
    leaving = jnp.maximum(moves[(curve * cross_size + cross) * 3], 0)
    low = lanes_iota() < 64
    for p in range(POPS):
        for v in range(2):
            base = leaving * (POPS * 32) + p * 32 + v * 8
            first = cells[aligned(base), :]
            second = cells[aligned(base + EDGE), :]
            outer = jnp.where(low, first, second)
            row = p * EDGE + v * 8
            up_msg[STRIP + row : STRIP + row + 8, :] = outer
            down_msg[STRIP + row : STRIP + row + 8, :] = outer
            inner_msg[row : row + 8, :] = jnp.where(low, second, first)
    for s in range(SLOTS):

        @pl.when(leaving == s)
        def _():
            for y in range(2):
                for k in range(3):
                    out = (y * 3 + k) * GROUP
                    row = s * POPS * 32 + y * EDGE + k
                    up2_msg[out : out + POPS, :] = cells[pl.ds(row + 13, POPS, stride=32), :]
                    down2_msg[out : out + POPS, :] = cells[pl.ds(row, POPS, stride=32), :]


def own_strip(cells, slot, y, x):
    return cells[pl.ds(slot * POPS * 32 + y * EDGE + x, POPS, stride=32), :]


def edge_kernel(
    curve_size,
    cross_size,
    moves,
    where,
    cells,
    low_msg,
    high_msg,
    low2_msg,
    high2_msg,
    north_msg,
    south_msg,
    outer,
):
    from_low, from_high, low_low, low_me, high_high, high_me, leaving = move_slots(
        moves, where, curve_size, cross_size
    )
    low = lanes_iota() < 64
    for q in range(PLANES):
        for v in range(2):
            first = cells[q * 32 + v * 8 : q * 32 + v * 8 + 8, :]
            second = cells[q * 32 + EDGE + v * 8 : q * 32 + EDGE + v * 8 + 8, :]
            outer[q * GROUP + v * 8 : q * GROUP + v * 8 + 8, :] = jnp.where(low, first, second)

    def both(first, second):
        lane = lax.broadcasted_iota(jnp.int32, first.shape, 1)
        return jnp.where(lane < 64, first, second)

    for msg, row0 in ((high_msg, 16), (low_msg, 21)):
        for k in range(3):
            outer[pl.ds(row0 + k, PLANES, stride=GROUP), :] = both(
                msg[k * PLANES : (k + 1) * PLANES, :],
                msg[(3 + k) * PLANES : (4 + k) * PLANES, :],
            )
    for slot, msg in ((from_low, low_msg), (from_high, high_msg)):

        @pl.when(slot >= 0)
        def _():
            for p in range(POPS):
                for v in range(2):
                    row = STRIP + p * EDGE + v * 8
                    base = slot * (POPS * GROUP) + p * GROUP + v * 8
                    outer[aligned(base), :] = msg[row : row + 8, :]

    for s in range(SLOTS):
        for slot, msg, row0 in ((low_low, low2_msg, 21), (high_high, high2_msg, 16)):

            @pl.when(slot == s)
            def _():
                for k in range(3):
                    outer[pl.ds(s * POPS * GROUP + row0 + k, POPS, stride=GROUP), :] = both(
                        msg[k * GROUP : k * GROUP + POPS, :],
                        msg[(3 + k) * GROUP : (3 + k) * GROUP + POPS, :],
                    )

        for mine in range(SLOTS):
            for slot, x0, row0 in ((low_me, 13, 21), (high_me, 0, 16)):

                @pl.when((slot == s) & (leaving == mine))
                def _():
                    for k in range(3):
                        outer[pl.ds(s * POPS * GROUP + row0 + k, POPS, stride=GROUP), :] = both(
                            own_strip(cells, mine, 0, x0 + k), own_strip(cells, mine, 1, x0 + k)
                        )

    for pair in range(PAIRS):
        for v in range(3):
            row = 2 * pair * GROUP + v * 8
            first = outer[row : row + 8, :]
            second = pltpu.roll(outer[row + GROUP : row + GROUP + 8, :], 64, axis=1)
            out = pair * GROUP + v * 8
            north_msg[out : out + 8, :] = jnp.where(low, second, first)
            south_msg[out : out + 8, :] = jnp.where(low, first, second)


def collided(h, is_fluid):
    shear = 1.0 / 0.6
    rest = h[0]
    sx, dx = h[1] + h[2], h[1] - h[2]
    sy, dy = h[3] + h[4], h[3] - h[4]
    sz, dz = h[5] + h[6], h[5] - h[6]
    s7, d7 = h[7] + h[8], h[7] - h[8]
    s9, d9 = h[9] + h[10], h[9] - h[10]
    s11, d11 = h[11] + h[12], h[11] - h[12]
    s13, d13 = h[13] + h[14], h[13] - h[14]
    s15, d15 = h[15] + h[16], h[15] - h[16]
    s17, d17 = h[17] + h[18], h[17] - h[18]
    txy, txz, tyz = s7 + s9, s11 + s13, s15 + s17
    pxy, pxz, pyz = s7 - s9, s11 - s13, s15 - s17
    ax, bx = d7 + d9, d11 + d13
    ay, by = d7 - d9, d15 + d17
    az, bz = d11 - d13, d15 - d17
    axes = sx + sy + sz
    diags = txy + txz + tyz
    rho = rest * (1.0 / 3.0) + axes * (1.0 / 18.0) + diags * (1.0 / 36.0)
    fx, fy, fz = ax + bx, ay + by, az + bz
    jx = dx * (1.0 / 18.0) + fx * (1.0 / 36.0)
    jy = dy * (1.0 / 18.0) + fy * (1.0 / 36.0)
    jz = dz * (1.0 / 18.0) + fz * (1.0 / 36.0)
    inverse = 1.0 / jnp.where(is_fluid, rho, 1.0)
    ux, uy, uz = jx * inverse, jy * inverse, jz * inverse
    qxx, qyy, qzz = jx * ux, jy * uy, jz * uz
    total = qxx + qyy + qzz

    energy = -10.0 * rest - axes * (11.0 / 18.0) + diags * (8.0 / 36.0)
    energy = (energy + 11.0 * rho - 19.0 * total) * (1.19 / 2394.0)
    square = 4.0 * rest - axes * (4.0 / 18.0) + diags * (1.0 / 36.0)
    square = (square - 3.0 * rho + 5.5 * total) * (1.4 / 252.0)
    axis_x = (3.0 * sx - axes) * (1.0 / 18.0)
    diag_x = (diags - 3.0 * tyz) * (1.0 / 36.0)
    want_x = 3.0 * qxx - total
    stress_x = (axis_x + diag_x - want_x) * (shear / 36.0)
    third_x = (diag_x - 2.0 * axis_x + 0.5 * want_x) * (1.4 / 72.0)
    axis_w = (sy - sz) * (1.0 / 18.0)
    diag_w = (txy - txz) * (1.0 / 36.0)
    want_w = qyy - qzz
    stress_w = (axis_w + diag_w - want_w) * (shear / 12.0)
    third_w = (diag_w - 2.0 * axis_w + 0.5 * want_w) * (1.4 / 24.0)

    rest_out = rest - 3.0 * (12.0 * square - 30.0 * energy)
    common = -18.0 * (11.0 * energy + 4.0 * square)
    along_x = 18.0 * (stress_x - 2.0 * third_x)
    along_w = 18.0 * (stress_w - 2.0 * third_w)
    ex = common + 2.0 * along_x
    ey = common - along_x + along_w
    ez = common - along_x - along_w
    common = 36.0 * (8.0 * energy + square)
    across_x = 36.0 * (stress_x + third_x)
    across_w = 36.0 * (stress_w + third_w)
    exy = common + across_x + across_w
    exz = common + across_x - across_w
    eyz = common - 2.0 * across_x
    cxy = shear * (0.25 * pxy - 9.0 * jx * uy)
    cxz = shear * (0.25 * pxz - 9.0 * jx * uz)
    cyz = shear * (0.25 * pyz - 9.0 * jy * uz)

    def flux(d, f, j):
        return (f * (1.0 / 36.0) - d * (4.0 / 18.0) + j * (2.0 / 3.0)) * (1.2 / 40.0)

    hx, hy, hz = flux(dx, fx, jx), flux(dy, fy, jy), flux(dz, fz, jz)
    mx = (ax - bx) * (1.98 / 8.0)
    my = (by - ay) * (1.98 / 8.0)
    mz = (az - bz) * (1.98 / 8.0)
    hx36, hy36, hz36 = 36.0 * hx, 36.0 * hy, 36.0 * hz
    xy_x, xz_x = hx36 + mx, hx36 - mx
    yz_y, xy_y = hy36 + my, hy36 - my
    xz_z, yz_z = hz36 + mz, hz36 - mz
    ox, oy, oz = -2.0 * hx36, -2.0 * hy36, -2.0 * hz36

    out = [rest_out]

    def pair(i, even, odd):
        out.append(h[i] - (even + odd))
        out.append(h[i + 1] - (even - odd))

    pair(1, ex, ox)
    pair(3, ey, oy)
    pair(5, ez, oz)
    pair(7, exy + cxy, xy_x + xy_y)
    pair(9, exy - cxy, xy_x - xy_y)
    pair(11, exz + cxz, xz_x + xz_z)
    pair(13, exz - cxz, xz_x - xz_z)
    pair(15, eyz + cyz, yz_y + yz_z)
    pair(17, eyz - cyz, yz_y - yz_z)
    return out


def collide_all(h_ref, post_ref, fluid):
    def chunk(s, c):
        base = s * SLOT + c * 8
        is_fluid = fluid[aligned(s * PLANE + c * 8), :] > 0.0
        h = [h_ref[aligned(base + p * PLANE), :] for p in range(POPS)]
        for p, value in enumerate(collided(h, is_fluid)):
            post_ref[aligned(base + p * PLANE), :] = jnp.where(is_fluid, value, jnp.nan)

    @pl.loop(0, SLOTS)
    def _(s):
        @pl.loop(0, PLANE // 8)
        def _(c):
            chunk(s, c)


def stream_all(post_ref, h_ref, fluid, table, groups, vregs):
    lane = lanes_iota()
    row = rows_iota()
    side = {0: -1, 1: 0, 2: 0, 3: 1}

    def one_slot(s):
        own = s * SLOT

        def look(i, j, offset):
            if offset == (0, 0, 0):
                return own
            region = (i + 1) * 3 + j + 1
            return table[(region * SLOTS + s) * 18 + VELOCITY.index(offset) - 1]

        def shifted(pop, group, j, dy, dz):
            cx = VELOCITY[pop][0]

            def rows(start, v):
                return post_ref[aligned(start + pop * PLANE + group * GROUP + v * 8), :]

            inner = look(0, j, (0, dy, dz))
            need_last = vregs == 3
            values = [rows(inner, 0), rows(inner, 1)]
            if need_last:
                if dy == 0 and dz == 0:
                    values.append(rows(inner, 2))
                else:
                    values.append(
                        jnp.where(
                            row < 4,
                            rows(look(1, j, (0, dy, dz)), 2),
                            rows(look(-1, j, (0, dy, dz)), 2),
                        )
                    )
            if cx == 0:
                return values
            turn = 1 if cx > 0 else 7
            rolled = [pltpu.roll(value, turn, axis=0) for value in values]
            if cx > 0:
                before = pltpu.roll(rows(look(0, j, (-1, dy, dz)), 2), 1, axis=0)
                result = [
                    jnp.where(row == 0, before, rolled[0]),
                    jnp.where(row == 0, rolled[0], rolled[1]),
                ]
                if need_last:
                    edge = pltpu.roll(rows(look(1, j, (-1, dy, dz)), 1), 1, axis=0)
                    result.append(jnp.where(row == 0, edge, rolled[2]))
                return result
            after = pltpu.roll(rows(look(0, j, (1, dy, dz)), 2), 7, axis=0)
            result = [
                jnp.where(row == 7, rolled[1], rolled[0]),
                jnp.where(row == 7, after, rolled[1]),
            ]
            if need_last:
                edge = pltpu.roll(rows(look(-1, j, (1, dy, dz)), 0), 7, axis=0)
                result.append(jnp.where(row == 7, edge, rolled[2]))
            return result

        for pop in range(POPS):
            cx, cy, cz = VELOCITY[pop]
            kept = {}

            def source(group, j, dy, dz):
                key = (group, j, dy, dz)
                if key not in kept:
                    kept[key] = shifted(pop, group, j, dy, dz)
                return kept[key]

            def along_y(group, dz):
                j = side[group]
                values = source(group, j, 0, dz)
                other = group - cy
                if cy == 0 or other < 0 or other > 3:
                    return values
                dy = 0 if side[other] == j else -cy
                carried = source(other, j, dy, dz)
                mask = lane >= 112 if cy > 0 else lane < 16
                return [jnp.where(mask, b, a) for a, b in zip(values, carried)]

            for group in groups:
                values = along_y(group, 0)
                turn = (16 * cy + cz) % 128
                if turn:
                    values = [pltpu.roll(value, turn, axis=1) for value in values]
                if cz:
                    turn = (16 * cy - 15 * cz) % 128
                    wrapped = [pltpu.roll(value, turn, axis=1) for value in along_y(group, -cz)]
                    mask = lane % 16 == (0 if cz > 0 else 15)
                    values = [jnp.where(mask, b, a) for a, b in zip(values, wrapped)]
                for v, value in enumerate(values[:vregs]):
                    place = group * GROUP + v * 8
                    if pop:
                        back = post_ref[aligned(own + OPPOSITE[pop] * PLANE + place), :]
                        value = jnp.where(value != value, back, value)
                    is_fluid = fluid[aligned(s * PLANE + place), :] > 0.0
                    h_ref[aligned(own + pop * PLANE + place), :] = jnp.where(is_fluid, value, 0.0)

    @pl.loop(0, SLOTS)
    def _(s):
        one_slot(s)


def steps_kernel(
    curve_size,
    cross_size,
    moves,
    where,
    table,
    cells,
    low_msg,
    high_msg,
    low2_msg,
    high2_msg,
    low_inner,
    high_inner,
    south_msg,
    north_msg,
    out,
    h_ref,
    post_ref,
    fluid,
):
    from_low, from_high, low_low, low_me, high_high, high_me, leaving = move_slots(
        moves, where, curve_size, cross_size
    )
    low = lanes_iota() < 64
    fluid[...] = jnp.zeros_like(fluid)
    post_ref[SLOTS * SLOT :, :] = jnp.full((SLOT, 128), jnp.nan, jnp.float32)

    def home(q):
        if q < FLAG0:
            return h_ref, q * PLANE
        return fluid, (q - FLAG0) * PLANE

    for q in range(PLANES):
        ref, base = home(q)
        for y in range(2):
            start = base + (1 + y) * GROUP
            ref[start : start + EDGE, :] = cells[q * 32 + y * EDGE : q * 32 + (y + 1) * EDGE, :]
    for slot, msg, inner in (
        (from_low, low_msg, low_inner),
        (from_high, high_msg, high_inner),
    ):

        @pl.when(slot >= 0)
        def _():
            for p in range(POPS):
                for v in range(2):
                    row = p * EDGE + v * 8
                    outside = msg[STRIP + row : STRIP + row + 8, :]
                    inside = inner[row : row + 8, :]
                    start = slot * SLOT + p * PLANE + GROUP + v * 8
                    h_ref[aligned(start), :] = jnp.where(low, outside, inside)
                    h_ref[aligned(start + GROUP), :] = jnp.where(low, inside, outside)

    for msg, row0 in ((high_msg, 16), (low_msg, 21)):
        for y in range(2):
            for k in range(3):
                row = (1 + y) * GROUP + row0 + k
                source = (y * 3 + k) * PLANES
                h_ref[pl.ds(row, FLAG0, stride=PLANE), :] = msg[source : source + FLAG0, :]
                fluid[pl.ds(row, SLOTS, stride=PLANE), :] = msg[source + FLAG0 : source + PLANES, :]
    for s in range(SLOTS):
        for slot, msg, row0 in ((low_low, low2_msg, 21), (high_high, high2_msg, 16)):

            @pl.when(slot == s)
            def _():
                for y in range(2):
                    for k in range(3):
                        row = s * SLOT + (1 + y) * GROUP + row0 + k
                        source = (y * 3 + k) * GROUP
                        h_ref[pl.ds(row, POPS, stride=PLANE), :] = msg[source : source + POPS, :]

        for mine in range(SLOTS):
            for slot, x0, row0 in ((low_me, 13, 21), (high_me, 0, 16)):

                @pl.when((slot == s) & (leaving == mine))
                def _():
                    for y in range(2):
                        for k in range(3):
                            row = s * SLOT + (1 + y) * GROUP + row0 + k
                            h_ref[pl.ds(row, POPS, stride=PLANE), :] = own_strip(
                                cells, mine, y, x0 + k
                            )

    for msg, group in ((south_msg, 0), (north_msg, 3)):
        for pair in range(PAIRS):
            for v in range(3):
                value = msg[pair * GROUP + v * 8 : pair * GROUP + v * 8 + 8, :]
                ref, base = home(2 * pair)
                row = base + group * GROUP + v * 8
                ref[row : row + 8, :] = value
                ref, base = home(2 * pair + 1)
                row = base + group * GROUP + v * 8
                ref[row : row + 8, :] = pltpu.roll(value, 64, axis=1)

    for step in range(STEPS):
        collide_all(h_ref, post_ref, fluid)
        if step < STEPS - 1:
            stream_all(post_ref, h_ref, fluid, table, (0, 1, 2, 3), 3)
        else:
            stream_all(post_ref, h_ref, fluid, table, (1, 2), 2)

    for s in range(SLOTS):
        for x in range(EDGE):
            for y in range(2):
                tile = 2 * x + y
                for p, size in ((0, 8), (8, 8), (16, 3)):
                    row = s * SLOT + p * PLANE + (1 + y) * GROUP + x
                    out[s, p : p + size, 128 * tile : 128 * tile + 128] = h_ref[
                        pl.ds(row, size, stride=PLANE), :
                    ]


def shifted_from(value, axis, step):
    count = lax.axis_size(axis)
    pairs = [(i, i + step) for i in range(count) if 0 <= i + step < count]
    return lax.ppermute(value, axis, pairs)


def rows128(count):
    return jax.ShapeDtypeStruct((count, 128), jnp.float32)


def call(kernel, outs, ins, scratch):
    smem = pl.BlockSpec(memory_space=pltpu.SMEM)
    vmem = pl.BlockSpec(memory_space=pltpu.VMEM)
    return pl.pallas_call(
        kernel,
        out_shape=outs,
        in_specs=[smem if x.ndim == 1 else vmem for x in ins],
        out_specs=jax.tree.map(lambda _: vmem, outs),
        scratch_shapes=scratch,
        compiler_params=pltpu.CompilerParams(vmem_limit_bytes=LIMIT),
    )(*ins)


def per_device(populations, site_flags, neighbours, migrations, counts):
    curve_size = lax.axis_size("curve")
    cross_size = lax.axis_size("cross")
    curve = lax.axis_index("curve")
    cross = lax.axis_index("cross")
    where = jnp.stack([curve, cross]).astype(jnp.int32)
    moves = migrations.reshape(-1)

    everyone = lax.all_gather(neighbours, ("curve", "cross"), tiled=True)
    ranks = [
        jnp.clip(curve + i, 0, curve_size - 1) * cross_size + jnp.clip(cross + j, 0, cross_size - 1)
        for i in (-1, 0, 1)
        for j in (-1, 0, 1)
    ]
    near = jnp.concatenate(
        [lax.dynamic_slice_in_dim(everyone, rank * SLOTS, SLOTS, axis=0) for rank in ranks]
    )
    table = (jnp.where(near >= 0, near % SLOTS, SLOTS) * SLOT).reshape(-1)

    sizes = (curve_size, cross_size)
    cells, up_msg, down_msg, up2_msg, down2_msg, inner_msg = call(
        functools.partial(pack_kernel, *sizes),
        [
            rows128(PLANES * 32),
            rows128(STRIP + HALF),
            rows128(STRIP + HALF),
            rows128(6 * GROUP),
            rows128(6 * GROUP),
            rows128(HALF),
        ],
        (moves, where, counts, populations, site_flags),
        [
            pltpu.VMEM((8, 5888), jnp.float32),
            pltpu.VMEM((128, 384), jnp.bfloat16),
            pltpu.VMEM((256, 128), jnp.float32),
        ],
    )
    low_msg = shifted_from(up_msg, "curve", 1)
    high_msg = shifted_from(down_msg, "curve", -1)
    low2_msg = shifted_from(up2_msg, "curve", 2)
    high2_msg = shifted_from(down2_msg, "curve", -2)
    low_inner = shifted_from(inner_msg, "curve", 1)
    high_inner = shifted_from(inner_msg, "curve", -1)
    north_msg, south_msg = call(
        functools.partial(edge_kernel, *sizes),
        [rows128(PAIRS * GROUP), rows128(PAIRS * GROUP)],
        (moves, where, cells, low_msg, high_msg, low2_msg, high2_msg),
        [pltpu.VMEM((PLANES * GROUP, 128), jnp.float32)],
    )
    from_south = shifted_from(north_msg, "cross", 1)
    from_north = shifted_from(south_msg, "cross", -1)
    return call(
        functools.partial(steps_kernel, *sizes),
        jax.ShapeDtypeStruct(populations.shape, jnp.float32),
        (
            moves,
            where,
            table,
            cells,
            low_msg,
            high_msg,
            low2_msg,
            high2_msg,
            low_inner,
            high_inner,
            from_south,
            from_north,
        ),
        [
            pltpu.VMEM((SLOTS * SLOT, 128), jnp.float32),
            pltpu.VMEM(((SLOTS + 1) * SLOT, 128), jnp.float32),
            pltpu.VMEM((SLOTS * PLANE, 128), jnp.float32),
        ],
    )


def solution(mesh):
    return jax.shard_map(
        per_device,
        mesh=mesh,
        in_specs=(
            P(("curve", "cross"), None, None),
            P(("curve", "cross"), None),
            P(("curve", "cross"), None),
            P(),
            P(("curve", "cross")),
        ),
        out_specs=P(("curve", "cross"), None, None),
        check_vma=False,
    )
```

profile of v0, /device:TPU:1, one launch (start us, length us, event | category | flops | bytes accessed | tf_op | source)
XLA Modules:
  0.0 88.4 jit_solution(552424969138649653)
XLA Ops:
  0.0 0.0 copy-start.2
  0.7 0.8 copy.8
  1.4 0.1 reshape.9.moves
  1.5 0.1 pad_add_fusion.where
  1.6 0.0 copy-start
  1.6 1.3 %copy-done = f32[3,19,4096]{2,1,0:T(8,128)S(1)} copy-done((f32[3,19,4096]{2,1,0:T(8,128)S(1)}, f32[3,19,4096]{2,1,0:T(8,128)}, u32[]{:S(2)}) %copy-start) | copy-done | bytes 933912
  2.9 0.0 copy-start.1
  2.9 0.9 %copy-done.1 = s32[3,5832]{1,0:T(4,128)S(1)} copy-done((s32[3,5832]{1,0:T(4,128)S(1)}, s32[3,5832]{1,0:T(4,128)}, u32[]{:S(2)}) %copy-start.1) | copy-done | bytes 70008
  3.8 1.8 %shard_map.55 = (f32[1920,128]{1,0:T(8,128)S(1)}, f32[664,128]{1,0:T(8,128)S(1)}, f32[664,128]{1,0:T(8,128)S(1)}, f32[144,128]{1,0:T(8,128)S(1)}, f32[144,128]{1,0:T(8,128)S(1)}, /*index=5*/f32[304,128]{1,0:T(8,128)S(1)}) custom-call(s32[96]{0:T(128)S(1)} %reshape.9.moves, s32[2]{0:T(128)S(1)} %pad_add_fusion.where, s32[1]{0:T(128)S(6)} %copy.9.counts, ...), custom_call_target="tpu_custom_call" | custom-call | tf_op jit(solution)/shard_map/pallas_call | solution.py:582
  5.6 4.0 %collective-permute-start.2 = (f32[144,128]{1,0:T(8,128)S(1)}, f32[144,128]{1,0:T(8,128)S(1)}, u32[]{:S(2)}, u32[]{:S(2)}) collective-permute-start(f32[144,128]{1,0:T(8,128)S(1)} %get-tuple-element.16), channel_id=1, source_target_pairs={{0,8},{4,12},{8,16},{12,20},{16,24},{20,28},{1,9},{5,13},{9,17},{1... | collective-permute-start | bytes 221192 | tf_op jit(solution)/shard_map/ppermute | solution.py:572
  9.6 1.3 %collective-permute-start.3 = (f32[144,128]{1,0:T(8,128)S(1)}, f32[144,128]{1,0:T(8,128)S(1)}, u32[]{:S(2)}, u32[]{:S(2)}) collective-permute-start(f32[144,128]{1,0:T(8,128)S(1)} %get-tuple-element.17), channel_id=1, source_target_pairs={{8,0},{12,4},{16,8},{20,12},{24,16},{28,20},{9,1},{13,5},{17,9},{2... | collective-permute-start | bytes 221192 | tf_op jit(solution)/shard_map/ppermute | solution.py:572
  10.9 1.3 %collective-permute-start.5 = (f32[304,128]{1,0:T(8,128)S(1)}, f32[304,128]{1,0:T(8,128)S(1)}, u32[]{:S(2)}, u32[]{:S(2)}) collective-permute-start(f32[304,128]{1,0:T(8,128)S(1)} %get-tuple-element.18), channel_id=1, source_target_pairs={{4,0},{8,4},{12,8},{16,12},{20,16},{24,20},{28,24},{5,1},{9,5},{13... | collective-permute-start | bytes 466952 | tf_op jit(solution)/shard_map/ppermute | solution.py:572
  12.2 4.0 %collective-permute-start = (f32[664,128]{1,0:T(8,128)S(1)}, f32[664,128]{1,0:T(8,128)S(1)}, u32[]{:S(2)}, u32[]{:S(2)}) collective-permute-start(f32[664,128]{1,0:T(8,128)S(1)} %get-tuple-element.14), channel_id=1, source_target_pairs={{0,4},{4,8},{8,12},{12,16},{16,20},{20,24},{24,28},{1,5},{5,9},{9,... | collective-permute-start | bytes 1019912 | tf_op jit(solution)/shard_map/ppermute | solution.py:572
  16.2 1.3 %collective-permute-start.1 = (f32[664,128]{1,0:T(8,128)S(1)}, f32[664,128]{1,0:T(8,128)S(1)}, u32[]{:S(2)}, u32[]{:S(2)}) collective-permute-start(f32[664,128]{1,0:T(8,128)S(1)} %get-tuple-element.15), channel_id=1, source_target_pairs={{4,0},{8,4},{12,8},{16,12},{20,16},{24,20},{28,24},{5,1},{9,5},{13... | collective-permute-start | bytes 1019912 | tf_op jit(solution)/shard_map/ppermute | solution.py:572
  17.6 0.0 copy-done.2
  17.6 45.5 %all-gather = s32[32,3,18]{2,1,0:T(4,128)S(1)} all-gather(s32[1,3,18]{2,1,0:T(4,128)S(1)} %bitcast.3), channel_id=1, replica_groups=mesh['curve'=8,'cross'=4] {'curve','cross'}, dimensions={0}, use_global_device_ids=true | all-gather | bytes 7128 | tf_op jit(solution)/shard_map/all_gather | solution.py:600
  63.1 0.1 constant_dynamic-slice_fusion
  63.2 0.2 concatenate.3
  63.4 0.1 ge.14
  63.5 0.0 collective-permute-done.2.low2_msg
  63.5 1.3 %collective-permute-start.4 = (f32[304,128]{1,0:T(8,128)S(1)}, f32[304,128]{1,0:T(8,128)S(1)}, u32[]{:S(2)}, u32[]{:S(2)}) collective-permute-start(f32[304,128]{1,0:T(8,128)S(1)} %get-tuple-element.18), channel_id=1, source_target_pairs={{0,4},{4,8},{8,12},{12,16},{16,20},{20,24},{24,28},{1,5},{5,9},{9,... | collective-permute-start | bytes 466952 | tf_op jit(solution)/shard_map/ppermute | solution.py:572
  64.8 0.0 collective-permute-done.3.high2_msg
  64.8 0.0 collective-permute-done.low_msg
  64.8 0.0 collective-permute-done.1.high_msg
  64.9 1.7 %shard_map.56 = (f32[720,128]{1,0:T(8,128)}, f32[720,128]{1,0:T(8,128)S(1)}) custom-call(s32[96]{0:T(128)S(1)} %reshape.9.moves, s32[2]{0:T(128)S(1)} %pad_add_fusion.where, f32[1920,128]{1,0:T(8,128)S(1)} %get-tuple-element.13.cells, f32[664,128]{1,0:T(8,128)S(1)} %collective-permute-done.low_msg, f32[664,128]{1,0:T(8,128)S(1)} %collective-permute-done.1.high_msg, ...), custom_call_target="tpu_custom_call" | custom-call | tf_op jit(solution)/shard_map/pallas_call | solution.py:582
  66.5 1.9 %collective-permute-start.6 = (f32[720,128]{1,0:T(8,128)}, f32[720,128]{1,0:T(8,128)S(1)}, u32[]{:S(2)}, u32[]{:S(2)}) collective-permute-start(f32[720,128]{1,0:T(8,128)} %get-tuple-element.19), channel_id=1, source_target_pairs={{0,1},{1,2},{2,3},{4,5},{5,6},{6,7},{8,9},{9,10},{10,11},{12,13},{... | collective-permute-start | bytes 1105928 | tf_op jit(solution)/shard_map/ppermute | solution.py:572
  68.4 2.4 %collective-permute-start.7 = (f32[720,128]{1,0:T(8,128)S(1)}, f32[720,128]{1,0:T(8,128)S(1)}, u32[]{:S(2)}, u32[]{:S(2)}) collective-permute-start(f32[720,128]{1,0:T(8,128)S(1)} %get-tuple-element.20), channel_id=1, source_target_pairs={{1,0},{2,1},{3,2},{5,4},{6,5},{7,6},{9,8},{10,9},{11,10},{13,12},{... | collective-permute-start | bytes 1105928 | tf_op jit(solution)/shard_map/ppermute | solution.py:572
  70.9 0.1 rem.16
  71.0 0.0 collective-permute-done.5.high_inner
  71.0 0.0 collective-permute-done.4.low_inner
  71.0 2.2 %collective-permute-done.6.south_msg = f32[720,128]{1,0:T(8,128)S(1)} collective-permute-done((f32[720,128]{1,0:T(8,128)}, f32[720,128]{1,0:T(8,128)S(1)}, u32[]{:S(2)}, u32[]{:S(2)}) %collective-permute-start.6) | collective-permute-done | bytes 368672 | tf_op jit(solution)/shard_map/ppermute | solution.py:572
  73.2 4.1 %collective-permute-done.7.north_msg = f32[720,128]{1,0:T(8,128)S(1)} collective-permute-done((f32[720,128]{1,0:T(8,128)S(1)}, f32[720,128]{1,0:T(8,128)S(1)}, u32[]{:S(2)}, u32[]{:S(2)}) %collective-permute-start.7) | collective-permute-done | bytes 368672 | tf_op jit(solution)/shard_map/ppermute | solution.py:572
  77.3 11.2 %shard_map.57 = f32[3,19,4096]{2,1,0:T(8,128)} custom-call(s32[96]{0:T(128)S(1)} %reshape.9.moves, s32[2]{0:T(128)S(1)} %pad_add_fusion.where, s32[486]{0:T(512)S(1)} %fusion.1.table, f32[1920,128]{1,0:T(8,128)S(1)} %get-tuple-element.13.cells, f32[664,128]{1,0:T(8,128)S(1)} %collective-permute-done.low_msg, f32[664,128]{1,0:T(8,128)S(1)} %collective-permute-done.1.high_msg, ...), custom_call_target="tpu_custom_call" | custom-call | tf_op jit(solution)/shard_map/pallas_call | solution.py:582
  (4 shorter events, 0.1 us)
Async XLA Ops:
  0.0 17.6 %copy-start.2 = (s32[3,18]{1,0:T(4,128)S(1)}, s32[3,18]{1,0:T(4,128)}, u32[]{:S(2)}) copy-start(s32[3,18]{1,0:T(4,128)} %param.7) | copy-start | bytes 652
  1.6 1.3 %copy-start = (f32[3,19,4096]{2,1,0:T(8,128)S(1)}, f32[3,19,4096]{2,1,0:T(8,128)}, u32[]{:S(2)}) copy-start(f32[3,19,4096]{2,1,0:T(8,128)} %pops.1) | copy-start | bytes 2801668
  2.9 0.9 %copy-start.1 = (s32[3,5832]{1,0:T(4,128)S(1)}, s32[3,5832]{1,0:T(4,128)}, u32[]{:S(2)}) copy-start(s32[3,5832]{1,0:T(4,128)} %flags.1) | copy-start | bytes 209956
  5.6 57.9 %collective-permute-start.2 = (f32[144,128]{1,0:T(8,128)S(1)}, f32[144,128]{1,0:T(8,128)S(1)}, u32[]{:S(2)}, u32[]{:S(2)}) collective-permute-start(f32[144,128]{1,0:T(8,128)S(1)} %get-tuple-element.16), channel_id=1, source_target_pairs={{0,8},{4,12},{8,16},{12,20},{16,24},{20,28},{1,9},{5,13},{9,17},{1... | collective-permute-start | bytes 221192 | tf_op jit(solution)/shard_map/ppermute | solution.py:572
  9.6 55.2 %collective-permute-start.3 = (f32[144,128]{1,0:T(8,128)S(1)}, f32[144,128]{1,0:T(8,128)S(1)}, u32[]{:S(2)}, u32[]{:S(2)}) collective-permute-start(f32[144,128]{1,0:T(8,128)S(1)} %get-tuple-element.17), channel_id=1, source_target_pairs={{8,0},{12,4},{16,8},{20,12},{24,16},{28,20},{9,1},{13,5},{17,9},{2... | collective-permute-start | bytes 221192 | tf_op jit(solution)/shard_map/ppermute | solution.py:572
  10.9 60.1 %collective-permute-start.5 = (f32[304,128]{1,0:T(8,128)S(1)}, f32[304,128]{1,0:T(8,128)S(1)}, u32[]{:S(2)}, u32[]{:S(2)}) collective-permute-start(f32[304,128]{1,0:T(8,128)S(1)} %get-tuple-element.18), channel_id=1, source_target_pairs={{4,0},{8,4},{12,8},{16,12},{20,16},{24,20},{28,24},{5,1},{9,5},{13... | collective-permute-start | bytes 466952 | tf_op jit(solution)/shard_map/ppermute | solution.py:572
  12.2 52.6 %collective-permute-start = (f32[664,128]{1,0:T(8,128)S(1)}, f32[664,128]{1,0:T(8,128)S(1)}, u32[]{:S(2)}, u32[]{:S(2)}) collective-permute-start(f32[664,128]{1,0:T(8,128)S(1)} %get-tuple-element.14), channel_id=1, source_target_pairs={{0,4},{4,8},{8,12},{12,16},{16,20},{20,24},{24,28},{1,5},{5,9},{9,... | collective-permute-start | bytes 1019912 | tf_op jit(solution)/shard_map/ppermute | solution.py:572
  16.2 48.6 %collective-permute-start.1 = (f32[664,128]{1,0:T(8,128)S(1)}, f32[664,128]{1,0:T(8,128)S(1)}, u32[]{:S(2)}, u32[]{:S(2)}) collective-permute-start(f32[664,128]{1,0:T(8,128)S(1)} %get-tuple-element.15), channel_id=1, source_target_pairs={{4,0},{8,4},{12,8},{16,12},{20,16},{24,20},{28,24},{5,1},{9,5},{13... | collective-permute-start | bytes 1019912 | tf_op jit(solution)/shard_map/ppermute | solution.py:572
  63.5 7.5 %collective-permute-start.4 = (f32[304,128]{1,0:T(8,128)S(1)}, f32[304,128]{1,0:T(8,128)S(1)}, u32[]{:S(2)}, u32[]{:S(2)}) collective-permute-start(f32[304,128]{1,0:T(8,128)S(1)} %get-tuple-element.18), channel_id=1, source_target_pairs={{0,4},{4,8},{8,12},{12,16},{16,20},{20,24},{24,28},{1,5},{5,9},{9,... | collective-permute-start | bytes 466952 | tf_op jit(solution)/shard_map/ppermute | solution.py:572
  66.5 6.7 %collective-permute-start.6 = (f32[720,128]{1,0:T(8,128)}, f32[720,128]{1,0:T(8,128)S(1)}, u32[]{:S(2)}, u32[]{:S(2)}) collective-permute-start(f32[720,128]{1,0:T(8,128)} %get-tuple-element.19), channel_id=1, source_target_pairs={{0,1},{1,2},{2,3},{4,5},{5,6},{6,7},{8,9},{9,10},{10,11},{12,13},{... | collective-permute-start | bytes 1105928 | tf_op jit(solution)/shard_map/ppermute | solution.py:572
  68.4 8.8 %collective-permute-start.7 = (f32[720,128]{1,0:T(8,128)S(1)}, f32[720,128]{1,0:T(8,128)S(1)}, u32[]{:S(2)}, u32[]{:S(2)}) collective-permute-start(f32[720,128]{1,0:T(8,128)S(1)} %get-tuple-element.20), channel_id=1, source_target_pairs={{1,0},{2,1},{3,2},{5,4},{6,5},{7,6},{9,8},{10,9},{11,10},{13,12},{... | collective-permute-start | bytes 1105928 | tf_op jit(solution)/shard_map/ppermute | solution.py:572
where the time goes:
time: 88.9 us; the launch traced here: 88.4 us
  blocking collectives  45.5 us (51%)
  starting transfers between devices  17.6 us (20%)
  Pallas kernels  14.6 us (16%)
  waiting for transfers between devices  6.26 us (7%)
  local copies, waits for them, and re-layouts  3.54 us (4%)
    all_gather x1, blocking collectives, per_device(): everyone = lax.all_gather(neighbours, ('curve', 'cross'), tiled=True)  45.5 us
    ppermute x8, starting transfers between devices, shifted_from(): return lax.ppermute(value, axis, pairs)  17.6 us
    pallas_call x3, Pallas kernels, call(): pl.pallas_call(kernel, out_shape=outs, in_specs=[smem if x.ndim == 1 else...  14.6 us
    ppermute x8, waiting for transfers between devices, shifted_from(): return lax.ppermute(value, axis, pairs)  6.26 us
    unnamed x8, local copies, waits for them, and re-layouts  2.95 us
  transfers between devices with their start and end apart: 8, of which 2 were waited for; matrix products, arithmetic and copies ran while one was open for 1% of the time, Pallas kernels for 2%

commit v1 on v0

--- a/solution.py
+++ b/solution.py
@@ -20,6 +20,8 @@
 STRIP = 6 * PLANES
 HALF = POPS * EDGE
 PAIRS = PLANES // 2
+TABLE = STRIP + HALF
+EDGE_TABLE = PAIRS * GROUP
 LIMIT = 48 * 1024 * 1024
 
 VELOCITY = [
@@ -65,8 +67,8 @@
         inside = (source >= 0) & (source < curve_size) & (target >= 0) & (target < curve_size)
         row = jnp.clip(source, 0, curve_size - 1) * cross_size + cross
         rank = target * cross_size + cross
-        hit = inside & (moves[row * 3] >= 0) & (moves[row * 3 + 1] == rank)
-        return jnp.where(hit, moves[row * 3 + 2], -1)
+        hit = inside & (moves[0, row] >= 0) & (moves[1, row] == rank)
+        return jnp.where(hit, moves[2, row], -1)
 
     here = curve * cross_size + cross
     return (
@@ -76,7 +78,7 @@
         landed(curve, curve - 1),
         landed(curve + 2, curve + 1),
         landed(curve, curve + 1),
-        jnp.maximum(moves[here * 3], 0),
+        jnp.maximum(moves[0, here], 0),
     )
 
 
@@ -86,19 +88,40 @@
     moves,
     where,
     counts,
-    pops,
-    flags,
+    pops_hbm,
+    flags_hbm,
+    neighbours,
     cells,
     up_msg,
     down_msg,
     up2_msg,
     down2_msg,
     inner_msg,
+    pops,
+    flags,
     wide_flags,
     plane_flags,
     site_flags,
+    near,
+    sems,
 ):
+    flags_copy = pltpu.make_async_copy(flags_hbm, flags, sems.at[SLOTS])
+    flags_copy.start()
+    copies = [
+        pltpu.make_async_copy(pops_hbm.at[s], pops.at[s], sems.at[s]) for s in range(SLOTS)
+    ]
+    for copy in copies:
+        copy.start()
+
+    near[...] = jnp.zeros_like(near)
+    named = neighbours[...]
+    slot = jnp.where(named >= 0, lax.rem(jnp.maximum(named, 0), SLOTS), SLOTS)
+    near[0:SLOTS, 0 : named.shape[1]] = slot.astype(jnp.float32)
+    for ref, row in ((cells, PLANES * 32), (up_msg, TABLE), (down_msg, TABLE)):
+        ref[row : row + 8, :] = near[...]
+
     wide_flags[...] = jnp.zeros_like(wide_flags)
+    flags_copy.wait()
     wide_flags[0:SLOTS, 0 : flags.shape[1]] = flags[...].astype(jnp.float32)
     span = EDGE + 2
     for x in range(EDGE):
@@ -126,6 +149,7 @@
             cells[row : row + EDGE, :] = jnp.where(is_fluid, 1.0, 0.0)
 
     for s in range(SLOTS):
+        copies[s].wait()
         for x in range(EDGE):
             for y in range(2):
                 tile = 2 * x + y
@@ -142,7 +166,7 @@
             down_msg[out : out + PLANES, :] = cells[pl.ds(y * EDGE + k, PLANES, stride=32), :]
 
     curve, cross = where[0], where[1]
-    leaving = jnp.maximum(moves[(curve * cross_size + cross) * 3], 0)
+    leaving = jnp.maximum(moves[0, curve * cross_size + cross], 0)
     low = lanes_iota() < 64
     for p in range(POPS):
         for v in range(2):
@@ -243,6 +267,11 @@
             out = pair * GROUP + v * 8
             north_msg[out : out + 8, :] = jnp.where(low, second, first)
             south_msg[out : out + 8, :] = jnp.where(low, first, second)
+    tables = (low_msg, TABLE), (cells, PLANES * 32), (high_msg, TABLE)
+    for i, (ref, row) in enumerate(tables):
+        out = EDGE_TABLE + 8 * i
+        north_msg[out : out + 8, :] = ref[row : row + 8, :]
+        south_msg[out : out + 8, :] = ref[row : row + 8, :]
 
 
 def collided(h, is_fluid):
@@ -352,7 +381,7 @@
             chunk(s, c)
 
 
-def stream_all(post_ref, h_ref, fluid, table, groups, vregs):
+def stream_all(post_ref, h_ref, fluid, table, groups, vregs, finish=None):
     lane = lanes_iota()
     row = rows_iota()
     side = {0: -1, 1: 0, 2: 0, 3: 1}
@@ -364,7 +393,7 @@
             if offset == (0, 0, 0):
                 return own
             region = (i + 1) * 3 + j + 1
-            return table[(region * SLOTS + s) * 18 + VELOCITY.index(offset) - 1]
+            return table[region * 8 + s, VELOCITY.index(offset) - 1]
 
         def shifted(pop, group, j, dy, dz):
             cx = VELOCITY[pop][0]
@@ -452,6 +481,8 @@
     @pl.loop(0, SLOTS)
     def _(s):
         one_slot(s)
+        if finish is not None:
+            finish(s)
 
 
 def steps_kernel(
@@ -459,7 +490,6 @@
     cross_size,
     moves,
     where,
-    table,
     cells,
     low_msg,
     high_msg,
@@ -469,11 +499,29 @@
     high_inner,
     south_msg,
     north_msg,
-    out,
+    out_hbm,
     h_ref,
     post_ref,
     fluid,
+    out,
+    slots,
+    table,
+    sems,
 ):
+    for i in range(3):
+        for j, (ref, row) in enumerate(
+            (
+                (south_msg, EDGE_TABLE + 8 * i),
+                ((low_msg, TABLE), (cells, PLANES * 32), (high_msg, TABLE))[i],
+                (north_msg, EDGE_TABLE + 8 * i),
+            )
+        ):
+            first = ref[row : row + 8, :].astype(jnp.int32) * SLOT
+            region = 8 * (3 * i + j)
+            slots[region : region + 8, :] = first
+    table_copy = pltpu.make_async_copy(slots, table, sems.at[SLOTS])
+    table_copy.start()
+
     from_low, from_high, low_low, low_me, high_high, high_me, leaving = move_slots(
         moves, where, curve_size, cross_size
     )
@@ -548,22 +596,27 @@
                 row = base + group * GROUP + v * 8
                 ref[row : row + 8, :] = pltpu.roll(value, 64, axis=1)
 
-    for step in range(STEPS):
-        collide_all(h_ref, post_ref, fluid)
-        if step < STEPS - 1:
-            stream_all(post_ref, h_ref, fluid, table, (0, 1, 2, 3), 3)
-        else:
-            stream_all(post_ref, h_ref, fluid, table, (1, 2), 2)
-
-    for s in range(SLOTS):
+    def finish(s):
         for x in range(EDGE):
             for y in range(2):
                 tile = 2 * x + y
                 for p, size in ((0, 8), (8, 8), (16, 3)):
-                    row = s * SLOT + p * PLANE + (1 + y) * GROUP + x
+                    row = s * SLOT + (p * PLANE + (1 + y) * GROUP + x)
                     out[s, p : p + size, 128 * tile : 128 * tile + 128] = h_ref[
                         pl.ds(row, size, stride=PLANE), :
                     ]
+        pltpu.make_async_copy(out.at[s], out_hbm.at[s], sems.at[s]).start()
+
+    for step in range(STEPS):
+        collide_all(h_ref, post_ref, fluid)
+        if step == 0:
+            table_copy.wait()
+        if step < STEPS - 1:
+            stream_all(post_ref, h_ref, fluid, table, (0, 1, 2, 3), 3)
+        else:
+            stream_all(post_ref, h_ref, fluid, table, (1, 2), 2, finish)
+    for s in range(SLOTS):
+        pltpu.make_async_copy(out.at[s], out_hbm.at[s], sems.at[s]).wait()
 
 
 def shifted_from(value, axis, step):
@@ -576,14 +629,17 @@
     return jax.ShapeDtypeStruct((count, 128), jnp.float32)
 
 
-def call(kernel, outs, ins, scratch):
-    smem = pl.BlockSpec(memory_space=pltpu.SMEM)
-    vmem = pl.BlockSpec(memory_space=pltpu.VMEM)
+def call(kernel, in_spaces, out_spaces, outs, ins, scratch):
+    spaces = {
+        "S": pl.BlockSpec(memory_space=pltpu.SMEM),
+        "V": pl.BlockSpec(memory_space=pltpu.VMEM),
+        "H": pl.BlockSpec(memory_space=pltpu.HBM),
+    }
     return pl.pallas_call(
         kernel,
         out_shape=outs,
-        in_specs=[smem if x.ndim == 1 else vmem for x in ins],
-        out_specs=jax.tree.map(lambda _: vmem, outs),
+        in_specs=[spaces[x] for x in in_spaces],
+        out_specs=[spaces[x] for x in out_spaces],
         scratch_shapes=scratch,
         compiler_params=pltpu.CompilerParams(vmem_limit_bytes=LIMIT),
     )(*ins)
@@ -595,35 +651,30 @@
     curve = lax.axis_index("curve")
     cross = lax.axis_index("cross")
     where = jnp.stack([curve, cross]).astype(jnp.int32)
-    moves = migrations.reshape(-1)
-
-    everyone = lax.all_gather(neighbours, ("curve", "cross"), tiled=True)
-    ranks = [
-        jnp.clip(curve + i, 0, curve_size - 1) * cross_size + jnp.clip(cross + j, 0, cross_size - 1)
-        for i in (-1, 0, 1)
-        for j in (-1, 0, 1)
-    ]
-    near = jnp.concatenate(
-        [lax.dynamic_slice_in_dim(everyone, rank * SLOTS, SLOTS, axis=0) for rank in ranks]
-    )
-    table = (jnp.where(near >= 0, near % SLOTS, SLOTS) * SLOT).reshape(-1)
+    moves = migrations.T
 
     sizes = (curve_size, cross_size)
     cells, up_msg, down_msg, up2_msg, down2_msg, inner_msg = call(
         functools.partial(pack_kernel, *sizes),
+        "SSSHHV",
+        "VVVVVV",
         [
-            rows128(PLANES * 32),
-            rows128(STRIP + HALF),
-            rows128(STRIP + HALF),
+            rows128(PLANES * 32 + 8),
+            rows128(STRIP + HALF + 8),
+            rows128(STRIP + HALF + 8),
             rows128(6 * GROUP),
             rows128(6 * GROUP),
             rows128(HALF),
         ],
-        (moves, where, counts, populations, site_flags),
+        (moves, where, counts, populations, site_flags, neighbours),
         [
+            pltpu.VMEM(populations.shape, jnp.float32),
+            pltpu.VMEM(site_flags.shape, jnp.int32),
             pltpu.VMEM((8, 5888), jnp.float32),
             pltpu.VMEM((128, 384), jnp.bfloat16),
             pltpu.VMEM((256, 128), jnp.float32),
+            pltpu.VMEM((8, 128), jnp.float32),
+            pltpu.SemaphoreType.DMA((SLOTS + 1,)),
         ],
     )
     low_msg = shifted_from(up_msg, "curve", 1)
@@ -634,7 +685,9 @@
     high_inner = shifted_from(inner_msg, "curve", -1)
     north_msg, south_msg = call(
         functools.partial(edge_kernel, *sizes),
-        [rows128(PAIRS * GROUP), rows128(PAIRS * GROUP)],
+        "SSVVVVV",
+        "VV",
+        [rows128(PAIRS * GROUP + 24), rows128(PAIRS * GROUP + 24)],
         (moves, where, cells, low_msg, high_msg, low2_msg, high2_msg),
         [pltpu.VMEM((PLANES * GROUP, 128), jnp.float32)],
     )
@@ -642,11 +695,12 @@
     from_north = shifted_from(south_msg, "cross", -1)
     return call(
         functools.partial(steps_kernel, *sizes),
-        jax.ShapeDtypeStruct(populations.shape, jnp.float32),
+        "SSVVVVVVVVV",
+        "H",
+        [jax.ShapeDtypeStruct(populations.shape, jnp.float32)],
         (
             moves,
             where,
-            table,
             cells,
             low_msg,
             high_msg,
@@ -661,8 +715,12 @@
             pltpu.VMEM((SLOTS * SLOT, 128), jnp.float32),
             pltpu.VMEM(((SLOTS + 1) * SLOT, 128), jnp.float32),
             pltpu.VMEM((SLOTS * PLANE, 128), jnp.float32),
+            pltpu.VMEM(populations.shape, jnp.float32),
+            pltpu.VMEM((72, 128), jnp.int32),
+            pltpu.SMEM((72, 128), jnp.int32),
+            pltpu.SemaphoreType.DMA((SLOTS + 1,)),
         ],
-    )
+    )[0]
 
 
 def solution(mesh):

time: 88.9 us -> 55.4 us (0.62)
  the two profiles are of different devices: /device:TPU:1 before, /device:TPU:10 now
where the time goes in v1:
time: 55.4 us; the launch traced here: 55.1 us
  starting transfers between devices  24 us (43%)
  Pallas kernels  14.8 us (27%)
  waiting for transfers between devices  12 us (22%)
  local copies, waits for them, and re-layouts  3.52 us (6%)
  between operations  0.74 us (1%)
    ppermute x8, starting transfers between devices, shifted_from(): return lax.ppermute(value, axis, pairs)  24 us
    pallas_call x3, Pallas kernels, call(): pl.pallas_call(kernel, out_shape=outs, in_specs=[spaces[x] for x in in_sp...  14.8 us
    ppermute x8, waiting for transfers between devices, shifted_from(): return lax.ppermute(value, axis, pairs)  12 us
    unnamed x8, local copies, waits for them, and re-layouts  3.52 us
  transfers between devices with their start and end apart: 8, of which 6 were waited for; matrix products, arithmetic and copies ran while one was open for 0% of the time, Pallas kernels for 0%

profile of v1, /device:TPU:10, one launch (start us, length us, event | category | flops | bytes accessed | tf_op | source)
XLA Modules:
  0.0 55.1 jit_solution(15403204963075807545)
XLA Ops:
  0.7 0.1 pad_add_fusion.where
  0.7 0.0 copy-start
  0.7 1.3 %copy-done = f32[3,19,4096]{2,1,0:T(8,128)S(1)} copy-done((f32[3,19,4096]{2,1,0:T(8,128)S(1)}, f32[3,19,4096]{2,1,0:T(8,128)}, u32[]{:S(2)}) %copy-start) | copy-done | bytes 933912
  2.0 0.0 copy-start.1
  2.0 0.9 %copy-done.1 = s32[3,5832]{1,0:T(4,128)S(1)} copy-done((s32[3,5832]{1,0:T(4,128)S(1)}, s32[3,5832]{1,0:T(4,128)}, u32[]{:S(2)}) %copy-start.1) | copy-done | bytes 70008
  2.9 0.0 copy-start.2
  2.9 0.7 %copy-done.2 = s32[32,3]{0,1:T(4,128)S(1)} copy-done((s32[32,3]{0,1:T(4,128)S(1)}, s32[32,3]{0,1:T(4,128)}, u32[]{:S(2)}) %copy-start.2) | copy-done | bytes 408
  3.6 0.0 copy-start.3
  3.6 0.7 %copy-done.3 = s32[3,18]{1,0:T(4,128)S(1)} copy-done((s32[3,18]{1,0:T(4,128)S(1)}, s32[3,18]{1,0:T(4,128)}, u32[]{:S(2)}) %copy-start.3) | copy-done | bytes 240
  4.3 2.7 %shard_map.55 = (f32[1928,128]{1,0:T(8,128)S(1)}, f32[672,128]{1,0:T(8,128)S(1)}, f32[672,128]{1,0:T(8,128)S(1)}, f32[144,128]{1,0:T(8,128)S(1)}, f32[144,128]{1,0:T(8,128)S(1)}, /*index=5*/f32[304,128]{1,0:T(8,128)S(1)}) custom-call(s32[3,32]{1,0:T(4,128)S(1)} %bitcast.3, s32[2]{0:T(128)S(1)} %pad_add_fusion.where, s32[1]{0:T(128)S(6)} %copy.6.counts, ...), custom_call_target="tpu_custom_call" | custom-call | tf_op jit(solution)/shard_map/pallas_call | solution.py:638
  7.0 3.4 %collective-permute-start = (f32[672,128]{1,0:T(8,128)S(1)}, f32[672,128]{1,0:T(8,128)S(1)}, u32[]{:S(2)}, u32[]{:S(2)}) collective-permute-start(f32[672,128]{1,0:T(8,128)S(1)} %get-tuple-element.14), channel_id=1, source_target_pairs={{0,4},{4,8},{8,12},{12,16},{16,20},{20,24},{24,28},{1,5},{5,9},{9,... | collective-permute-start | bytes 1032200 | tf_op jit(solution)/shard_map/ppermute | solution.py:625
  10.4 3.3 %collective-permute-start.1 = (f32[672,128]{1,0:T(8,128)S(1)}, f32[672,128]{1,0:T(8,128)S(1)}, u32[]{:S(2)}, u32[]{:S(2)}) collective-permute-start(f32[672,128]{1,0:T(8,128)S(1)} %get-tuple-element.15), channel_id=1, source_target_pairs={{4,0},{8,4},{12,8},{16,12},{20,16},{24,20},{28,24},{5,1},{9,5},{13... | collective-permute-start | bytes 1032200 | tf_op jit(solution)/shard_map/ppermute | solution.py:625
  13.7 3.5 %collective-permute-start.2 = (f32[144,128]{1,0:T(8,128)S(1)}, f32[144,128]{1,0:T(8,128)S(1)}, u32[]{:S(2)}, u32[]{:S(2)}) collective-permute-start(f32[144,128]{1,0:T(8,128)S(1)} %get-tuple-element.16), channel_id=1, source_target_pairs={{0,8},{4,12},{8,16},{12,20},{16,24},{20,28},{1,9},{5,13},{9,17},{1... | collective-permute-start | bytes 221192 | tf_op jit(solution)/shard_map/ppermute | solution.py:625
  17.2 2.4 %collective-permute-start.3 = (f32[144,128]{1,0:T(8,128)S(1)}, f32[144,128]{1,0:T(8,128)S(1)}, u32[]{:S(2)}, u32[]{:S(2)}) collective-permute-start(f32[144,128]{1,0:T(8,128)S(1)} %get-tuple-element.17), channel_id=1, source_target_pairs={{8,0},{12,4},{16,8},{20,12},{24,16},{28,20},{9,1},{13,5},{17,9},{2... | collective-permute-start | bytes 221192 | tf_op jit(solution)/shard_map/ppermute | solution.py:625
  19.6 0.4 collective-permute-done.2.low2_msg
  20.0 4.4 %collective-permute-done.3.high2_msg = f32[144,128]{1,0:T(8,128)S(1)} collective-permute-done((f32[144,128]{1,0:T(8,128)S(1)}, f32[144,128]{1,0:T(8,128)S(1)}, u32[]{:S(2)}, u32[]{:S(2)}) %collective-permute-start.3) | collective-permute-done | bytes 73760 | tf_op jit(solution)/shard_map/ppermute | solution.py:625
  24.4 0.7 %collective-permute-done.low_msg = f32[672,128]{1,0:T(8,128)S(1)} collective-permute-done((f32[672,128]{1,0:T(8,128)S(1)}, f32[672,128]{1,0:T(8,128)S(1)}, u32[]{:S(2)}, u32[]{:S(2)}) %collective-permute-start) | collective-permute-done | bytes 344096 | tf_op jit(solution)/shard_map/ppermute | solution.py:625
  25.1 1.9 %collective-permute-done.1.high_msg = f32[672,128]{1,0:T(8,128)S(1)} collective-permute-done((f32[672,128]{1,0:T(8,128)S(1)}, f32[672,128]{1,0:T(8,128)S(1)}, u32[]{:S(2)}, u32[]{:S(2)}) %collective-permute-start.1) | collective-permute-done | bytes 344096 | tf_op jit(solution)/shard_map/ppermute | solution.py:625
  26.9 1.0 %shard_map.56 = (f32[744,128]{1,0:T(8,128)S(1)}, f32[744,128]{1,0:T(8,128)S(1)}) custom-call(s32[3,32]{1,0:T(4,128)S(1)} %bitcast.4, s32[2]{0:T(128)S(1)} %pad_add_fusion.where, f32[1928,128]{1,0:T(8,128)S(1)} %get-tuple-element.13.cells, f32[672,128]{1,0:T(8,128)S(1)} %collective-permute-done.low_msg, f32[672,128]{1,0:T(8,128)S(1)} %collective-permute-done.1.high_msg, ...), custom_call_target="tpu_custom_call" | custom-call | tf_op jit(solution)/shard_map/pallas_call | solution.py:638
  27.9 1.9 %collective-permute-start.6 = (f32[744,128]{1,0:T(8,128)S(1)}, f32[744,128]{1,0:T(8,128)S(1)}, u32[]{:S(2)}, u32[]{:S(2)}) collective-permute-start(f32[744,128]{1,0:T(8,128)S(1)} %get-tuple-element.19), channel_id=1, source_target_pairs={{0,1},{1,2},{2,3},{4,5},{5,6},{6,7},{8,9},{9,10},{10,11},{12,13},{... | collective-permute-start | bytes 1142792 | tf_op jit(solution)/shard_map/ppermute | solution.py:625
  29.9 3.6 %collective-permute-start.7 = (f32[744,128]{1,0:T(8,128)S(1)}, f32[744,128]{1,0:T(8,128)S(1)}, u32[]{:S(2)}, u32[]{:S(2)}) collective-permute-start(f32[744,128]{1,0:T(8,128)S(1)} %get-tuple-element.20), channel_id=1, source_target_pairs={{1,0},{2,1},{3,2},{5,4},{6,5},{7,6},{9,8},{10,9},{11,10},{13,12},{... | collective-permute-start | bytes 1142792 | tf_op jit(solution)/shard_map/ppermute | solution.py:625
  33.5 2.4 %collective-permute-start.5 = (f32[304,128]{1,0:T(8,128)S(1)}, f32[304,128]{1,0:T(8,128)S(1)}, u32[]{:S(2)}, u32[]{:S(2)}) collective-permute-start(f32[304,128]{1,0:T(8,128)S(1)} %get-tuple-element.18), channel_id=1, source_target_pairs={{4,0},{8,4},{12,8},{16,12},{20,16},{24,20},{28,24},{5,1},{9,5},{13... | collective-permute-start | bytes 466952 | tf_op jit(solution)/shard_map/ppermute | solution.py:625
  35.9 3.4 %collective-permute-start.4 = (f32[304,128]{1,0:T(8,128)S(1)}, f32[304,128]{1,0:T(8,128)S(1)}, u32[]{:S(2)}, u32[]{:S(2)}) collective-permute-start(f32[304,128]{1,0:T(8,128)S(1)} %get-tuple-element.18), channel_id=1, source_target_pairs={{0,4},{4,8},{8,12},{12,16},{16,20},{20,24},{24,28},{1,5},{5,9},{9,... | collective-permute-start | bytes 466952 | tf_op jit(solution)/shard_map/ppermute | solution.py:625
  39.4 2.9 %collective-permute-done.5.high_inner = f32[304,128]{1,0:T(8,128)S(1)} collective-permute-done((f32[304,128]{1,0:T(8,128)S(1)}, f32[304,128]{1,0:T(8,128)S(1)}, u32[]{:S(2)}, u32[]{:S(2)}) %collective-permute-start.5) | collective-permute-done | bytes 155680 | tf_op jit(solution)/shard_map/ppermute | solution.py:625
  42.3 1.7 %collective-permute-done.4.low_inner = f32[304,128]{1,0:T(8,128)S(1)} collective-permute-done((f32[304,128]{1,0:T(8,128)S(1)}, f32[304,128]{1,0:T(8,128)S(1)}, u32[]{:S(2)}, u32[]{:S(2)}) %collective-permute-start.4) | collective-permute-done | bytes 155680 | tf_op jit(solution)/shard_map/ppermute | solution.py:625
  44.0 0.0 collective-permute-done.6.south_msg
  44.0 0.0 collective-permute-done.7.north_msg
  44.0 11.1 %shard_map.57 = f32[3,19,4096]{2,1,0:T(8,128)} custom-call(s32[3,32]{1,0:T(4,128)S(1)} %bitcast.5, s32[2]{0:T(128)S(1)} %pad_add_fusion.where, f32[1928,128]{1,0:T(8,128)S(1)} %get-tuple-element.13.cells, f32[672,128]{1,0:T(8,128)S(1)} %collective-permute-done.low_msg, f32[672,128]{1,0:T(8,128)S(1)} %collective-permute-done.1.high_msg, ...), custom_call_target="tpu_custom_call" | custom-call | tf_op jit(solution)/shard_map/pallas_call | solution.py:638
Async XLA Ops:
  0.7 1.3 %copy-start = (f32[3,19,4096]{2,1,0:T(8,128)S(1)}, f32[3,19,4096]{2,1,0:T(8,128)}, u32[]{:S(2)}) copy-start(f32[3,19,4096]{2,1,0:T(8,128)} %pops_hbm.1) | copy-start | bytes 2801668
  2.0 0.9 %copy-start.1 = (s32[3,5832]{1,0:T(4,128)S(1)}, s32[3,5832]{1,0:T(4,128)}, u32[]{:S(2)}) copy-start(s32[3,5832]{1,0:T(4,128)} %flags_hbm.1) | copy-start | bytes 209956
  2.9 0.7 %copy-start.2 = (s32[32,3]{0,1:T(4,128)S(1)}, s32[32,3]{0,1:T(4,128)}, u32[]{:S(2)}) copy-start(s32[32,3]{0,1:T(4,128)} %param.8) | copy-start | bytes 1156
  3.6 0.7 %copy-start.3 = (s32[3,18]{1,0:T(4,128)S(1)}, s32[3,18]{1,0:T(4,128)}, u32[]{:S(2)}) copy-start(s32[3,18]{1,0:T(4,128)} %neighbours.1) | copy-start | bytes 652
  7.0 18.1 %collective-permute-start = (f32[672,128]{1,0:T(8,128)S(1)}, f32[672,128]{1,0:T(8,128)S(1)}, u32[]{:S(2)}, u32[]{:S(2)}) collective-permute-start(f32[672,128]{1,0:T(8,128)S(1)} %get-tuple-element.14), channel_id=1, source_target_pairs={{0,4},{4,8},{8,12},{12,16},{16,20},{20,24},{24,28},{1,5},{5,9},{9,... | collective-permute-start | bytes 1032200 | tf_op jit(solution)/shard_map/ppermute | solution.py:625
  10.4 16.5 %collective-permute-start.1 = (f32[672,128]{1,0:T(8,128)S(1)}, f32[672,128]{1,0:T(8,128)S(1)}, u32[]{:S(2)}, u32[]{:S(2)}) collective-permute-start(f32[672,128]{1,0:T(8,128)S(1)} %get-tuple-element.15), channel_id=1, source_target_pairs={{4,0},{8,4},{12,8},{16,12},{20,16},{24,20},{28,24},{5,1},{9,5},{13... | collective-permute-start | bytes 1032200 | tf_op jit(solution)/shard_map/ppermute | solution.py:625
  13.7 6.2 %collective-permute-start.2 = (f32[144,128]{1,0:T(8,128)S(1)}, f32[144,128]{1,0:T(8,128)S(1)}, u32[]{:S(2)}, u32[]{:S(2)}) collective-permute-start(f32[144,128]{1,0:T(8,128)S(1)} %get-tuple-element.16), channel_id=1, source_target_pairs={{0,8},{4,12},{8,16},{12,20},{16,24},{20,28},{1,9},{5,13},{9,17},{1... | collective-permute-start | bytes 221192 | tf_op jit(solution)/shard_map/ppermute | solution.py:625
  17.2 7.2 %collective-permute-start.3 = (f32[144,128]{1,0:T(8,128)S(1)}, f32[144,128]{1,0:T(8,128)S(1)}, u32[]{:S(2)}, u32[]{:S(2)}) collective-permute-start(f32[144,128]{1,0:T(8,128)S(1)} %get-tuple-element.17), channel_id=1, source_target_pairs={{8,0},{12,4},{16,8},{20,12},{24,16},{28,20},{9,1},{13,5},{17,9},{2... | collective-permute-start | bytes 221192 | tf_op jit(solution)/shard_map/ppermute | solution.py:625
  27.9 16.0 %collective-permute-start.6 = (f32[744,128]{1,0:T(8,128)S(1)}, f32[744,128]{1,0:T(8,128)S(1)}, u32[]{:S(2)}, u32[]{:S(2)}) collective-permute-start(f32[744,128]{1,0:T(8,128)S(1)} %get-tuple-element.19), channel_id=1, source_target_pairs={{0,1},{1,2},{2,3},{4,5},{5,6},{6,7},{8,9},{9,10},{10,11},{12,13},{... | collective-permute-start | bytes 1142792 | tf_op jit(solution)/shard_map/ppermute | solution.py:625
  29.9 14.1 %collective-permute-start.7 = (f32[744,128]{1,0:T(8,128)S(1)}, f32[744,128]{1,0:T(8,128)S(1)}, u32[]{:S(2)}, u32[]{:S(2)}) collective-permute-start(f32[744,128]{1,0:T(8,128)S(1)} %get-tuple-element.20), channel_id=1, source_target_pairs={{1,0},{2,1},{3,2},{5,4},{6,5},{7,6},{9,8},{10,9},{11,10},{13,12},{... | collective-permute-start | bytes 1142792 | tf_op jit(solution)/shard_map/ppermute | solution.py:625
  33.5 8.8 %collective-permute-start.5 = (f32[304,128]{1,0:T(8,128)S(1)}, f32[304,128]{1,0:T(8,128)S(1)}, u32[]{:S(2)}, u32[]{:S(2)}) collective-permute-start(f32[304,128]{1,0:T(8,128)S(1)} %get-tuple-element.18), channel_id=1, source_target_pairs={{4,0},{8,4},{12,8},{16,12},{20,16},{24,20},{28,24},{5,1},{9,5},{13... | collective-permute-start | bytes 466952 | tf_op jit(solution)/shard_map/ppermute | solution.py:625
  35.9 8.0 %collective-permute-start.4 = (f32[304,128]{1,0:T(8,128)S(1)}, f32[304,128]{1,0:T(8,128)S(1)}, u32[]{:S(2)}, u32[]{:S(2)}) collective-permute-start(f32[304,128]{1,0:T(8,128)S(1)} %get-tuple-element.18), channel_id=1, source_target_pairs={{0,4},{4,8},{8,12},{12,16},{16,20},{20,24},{24,28},{1,5},{5,9},{9,... | collective-permute-start | bytes 466952 | tf_op jit(solution)/shard_map/ppermute | solution.py:625

commit v2 on v1

--- a/solution.py
+++ b/solution.py
@@ -15,14 +15,18 @@
 PLANES = SLOTS * POPS + SLOTS
 FLAG0 = SLOTS * POPS
 GROUP = 24
-PLANE = 4 * GROUP
+PLANE = 3 * GROUP
 SLOT = POPS * PLANE
-STRIP = 6 * PLANES
+OUTWARD = SLOTS * 5 + SLOTS
+LAYERS = 2 * PLANES + OUTWARD
 HALF = POPS * EDGE
 PAIRS = PLANES // 2
-TABLE = STRIP + HALF
+TABLE = HALF
+STRIPS = HALF + 8
 EDGE_TABLE = PAIRS * GROUP
+NOWHERE = PLANES * PLANE
 LIMIT = 48 * 1024 * 1024
+WIDE_LIMIT = 127 * 512 * 1024
 
 VELOCITY = [
     (0, 0, 0),
@@ -159,11 +163,34 @@
                         s, p : p + size, 128 * tile : 128 * tile + 128
                     ]
 
+    @pl.loop(0, SLOTS)
+    def _(s):
+        @pl.loop(0, 4)
+        def _(c):
+            base = s * (POPS * 32) + c * 8
+            h = [cells[aligned(base + p * 32), :] for p in range(POPS)]
+            for p, value in enumerate(collided(h, True)):
+                cells[aligned(base + p * 32), :] = value
+
     for y in range(2):
-        for k in range(3):
-            out = (y * 3 + k) * PLANES
-            up_msg[out : out + PLANES, :] = cells[pl.ds(y * EDGE + 13 + k, PLANES, stride=32), :]
-            down_msg[out : out + PLANES, :] = cells[pl.ds(y * EDGE + k, PLANES, stride=32), :]
+        for msg, x0, first in ((up_msg, 15, 1), (down_msg, 0, 2)):
+            step = -1 if x0 else 1
+            for k in range(2):
+                out = STRIPS + y * LAYERS + k * PLANES
+                msg[out : out + PLANES, :] = cells[
+                    pl.ds(y * EDGE + x0 + step * k, PLANES, stride=32), :
+                ]
+            row = y * EDGE + x0 + 2 * step
+            out = STRIPS + y * LAYERS + 2 * PLANES
+            for s in range(SLOTS):
+                base = s * POPS * 32 + row
+                msg[out + 5 * s : out + 5 * s + 1, :] = cells[pl.ds(base + first * 32, 1), :]
+                msg[out + 5 * s + 1 : out + 5 * s + 5, :] = cells[
+                    pl.ds(base + (first + 6) * 32, 4, stride=64), :
+                ]
+            msg[out + 5 * SLOTS : out + OUTWARD, :] = cells[
+                pl.ds(FLAG0 * 32 + row, SLOTS, stride=32), :
+            ]
 
     curve, cross = where[0], where[1]
     leaving = jnp.maximum(moves[0, curve * cross_size + cross], 0)
@@ -175,8 +202,8 @@
             second = cells[aligned(base + EDGE), :]
             outer = jnp.where(low, first, second)
             row = p * EDGE + v * 8
-            up_msg[STRIP + row : STRIP + row + 8, :] = outer
-            down_msg[STRIP + row : STRIP + row + 8, :] = outer
+            up_msg[row : row + 8, :] = outer
+            down_msg[row : row + 8, :] = outer
             inner_msg[row : row + 8, :] = jnp.where(low, second, first)
     for s in range(SLOTS):
 
@@ -188,6 +215,33 @@
                     row = s * POPS * 32 + y * EDGE + k
                     up2_msg[out : out + POPS, :] = cells[pl.ds(row + 13, POPS, stride=32), :]
                     down2_msg[out : out + POPS, :] = cells[pl.ds(row, POPS, stride=32), :]
+
+
+def strip_rows(first, row0, step):
+    pieces = []
+    for k in range(2):
+        pieces.append(
+            (PLANES, lambda size, row: pl.ds(row, PLANES, stride=size), row0 + step * k, STRIPS + k * PLANES)
+        )
+    row, source = row0 + 2 * step, STRIPS + 2 * PLANES
+    for s in range(SLOTS):
+        plane = s * POPS + first
+        pieces.append((1, lambda size, row, plane=plane: pl.ds(plane * size + row, 1), row, source))
+        pieces.append(
+            (
+                4,
+                lambda size, row, plane=plane: pl.ds(
+                    (plane + 6) * size + row, 4, stride=2 * size
+                ),
+                row,
+                source + 1,
+            )
+        )
+        source += 5
+    pieces.append(
+        (SLOTS, lambda size, row: pl.ds(FLAG0 * size + row, SLOTS, stride=size), row, source)
+    )
+    return pieces
 
 
 def own_strip(cells, slot, y, x):
@@ -222,11 +276,11 @@
         lane = lax.broadcasted_iota(jnp.int32, first.shape, 1)
         return jnp.where(lane < 64, first, second)
 
-    for msg, row0 in ((high_msg, 16), (low_msg, 21)):
-        for k in range(3):
-            outer[pl.ds(row0 + k, PLANES, stride=GROUP), :] = both(
-                msg[k * PLANES : (k + 1) * PLANES, :],
-                msg[(3 + k) * PLANES : (4 + k) * PLANES, :],
+    for msg, row0, step, first in ((high_msg, 16, 1, 2), (low_msg, 23, -1, 1)):
+        for count, planes, row, source in strip_rows(first, row0, step):
+            outer[planes(GROUP, row), :] = both(
+                msg[source : source + count, :],
+                msg[LAYERS + source : LAYERS + source + count, :],
             )
     for slot, msg in ((from_low, low_msg), (from_high, high_msg)):
 
@@ -234,7 +288,7 @@
         def _():
             for p in range(POPS):
                 for v in range(2):
-                    row = STRIP + p * EDGE + v * 8
+                    row = p * EDGE + v * 8
                     base = slot * (POPS * GROUP) + p * GROUP + v * 8
                     outer[aligned(base), :] = msg[row : row + 8, :]
 
@@ -366,76 +420,83 @@
     return out
 
 
-def collide_all(h_ref, post_ref, fluid):
-    def chunk(s, c):
-        base = s * SLOT + c * 8
-        is_fluid = fluid[aligned(s * PLANE + c * 8), :] > 0.0
-        h = [h_ref[aligned(base + p * PLANE), :] for p in range(POPS)]
-        for p, value in enumerate(collided(h, is_fluid)):
-            post_ref[aligned(base + p * PLANE), :] = jnp.where(is_fluid, value, jnp.nan)
-
+def fluid_at(post_ref, s, row):
+    return post_ref[aligned((FLAG0 + s) * PLANE + row), :] > 0.0
+
+
+def collide_all(h_ref, post_ref):
     @pl.loop(0, SLOTS)
     def _(s):
         @pl.loop(0, PLANE // 8)
         def _(c):
-            chunk(s, c)
-
-
-def stream_all(post_ref, h_ref, fluid, table, groups, vregs, finish=None):
+            base = s * SLOT + c * 8
+            is_fluid = fluid_at(post_ref, s, c * 8)
+            h = [h_ref[aligned(base + p * PLANE), :] for p in range(POPS)]
+            for p, value in enumerate(collided(h, is_fluid)):
+                post_ref[aligned(base + p * PLANE), :] = jnp.where(is_fluid, value, jnp.nan)
+
+
+def hide_walls(post_ref):
+    @pl.loop(0, SLOTS)
+    def _(s):
+        @pl.loop(0, PLANE // 8)
+        def _(c):
+            is_fluid = fluid_at(post_ref, s, c * 8)
+            for p in range(POPS):
+                place = aligned(s * SLOT + p * PLANE + c * 8)
+                post_ref[place, :] = jnp.where(is_fluid, post_ref[place, :], jnp.nan)
+
+
+def stream_all(post_ref, h_ref, table, groups, vregs, finish=None):
     lane = lanes_iota()
     row = rows_iota()
-    side = {0: -1, 1: 0, 2: 0, 3: 1}
+    low = lane < 64
 
     def one_slot(s):
         own = s * SLOT
 
-        def look(i, j, offset):
-            if offset == (0, 0, 0):
-                return own
-            region = (i + 1) * 3 + j + 1
-            return table[region * 8 + s, VELOCITY.index(offset) - 1]
-
         def shifted(pop, group, j, dy, dz):
             cx = VELOCITY[pop][0]
 
             def rows(start, v):
                 return post_ref[aligned(start + pop * PLANE + group * GROUP + v * 8), :]
 
-            inner = look(0, j, (0, dy, dz))
+            def look(i, j, dx, v):
+                if (dx, dy, dz) == (0, 0, 0):
+                    return rows(own, v)
+                if j is None:
+                    return jnp.where(low, look(i, 1, dx, v), look(i, -1, dx, v))
+                region = (i + 1) * 3 + j + 1
+                return rows(table[region * 8 + s, VELOCITY.index((dx, dy, dz)) - 1], v)
+
             need_last = vregs == 3
-            values = [rows(inner, 0), rows(inner, 1)]
+            values = [look(0, j, 0, 0), look(0, j, 0, 1)]
             if need_last:
                 if dy == 0 and dz == 0:
-                    values.append(rows(inner, 2))
+                    values.append(rows(own, 2))
                 else:
-                    values.append(
-                        jnp.where(
-                            row < 4,
-                            rows(look(1, j, (0, dy, dz)), 2),
-                            rows(look(-1, j, (0, dy, dz)), 2),
-                        )
-                    )
+                    values.append(jnp.where(row < 4, look(1, j, 0, 2), look(-1, j, 0, 2)))
             if cx == 0:
                 return values
             turn = 1 if cx > 0 else 7
             rolled = [pltpu.roll(value, turn, axis=0) for value in values]
             if cx > 0:
-                before = pltpu.roll(rows(look(0, j, (-1, dy, dz)), 2), 1, axis=0)
+                before = pltpu.roll(look(0, j, -1, 2), 1, axis=0)
                 result = [
                     jnp.where(row == 0, before, rolled[0]),
                     jnp.where(row == 0, rolled[0], rolled[1]),
                 ]
                 if need_last:
-                    edge = pltpu.roll(rows(look(1, j, (-1, dy, dz)), 1), 1, axis=0)
+                    edge = pltpu.roll(look(1, j, -1, 1), 1, axis=0)
                     result.append(jnp.where(row == 0, edge, rolled[2]))
                 return result
-            after = pltpu.roll(rows(look(0, j, (1, dy, dz)), 2), 7, axis=0)
+            after = pltpu.roll(look(0, j, 1, 2), 7, axis=0)
             result = [
                 jnp.where(row == 7, rolled[1], rolled[0]),
                 jnp.where(row == 7, after, rolled[1]),
             ]
             if need_last:
-                edge = pltpu.roll(rows(look(-1, j, (1, dy, dz)), 0), 7, axis=0)
+                edge = pltpu.roll(look(-1, j, 1, 0), 7, axis=0)
                 result.append(jnp.where(row == 7, edge, rolled[2]))
             return result
 
@@ -443,20 +504,20 @@
             cx, cy, cz = VELOCITY[pop]
             kept = {}
 
-            def source(group, j, dy, dz):
-                key = (group, j, dy, dz)
+            def source(*key):
                 if key not in kept:
-                    kept[key] = shifted(pop, group, j, dy, dz)
+                    kept[key] = shifted(pop, *key)
                 return kept[key]
 
             def along_y(group, dz):
-                j = side[group]
-                values = source(group, j, 0, dz)
-                other = group - cy
-                if cy == 0 or other < 0 or other > 3:
+                values = source(group, None if group == 2 else 0, 0, dz)
+                if cy == 0:
                     return values
-                dy = 0 if side[other] == j else -cy
-                carried = source(other, j, dy, dz)
+                other = (group - cy) % 3
+                if group != 2 and other != 2:
+                    carried = source(other, 0, 0, dz)
+                else:
+                    carried = source(other, cy if group == 2 else 0, -cy, dz)
                 mask = lane >= 112 if cy > 0 else lane < 16
                 return [jnp.where(mask, b, a) for a, b in zip(values, carried)]
 
@@ -475,7 +536,7 @@
                     if pop:
                         back = post_ref[aligned(own + OPPOSITE[pop] * PLANE + place), :]
                         value = jnp.where(value != value, back, value)
-                    is_fluid = fluid[aligned(s * PLANE + place), :] > 0.0
+                    is_fluid = fluid_at(post_ref, s, place)
                     h_ref[aligned(own + pop * PLANE + place), :] = jnp.where(is_fluid, value, 0.0)
 
     @pl.loop(0, SLOTS)
@@ -502,7 +563,6 @@
     out_hbm,
     h_ref,
     post_ref,
-    fluid,
     out,
     slots,
     table,
@@ -516,9 +576,9 @@
                 (north_msg, EDGE_TABLE + 8 * i),
             )
         ):
-            first = ref[row : row + 8, :].astype(jnp.int32) * SLOT
+            slot = ref[row : row + 8, :].astype(jnp.int32)
             region = 8 * (3 * i + j)
-            slots[region : region + 8, :] = first
+            slots[region : region + 8, :] = jnp.where(slot == SLOTS, NOWHERE, slot * SLOT)
     table_copy = pltpu.make_async_copy(slots, table, sems.at[SLOTS])
     table_copy.start()
 
@@ -526,19 +586,14 @@
         moves, where, curve_size, cross_size
     )
     low = lanes_iota() < 64
-    fluid[...] = jnp.zeros_like(fluid)
-    post_ref[SLOTS * SLOT :, :] = jnp.full((SLOT, 128), jnp.nan, jnp.float32)
-
-    def home(q):
-        if q < FLAG0:
-            return h_ref, q * PLANE
-        return fluid, (q - FLAG0) * PLANE
+    post_ref[NOWHERE:, :] = jnp.full((SLOT, 128), jnp.nan, jnp.float32)
 
     for q in range(PLANES):
-        ref, base = home(q)
         for y in range(2):
-            start = base + (1 + y) * GROUP
-            ref[start : start + EDGE, :] = cells[q * 32 + y * EDGE : q * 32 + (y + 1) * EDGE, :]
+            start = q * PLANE + y * GROUP
+            post_ref[start : start + EDGE, :] = cells[
+                q * 32 + y * EDGE : q * 32 + (y + 1) * EDGE, :
+            ]
     for slot, msg, inner in (
         (from_low, low_msg, low_inner),
         (from_high, high_msg, high_inner),
@@ -549,19 +604,17 @@
             for p in range(POPS):
                 for v in range(2):
                     row = p * EDGE + v * 8
-                    outside = msg[STRIP + row : STRIP + row + 8, :]
+                    outside = msg[row : row + 8, :]
                     inside = inner[row : row + 8, :]
-                    start = slot * SLOT + p * PLANE + GROUP + v * 8
-                    h_ref[aligned(start), :] = jnp.where(low, outside, inside)
-                    h_ref[aligned(start + GROUP), :] = jnp.where(low, inside, outside)
-
-    for msg, row0 in ((high_msg, 16), (low_msg, 21)):
+                    start = slot * SLOT + p * PLANE + v * 8
+                    post_ref[aligned(start), :] = jnp.where(low, outside, inside)
+                    post_ref[aligned(start + GROUP), :] = jnp.where(low, inside, outside)
+
+    for msg, row0, step, first in ((high_msg, 16, 1, 2), (low_msg, 23, -1, 1)):
         for y in range(2):
-            for k in range(3):
-                row = (1 + y) * GROUP + row0 + k
-                source = (y * 3 + k) * PLANES
-                h_ref[pl.ds(row, FLAG0, stride=PLANE), :] = msg[source : source + FLAG0, :]
-                fluid[pl.ds(row, SLOTS, stride=PLANE), :] = msg[source + FLAG0 : source + PLANES, :]
+            for count, planes, row, source in strip_rows(first, row0, step):
+                source += y * LAYERS
+                post_ref[planes(PLANE, row + y * GROUP), :] = msg[source : source + count, :]
     for s in range(SLOTS):
         for slot, msg, row0 in ((low_low, low2_msg, 21), (high_high, high2_msg, 16)):
 
@@ -569,9 +622,11 @@
             def _():
                 for y in range(2):
                     for k in range(3):
-                        row = s * SLOT + (1 + y) * GROUP + row0 + k
+                        row = s * SLOT + y * GROUP + row0 + k
                         source = (y * 3 + k) * GROUP
-                        h_ref[pl.ds(row, POPS, stride=PLANE), :] = msg[source : source + POPS, :]
+                        post_ref[pl.ds(row, POPS, stride=PLANE), :] = msg[
+                            source : source + POPS, :
+                        ]
 
         for mine in range(SLOTS):
             for slot, x0, row0 in ((low_me, 13, 21), (high_me, 0, 16)):
@@ -580,41 +635,38 @@
                 def _():
                     for y in range(2):
                         for k in range(3):
-                            row = s * SLOT + (1 + y) * GROUP + row0 + k
-                            h_ref[pl.ds(row, POPS, stride=PLANE), :] = own_strip(
+                            row = s * SLOT + y * GROUP + row0 + k
+                            post_ref[pl.ds(row, POPS, stride=PLANE), :] = own_strip(
                                 cells, mine, y, x0 + k
                             )
 
-    for msg, group in ((south_msg, 0), (north_msg, 3)):
-        for pair in range(PAIRS):
-            for v in range(3):
-                value = msg[pair * GROUP + v * 8 : pair * GROUP + v * 8 + 8, :]
-                ref, base = home(2 * pair)
-                row = base + group * GROUP + v * 8
-                ref[row : row + 8, :] = value
-                ref, base = home(2 * pair + 1)
-                row = base + group * GROUP + v * 8
-                ref[row : row + 8, :] = pltpu.roll(value, 64, axis=1)
+    for pair in range(PAIRS):
+        for v in range(3):
+            row = pair * GROUP + v * 8
+            south, north = south_msg[row : row + 8, :], north_msg[row : row + 8, :]
+            row = 2 * pair * PLANE + 2 * GROUP + v * 8
+            post_ref[row : row + 8, :] = jnp.where(low, north, south)
+            post_ref[row + PLANE : row + PLANE + 8, :] = pltpu.roll(
+                jnp.where(low, south, north), 64, axis=1
+            )
 
     def finish(s):
         for x in range(EDGE):
             for y in range(2):
                 tile = 2 * x + y
                 for p, size in ((0, 8), (8, 8), (16, 3)):
-                    row = s * SLOT + (p * PLANE + (1 + y) * GROUP + x)
+                    row = s * SLOT + (p * PLANE + y * GROUP + x)
                     out[s, p : p + size, 128 * tile : 128 * tile + 128] = h_ref[
                         pl.ds(row, size, stride=PLANE), :
                     ]
         pltpu.make_async_copy(out.at[s], out_hbm.at[s], sems.at[s]).start()
 
-    for step in range(STEPS):
-        collide_all(h_ref, post_ref, fluid)
-        if step == 0:
-            table_copy.wait()
-        if step < STEPS - 1:
-            stream_all(post_ref, h_ref, fluid, table, (0, 1, 2, 3), 3)
-        else:
-            stream_all(post_ref, h_ref, fluid, table, (1, 2), 2, finish)
+    hide_walls(post_ref)
+    table_copy.wait()
+    for step in range(STEPS - 1):
+        stream_all(post_ref, h_ref, table, (0, 1, 2), 3)
+        collide_all(h_ref, post_ref)
+    stream_all(post_ref, h_ref, table, (0, 1), 2, finish)
     for s in range(SLOTS):
         pltpu.make_async_copy(out.at[s], out_hbm.at[s], sems.at[s]).wait()
 
@@ -629,7 +681,7 @@
     return jax.ShapeDtypeStruct((count, 128), jnp.float32)
 
 
-def call(kernel, in_spaces, out_spaces, outs, ins, scratch):
+def call(kernel, in_spaces, out_spaces, outs, ins, scratch, limit=LIMIT):
     spaces = {
         "S": pl.BlockSpec(memory_space=pltpu.SMEM),
         "V": pl.BlockSpec(memory_space=pltpu.VMEM),
@@ -641,7 +693,7 @@
         in_specs=[spaces[x] for x in in_spaces],
         out_specs=[spaces[x] for x in out_spaces],
         scratch_shapes=scratch,
-        compiler_params=pltpu.CompilerParams(vmem_limit_bytes=LIMIT),
+        compiler_params=pltpu.CompilerParams(vmem_limit_bytes=limit),
     )(*ins)
 
 
@@ -660,8 +712,8 @@
         "VVVVVV",
         [
             rows128(PLANES * 32 + 8),
-            rows128(STRIP + HALF + 8),
-            rows128(STRIP + HALF + 8),
+            rows128(STRIPS + 2 * LAYERS),
+            rows128(STRIPS + 2 * LAYERS),
             rows128(6 * GROUP),
             rows128(6 * GROUP),
             rows128(HALF),
@@ -676,6 +728,7 @@
             pltpu.VMEM((8, 128), jnp.float32),
             pltpu.SemaphoreType.DMA((SLOTS + 1,)),
         ],
+        WIDE_LIMIT,
     )
     low_msg = shifted_from(up_msg, "curve", 1)
     high_msg = shifted_from(down_msg, "curve", -1)
@@ -713,8 +766,7 @@
         ),
         [
             pltpu.VMEM((SLOTS * SLOT, 128), jnp.float32),
-            pltpu.VMEM(((SLOTS + 1) * SLOT, 128), jnp.float32),
-            pltpu.VMEM((SLOTS * PLANE, 128), jnp.float32),
+            pltpu.VMEM((NOWHERE + SLOT, 128), jnp.float32),
             pltpu.VMEM(populations.shape, jnp.float32),
             pltpu.VMEM((72, 128), jnp.int32),
             pltpu.SMEM((72, 128), jnp.int32),

time: 55.4 us -> 51.3 us (0.926)
  the two profiles are of different devices: /device:TPU:10 before, /device:TPU:18 now
where the time goes in v2:
time: 51.3 us; the launch traced here: 50.9 us
  starting transfers between devices  24 us (47%)
  Pallas kernels  13.8 us (27%)
  waiting for transfers between devices  10.4 us (20%)
  local copies, waits for them, and re-layouts  1.22 us (2%)
  between operations  0.76 us (1%)
  other arithmetic  0.65 us (1%)
    ppermute x8, starting transfers between devices, shifted_from(): return lax.ppermute(value, axis, pairs)  24 us
    pallas_call x3, Pallas kernels, call(): pl.pallas_call(kernel, out_shape=outs, in_specs=[spaces[x] for x in in_sp...  13.8 us
    ppermute x8, waiting for transfers between devices, shifted_from(): return lax.ppermute(value, axis, pairs)  10.4 us
    unnamed x8, local copies, waits for them, and re-layouts  1.22 us
  transfers between devices with their start and end apart: 8, of which 5 were waited for; matrix products, arithmetic and copies ran while one was open for 0% of the time, Pallas kernels for 0%

profile of v2, /device:TPU:18, one launch (start us, length us, event | category | flops | bytes accessed | tf_op | source)
XLA Modules:
  0.0 50.9 jit_solution(17470712026000589763)
XLA Ops:
  0.0 0.0 copy-start.1
  0.7 0.6 %pad_add_fusion.where = s32[2]{0:T(128)} fusion(s32[1]{0:T(128)} %bitcast.2, s32[1]{0:T(128)} %bitcast.1), kind=kLoop, calls=%fused_computation | loop fusion | flops 2 | bytes 16 | tf_op jit(solution)/shard_map/stack | solution.py:705
  1.3 0.0 copy-start.2
  1.3 4.8 %shard_map.55 = (f32[1928,128]{1,0:T(8,128)}, f32[588,128]{1,0:T(8,128)}, f32[588,128]{1,0:T(8,128)}, f32[144,128]{1,0:T(8,128)}, f32[144,128]{1,0:T(8,128)}, /*index=5*/f32[304,128]{1,0:T(8,128)}) custom-call(s32[3,32]{1,0:T(4,128)} %bitcast.3, s32[2]{0:T(128)} %pad_add_fusion.where, s32[1]{0:T(128)S(6)} %copy.6.counts, f32[3,19,4096]{2,1,0:T(8,128)} %pops_hbm.1, ...), custom_call_target="tpu_custom_call" | custom-call | tf_op jit(solution)/shard_map/pallas_call | solution.py:690
  6.1 3.4 %collective-permute-start = (f32[588,128]{1,0:T(8,128)}, f32[588,128]{1,0:T(8,128)S(1)}, u32[]{:S(2)}, u32[]{:S(2)}) collective-permute-start(f32[588,128]{1,0:T(8,128)} %get-tuple-element.14), channel_id=1, source_target_pairs={{0,4},{4,8},{8,12},{12,16},{16,20},{20,24},{24,28},{1,5},{5,9},{9,... | collective-permute-start | bytes 903176 | tf_op jit(solution)/shard_map/ppermute | solution.py:677
  9.6 3.3 %collective-permute-start.1 = (f32[588,128]{1,0:T(8,128)}, f32[588,128]{1,0:T(8,128)S(1)}, u32[]{:S(2)}, u32[]{:S(2)}) collective-permute-start(f32[588,128]{1,0:T(8,128)} %get-tuple-element.15), channel_id=1, source_target_pairs={{4,0},{8,4},{12,8},{16,12},{20,16},{24,20},{28,24},{5,1},{9,5},{13... | collective-permute-start | bytes 903176 | tf_op jit(solution)/shard_map/ppermute | solution.py:677
  12.9 3.5 %collective-permute-start.2 = (f32[144,128]{1,0:T(8,128)}, f32[144,128]{1,0:T(8,128)S(1)}, u32[]{:S(2)}, u32[]{:S(2)}) collective-permute-start(f32[144,128]{1,0:T(8,128)} %get-tuple-element.16), channel_id=1, source_target_pairs={{0,8},{4,12},{8,16},{12,20},{16,24},{20,28},{1,9},{5,13},{9,17},{1... | collective-permute-start | bytes 221192 | tf_op jit(solution)/shard_map/ppermute | solution.py:677
  16.4 2.4 %collective-permute-start.3 = (f32[144,128]{1,0:T(8,128)}, f32[144,128]{1,0:T(8,128)S(1)}, u32[]{:S(2)}, u32[]{:S(2)}) collective-permute-start(f32[144,128]{1,0:T(8,128)} %get-tuple-element.17), channel_id=1, source_target_pairs={{8,0},{12,4},{16,8},{20,12},{24,16},{28,20},{9,1},{13,5},{17,9},{2... | collective-permute-start | bytes 221192 | tf_op jit(solution)/shard_map/ppermute | solution.py:677
  18.8 0.6 %collective-permute-done.2.low2_msg = f32[144,128]{1,0:T(8,128)S(1)} collective-permute-done((f32[144,128]{1,0:T(8,128)}, f32[144,128]{1,0:T(8,128)S(1)}, u32[]{:S(2)}, u32[]{:S(2)}) %collective-permute-start.2) | collective-permute-done | bytes 73760 | tf_op jit(solution)/shard_map/ppermute | solution.py:677
  19.4 3.5 %collective-permute-done.3.high2_msg = f32[144,128]{1,0:T(8,128)S(1)} collective-permute-done((f32[144,128]{1,0:T(8,128)}, f32[144,128]{1,0:T(8,128)S(1)}, u32[]{:S(2)}, u32[]{:S(2)}) %collective-permute-start.3) | collective-permute-done | bytes 73760 | tf_op jit(solution)/shard_map/ppermute | solution.py:677
  22.9 0.0 collective-permute-done.low_msg
  22.9 1.7 %collective-permute-done.1.high_msg = f32[588,128]{1,0:T(8,128)S(1)} collective-permute-done((f32[588,128]{1,0:T(8,128)}, f32[588,128]{1,0:T(8,128)S(1)}, u32[]{:S(2)}, u32[]{:S(2)}) %collective-permute-start.1) | collective-permute-done | bytes 301088 | tf_op jit(solution)/shard_map/ppermute | solution.py:677
  24.6 0.0 copy-done.1
  24.6 0.0 copy-done.2
  24.6 0.0 copy-start
  24.6 1.2 %copy-done = f32[1928,128]{1,0:T(8,128)S(1)} copy-done((f32[1928,128]{1,0:T(8,128)S(1)}, f32[1928,128]{1,0:T(8,128)}, u32[]{:S(2)}) %copy-start) | copy-done | bytes 987160
  25.8 0.0 copy-start.3
  25.8 0.9 %shard_map.56 = (f32[744,128]{1,0:T(8,128)S(1)}, f32[744,128]{1,0:T(8,128)S(1)}) custom-call(s32[3,32]{1,0:T(4,128)S(1)} %bitcast.4, s32[2]{0:T(128)S(1)} %copy-done.2, f32[1928,128]{1,0:T(8,128)S(1)} %copy-done, f32[588,128]{1,0:T(8,128)S(1)} %collective-permute-done.low_msg, f32[588,128]{1,0:T(8,128)S(1)} %collective-permute-done.1.high_msg, ...), custom_call_target="tpu_custom_call" | custom-call | tf_op jit(solution)/shard_map/pallas_call | solution.py:690
  26.7 2.0 %collective-permute-start.6 = (f32[744,128]{1,0:T(8,128)S(1)}, f32[744,128]{1,0:T(8,128)S(1)}, u32[]{:S(2)}, u32[]{:S(2)}) collective-permute-start(f32[744,128]{1,0:T(8,128)S(1)} %get-tuple-element.19), channel_id=1, source_target_pairs={{0,1},{1,2},{2,3},{4,5},{5,6},{6,7},{8,9},{9,10},{10,11},{12,13},{... | collective-permute-start | bytes 1142792 | tf_op jit(solution)/shard_map/ppermute | solution.py:677
  28.7 3.6 %collective-permute-start.7 = (f32[744,128]{1,0:T(8,128)S(1)}, f32[744,128]{1,0:T(8,128)S(1)}, u32[]{:S(2)}, u32[]{:S(2)}) collective-permute-start(f32[744,128]{1,0:T(8,128)S(1)} %get-tuple-element.20), channel_id=1, source_target_pairs={{1,0},{2,1},{3,2},{5,4},{6,5},{7,6},{9,8},{10,9},{11,10},{13,12},{... | collective-permute-start | bytes 1142792 | tf_op jit(solution)/shard_map/ppermute | solution.py:677
  32.3 0.0 copy-done.3
  32.3 2.4 %collective-permute-start.5 = (f32[304,128]{1,0:T(8,128)S(1)}, f32[304,128]{1,0:T(8,128)S(1)}, u32[]{:S(2)}, u32[]{:S(2)}) collective-permute-start(f32[304,128]{1,0:T(8,128)S(1)} %copy-done.3), channel_id=1, source_target_pairs={{4,0},{8,4},{12,8},{16,12},{20,16},{24,20},{28,24},{5,1},{9,5},{13... | collective-permute-start | bytes 466952 | tf_op jit(solution)/shard_map/ppermute | solution.py:677
  34.8 3.4 %collective-permute-start.4 = (f32[304,128]{1,0:T(8,128)S(1)}, f32[304,128]{1,0:T(8,128)S(1)}, u32[]{:S(2)}, u32[]{:S(2)}) collective-permute-start(f32[304,128]{1,0:T(8,128)S(1)} %copy-done.3), channel_id=1, source_target_pairs={{0,4},{4,8},{8,12},{12,16},{16,20},{20,24},{24,28},{1,5},{5,9},{9,... | collective-permute-start | bytes 466952 | tf_op jit(solution)/shard_map/ppermute | solution.py:677
  38.2 2.9 %collective-permute-done.5.high_inner = f32[304,128]{1,0:T(8,128)S(1)} collective-permute-done((f32[304,128]{1,0:T(8,128)S(1)}, f32[304,128]{1,0:T(8,128)S(1)}, u32[]{:S(2)}, u32[]{:S(2)}) %collective-permute-start.5) | collective-permute-done | bytes 155680 | tf_op jit(solution)/shard_map/ppermute | solution.py:677
  41.1 1.7 %collective-permute-done.4.low_inner = f32[304,128]{1,0:T(8,128)S(1)} collective-permute-done((f32[304,128]{1,0:T(8,128)S(1)}, f32[304,128]{1,0:T(8,128)S(1)}, u32[]{:S(2)}, u32[]{:S(2)}) %collective-permute-start.4) | collective-permute-done | bytes 155680 | tf_op jit(solution)/shard_map/ppermute | solution.py:677
  42.8 0.0 collective-permute-done.6.south_msg
  42.8 0.0 collective-permute-done.7.north_msg
  42.8 8.1 %shard_map.57 = f32[3,19,4096]{2,1,0:T(8,128)} custom-call(s32[3,32]{1,0:T(4,128)S(1)} %bitcast.5, s32[2]{0:T(128)S(1)} %copy-done.2, f32[1928,128]{1,0:T(8,128)S(1)} %copy-done, f32[588,128]{1,0:T(8,128)S(1)} %collective-permute-done.low_msg, f32[588,128]{1,0:T(8,128)S(1)} %collective-permute-done.1.high_msg, ...), custom_call_target="tpu_custom_call" | custom-call | tf_op jit(solution)/shard_map/pallas_call | solution.py:690
Async XLA Ops:
  0.0 24.6 %copy-start.1 = (s32[32,3]{0,1:T(4,128)S(1)}, s32[32,3]{0,1:T(4,128)}, u32[]{:S(2)}) copy-start(s32[32,3]{0,1:T(4,128)} %param.8) | copy-start | bytes 1156
  1.3 23.3 %copy-start.2 = (s32[2]{0:T(128)S(1)}, s32[2]{0:T(128)}, u32[]{:S(2)}) copy-start(s32[2]{0:T(128)} %pad_add_fusion.where) | copy-start | bytes 28
  6.1 16.8 %collective-permute-start = (f32[588,128]{1,0:T(8,128)}, f32[588,128]{1,0:T(8,128)S(1)}, u32[]{:S(2)}, u32[]{:S(2)}) collective-permute-start(f32[588,128]{1,0:T(8,128)} %get-tuple-element.14), channel_id=1, source_target_pairs={{0,4},{4,8},{8,12},{12,16},{16,20},{20,24},{24,28},{1,5},{5,9},{9,... | collective-permute-start | bytes 903176 | tf_op jit(solution)/shard_map/ppermute | solution.py:677
  9.6 15.0 %collective-permute-start.1 = (f32[588,128]{1,0:T(8,128)}, f32[588,128]{1,0:T(8,128)S(1)}, u32[]{:S(2)}, u32[]{:S(2)}) collective-permute-start(f32[588,128]{1,0:T(8,128)} %get-tuple-element.15), channel_id=1, source_target_pairs={{4,0},{8,4},{12,8},{16,12},{20,16},{24,20},{28,24},{5,1},{9,5},{13... | collective-permute-start | bytes 903176 | tf_op jit(solution)/shard_map/ppermute | solution.py:677
  12.9 6.5 %collective-permute-start.2 = (f32[144,128]{1,0:T(8,128)}, f32[144,128]{1,0:T(8,128)S(1)}, u32[]{:S(2)}, u32[]{:S(2)}) collective-permute-start(f32[144,128]{1,0:T(8,128)} %get-tuple-element.16), channel_id=1, source_target_pairs={{0,8},{4,12},{8,16},{12,20},{16,24},{20,28},{1,9},{5,13},{9,17},{1... | collective-permute-start | bytes 221192 | tf_op jit(solution)/shard_map/ppermute | solution.py:677
  16.4 6.5 %collective-permute-start.3 = (f32[144,128]{1,0:T(8,128)}, f32[144,128]{1,0:T(8,128)S(1)}, u32[]{:S(2)}, u32[]{:S(2)}) collective-permute-start(f32[144,128]{1,0:T(8,128)} %get-tuple-element.17), channel_id=1, source_target_pairs={{8,0},{12,4},{16,8},{20,12},{24,16},{28,20},{9,1},{13,5},{17,9},{2... | collective-permute-start | bytes 221192 | tf_op jit(solution)/shard_map/ppermute | solution.py:677
  24.6 1.2 %copy-start = (f32[1928,128]{1,0:T(8,128)S(1)}, f32[1928,128]{1,0:T(8,128)}, u32[]{:S(2)}) copy-start(f32[1928,128]{1,0:T(8,128)} %get-tuple-element.13.cells) | copy-start | bytes 2961412
  25.8 6.5 %copy-start.3 = (f32[304,128]{1,0:T(8,128)S(1)}, f32[304,128]{1,0:T(8,128)}, u32[]{:S(2)}) copy-start(f32[304,128]{1,0:T(8,128)} %get-tuple-element.18) | copy-start | bytes 466948
  26.7 16.1 %collective-permute-start.6 = (f32[744,128]{1,0:T(8,128)S(1)}, f32[744,128]{1,0:T(8,128)S(1)}, u32[]{:S(2)}, u32[]{:S(2)}) collective-permute-start(f32[744,128]{1,0:T(8,128)S(1)} %get-tuple-element.19), channel_id=1, source_target_pairs={{0,1},{1,2},{2,3},{4,5},{5,6},{6,7},{8,9},{9,10},{10,11},{12,13},{... | collective-permute-start | bytes 1142792 | tf_op jit(solution)/shard_map/ppermute | solution.py:677
  28.7 14.1 %collective-permute-start.7 = (f32[744,128]{1,0:T(8,128)S(1)}, f32[744,128]{1,0:T(8,128)S(1)}, u32[]{:S(2)}, u32[]{:S(2)}) collective-permute-start(f32[744,128]{1,0:T(8,128)S(1)} %get-tuple-element.20), channel_id=1, source_target_pairs={{1,0},{2,1},{3,2},{5,4},{6,5},{7,6},{9,8},{10,9},{11,10},{13,12},{... | collective-permute-start | bytes 1142792 | tf_op jit(solution)/shard_map/ppermute | solution.py:677
  32.3 8.8 %collective-permute-start.5 = (f32[304,128]{1,0:T(8,128)S(1)}, f32[304,128]{1,0:T(8,128)S(1)}, u32[]{:S(2)}, u32[]{:S(2)}) collective-permute-start(f32[304,128]{1,0:T(8,128)S(1)} %copy-done.3), channel_id=1, source_target_pairs={{4,0},{8,4},{12,8},{16,12},{20,16},{24,20},{28,24},{5,1},{9,5},{13... | collective-permute-start | bytes 466952 | tf_op jit(solution)/shard_map/ppermute | solution.py:677
  34.8 8.0 %collective-permute-start.4 = (f32[304,128]{1,0:T(8,128)S(1)}, f32[304,128]{1,0:T(8,128)S(1)}, u32[]{:S(2)}, u32[]{:S(2)}) collective-permute-start(f32[304,128]{1,0:T(8,128)S(1)} %copy-done.3), channel_id=1, source_target_pairs={{0,4},{4,8},{8,12},{12,16},{16,20},{20,24},{24,28},{1,5},{5,9},{9,... | collective-permute-start | bytes 466952 | tf_op jit(solution)/shard_map/ppermute | solution.py:677

commit v3 on v2

--- a/solution.py
+++ b/solution.py
@@ -25,7 +25,7 @@
 STRIPS = HALF + 8
 EDGE_TABLE = PAIRS * GROUP
 NOWHERE = PLANES * PLANE
-LIMIT = 48 * 1024 * 1024
+LIMIT = 20 * 1024 * 1024
 WIDE_LIMIT = 127 * 512 * 1024
 
 VELOCITY = [
@@ -64,8 +64,8 @@
     return pl.ds(pl.multiple_of(start, 8), size)
 
 
-def move_slots(moves, where, curve_size, cross_size):
-    curve, cross = where[0], where[1]
+def move_slots(moves, curve_size, cross_size):
+    curve, cross = lax.axis_index("curve"), lax.axis_index("cross")
 
     def landed(source, target):
         inside = (source >= 0) & (source < curve_size) & (target >= 0) & (target < curve_size)
@@ -74,7 +74,6 @@
         hit = inside & (moves[0, row] >= 0) & (moves[1, row] == rank)
         return jnp.where(hit, moves[2, row], -1)
 
-    here = curve * cross_size + cross
     return (
         landed(curve - 1, curve),
         landed(curve + 1, curve),
@@ -82,18 +81,26 @@
         landed(curve, curve - 1),
         landed(curve + 2, curve + 1),
         landed(curve, curve + 1),
-        jnp.maximum(moves[0, here], 0),
     )
 
 
 def pack_kernel(
-    curve_size,
     cross_size,
-    moves,
-    where,
-    counts,
+    moves_hbm,
+    counts_hbm,
     pops_hbm,
     flags_hbm,
+    neighbours_hbm,
+    cells_hbm,
+    up_hbm,
+    down_hbm,
+    up2_hbm,
+    down2_hbm,
+    inner_hbm,
+    moves,
+    counts,
+    pops,
+    flags,
     neighbours,
     cells,
     up_msg,
@@ -101,21 +108,29 @@
     up2_msg,
     down2_msg,
     inner_msg,
-    pops,
-    flags,
     wide_flags,
     plane_flags,
     site_flags,
     near,
     sems,
 ):
-    flags_copy = pltpu.make_async_copy(flags_hbm, flags, sems.at[SLOTS])
-    flags_copy.start()
-    copies = [
-        pltpu.make_async_copy(pops_hbm.at[s], pops.at[s], sems.at[s]) for s in range(SLOTS)
+    started = []
+
+    def copy(source, target):
+        one = pltpu.make_async_copy(source, target, sems.at[len(started)])
+        one.start()
+        started.append(one)
+        return one
+
+    flags_copy = copy(flags_hbm, flags)
+    copies = [copy(pops_hbm.at[s], pops.at[s]) for s in range(SLOTS)]
+    small = [
+        copy(neighbours_hbm, neighbours),
+        copy(counts_hbm, counts),
+        copy(moves_hbm, moves),
     ]
-    for copy in copies:
-        copy.start()
+    for one in small:
+        one.wait()
 
     near[...] = jnp.zeros_like(near)
     named = neighbours[...]
@@ -172,6 +187,8 @@
             for p, value in enumerate(collided(h, True)):
                 cells[aligned(base + p * 32), :] = value
 
+    cells_copy = copy(cells, cells_hbm)
+
     for y in range(2):
         for msg, x0, first in ((up_msg, 15, 1), (down_msg, 0, 2)):
             step = -1 if x0 else 1
@@ -192,8 +209,8 @@
                 pl.ds(FLAG0 * 32 + row, SLOTS, stride=32), :
             ]
 
-    curve, cross = where[0], where[1]
-    leaving = jnp.maximum(moves[0, curve * cross_size + cross], 0)
+    here = lax.axis_index("curve") * cross_size + lax.axis_index("cross")
+    leaving = jnp.maximum(moves[0, here], 0)
     low = lanes_iota() < 64
     for p in range(POPS):
         for v in range(2):
@@ -215,6 +232,38 @@
                     row = s * POPS * 32 + y * EDGE + k
                     up2_msg[out : out + POPS, :] = cells[pl.ds(row + 13, POPS, stride=32), :]
                     down2_msg[out : out + POPS, :] = cells[pl.ds(row, POPS, stride=32), :]
+
+    last = [
+        copy(up_msg, up_hbm),
+        copy(down_msg, down_hbm),
+        copy(up2_msg, up2_hbm),
+        copy(down2_msg, down2_hbm),
+        copy(inner_msg, inner_hbm),
+    ]
+    cells_copy.wait()
+    for one in last:
+        one.wait()
+
+
+def spread_kernel(
+    curve_size, cross_size, moves, cells, up2_msg, down2_msg, post, outer, own2, landings
+):
+    low = lanes_iota() < 64
+    own2[0 : 6 * GROUP, :] = up2_msg[...]
+    own2[6 * GROUP :, :] = down2_msg[...]
+    for i, slot in enumerate(move_slots(moves, curve_size, cross_size)):
+        landings[i : i + 1, :] = jnp.full((1, 128), slot, jnp.int32)
+    post[NOWHERE:, :] = jnp.full((SLOT, 128), jnp.nan, jnp.float32)
+    for q in range(PLANES):
+        for v in range(2):
+            row = q * 32 + v * 8
+            first, second = cells[row : row + 8, :], cells[row + EDGE : row + EDGE + 8, :]
+            row = q * PLANE + v * 8
+            post[row : row + 8, :] = first
+            post[row + GROUP : row + GROUP + 8, :] = second
+            row = q * GROUP + v * 8
+            outer[row : row + 8, :] = jnp.where(low, first, second)
+    outer[PLANES * GROUP :, :] = cells[PLANES * 32 :, :]
 
 
 def strip_rows(first, row0, step):
@@ -244,33 +293,24 @@
     return pieces
 
 
-def own_strip(cells, slot, y, x):
-    return cells[pl.ds(slot * POPS * 32 + y * EDGE + x, POPS, stride=32), :]
-
-
 def edge_kernel(
-    curve_size,
-    cross_size,
-    moves,
-    where,
-    cells,
+    landings,
+    own_outer,
     low_msg,
     high_msg,
     low2_msg,
     high2_msg,
+    own2,
     north_msg,
     south_msg,
     outer,
 ):
-    from_low, from_high, low_low, low_me, high_high, high_me, leaving = move_slots(
-        moves, where, curve_size, cross_size
-    )
+    from_low, from_high, low_low, low_me, high_high, high_me = (landings[i, 0] for i in range(6))
     low = lanes_iota() < 64
     for q in range(PLANES):
         for v in range(2):
-            first = cells[q * 32 + v * 8 : q * 32 + v * 8 + 8, :]
-            second = cells[q * 32 + EDGE + v * 8 : q * 32 + EDGE + v * 8 + 8, :]
-            outer[q * GROUP + v * 8 : q * GROUP + v * 8 + 8, :] = jnp.where(low, first, second)
+            row = q * GROUP + v * 8
+            outer[row : row + 8, :] = own_outer[row : row + 8, :]
 
     def both(first, second):
         lane = lax.broadcasted_iota(jnp.int32, first.shape, 1)
@@ -293,7 +333,12 @@
                     outer[aligned(base), :] = msg[row : row + 8, :]
 
     for s in range(SLOTS):
-        for slot, msg, row0 in ((low_low, low2_msg, 21), (high_high, high2_msg, 16)):
+        for slot, msg, row0 in (
+            (low_low, low2_msg, 21),
+            (low_me, own2, 21),
+            (high_high, high2_msg, 16),
+            (high_me, own2.at[6 * GROUP :], 16),
+        ):
 
             @pl.when(slot == s)
             def _():
@@ -302,16 +347,6 @@
                         msg[k * GROUP : k * GROUP + POPS, :],
                         msg[(3 + k) * GROUP : (3 + k) * GROUP + POPS, :],
                     )
-
-        for mine in range(SLOTS):
-            for slot, x0, row0 in ((low_me, 13, 21), (high_me, 0, 16)):
-
-                @pl.when((slot == s) & (leaving == mine))
-                def _():
-                    for k in range(3):
-                        outer[pl.ds(s * POPS * GROUP + row0 + k, POPS, stride=GROUP), :] = both(
-                            own_strip(cells, mine, 0, x0 + k), own_strip(cells, mine, 1, x0 + k)
-                        )
 
     for pair in range(PAIRS):
         for v in range(3):
@@ -321,7 +356,7 @@
             out = pair * GROUP + v * 8
             north_msg[out : out + 8, :] = jnp.where(low, second, first)
             south_msg[out : out + 8, :] = jnp.where(low, first, second)
-    tables = (low_msg, TABLE), (cells, PLANES * 32), (high_msg, TABLE)
+    tables = (low_msg, TABLE), (own_outer, PLANES * GROUP), (high_msg, TABLE)
     for i, (ref, row) in enumerate(tables):
         out = EDGE_TABLE + 8 * i
         north_msg[out : out + 8, :] = ref[row : row + 8, :]
@@ -424,16 +459,16 @@
     return post_ref[aligned((FLAG0 + s) * PLANE + row), :] > 0.0
 
 
-def collide_all(h_ref, post_ref):
+def collide_all(h_ref, post_ref, put, chunks):
     @pl.loop(0, SLOTS)
     def _(s):
-        @pl.loop(0, PLANE // 8)
+        @pl.loop(*chunks)
         def _(c):
             base = s * SLOT + c * 8
             is_fluid = fluid_at(post_ref, s, c * 8)
             h = [h_ref[aligned(base + p * PLANE), :] for p in range(POPS)]
             for p, value in enumerate(collided(h, is_fluid)):
-                post_ref[aligned(base + p * PLANE), :] = jnp.where(is_fluid, value, jnp.nan)
+                put(s, c, p, jnp.where(is_fluid, value, jnp.nan))
 
 
 def hide_walls(post_ref):
@@ -546,69 +581,52 @@
             finish(s)
 
 
-def steps_kernel(
-    curve_size,
-    cross_size,
-    moves,
-    where,
-    cells,
+def widen_kernel(
+    landings,
+    own_post,
+    own_outer,
     low_msg,
     high_msg,
     low2_msg,
     high2_msg,
-    low_inner,
-    high_inner,
+    own2,
     south_msg,
     north_msg,
-    out_hbm,
+    post_ref,
+    slots,
+    next_outer,
     h_ref,
-    post_ref,
-    out,
-    slots,
     table,
-    sems,
+    sem,
 ):
     for i in range(3):
         for j, (ref, row) in enumerate(
             (
                 (south_msg, EDGE_TABLE + 8 * i),
-                ((low_msg, TABLE), (cells, PLANES * 32), (high_msg, TABLE))[i],
+                ((low_msg, TABLE), (own_outer, PLANES * GROUP), (high_msg, TABLE))[i],
                 (north_msg, EDGE_TABLE + 8 * i),
             )
         ):
             slot = ref[row : row + 8, :].astype(jnp.int32)
             region = 8 * (3 * i + j)
             slots[region : region + 8, :] = jnp.where(slot == SLOTS, NOWHERE, slot * SLOT)
-    table_copy = pltpu.make_async_copy(slots, table, sems.at[SLOTS])
+    table_copy = pltpu.make_async_copy(slots, table, sem)
     table_copy.start()
 
-    from_low, from_high, low_low, low_me, high_high, high_me, leaving = move_slots(
-        moves, where, curve_size, cross_size
-    )
+    from_low, from_high, low_low, low_me, high_high, high_me = (landings[i, 0] for i in range(6))
     low = lanes_iota() < 64
-    post_ref[NOWHERE:, :] = jnp.full((SLOT, 128), jnp.nan, jnp.float32)
-
-    for q in range(PLANES):
-        for y in range(2):
-            start = q * PLANE + y * GROUP
-            post_ref[start : start + EDGE, :] = cells[
-                q * 32 + y * EDGE : q * 32 + (y + 1) * EDGE, :
-            ]
-    for slot, msg, inner in (
-        (from_low, low_msg, low_inner),
-        (from_high, high_msg, high_inner),
-    ):
+    post_ref[...] = own_post[...]
+    for slot, msg in ((from_low, low_msg), (from_high, high_msg)):
 
         @pl.when(slot >= 0)
         def _():
             for p in range(POPS):
                 for v in range(2):
                     row = p * EDGE + v * 8
-                    outside = msg[row : row + 8, :]
-                    inside = inner[row : row + 8, :]
+                    value = msg[row : row + 8, :]
                     start = slot * SLOT + p * PLANE + v * 8
-                    post_ref[aligned(start), :] = jnp.where(low, outside, inside)
-                    post_ref[aligned(start + GROUP), :] = jnp.where(low, inside, outside)
+                    post_ref[aligned(start), :] = value
+                    post_ref[aligned(start + GROUP), :] = value
 
     for msg, row0, step, first in ((high_msg, 16, 1, 2), (low_msg, 23, -1, 1)):
         for y in range(2):
@@ -616,7 +634,12 @@
                 source += y * LAYERS
                 post_ref[planes(PLANE, row + y * GROUP), :] = msg[source : source + count, :]
     for s in range(SLOTS):
-        for slot, msg, row0 in ((low_low, low2_msg, 21), (high_high, high2_msg, 16)):
+        for slot, msg, row0 in (
+            (low_low, low2_msg, 21),
+            (low_me, own2, 21),
+            (high_high, high2_msg, 16),
+            (high_me, own2.at[6 * GROUP :], 16),
+        ):
 
             @pl.when(slot == s)
             def _():
@@ -628,18 +651,6 @@
                             source : source + POPS, :
                         ]
 
-        for mine in range(SLOTS):
-            for slot, x0, row0 in ((low_me, 13, 21), (high_me, 0, 16)):
-
-                @pl.when((slot == s) & (leaving == mine))
-                def _():
-                    for y in range(2):
-                        for k in range(3):
-                            row = s * SLOT + y * GROUP + row0 + k
-                            post_ref[pl.ds(row, POPS, stride=PLANE), :] = own_strip(
-                                cells, mine, y, x0 + k
-                            )
-
     for pair in range(PAIRS):
         for v in range(3):
             row = pair * GROUP + v * 8
@@ -649,6 +660,46 @@
             post_ref[row + PLANE : row + PLANE + 8, :] = pltpu.roll(
                 jnp.where(low, south, north), 64, axis=1
             )
+
+    hide_walls(post_ref)
+    table_copy.wait()
+    stream_all(post_ref, h_ref, table, (2,), 3)
+
+    def put(s, c, p, value):
+        next_outer[aligned(s * (POPS * GROUP) + p * GROUP + (c - 6) * 8), :] = value
+
+    collide_all(h_ref, post_ref, put, (6, 9))
+
+
+def steps_kernel(
+    landings,
+    table,
+    wide_post,
+    next_outer,
+    low_inner,
+    high_inner,
+    out_hbm,
+    h_ref,
+    post_ref,
+    out,
+    sems,
+):
+    low = lanes_iota() < 64
+    post_ref[...] = wide_post[...]
+    for slot, inner in ((landings[0, 0], low_inner), (landings[1, 0], high_inner)):
+
+        @pl.when(slot >= 0)
+        def _():
+            for v in range(2):
+                fluid = [fluid_at(post_ref, slot, y * GROUP + v * 8) for y in range(2)]
+                for p in range(POPS):
+                    row = p * EDGE + v * 8
+                    value = inner[row : row + 8, :]
+                    for y in range(2):
+                        start = aligned(slot * SLOT + p * PLANE + y * GROUP + v * 8)
+                        is_here = low if y else jnp.logical_not(low)
+                        hidden = jnp.where(fluid[y], value, jnp.nan)
+                        post_ref[start, :] = jnp.where(is_here, hidden, post_ref[start, :])
 
     def finish(s):
         for x in range(EDGE):
@@ -661,11 +712,17 @@
                     ]
         pltpu.make_async_copy(out.at[s], out_hbm.at[s], sems.at[s]).start()
 
-    hide_walls(post_ref)
-    table_copy.wait()
-    for step in range(STEPS - 1):
+    def put(s, c, p, value):
+        post_ref[aligned(s * SLOT + p * PLANE + c * 8), :] = value
+
+    stream_all(post_ref, h_ref, table, (0, 1), 3)
+    collide_all(h_ref, post_ref, put, (0, 6))
+    for q in range(SLOTS * POPS):
+        row = q * PLANE + 2 * GROUP
+        post_ref[row : row + GROUP, :] = next_outer[q * GROUP : (q + 1) * GROUP, :]
+    for _ in range(STEPS - 2):
         stream_all(post_ref, h_ref, table, (0, 1, 2), 3)
-        collide_all(h_ref, post_ref)
+        collide_all(h_ref, post_ref, put, (0, 9))
     stream_all(post_ref, h_ref, table, (0, 1), 2, finish)
     for s in range(SLOTS):
         pltpu.make_async_copy(out.at[s], out_hbm.at[s], sems.at[s]).wait()
@@ -698,35 +755,35 @@
 
 
 def per_device(populations, site_flags, neighbours, migrations, counts):
-    curve_size = lax.axis_size("curve")
-    cross_size = lax.axis_size("cross")
-    curve = lax.axis_index("curve")
-    cross = lax.axis_index("cross")
-    where = jnp.stack([curve, cross]).astype(jnp.int32)
+    sizes = (lax.axis_size("curve"), lax.axis_size("cross"))
     moves = migrations.T
-
-    sizes = (curve_size, cross_size)
+    floats = lambda rows: pltpu.VMEM((rows, 128), jnp.float32)
+    messages = [
+        PLANES * 32 + 8,
+        STRIPS + 2 * LAYERS,
+        STRIPS + 2 * LAYERS,
+        6 * GROUP,
+        6 * GROUP,
+        HALF,
+    ]
     cells, up_msg, down_msg, up2_msg, down2_msg, inner_msg = call(
-        functools.partial(pack_kernel, *sizes),
-        "SSSHHV",
-        "VVVVVV",
+        functools.partial(pack_kernel, sizes[1]),
+        "HHHHH",
+        "HHHHHH",
+        [rows128(rows) for rows in messages],
+        (moves, counts, populations, site_flags, neighbours),
         [
-            rows128(PLANES * 32 + 8),
-            rows128(STRIPS + 2 * LAYERS),
-            rows128(STRIPS + 2 * LAYERS),
-            rows128(6 * GROUP),
-            rows128(6 * GROUP),
-            rows128(HALF),
-        ],
-        (moves, where, counts, populations, site_flags, neighbours),
-        [
+            pltpu.SMEM(moves.shape, jnp.int32),
+            pltpu.SMEM(counts.shape, jnp.int32),
             pltpu.VMEM(populations.shape, jnp.float32),
             pltpu.VMEM(site_flags.shape, jnp.int32),
+            pltpu.VMEM(neighbours.shape, jnp.int32),
+            *[floats(rows) for rows in messages],
             pltpu.VMEM((8, 5888), jnp.float32),
             pltpu.VMEM((128, 384), jnp.bfloat16),
-            pltpu.VMEM((256, 128), jnp.float32),
-            pltpu.VMEM((8, 128), jnp.float32),
-            pltpu.SemaphoreType.DMA((SLOTS + 1,)),
+            floats(256),
+            floats(8),
+            pltpu.SemaphoreType.DMA((4 + SLOTS + 6,)),
         ],
         WIDE_LIMIT,
     )
@@ -736,41 +793,57 @@
     high2_msg = shifted_from(down2_msg, "curve", -2)
     low_inner = shifted_from(inner_msg, "curve", 1)
     high_inner = shifted_from(inner_msg, "curve", -1)
+    post, outer, own2, landings = call(
+        functools.partial(spread_kernel, *sizes),
+        "SVVV",
+        "VVVV",
+        [
+            rows128(NOWHERE + SLOT),
+            rows128(PLANES * GROUP + 8),
+            rows128(12 * GROUP),
+            jax.ShapeDtypeStruct((8, 128), jnp.int32),
+        ],
+        (moves, cells, up2_msg, down2_msg),
+        [],
+    )
+    strips = (low_msg, high_msg, low2_msg, high2_msg, own2)
     north_msg, south_msg = call(
-        functools.partial(edge_kernel, *sizes),
-        "SSVVVVV",
+        edge_kernel,
+        "SVVVVVV",
         "VV",
         [rows128(PAIRS * GROUP + 24), rows128(PAIRS * GROUP + 24)],
-        (moves, where, cells, low_msg, high_msg, low2_msg, high2_msg),
-        [pltpu.VMEM((PLANES * GROUP, 128), jnp.float32)],
+        (landings, outer, *strips),
+        [floats(PLANES * GROUP)],
     )
     from_south = shifted_from(north_msg, "cross", 1)
     from_north = shifted_from(south_msg, "cross", -1)
+    post, table, next_outer = call(
+        widen_kernel,
+        "SVVVVVVVVV",
+        "VVV",
+        [
+            rows128(NOWHERE + SLOT),
+            jax.ShapeDtypeStruct((72, 128), jnp.int32),
+            rows128(SLOTS * POPS * GROUP),
+        ],
+        (landings, post, outer, *strips, from_south, from_north),
+        [
+            floats(SLOTS * SLOT),
+            pltpu.SMEM((72, 128), jnp.int32),
+            pltpu.SemaphoreType.DMA,
+        ],
+    )
     return call(
-        functools.partial(steps_kernel, *sizes),
-        "SSVVVVVVVVV",
+        steps_kernel,
+        "SSVVVV",
         "H",
         [jax.ShapeDtypeStruct(populations.shape, jnp.float32)],
-        (
-            moves,
-            where,
-            cells,
-            low_msg,
-            high_msg,
-            low2_msg,
-            high2_msg,
-            low_inner,
-            high_inner,
-            from_south,
-            from_north,
-        ),
+        (landings, table, post, next_outer, low_inner, high_inner),
         [
-            pltpu.VMEM((SLOTS * SLOT, 128), jnp.float32),
-            pltpu.VMEM((NOWHERE + SLOT, 128), jnp.float32),
+            floats(SLOTS * SLOT),
+            floats(NOWHERE + SLOT),
             pltpu.VMEM(populations.shape, jnp.float32),
-            pltpu.VMEM((72, 128), jnp.int32),
-            pltpu.SMEM((72, 128), jnp.int32),
-            pltpu.SemaphoreType.DMA((SLOTS + 1,)),
+            pltpu.SemaphoreType.DMA((SLOTS,)),
         ],
     )[0]
 

time: 51.3 us -> 48.5 us (0.945)
  the two profiles are of different devices: /device:TPU:18 before, /device:TPU:22 now
where the time goes in v3:
time: 48.5 us; the launch traced here: 48.1 us
  starting transfers between devices  23.5 us (48%)
  Pallas kernels  15.3 us (32%)
  waiting for transfers between devices  4.86 us (10%)
  local copies, waits for them, and re-layouts  3.65 us (8%)
  between operations  0.8 us (2%)
    ppermute x8, starting transfers between devices, shifted_from(): return lax.ppermute(value, axis, pairs)  23.5 us
    pallas_call x5, Pallas kernels, call(): pl.pallas_call(kernel, out_shape=outs, in_specs=[spaces[x] for x in in_sp...  15.3 us
    ppermute x8, waiting for transfers between devices, shifted_from(): return lax.ppermute(value, axis, pairs)  4.86 us
    unnamed x8, local copies, waits for them, and re-layouts  3.65 us
  transfers between devices with their start and end apart: 8, of which 2 were waited for; matrix products, arithmetic and copies ran while one was open for 0% of the time, Pallas kernels for 7%

profile of v3, /device:TPU:22, one launch (start us, length us, event | category | flops | bytes accessed | tf_op | source)
XLA Modules:
  0.0 48.1 jit_solution(5008591779058258596)
XLA Ops:
  0.7 4.1 %shard_map.55 = (f32[1928,128]{1,0:T(8,128)}, f32[588,128]{1,0:T(8,128)}, f32[588,128]{1,0:T(8,128)}, f32[144,128]{1,0:T(8,128)}, f32[144,128]{1,0:T(8,128)}, /*index=5*/f32[304,128]{1,0:T(8,128)}) custom-call(s32[3,32]{1,0:T(4,128)} %bitcast.1, s32[1]{0:T(128)S(6)} %copy.6.counts_hbm, f32[3,19,4096]{2,1,0:T(8,128)} %pops_hbm.1, s32[3,5832]{1,0:T(4,128)} %flags_hbm.1, ...), custom_call_target="tpu_custom_call" | custom-call | tf_op jit(solution)/shard_map/pallas_call | solution.py:747
  4.8 3.4 %collective-permute-start = (f32[588,128]{1,0:T(8,128)}, f32[588,128]{1,0:T(8,128)S(1)}, u32[]{:S(2)}, u32[]{:S(2)}) collective-permute-start(f32[588,128]{1,0:T(8,128)} %get-tuple-element.26), channel_id=1, source_target_pairs={{0,4},{4,8},{8,12},{12,16},{16,20},{20,24},{24,28},{1,5},{5,9},{9,... | collective-permute-start | bytes 903176 | tf_op jit(solution)/shard_map/ppermute | solution.py:734
  8.2 2.4 %collective-permute-start.1 = (f32[588,128]{1,0:T(8,128)}, f32[588,128]{1,0:T(8,128)S(1)}, u32[]{:S(2)}, u32[]{:S(2)}) collective-permute-start(f32[588,128]{1,0:T(8,128)} %get-tuple-element.27), channel_id=1, source_target_pairs={{4,0},{8,4},{12,8},{16,12},{20,16},{24,20},{28,24},{5,1},{9,5},{13... | collective-permute-start | bytes 903176 | tf_op jit(solution)/shard_map/ppermute | solution.py:734
  10.6 3.5 %collective-permute-start.2 = (f32[144,128]{1,0:T(8,128)}, f32[144,128]{1,0:T(8,128)S(1)}, u32[]{:S(2)}, u32[]{:S(2)}) collective-permute-start(f32[144,128]{1,0:T(8,128)} %get-tuple-element.21.up2_msg), channel_id=1, source_target_pairs={{0,8},{4,12},{8,16},{12,20},{16,24},{20,28},{1,9},{5,13},{9,17},{1... | collective-permute-start | bytes 221192 | tf_op jit(solution)/shard_map/ppermute | solution.py:734
  14.1 2.3 %collective-permute-start.3 = (f32[144,128]{1,0:T(8,128)}, f32[144,128]{1,0:T(8,128)S(1)}, u32[]{:S(2)}, u32[]{:S(2)}) collective-permute-start(f32[144,128]{1,0:T(8,128)} %get-tuple-element.22.down2_msg), channel_id=1, source_target_pairs={{8,0},{12,4},{16,8},{20,12},{24,16},{28,20},{9,1},{13,5},{17,9},{2... | collective-permute-start | bytes 221192 | tf_op jit(solution)/shard_map/ppermute | solution.py:734
  16.5 0.0 copy-start
  16.5 1.2 %copy-done = f32[1928,128]{1,0:T(8,128)S(1)} copy-done((f32[1928,128]{1,0:T(8,128)S(1)}, f32[1928,128]{1,0:T(8,128)}, u32[]{:S(2)}) %copy-start) | copy-done | bytes 987160
  17.7 0.0 copy-start.1
  17.7 0.9 %copy-done.1 = f32[144,128]{1,0:T(8,128)S(1)} copy-done((f32[144,128]{1,0:T(8,128)S(1)}, f32[144,128]{1,0:T(8,128)}, u32[]{:S(2)}) %copy-start.1) | copy-done | bytes 73752
  18.6 0.0 copy-start.2
  18.6 0.9 %copy-done.2 = f32[144,128]{1,0:T(8,128)S(1)} copy-done((f32[144,128]{1,0:T(8,128)S(1)}, f32[144,128]{1,0:T(8,128)}, u32[]{:S(2)}) %copy-start.2) | copy-done | bytes 73752
  19.5 0.0 copy-start.3
  19.5 0.7 %copy-done.3 = s32[32,3]{0,1:T(4,128)S(1)} copy-done((s32[32,3]{0,1:T(4,128)S(1)}, s32[32,3]{0,1:T(4,128)}, u32[]{:S(2)}) %copy-start.3) | copy-done | bytes 408
  20.1 0.7 %shard_map.56 = (f32[5688,128]{1,0:T(8,128)S(1)}, f32[1448,128]{1,0:T(8,128)S(1)}, f32[288,128]{1,0:T(8,128)S(1)}, s32[8,128]{1,0:T(8,128)S(1)}) custom-call(s32[3,32]{1,0:T(4,128)S(1)} %bitcast.2, f32[1928,128]{1,0:T(8,128)S(1)} %copy-done, f32[144,128]{1,0:T(8,128)S(1)} %copy-done.2, f32[144,128]{1,0:T(8,128)S(1)} %copy-done.1), custom_call_target="tpu_custom_call" | custom-call | tf_op jit(solution)/shard_map/pallas_call | solution.py:747
  20.9 0.0 collective-permute-done.2.low2_msg
  20.9 0.0 collective-permute-done.3.high2_msg
  20.9 1.4 %collective-permute-done.low_msg = f32[588,128]{1,0:T(8,128)S(1)} collective-permute-done((f32[588,128]{1,0:T(8,128)}, f32[588,128]{1,0:T(8,128)S(1)}, u32[]{:S(2)}, u32[]{:S(2)}) %collective-permute-start) | collective-permute-done | bytes 301088 | tf_op jit(solution)/shard_map/ppermute | solution.py:734
  22.3 0.0 collective-permute-done.1.high_msg
  22.3 0.9 %shard_map.57 = (f32[744,128]{1,0:T(8,128)S(1)}, f32[744,128]{1,0:T(8,128)S(1)}) custom-call(s32[8,128]{1,0:T(8,128)S(1)} %get-tuple-element.23.landings, f32[1448,128]{1,0:T(8,128)S(1)} %get-tuple-element.25.own_outer, f32[588,128]{1,0:T(8,128)S(1)} %collective-permute-done.low_msg, f32[588,128]{1,0:T(8,128)S(1)} %collective-permute-done.1.high_msg, ...), custom_call_target="tpu_custom_call" | custom-call | tf_op jit(solution)/shard_map/pallas_call | solution.py:747
  23.2 1.9 %collective-permute-start.4 = (f32[744,128]{1,0:T(8,128)S(1)}, f32[744,128]{1,0:T(8,128)S(1)}, u32[]{:S(2)}, u32[]{:S(2)}) collective-permute-start(f32[744,128]{1,0:T(8,128)S(1)} %get-tuple-element.29), channel_id=1, source_target_pairs={{0,1},{1,2},{2,3},{4,5},{5,6},{6,7},{8,9},{9,10},{10,11},{12,13},{... | collective-permute-start | bytes 1142792 | tf_op jit(solution)/shard_map/ppermute | solution.py:734
  25.1 3.6 %collective-permute-start.5 = (f32[744,128]{1,0:T(8,128)S(1)}, f32[744,128]{1,0:T(8,128)S(1)}, u32[]{:S(2)}, u32[]{:S(2)}) collective-permute-start(f32[744,128]{1,0:T(8,128)S(1)} %get-tuple-element.30), channel_id=1, source_target_pairs={{1,0},{2,1},{3,2},{5,4},{6,5},{7,6},{9,8},{10,9},{11,10},{13,12},{... | collective-permute-start | bytes 1142792 | tf_op jit(solution)/shard_map/ppermute | solution.py:734
  28.8 4.3 %collective-permute-start.6 = (f32[304,128]{1,0:T(8,128)}, f32[304,128]{1,0:T(8,128)S(1)}, u32[]{:S(2)}, u32[]{:S(2)}) collective-permute-start(f32[304,128]{1,0:T(8,128)} %get-tuple-element.34), channel_id=1, source_target_pairs={{0,4},{4,8},{8,12},{12,16},{16,20},{20,24},{24,28},{1,5},{5,9},{9,... | collective-permute-start | bytes 466952 | tf_op jit(solution)/shard_map/ppermute | solution.py:734
  33.1 1.9 %collective-permute-start.7 = (f32[304,128]{1,0:T(8,128)}, f32[304,128]{1,0:T(8,128)S(1)}, u32[]{:S(2)}, u32[]{:S(2)}) collective-permute-start(f32[304,128]{1,0:T(8,128)} %get-tuple-element.34), channel_id=1, source_target_pairs={{4,0},{8,4},{12,8},{16,12},{20,16},{24,20},{28,24},{5,1},{9,5},{13... | collective-permute-start | bytes 466952 | tf_op jit(solution)/shard_map/ppermute | solution.py:734
  35.1 0.0 collective-permute-done.4.south_msg
  35.1 0.0 collective-permute-done.5.north_msg
  35.1 2.8 %shard_map.58 = (f32[5688,128]{1,0:T(8,128)S(1)}, s32[72,128]{1,0:T(8,128)S(1)}, f32[1368,128]{1,0:T(8,128)S(1)}) custom-call(s32[8,128]{1,0:T(8,128)S(1)} %get-tuple-element.23.landings, f32[5688,128]{1,0:T(8,128)S(1)} %get-tuple-element.24.own_post, f32[1448,128]{1,0:T(8,128)S(1)} %get-tuple-element.25.own_outer, ...), custom_call_target="tpu_custom_call" | custom-call | tf_op jit(solution)/shard_map/pallas_call | solution.py:747
  37.9 0.0 collective-permute-done.6.low_inner
  37.9 3.4 %collective-permute-done.7.high_inner = f32[304,128]{1,0:T(8,128)S(1)} collective-permute-done((f32[304,128]{1,0:T(8,128)}, f32[304,128]{1,0:T(8,128)S(1)}, u32[]{:S(2)}, u32[]{:S(2)}) %collective-permute-start.7) | collective-permute-done | bytes 155680 | tf_op jit(solution)/shard_map/ppermute | solution.py:734
  41.4 6.7 %shard_map.59 = f32[3,19,4096]{2,1,0:T(8,128)} custom-call(s32[8,128]{1,0:T(8,128)S(1)} %get-tuple-element.23.landings, s32[72,128]{1,0:T(8,128)S(1)} %get-tuple-element.31.table, f32[5688,128]{1,0:T(8,128)S(1)} %get-tuple-element.32.wide_post, f32[1368,128]{1,0:T(8,128)S(1)} %get-tuple-element.33.next_outer, ...), custom_call_target="tpu_custom_call" | custom-call | tf_op jit(solution)/shard_map/pallas_call | solution.py:747
Async XLA Ops:
  4.8 17.5 %collective-permute-start = (f32[588,128]{1,0:T(8,128)}, f32[588,128]{1,0:T(8,128)S(1)}, u32[]{:S(2)}, u32[]{:S(2)}) collective-permute-start(f32[588,128]{1,0:T(8,128)} %get-tuple-element.26), channel_id=1, source_target_pairs={{0,4},{4,8},{8,12},{12,16},{16,20},{20,24},{24,28},{1,5},{5,9},{9,... | collective-permute-start | bytes 903176 | tf_op jit(solution)/shard_map/ppermute | solution.py:734
  8.2 14.1 %collective-permute-start.1 = (f32[588,128]{1,0:T(8,128)}, f32[588,128]{1,0:T(8,128)S(1)}, u32[]{:S(2)}, u32[]{:S(2)}) collective-permute-start(f32[588,128]{1,0:T(8,128)} %get-tuple-element.27), channel_id=1, source_target_pairs={{4,0},{8,4},{12,8},{16,12},{20,16},{24,20},{28,24},{5,1},{9,5},{13... | collective-permute-start | bytes 903176 | tf_op jit(solution)/shard_map/ppermute | solution.py:734
  10.6 10.2 %collective-permute-start.2 = (f32[144,128]{1,0:T(8,128)}, f32[144,128]{1,0:T(8,128)S(1)}, u32[]{:S(2)}, u32[]{:S(2)}) collective-permute-start(f32[144,128]{1,0:T(8,128)} %get-tuple-element.21.up2_msg), channel_id=1, source_target_pairs={{0,8},{4,12},{8,16},{12,20},{16,24},{20,28},{1,9},{5,13},{9,17},{1... | collective-permute-start | bytes 221192 | tf_op jit(solution)/shard_map/ppermute | solution.py:734
  14.1 6.7 %collective-permute-start.3 = (f32[144,128]{1,0:T(8,128)}, f32[144,128]{1,0:T(8,128)S(1)}, u32[]{:S(2)}, u32[]{:S(2)}) collective-permute-start(f32[144,128]{1,0:T(8,128)} %get-tuple-element.22.down2_msg), channel_id=1, source_target_pairs={{8,0},{12,4},{16,8},{20,12},{24,16},{28,20},{9,1},{13,5},{17,9},{2... | collective-permute-start | bytes 221192 | tf_op jit(solution)/shard_map/ppermute | solution.py:734
  16.5 1.2 %copy-start = (f32[1928,128]{1,0:T(8,128)S(1)}, f32[1928,128]{1,0:T(8,128)}, u32[]{:S(2)}) copy-start(f32[1928,128]{1,0:T(8,128)} %get-tuple-element.20.cells) | copy-start | bytes 2961412
  17.7 0.9 %copy-start.1 = (f32[144,128]{1,0:T(8,128)S(1)}, f32[144,128]{1,0:T(8,128)}, u32[]{:S(2)}) copy-start(f32[144,128]{1,0:T(8,128)} %get-tuple-element.22.down2_msg) | copy-start | bytes 221188
  18.6 0.9 %copy-start.2 = (f32[144,128]{1,0:T(8,128)S(1)}, f32[144,128]{1,0:T(8,128)}, u32[]{:S(2)}) copy-start(f32[144,128]{1,0:T(8,128)} %get-tuple-element.21.up2_msg) | copy-start | bytes 221188
  19.5 0.7 %copy-start.3 = (s32[32,3]{0,1:T(4,128)S(1)}, s32[32,3]{0,1:T(4,128)}, u32[]{:S(2)}) copy-start(s32[32,3]{0,1:T(4,128)} %param.8) | copy-start | bytes 1156
  23.2 11.8 %collective-permute-start.4 = (f32[744,128]{1,0:T(8,128)S(1)}, f32[744,128]{1,0:T(8,128)S(1)}, u32[]{:S(2)}, u32[]{:S(2)}) collective-permute-start(f32[744,128]{1,0:T(8,128)S(1)} %get-tuple-element.29), channel_id=1, source_target_pairs={{0,1},{1,2},{2,3},{4,5},{5,6},{6,7},{8,9},{9,10},{10,11},{12,13},{... | collective-permute-start | bytes 1142792 | tf_op jit(solution)/shard_map/ppermute | solution.py:734
  25.1 9.9 %collective-permute-start.5 = (f32[744,128]{1,0:T(8,128)S(1)}, f32[744,128]{1,0:T(8,128)S(1)}, u32[]{:S(2)}, u32[]{:S(2)}) collective-permute-start(f32[744,128]{1,0:T(8,128)S(1)} %get-tuple-element.30), channel_id=1, source_target_pairs={{1,0},{2,1},{3,2},{5,4},{6,5},{7,6},{9,8},{10,9},{11,10},{13,12},{... | collective-permute-start | bytes 1142792 | tf_op jit(solution)/shard_map/ppermute | solution.py:734
  28.8 9.1 %collective-permute-start.6 = (f32[304,128]{1,0:T(8,128)}, f32[304,128]{1,0:T(8,128)S(1)}, u32[]{:S(2)}, u32[]{:S(2)}) collective-permute-start(f32[304,128]{1,0:T(8,128)} %get-tuple-element.34), channel_id=1, source_target_pairs={{0,4},{4,8},{8,12},{12,16},{16,20},{20,24},{24,28},{1,5},{5,9},{9,... | collective-permute-start | bytes 466952 | tf_op jit(solution)/shard_map/ppermute | solution.py:734
  33.1 8.2 %collective-permute-start.7 = (f32[304,128]{1,0:T(8,128)}, f32[304,128]{1,0:T(8,128)S(1)}, u32[]{:S(2)}, u32[]{:S(2)}) collective-permute-start(f32[304,128]{1,0:T(8,128)} %get-tuple-element.34), channel_id=1, source_target_pairs={{4,0},{8,4},{12,8},{16,12},{20,16},{24,20},{28,24},{5,1},{9,5},{13... | collective-permute-start | bytes 466952 | tf_op jit(solution)/shard_map/ppermute | solution.py:734

commit v4 on v3

--- a/solution.py
+++ b/solution.py
@@ -180,7 +180,7 @@
 
     @pl.loop(0, SLOTS)
     def _(s):
-        @pl.loop(0, 4)
+        @pl.loop(0, 4, unroll=2)
         def _(c):
             base = s * (POPS * 32) + c * 8
             h = [cells[aligned(base + p * 32), :] for p in range(POPS)]
@@ -301,6 +301,7 @@
     low2_msg,
     high2_msg,
     own2,
+    mate_inner,
     north_msg,
     south_msg,
     outer,
@@ -462,7 +463,7 @@
 def collide_all(h_ref, post_ref, put, chunks):
     @pl.loop(0, SLOTS)
     def _(s):
-        @pl.loop(*chunks)
+        @pl.loop(*chunks, unroll=3)
         def _(c):
             base = s * SLOT + c * 8
             is_fluid = fluid_at(post_ref, s, c * 8)
@@ -676,8 +677,8 @@
     table,
     wide_post,
     next_outer,
-    low_inner,
-    high_inner,
+    mate_inner,
+    passed_inner,
     out_hbm,
     h_ref,
     post_ref,
@@ -686,9 +687,16 @@
 ):
     low = lanes_iota() < 64
     post_ref[...] = wide_post[...]
-    for slot, inner in ((landings[0, 0], low_inner), (landings[1, 0], high_inner)):
-
-        @pl.when(slot >= 0)
+    odd = lax.rem(lax.axis_index("curve"), 2) == 1
+    even = jnp.logical_not(odd)
+    for slot, wanted, inner in (
+        (landings[0, 0], odd, mate_inner),
+        (landings[0, 0], even, passed_inner),
+        (landings[1, 0], even, mate_inner),
+        (landings[1, 0], odd, passed_inner),
+    ):
+
+        @pl.when((slot >= 0) & wanted)
         def _():
             for v in range(2):
                 fluid = [fluid_at(post_ref, slot, y * GROUP + v * 8) for y in range(2)]
@@ -791,8 +799,12 @@
     high_msg = shifted_from(down_msg, "curve", -1)
     low2_msg = shifted_from(up2_msg, "curve", 2)
     high2_msg = shifted_from(down2_msg, "curve", -2)
-    low_inner = shifted_from(inner_msg, "curve", 1)
-    high_inner = shifted_from(inner_msg, "curve", -1)
+    assert sizes[0] % 2 == 0
+    pairs = [(i, i ^ 1) for i in range(sizes[0])]
+    mate_inner = lax.ppermute(inner_msg, "curve", pairs)
+    pairs = [(i, i - 2 if i % 2 else i + 2) for i in range(sizes[0])]
+    pairs = [pair for pair in pairs if 0 <= pair[1] < sizes[0]]
+    passed_inner = lax.ppermute(mate_inner, "curve", pairs)
     post, outer, own2, landings = call(
         functools.partial(spread_kernel, *sizes),
         "SVVV",
@@ -809,10 +821,10 @@
     strips = (low_msg, high_msg, low2_msg, high2_msg, own2)
     north_msg, south_msg = call(
         edge_kernel,
-        "SVVVVVV",
+        "SVVVVVVV",
         "VV",
         [rows128(PAIRS * GROUP + 24), rows128(PAIRS * GROUP + 24)],
-        (landings, outer, *strips),
+        (landings, outer, *strips, mate_inner),
         [floats(PLANES * GROUP)],
     )
     from_south = shifted_from(north_msg, "cross", 1)
@@ -838,7 +850,7 @@
         "SSVVVV",
         "H",
         [jax.ShapeDtypeStruct(populations.shape, jnp.float32)],
-        (landings, table, post, next_outer, low_inner, high_inner),
+        (landings, table, post, next_outer, mate_inner, passed_inner),
         [
             floats(SLOTS * SLOT),
             floats(NOWHERE + SLOT),

time: 48.5 us -> 49.7 us (1.025)
  the two profiles are of different devices: /device:TPU:22 before, /device:TPU:25 now
where the time goes in v4:
time: 49.7 us; the launch traced here: 49.3 us
  starting transfers between devices  18.6 us (37%)
  Pallas kernels  15 us (30%)
  waiting for transfers between devices  11.4 us (23%)
  local copies, waits for them, and re-layouts  3.65 us (7%)
  between operations  0.78 us (2%)
    ppermute x6, starting transfers between devices, shifted_from(): return lax.ppermute(value, axis, pairs)  16.9 us
    pallas_call x5, Pallas kernels, call(): pl.pallas_call(kernel, out_shape=outs, in_specs=[spaces[x] for x in in_sp...  15 us
    ppermute x6, waiting for transfers between devices, shifted_from(): return lax.ppermute(value, axis, pairs)  5.75 us
    ppermute x1, waiting for transfers between devices, per_device(): mate_inner = lax.ppermute(inner_msg, 'curve', pairs)  5.63 us
    unnamed x8, local copies, waits for them, and re-layouts  3.65 us
    ppermute x1, starting transfers between devices, per_device(): passed_inner = lax.ppermute(mate_inner, 'curve', pairs)  1.29 us
  transfers between devices with their start and end apart: 8, of which 3 were waited for; matrix products, arithmetic and copies ran while one was open for 0% of the time, Pallas kernels for 7%

profile of v4, /device:TPU:25, one launch (start us, length us, event | category | flops | bytes accessed | tf_op | source)
XLA Modules:
  0.0 49.3 jit_solution(11608844030259029732)
XLA Ops:
  0.7 4.0 %shard_map.55 = (f32[1928,128]{1,0:T(8,128)}, f32[588,128]{1,0:T(8,128)}, f32[588,128]{1,0:T(8,128)}, f32[144,128]{1,0:T(8,128)}, f32[144,128]{1,0:T(8,128)}, /*index=5*/f32[304,128]{1,0:T(8,128)}) custom-call(s32[3,32]{1,0:T(4,128)} %bitcast.1, s32[1]{0:T(128)S(6)} %copy.6.counts_hbm, f32[3,19,4096]{2,1,0:T(8,128)} %pops_hbm.1, s32[3,5832]{1,0:T(4,128)} %flags_hbm.1, ...), custom_call_target="tpu_custom_call" | custom-call | tf_op jit(solution)/shard_map/pallas_call | solution.py:755
  4.7 3.1 %collective-permute-start = (f32[588,128]{1,0:T(8,128)}, f32[588,128]{1,0:T(8,128)S(1)}, u32[]{:S(2)}, u32[]{:S(2)}) collective-permute-start(f32[588,128]{1,0:T(8,128)} %get-tuple-element.26), channel_id=1, source_target_pairs={{0,4},{4,8},{8,12},{12,16},{16,20},{20,24},{24,28},{1,5},{5,9},{9,... | collective-permute-start | bytes 903176 | tf_op jit(solution)/shard_map/ppermute | solution.py:742
  7.9 3.0 %collective-permute-start.1 = (f32[588,128]{1,0:T(8,128)}, f32[588,128]{1,0:T(8,128)S(1)}, u32[]{:S(2)}, u32[]{:S(2)}) collective-permute-start(f32[588,128]{1,0:T(8,128)} %get-tuple-element.27), channel_id=1, source_target_pairs={{4,0},{8,4},{12,8},{16,12},{20,16},{24,20},{28,24},{5,1},{9,5},{13... | collective-permute-start | bytes 903176 | tf_op jit(solution)/shard_map/ppermute | solution.py:742
  10.9 0.4 collective-permute-start.4
  11.3 1.3 %collective-permute-start.2 = (f32[144,128]{1,0:T(8,128)}, f32[144,128]{1,0:T(8,128)S(1)}, u32[]{:S(2)}, u32[]{:S(2)}) collective-permute-start(f32[144,128]{1,0:T(8,128)} %get-tuple-element.21.up2_msg), channel_id=1, source_target_pairs={{0,8},{4,12},{8,16},{12,20},{16,24},{20,28},{1,9},{5,13},{9,17},{1... | collective-permute-start | bytes 221192 | tf_op jit(solution)/shard_map/ppermute | solution.py:742
  12.6 4.0 %collective-permute-start.3 = (f32[144,128]{1,0:T(8,128)}, f32[144,128]{1,0:T(8,128)S(1)}, u32[]{:S(2)}, u32[]{:S(2)}) collective-permute-start(f32[144,128]{1,0:T(8,128)} %get-tuple-element.22.down2_msg), channel_id=1, source_target_pairs={{8,0},{12,4},{16,8},{20,12},{24,16},{28,20},{9,1},{13,5},{17,9},{2... | collective-permute-start | bytes 221192 | tf_op jit(solution)/shard_map/ppermute | solution.py:742
  16.6 0.0 copy-start
  16.6 1.2 %copy-done = f32[1928,128]{1,0:T(8,128)S(1)} copy-done((f32[1928,128]{1,0:T(8,128)S(1)}, f32[1928,128]{1,0:T(8,128)}, u32[]{:S(2)}) %copy-start) | copy-done | bytes 987160
  17.8 0.0 copy-start.1
  17.8 0.9 %copy-done.1 = f32[144,128]{1,0:T(8,128)S(1)} copy-done((f32[144,128]{1,0:T(8,128)S(1)}, f32[144,128]{1,0:T(8,128)}, u32[]{:S(2)}) %copy-start.1) | copy-done | bytes 73752
  18.7 0.0 copy-start.2
  18.7 0.9 %copy-done.2 = f32[144,128]{1,0:T(8,128)S(1)} copy-done((f32[144,128]{1,0:T(8,128)S(1)}, f32[144,128]{1,0:T(8,128)}, u32[]{:S(2)}) %copy-start.2) | copy-done | bytes 73752
  19.6 0.0 copy-start.3
  19.6 0.7 %copy-done.3 = s32[32,3]{0,1:T(4,128)S(1)} copy-done((s32[32,3]{0,1:T(4,128)S(1)}, s32[32,3]{0,1:T(4,128)}, u32[]{:S(2)}) %copy-start.3) | copy-done | bytes 408
  20.3 0.7 %shard_map.56 = (f32[5688,128]{1,0:T(8,128)S(1)}, f32[1448,128]{1,0:T(8,128)S(1)}, f32[288,128]{1,0:T(8,128)S(1)}, s32[8,128]{1,0:T(8,128)S(1)}) custom-call(s32[3,32]{1,0:T(4,128)S(1)} %bitcast.2, f32[1928,128]{1,0:T(8,128)S(1)} %copy-done, f32[144,128]{1,0:T(8,128)S(1)} %copy-done.2, f32[144,128]{1,0:T(8,128)S(1)} %copy-done.1), custom_call_target="tpu_custom_call" | custom-call | tf_op jit(solution)/shard_map/pallas_call | solution.py:755
  21.0 0.0 collective-permute-done.2.low2_msg
  21.0 0.0 collective-permute-done.3.high2_msg
  21.0 5.6 %collective-permute-done.4.mate_inner = f32[304,128]{1,0:T(8,128)S(1)} collective-permute-done((f32[304,128]{1,0:T(8,128)}, f32[304,128]{1,0:T(8,128)S(1)}, u32[]{:S(2)}, u32[]{:S(2)}) %collective-permute-start.4) | collective-permute-done | bytes 155680 | tf_op jit(solution)/shard_map/ppermute | solution.py:804
  26.6 0.0 collective-permute-done.low_msg
  26.6 0.0 collective-permute-done.1.high_msg
  26.7 0.9 %shard_map.57 = (f32[744,128]{1,0:T(8,128)S(1)}, f32[744,128]{1,0:T(8,128)S(1)}) custom-call(s32[8,128]{1,0:T(8,128)S(1)} %get-tuple-element.23.landings, f32[1448,128]{1,0:T(8,128)S(1)} %get-tuple-element.25.own_outer, f32[588,128]{1,0:T(8,128)S(1)} %collective-permute-done.low_msg, f32[588,128]{1,0:T(8,128)S(1)} %collective-permute-done.1.high_msg, ...), custom_call_target="tpu_custom_call" | custom-call | tf_op jit(solution)/shard_map/pallas_call | solution.py:755
  27.6 3.5 %collective-permute-start.5 = (f32[744,128]{1,0:T(8,128)S(1)}, f32[744,128]{1,0:T(8,128)S(1)}, u32[]{:S(2)}, u32[]{:S(2)}) collective-permute-start(f32[744,128]{1,0:T(8,128)S(1)} %get-tuple-element.30), channel_id=1, source_target_pairs={{0,1},{1,2},{2,3},{4,5},{5,6},{6,7},{8,9},{9,10},{10,11},{12,13},{... | collective-permute-start | bytes 1142792 | tf_op jit(solution)/shard_map/ppermute | solution.py:742
  31.1 1.9 %collective-permute-start.6 = (f32[744,128]{1,0:T(8,128)S(1)}, f32[744,128]{1,0:T(8,128)S(1)}, u32[]{:S(2)}, u32[]{:S(2)}) collective-permute-start(f32[744,128]{1,0:T(8,128)S(1)} %get-tuple-element.31), channel_id=1, source_target_pairs={{1,0},{2,1},{3,2},{5,4},{6,5},{7,6},{9,8},{10,9},{11,10},{13,12},{... | collective-permute-start | bytes 1142792 | tf_op jit(solution)/shard_map/ppermute | solution.py:742
  33.0 1.3 %collective-permute-start.7 = (f32[304,128]{1,0:T(8,128)S(1)}, f32[304,128]{1,0:T(8,128)S(1)}, u32[]{:S(2)}, u32[]{:S(2)}) collective-permute-start(f32[304,128]{1,0:T(8,128)S(1)} %collective-permute-done.4.mate_inner), channel_id=1, source_target_pairs={{0,8},{8,16},{12,4},{16,24},{20,12},{28,20},{1,9},{9,17},{13,5},{1... | collective-permute-start | bytes 466952 | tf_op jit(solution)/shard_map/ppermute | solution.py:807
  34.3 1.3 %collective-permute-done.5.south_msg = f32[744,128]{1,0:T(8,128)S(1)} collective-permute-done((f32[744,128]{1,0:T(8,128)S(1)}, f32[744,128]{1,0:T(8,128)S(1)}, u32[]{:S(2)}, u32[]{:S(2)}) %collective-permute-start.5) | collective-permute-done | bytes 380960 | tf_op jit(solution)/shard_map/ppermute | solution.py:742
  35.6 4.4 %collective-permute-done.6.north_msg = f32[744,128]{1,0:T(8,128)S(1)} collective-permute-done((f32[744,128]{1,0:T(8,128)S(1)}, f32[744,128]{1,0:T(8,128)S(1)}, u32[]{:S(2)}, u32[]{:S(2)}) %collective-permute-start.6) | collective-permute-done | bytes 380960 | tf_op jit(solution)/shard_map/ppermute | solution.py:742
  40.0 2.8 %shard_map.58 = (f32[5688,128]{1,0:T(8,128)S(1)}, s32[72,128]{1,0:T(8,128)S(1)}, f32[1368,128]{1,0:T(8,128)S(1)}) custom-call(s32[8,128]{1,0:T(8,128)S(1)} %get-tuple-element.23.landings, f32[5688,128]{1,0:T(8,128)S(1)} %get-tuple-element.24.own_post, f32[1448,128]{1,0:T(8,128)S(1)} %get-tuple-element.25.own_outer, ...), custom_call_target="tpu_custom_call" | custom-call | tf_op jit(solution)/shard_map/pallas_call | solution.py:755
  42.8 0.0 collective-permute-done.7.passed_inner
  42.8 6.5 %shard_map.59 = f32[3,19,4096]{2,1,0:T(8,128)} custom-call(s32[8,128]{1,0:T(8,128)S(1)} %get-tuple-element.23.landings, s32[72,128]{1,0:T(8,128)S(1)} %get-tuple-element.32.table, f32[5688,128]{1,0:T(8,128)S(1)} %get-tuple-element.33.wide_post, f32[1368,128]{1,0:T(8,128)S(1)} %get-tuple-element.34.next_outer, ...), custom_call_target="tpu_custom_call" | custom-call | tf_op jit(solution)/shard_map/pallas_call | solution.py:755
Async XLA Ops:
  4.7 21.9 %collective-permute-start = (f32[588,128]{1,0:T(8,128)}, f32[588,128]{1,0:T(8,128)S(1)}, u32[]{:S(2)}, u32[]{:S(2)}) collective-permute-start(f32[588,128]{1,0:T(8,128)} %get-tuple-element.26), channel_id=1, source_target_pairs={{0,4},{4,8},{8,12},{12,16},{16,20},{20,24},{24,28},{1,5},{5,9},{9,... | collective-permute-start | bytes 903176 | tf_op jit(solution)/shard_map/ppermute | solution.py:742
  7.9 18.8 %collective-permute-start.1 = (f32[588,128]{1,0:T(8,128)}, f32[588,128]{1,0:T(8,128)S(1)}, u32[]{:S(2)}, u32[]{:S(2)}) collective-permute-start(f32[588,128]{1,0:T(8,128)} %get-tuple-element.27), channel_id=1, source_target_pairs={{4,0},{8,4},{12,8},{16,12},{20,16},{24,20},{28,24},{5,1},{9,5},{13... | collective-permute-start | bytes 903176 | tf_op jit(solution)/shard_map/ppermute | solution.py:742
  10.9 15.7 %collective-permute-start.4 = (f32[304,128]{1,0:T(8,128)}, f32[304,128]{1,0:T(8,128)S(1)}, u32[]{:S(2)}, u32[]{:S(2)}) collective-permute-start(f32[304,128]{1,0:T(8,128)} %get-tuple-element.29), channel_id=1, source_target_pairs={{0,4},{4,0},{8,12},{12,8},{16,20},{20,16},{24,28},{28,24},{1,5},{5... | collective-permute-start | bytes 466952 | tf_op jit(solution)/shard_map/ppermute | solution.py:804
  11.3 9.7 %collective-permute-start.2 = (f32[144,128]{1,0:T(8,128)}, f32[144,128]{1,0:T(8,128)S(1)}, u32[]{:S(2)}, u32[]{:S(2)}) collective-permute-start(f32[144,128]{1,0:T(8,128)} %get-tuple-element.21.up2_msg), channel_id=1, source_target_pairs={{0,8},{4,12},{8,16},{12,20},{16,24},{20,28},{1,9},{5,13},{9,17},{1... | collective-permute-start | bytes 221192 | tf_op jit(solution)/shard_map/ppermute | solution.py:742
  12.6 8.4 %collective-permute-start.3 = (f32[144,128]{1,0:T(8,128)}, f32[144,128]{1,0:T(8,128)S(1)}, u32[]{:S(2)}, u32[]{:S(2)}) collective-permute-start(f32[144,128]{1,0:T(8,128)} %get-tuple-element.22.down2_msg), channel_id=1, source_target_pairs={{8,0},{12,4},{16,8},{20,12},{24,16},{28,20},{9,1},{13,5},{17,9},{2... | collective-permute-start | bytes 221192 | tf_op jit(solution)/shard_map/ppermute | solution.py:742
  16.6 1.2 %copy-start = (f32[1928,128]{1,0:T(8,128)S(1)}, f32[1928,128]{1,0:T(8,128)}, u32[]{:S(2)}) copy-start(f32[1928,128]{1,0:T(8,128)} %get-tuple-element.20.cells) | copy-start | bytes 2961412
  17.8 0.9 %copy-start.1 = (f32[144,128]{1,0:T(8,128)S(1)}, f32[144,128]{1,0:T(8,128)}, u32[]{:S(2)}) copy-start(f32[144,128]{1,0:T(8,128)} %get-tuple-element.22.down2_msg) | copy-start | bytes 221188
  18.7 0.9 %copy-start.2 = (f32[144,128]{1,0:T(8,128)S(1)}, f32[144,128]{1,0:T(8,128)}, u32[]{:S(2)}) copy-start(f32[144,128]{1,0:T(8,128)} %get-tuple-element.21.up2_msg) | copy-start | bytes 221188
  19.6 0.7 %copy-start.3 = (s32[32,3]{0,1:T(4,128)S(1)}, s32[32,3]{0,1:T(4,128)}, u32[]{:S(2)}) copy-start(s32[32,3]{0,1:T(4,128)} %param.8) | copy-start | bytes 1156
  27.6 8.1 %collective-permute-start.5 = (f32[744,128]{1,0:T(8,128)S(1)}, f32[744,128]{1,0:T(8,128)S(1)}, u32[]{:S(2)}, u32[]{:S(2)}) collective-permute-start(f32[744,128]{1,0:T(8,128)S(1)} %get-tuple-element.30), channel_id=1, source_target_pairs={{0,1},{1,2},{2,3},{4,5},{5,6},{6,7},{8,9},{9,10},{10,11},{12,13},{... | collective-permute-start | bytes 1142792 | tf_op jit(solution)/shard_map/ppermute | solution.py:742
  31.1 9.0 %collective-permute-start.6 = (f32[744,128]{1,0:T(8,128)S(1)}, f32[744,128]{1,0:T(8,128)S(1)}, u32[]{:S(2)}, u32[]{:S(2)}) collective-permute-start(f32[744,128]{1,0:T(8,128)S(1)} %get-tuple-element.31), channel_id=1, source_target_pairs={{1,0},{2,1},{3,2},{5,4},{6,5},{7,6},{9,8},{10,9},{11,10},{13,12},{... | collective-permute-start | bytes 1142792 | tf_op jit(solution)/shard_map/ppermute | solution.py:742
  33.0 9.8 %collective-permute-start.7 = (f32[304,128]{1,0:T(8,128)S(1)}, f32[304,128]{1,0:T(8,128)S(1)}, u32[]{:S(2)}, u32[]{:S(2)}) collective-permute-start(f32[304,128]{1,0:T(8,128)S(1)} %collective-permute-done.4.mate_inner), channel_id=1, source_target_pairs={{0,8},{8,16},{12,4},{16,24},{20,12},{28,20},{1,9},{9,17},{13,5},{1... | collective-permute-start | bytes 466952 | tf_op jit(solution)/shard_map/ppermute | solution.py:807

commit v5 on v4

--- a/solution.py
+++ b/solution.py
@@ -20,10 +20,12 @@
 OUTWARD = SLOTS * 5 + SLOTS
 LAYERS = 2 * PLANES + OUTWARD
 HALF = POPS * EDGE
-PAIRS = PLANES // 2
+QUADS = PLANES // 4
 TABLE = HALF
 STRIPS = HALF + 8
-EDGE_TABLE = PAIRS * GROUP
+FAR = QUADS * GROUP
+EDGE_TABLE = FAR + 3 * GROUP
+EDGE_ROWS = EDGE_TABLE + 24
 NOWHERE = PLANES * PLANE
 LIMIT = 20 * 1024 * 1024
 WIDE_LIMIT = 127 * 512 * 1024
@@ -49,11 +51,20 @@
     (0, 1, -1),
     (0, -1, 1),
 ]
+NORTHWARD, SOUTHWARD = (
+    [s * POPS + p for s in range(SLOTS) for p in range(POPS) if VELOCITY[p][1] == side]
+    + [FLAG0 + s for s in range(SLOTS)]
+    for side in (1, -1)
+)
 OPPOSITE = [0, 2, 1, 4, 3, 6, 5, 8, 7, 10, 9, 12, 11, 14, 13, 16, 15, 18, 17]
 
 
 def lanes_iota():
     return lax.broadcasted_iota(jnp.int32, (8, 128), 1)
+
+
+def is_even(axis, unit=1):
+    return lax.rem(lax.axis_index(axis) // unit, 2) == 0
 
 
 def rows_iota():
@@ -92,8 +103,10 @@
     flags_hbm,
     neighbours_hbm,
     cells_hbm,
-    up_hbm,
-    down_hbm,
+    mate_hbm,
+    other_hbm,
+    mate2_hbm,
+    other2_hbm,
     up2_hbm,
     down2_hbm,
     inner_hbm,
@@ -233,13 +246,26 @@
                     up2_msg[out : out + POPS, :] = cells[pl.ds(row + 13, POPS, stride=32), :]
                     down2_msg[out : out + POPS, :] = cells[pl.ds(row, POPS, stride=32), :]
 
-    last = [
-        copy(up_msg, up_hbm),
-        copy(down_msg, down_hbm),
-        copy(up2_msg, up2_hbm),
-        copy(down2_msg, down2_hbm),
-        copy(inner_msg, inner_hbm),
-    ]
+    last = [copy(up2_msg, up2_hbm), copy(down2_msg, down2_hbm), copy(inner_msg, inner_hbm)]
+    count = len(started)
+    for i, (up, down, mate, other, unit) in enumerate(
+        ((up_msg, down_msg, mate_hbm, other_hbm, 1), (up2_msg, down2_msg, mate2_hbm, other2_hbm, 2))
+    ):
+        first, second = sems.at[count + 2 * i], sems.at[count + 2 * i + 1]
+        even = is_even("curve", unit)
+
+        @pl.when(even)
+        def _():
+            pltpu.make_async_copy(up, mate, first).start()
+            pltpu.make_async_copy(down, other, second).start()
+
+        @pl.when(jnp.logical_not(even))
+        def _():
+            pltpu.make_async_copy(down, mate, first).start()
+            pltpu.make_async_copy(up, other, second).start()
+
+        last.append(pltpu.make_async_copy(up, mate, first))
+        last.append(pltpu.make_async_copy(down, other, second))
     cells_copy.wait()
     for one in last:
         one.wait()
@@ -264,6 +290,30 @@
             row = q * GROUP + v * 8
             outer[row : row + 8, :] = jnp.where(low, first, second)
     outer[PLANES * GROUP :, :] = cells[PLANES * 32 :, :]
+
+
+def sort_messages(mate_msg, other_msg, mate2_msg, other2_msg, low_msg, high_msg, low2, high2):
+    for mate, other, low, high, unit in (
+        (mate_msg, other_msg, low_msg, high_msg, 1),
+        (mate2_msg, other2_msg, low2, high2, 2),
+    ):
+        even = is_even("curve", unit)
+
+        @pl.when(even)
+        def _():
+            low[...] = other[...]
+            high[...] = mate[...]
+
+        @pl.when(jnp.logical_not(even))
+        def _():
+            low[...] = mate[...]
+            high[...] = other[...]
+
+
+def sel4(parts, lane):
+    first = jnp.where(lane < 32, parts[0], parts[1])
+    second = jnp.where(lane < 96, parts[2], parts[3])
+    return jnp.where(lane < 64, first, second)
 
 
 def strip_rows(first, row0, step):
@@ -296,16 +346,22 @@
 def edge_kernel(
     landings,
     own_outer,
+    mate_msg,
+    other_msg,
+    mate2_msg,
+    other2_msg,
+    own2,
+    near_msg,
+    far_msg,
+    outer,
     low_msg,
     high_msg,
     low2_msg,
     high2_msg,
-    own2,
-    mate_inner,
-    north_msg,
-    south_msg,
-    outer,
 ):
+    sort_messages(
+        mate_msg, other_msg, mate2_msg, other2_msg, low_msg, high_msg, low2_msg, high2_msg
+    )
     from_low, from_high, low_low, low_me, high_high, high_me = (landings[i, 0] for i in range(6))
     low = lanes_iota() < 64
     for q in range(PLANES):
@@ -349,19 +405,35 @@
                         msg[(3 + k) * GROUP : (3 + k) * GROUP + POPS, :],
                     )
 
-    for pair in range(PAIRS):
-        for v in range(3):
-            row = 2 * pair * GROUP + v * 8
-            first = outer[row : row + 8, :]
-            second = pltpu.roll(outer[row + GROUP : row + GROUP + 8, :], 64, axis=1)
-            out = pair * GROUP + v * 8
-            north_msg[out : out + 8, :] = jnp.where(low, second, first)
-            south_msg[out : out + 8, :] = jnp.where(low, first, second)
+    even = is_even("cross")
+    lane = lanes_iota()
+
+    def send(row, north, south):
+        near_msg[row : row + 8, :] = jnp.where(even, north, south)
+        far_msg[row : row + 8, :] = jnp.where(even, south, north)
+
+    for v in range(3):
+
+        def plane(q):
+            return outer[q * GROUP + v * 8 : q * GROUP + v * 8 + 8, :]
+
+        for quad in range(QUADS):
+            parts = [plane(4 * quad)]
+            parts += [pltpu.roll(plane(4 * quad + k), 32 * k, axis=1) for k in (1, 2, 3)]
+            send(quad * GROUP + v * 8, sel4(parts[1:] + parts[:1], lane), sel4(parts, lane))
+        for part in range(3):
+            values = []
+            for planes, source in ((NORTHWARD, 80), (SOUTHWARD, 32)):
+                value = None
+                for k, q in enumerate(planes[8 * part : 8 * part + 8]):
+                    moved = pltpu.roll(plane(q), (16 * k - source) % 128, axis=1)
+                    value = moved if value is None else jnp.where(lane < 16 * k, value, moved)
+                values.append(value)
+            send(FAR + part * GROUP + v * 8, *values)
     tables = (low_msg, TABLE), (own_outer, PLANES * GROUP), (high_msg, TABLE)
     for i, (ref, row) in enumerate(tables):
-        out = EDGE_TABLE + 8 * i
-        north_msg[out : out + 8, :] = ref[row : row + 8, :]
-        south_msg[out : out + 8, :] = ref[row : row + 8, :]
+        value = ref[row : row + 8, :]
+        send(EDGE_TABLE + 8 * i, value, value)
 
 
 def collided(h, is_fluid):
@@ -586,29 +658,38 @@
     landings,
     own_post,
     own_outer,
+    mate_msg,
+    other_msg,
+    mate2_msg,
+    other2_msg,
+    own2,
+    near_msg,
+    far_msg,
+    post_ref,
+    slots,
+    next_outer,
+    h_ref,
     low_msg,
     high_msg,
     low2_msg,
     high2_msg,
-    own2,
-    south_msg,
-    north_msg,
-    post_ref,
-    slots,
-    next_outer,
-    h_ref,
     table,
     sem,
 ):
+    sort_messages(
+        mate_msg, other_msg, mate2_msg, other2_msg, low_msg, high_msg, low2_msg, high2_msg
+    )
+    even = is_even("cross")
+
+    def received(row):
+        near, far = near_msg[row : row + 8, :], far_msg[row : row + 8, :]
+        return jnp.where(even, far, near), jnp.where(even, near, far)
+
     for i in range(3):
-        for j, (ref, row) in enumerate(
-            (
-                (south_msg, EDGE_TABLE + 8 * i),
-                ((low_msg, TABLE), (own_outer, PLANES * GROUP), (high_msg, TABLE))[i],
-                (north_msg, EDGE_TABLE + 8 * i),
-            )
-        ):
-            slot = ref[row : row + 8, :].astype(jnp.int32)
+        south, north = received(EDGE_TABLE + 8 * i)
+        ref, row = ((low_msg, TABLE), (own_outer, PLANES * GROUP), (high_msg, TABLE))[i]
+        for j, value in enumerate((south, ref[row : row + 8, :], north)):
+            slot = value.astype(jnp.int32)
             region = 8 * (3 * i + j)
             slots[region : region + 8, :] = jnp.where(slot == SLOTS, NOWHERE, slot * SLOT)
     table_copy = pltpu.make_async_copy(slots, table, sem)
@@ -652,15 +733,28 @@
                             source : source + POPS, :
                         ]
 
-    for pair in range(PAIRS):
-        for v in range(3):
-            row = pair * GROUP + v * 8
-            south, north = south_msg[row : row + 8, :], north_msg[row : row + 8, :]
-            row = 2 * pair * PLANE + 2 * GROUP + v * 8
-            post_ref[row : row + 8, :] = jnp.where(low, north, south)
-            post_ref[row + PLANE : row + PLANE + 8, :] = pltpu.roll(
-                jnp.where(low, south, north), 64, axis=1
-            )
+    lane = lanes_iota()
+    for v in range(3):
+
+        def place(q):
+            row = q * PLANE + 2 * GROUP + v * 8
+            return slice(row, row + 8)
+
+        for quad in range(QUADS):
+            south, north = received(quad * GROUP + v * 8)
+            for k in range(4):
+                value = jnp.where(lane // 32 == (k + 3) % 4, south, north)
+                if k:
+                    value = pltpu.roll(value, 128 - 32 * k, axis=1)
+                post_ref[place(4 * quad + k), :] = value
+        for part in range(3):
+            values = received(FAR + part * GROUP + v * 8)
+            for planes, target, value in zip((NORTHWARD, SOUTHWARD), (80, 32), values):
+                for k, q in enumerate(planes[8 * part : 8 * part + 8]):
+                    moved = pltpu.roll(value, (target - 16 * k) % 128, axis=1)
+                    post_ref[place(q), :] = jnp.where(
+                        lane // 16 == target // 16, moved, post_ref[place(q), :]
+                    )
 
     hide_walls(post_ref)
     table_copy.wait()
@@ -678,7 +772,7 @@
     wide_post,
     next_outer,
     mate_inner,
-    passed_inner,
+    other_inner,
     out_hbm,
     h_ref,
     post_ref,
@@ -687,13 +781,13 @@
 ):
     low = lanes_iota() < 64
     post_ref[...] = wide_post[...]
-    odd = lax.rem(lax.axis_index("curve"), 2) == 1
-    even = jnp.logical_not(odd)
+    even = is_even("curve")
+    odd = jnp.logical_not(even)
     for slot, wanted, inner in (
         (landings[0, 0], odd, mate_inner),
-        (landings[0, 0], even, passed_inner),
+        (landings[0, 0], even, other_inner),
         (landings[1, 0], even, mate_inner),
-        (landings[1, 0], odd, passed_inner),
+        (landings[1, 0], odd, other_inner),
     ):
 
         @pl.when((slot >= 0) & wanted)
@@ -736,10 +830,14 @@
         pltpu.make_async_copy(out.at[s], out_hbm.at[s], sems.at[s]).wait()
 
 
-def shifted_from(value, axis, step):
+def swapped(value, axis, unit=1):
     count = lax.axis_size(axis)
-    pairs = [(i, i + step) for i in range(count) if 0 <= i + step < count]
-    return lax.ppermute(value, axis, pairs)
+    results = []
+    for which in (0, 1):
+        sides = [unit if i // unit % 2 == which else -unit for i in range(count)]
+        pairs = [(i, i + side) for i, side in enumerate(sides) if 0 <= i + side < count]
+        results.append(lax.ppermute(value[which], axis, pairs))
+    return results
 
 
 def rows128(count):
@@ -774,11 +872,12 @@
         6 * GROUP,
         HALF,
     ]
-    cells, up_msg, down_msg, up2_msg, down2_msg, inner_msg = call(
+    results = messages[:5] + messages[3:]
+    cells, mate_msg, other_msg, mate2_msg, other2_msg, up2_msg, down2_msg, inner_msg = call(
         functools.partial(pack_kernel, sizes[1]),
         "HHHHH",
-        "HHHHHH",
-        [rows128(rows) for rows in messages],
+        "HHHHHHHH",
+        [rows128(rows) for rows in results],
         (moves, counts, populations, site_flags, neighbours),
         [
             pltpu.SMEM(moves.shape, jnp.int32),
@@ -791,20 +890,13 @@
             pltpu.VMEM((128, 384), jnp.bfloat16),
             floats(256),
             floats(8),
-            pltpu.SemaphoreType.DMA((4 + SLOTS + 6,)),
+            pltpu.SemaphoreType.DMA((4 + SLOTS + 8,)),
         ],
         WIDE_LIMIT,
     )
-    low_msg = shifted_from(up_msg, "curve", 1)
-    high_msg = shifted_from(down_msg, "curve", -1)
-    low2_msg = shifted_from(up2_msg, "curve", 2)
-    high2_msg = shifted_from(down2_msg, "curve", -2)
-    assert sizes[0] % 2 == 0
-    pairs = [(i, i ^ 1) for i in range(sizes[0])]
-    mate_inner = lax.ppermute(inner_msg, "curve", pairs)
-    pairs = [(i, i - 2 if i % 2 else i + 2) for i in range(sizes[0])]
-    pairs = [pair for pair in pairs if 0 <= pair[1] < sizes[0]]
-    passed_inner = lax.ppermute(mate_inner, "curve", pairs)
+    mate_msg, other_msg = swapped((mate_msg, other_msg), "curve")
+    mate2_msg, other2_msg = swapped((mate2_msg, other2_msg), "curve", 2)
+    mate_inner, other_inner = swapped((inner_msg, inner_msg), "curve")
     post, outer, own2, landings = call(
         functools.partial(spread_kernel, *sizes),
         "SVVV",
@@ -818,17 +910,17 @@
         (moves, cells, up2_msg, down2_msg),
         [],
     )
-    strips = (low_msg, high_msg, low2_msg, high2_msg, own2)
-    north_msg, south_msg = call(
+    strips = (mate_msg, other_msg, mate2_msg, other2_msg, own2)
+    sorted_rows = [messages[1], messages[1], messages[3], messages[3]]
+    near_msg, far_msg = call(
         edge_kernel,
-        "SVVVVVVV",
+        "SVVVVVV",
         "VV",
-        [rows128(PAIRS * GROUP + 24), rows128(PAIRS * GROUP + 24)],
-        (landings, outer, *strips, mate_inner),
-        [floats(PLANES * GROUP)],
+        [rows128(EDGE_ROWS), rows128(EDGE_ROWS)],
+        (landings, outer, *strips),
+        [floats(rows) for rows in [PLANES * GROUP] + sorted_rows],
     )
-    from_south = shifted_from(north_msg, "cross", 1)
-    from_north = shifted_from(south_msg, "cross", -1)
+    near_msg, far_msg = swapped((near_msg, far_msg), "cross")
     post, table, next_outer = call(
         widen_kernel,
         "SVVVVVVVVV",
@@ -838,9 +930,9 @@
             jax.ShapeDtypeStruct((72, 128), jnp.int32),
             rows128(SLOTS * POPS * GROUP),
         ],
-        (landings, post, outer, *strips, from_south, from_north),
+        (landings, post, outer, *strips, near_msg, far_msg),
         [
-            floats(SLOTS * SLOT),
+            *[floats(rows) for rows in [SLOTS * SLOT] + sorted_rows],
             pltpu.SMEM((72, 128), jnp.int32),
             pltpu.SemaphoreType.DMA,
         ],
@@ -850,7 +942,7 @@
         "SSVVVV",
         "H",
         [jax.ShapeDtypeStruct(populations.shape, jnp.float32)],
-        (landings, table, post, next_outer, mate_inner, passed_inner),
+        (landings, table, post, next_outer, mate_inner, other_inner),
         [
             floats(SLOTS * SLOT),
             floats(NOWHERE + SLOT),

time: 49.7 us -> 40.8 us (0.82)
  the two profiles are of different devices: /device:TPU:25 before, /device:TPU:10 now
where the time goes in v5:
time: 40.8 us; the launch traced here: 40.5 us
  Pallas kernels  15.3 us (38%)
  starting transfers between devices  15.1 us (37%)
  waiting for transfers between devices  5.74 us (14%)
  local copies, waits for them, and re-layouts  3.65 us (9%)
  between operations  0.77 us (2%)
    pallas_call x5, Pallas kernels, call(): pl.pallas_call(kernel, out_shape=outs, in_specs=[spaces[x] for x in in_sp...  15.3 us
    ppermute x8, starting transfers between devices, swapped(): results.append(lax.ppermute(value[which], axis, pairs))  15.1 us
    ppermute x8, waiting for transfers between devices, swapped(): results.append(lax.ppermute(value[which], axis, pairs))  5.74 us
    unnamed x8, local copies, waits for them, and re-layouts  3.65 us
  transfers between devices with their start and end apart: 8, of which 4 were waited for; matrix products, arithmetic and copies ran while one was open for 0% of the time, Pallas kernels for 9%

profile of v5, /device:TPU:10, one launch (start us, length us, event | category | flops | bytes accessed | tf_op | source)
XLA Modules:
  0.0 40.5 jit_solution(2724971636994358150)
XLA Ops:
  0.7 4.1 %shard_map.55 = (f32[1928,128]{1,0:T(8,128)}, f32[588,128]{1,0:T(8,128)}, f32[588,128]{1,0:T(8,128)}, f32[144,128]{1,0:T(8,128)}, f32[144,128]{1,0:T(8,128)}, /*...) custom-call(s32[3,32]{1,0:T(4,128)} %bitcast.1, s32[1]{0:T(128)S(6)} %copy.6.counts_hbm, ...), custom_call_target="tpu_custom_call" | custom-call | tf_op jit(solution)/shard_map/pallas_call | solution.py:853
  4.8 1.6 %collective-permute-start = (f32[588,128]{1,0:T(8,128)}, f32[588,128]{1,0:T(8,128)S(1)}, u32[]{:S(2)}, u32[]{:S(2)}) collective-permute-start(f32[588,128]{1,0:T(8,128)} %get-tuple-element.28), channel_id=1, source_target_pairs={{0,4},{4,0},{8,12},{12,8},{16,20},{20,16},{24,28},{28,24},{1,5},{5... | collective-permute-start | bytes 903176 | tf_op jit(solution)/shard_map/ppermute | solution.py:839
  6.3 2.3 %collective-permute-start.1 = (f32[588,128]{1,0:T(8,128)}, f32[588,128]{1,0:T(8,128)S(1)}, u32[]{:S(2)}, u32[]{:S(2)}) collective-permute-start(f32[588,128]{1,0:T(8,128)} %get-tuple-element.29), channel_id=1, source_target_pairs={{4,8},{8,4},{12,16},{16,12},{20,24},{24,20},{5,9},{9,5},{13,17},{1... | collective-permute-start | bytes 903176 | tf_op jit(solution)/shard_map/ppermute | solution.py:839
  8.6 0.1 collective-permute-start.2
  8.7 5.0 %collective-permute-start.3 = (f32[144,128]{1,0:T(8,128)}, f32[144,128]{1,0:T(8,128)S(1)}, u32[]{:S(2)}, u32[]{:S(2)}) collective-permute-start(f32[144,128]{1,0:T(8,128)} %get-tuple-element.31), channel_id=1, source_target_pairs={{8,16},{12,20},{16,8},{20,12},{9,17},{13,21},{17,9},{21,13},{10,18... | collective-permute-start | bytes 221192 | tf_op jit(solution)/shard_map/ppermute | solution.py:839
  13.8 0.0 copy-start
  13.8 1.2 %copy-done = f32[1928,128]{1,0:T(8,128)S(1)} copy-done((f32[1928,128]{1,0:T(8,128)S(1)}, f32[1928,128]{1,0:T(8,128)}, u32[]{:S(2)}) %copy-start) | copy-done | bytes 987160
  15.0 0.0 copy-start.1
  15.0 0.9 %copy-done.1 = f32[144,128]{1,0:T(8,128)S(1)} copy-done((f32[144,128]{1,0:T(8,128)S(1)}, f32[144,128]{1,0:T(8,128)}, u32[]{:S(2)}) %copy-start.1) | copy-done | bytes 73752
  15.8 0.0 copy-start.2
  15.8 0.9 %copy-done.2 = f32[144,128]{1,0:T(8,128)S(1)} copy-done((f32[144,128]{1,0:T(8,128)S(1)}, f32[144,128]{1,0:T(8,128)}, u32[]{:S(2)}) %copy-start.2) | copy-done | bytes 73752
  16.7 0.0 copy-start.3
  16.7 0.7 %copy-done.3 = s32[32,3]{0,1:T(4,128)S(1)} copy-done((s32[32,3]{0,1:T(4,128)S(1)}, s32[32,3]{0,1:T(4,128)}, u32[]{:S(2)}) %copy-start.3) | copy-done | bytes 408
  17.4 0.7 %shard_map.56 = (f32[5688,128]{1,0:T(8,128)S(1)}, f32[1448,128]{1,0:T(8,128)S(1)}, f32[288,128]{1,0:T(8,128)S(1)}, s32[8,128]{1,0:T(8,128)S(1)}) custom-call(s32[3,32]{1,0:T(4,128)S(1)} %bitcast.2, f32[1928,128]{1,0:T(8,128)S(1)} %copy-done, f32[144,128]{1,0:T(8,128)S(1)} %copy-done.1, f32[144,128]{1,0:T(8,128)S(1)} %copy-done.2), custom_call_target="tpu_custom_call" | custom-call | tf_op jit(solution)/shard_map/pallas_call | solution.py:853
  18.1 0.0 collective-permute-done.2.mate2_msg
  18.1 0.5 %collective-permute-done.3.other2_msg = f32[144,128]{1,0:T(8,128)S(1)} collective-permute-done((f32[144,128]{1,0:T(8,128)}, f32[144,128]{1,0:T(8,128)S(1)}, u32[]{:S(2)}, u32[]{:S(2)}) %collective-permute-start.3) | collective-permute-done | bytes 73760 | tf_op jit(solution)/shard_map/ppermute | solution.py:839
  18.6 1.8 %collective-permute-done.mate_msg = f32[588,128]{1,0:T(8,128)S(1)} collective-permute-done((f32[588,128]{1,0:T(8,128)}, f32[588,128]{1,0:T(8,128)S(1)}, u32[]{:S(2)}, u32[]{:S(2)}) %collective-permute-start) | collective-permute-done | bytes 301088 | tf_op jit(solution)/shard_map/ppermute | solution.py:839
  20.4 0.0 collective-permute-done.1.other_msg
  20.4 1.1 %shard_map.57 = (f32[456,128]{1,0:T(8,128)S(1)}, f32[456,128]{1,0:T(8,128)S(1)}) custom-call(s32[8,128]{1,0:T(8,128)S(1)} %get-tuple-element.25.landings, f32[1448,128]{1,0:T(8,128)S(1)} %get-tuple-element.27.own_outer, f32[588,128]{1,0:T(8,128)S(1)} %collective-permute-done.mate_msg, f32[588,128]{1,0:T(8,128)S(1)} %collective-permute-done.1.other_msg, ...), custom_call_target="tpu_custom_call" | custom-call | tf_op jit(solution)/shard_map/pallas_call | solution.py:853
  21.6 0.1 collective-permute-start.4
  21.7 2.5 %collective-permute-start.5 = (f32[456,128]{1,0:T(8,128)S(1)}, f32[456,128]{1,0:T(8,128)S(1)}, u32[]{:S(2)}, u32[]{:S(2)}) collective-permute-start(f32[456,128]{1,0:T(8,128)S(1)} %get-tuple-element.34), channel_id=1, source_target_pairs={{1,2},{2,1},{5,6},{6,5},{9,10},{10,9},{13,14},{14,13},{17,18},{18,... | collective-permute-start | bytes 700424 | tf_op jit(solution)/shard_map/ppermute | solution.py:839
  24.2 1.6 %collective-permute-start.6 = (f32[304,128]{1,0:T(8,128)}, f32[304,128]{1,0:T(8,128)S(1)}, u32[]{:S(2)}, u32[]{:S(2)}) collective-permute-start(f32[304,128]{1,0:T(8,128)} %get-tuple-element.38), channel_id=1, source_target_pairs={{0,4},{4,0},{8,12},{12,8},{16,20},{20,16},{24,28},{28,24},{1,5},{5... | collective-permute-start | bytes 466952 | tf_op jit(solution)/shard_map/ppermute | solution.py:839
  25.8 1.9 %collective-permute-start.7 = (f32[304,128]{1,0:T(8,128)}, f32[304,128]{1,0:T(8,128)S(1)}, u32[]{:S(2)}, u32[]{:S(2)}) collective-permute-start(f32[304,128]{1,0:T(8,128)} %get-tuple-element.38), channel_id=1, source_target_pairs={{4,8},{8,4},{12,16},{16,12},{20,24},{24,20},{5,9},{9,5},{13,17},{1... | collective-permute-start | bytes 466952 | tf_op jit(solution)/shard_map/ppermute | solution.py:839
  27.7 0.0 collective-permute-done.4.near_msg
  27.7 1.3 %collective-permute-done.5.far_msg = f32[456,128]{1,0:T(8,128)S(1)} collective-permute-done((f32[456,128]{1,0:T(8,128)S(1)}, f32[456,128]{1,0:T(8,128)S(1)}, u32[]{:S(2)}, u32[]{:S(2)}) %collective-permute-start.5) | collective-permute-done | bytes 233504 | tf_op jit(solution)/shard_map/ppermute | solution.py:839
  29.0 2.8 %shard_map.58 = (f32[5688,128]{1,0:T(8,128)S(1)}, s32[72,128]{1,0:T(8,128)S(1)}, f32[1368,128]{1,0:T(8,128)S(1)}) custom-call(s32[8,128]{1,0:T(8,128)S(1)} %get-tuple-element.25.landings, f32[5688,128]{1,0:T(8,128)S(1)} %get-tuple-element.26.own_post, f32[1448,128]{1,0:T(8,128)S(1)} %get-tuple-element.27.own_outer, ...), custom_call_target="tpu_custom_call" | custom-call | tf_op jit(solution)/shard_map/pallas_call | solution.py:853
  31.9 0.0 collective-permute-done.6.mate_inner
  31.9 2.1 %collective-permute-done.7.other_inner = f32[304,128]{1,0:T(8,128)S(1)} collective-permute-done((f32[304,128]{1,0:T(8,128)}, f32[304,128]{1,0:T(8,128)S(1)}, u32[]{:S(2)}, u32[]{:S(2)}) %collective-permute-start.7) | collective-permute-done | bytes 155680 | tf_op jit(solution)/shard_map/ppermute | solution.py:839
  34.0 6.5 %shard_map.59 = f32[3,19,4096]{2,1,0:T(8,128)} custom-call(s32[8,128]{1,0:T(8,128)S(1)} %get-tuple-element.25.landings, s32[72,128]{1,0:T(8,128)S(1)} %get-tuple-element.35.table, f32[5688,128]{1,0:T(8,128)S(1)} %get-tuple-element.36.wide_post, f32[1368,128]{1,0:T(8,128)S(1)} %get-tuple-element.37.next_outer, ...), custom_call_target="tpu_custom_call" | custom-call | tf_op jit(solution)/shard_map/pallas_call | solution.py:853
Async XLA Ops:
  4.8 15.7 %collective-permute-start = (f32[588,128]{1,0:T(8,128)}, f32[588,128]{1,0:T(8,128)S(1)}, u32[]{:S(2)}, u32[]{:S(2)}) collective-permute-start(f32[588,128]{1,0:T(8,128)} %get-tuple-element.28), channel_id=1, source_target_pairs={{0,4},{4,0},{8,12},{12,8},{16,20},{20,16},{24,28},{28,24},{1,5},{5... | collective-permute-start | bytes 903176 | tf_op jit(solution)/shard_map/ppermute | solution.py:839
  6.3 14.1 %collective-permute-start.1 = (f32[588,128]{1,0:T(8,128)}, f32[588,128]{1,0:T(8,128)S(1)}, u32[]{:S(2)}, u32[]{:S(2)}) collective-permute-start(f32[588,128]{1,0:T(8,128)} %get-tuple-element.29), channel_id=1, source_target_pairs={{4,8},{8,4},{12,16},{16,12},{20,24},{24,20},{5,9},{9,5},{13,17},{1... | collective-permute-start | bytes 903176 | tf_op jit(solution)/shard_map/ppermute | solution.py:839
  8.6 9.5 %collective-permute-start.2 = (f32[144,128]{1,0:T(8,128)}, f32[144,128]{1,0:T(8,128)S(1)}, u32[]{:S(2)}, u32[]{:S(2)}) collective-permute-start(f32[144,128]{1,0:T(8,128)} %get-tuple-element.30), channel_id=1, source_target_pairs={{0,8},{4,12},{8,0},{12,4},{16,24},{20,28},{24,16},{28,20},{1,9},{5... | collective-permute-start | bytes 221192 | tf_op jit(solution)/shard_map/ppermute | solution.py:839
  8.7 9.9 %collective-permute-start.3 = (f32[144,128]{1,0:T(8,128)}, f32[144,128]{1,0:T(8,128)S(1)}, u32[]{:S(2)}, u32[]{:S(2)}) collective-permute-start(f32[144,128]{1,0:T(8,128)} %get-tuple-element.31), channel_id=1, source_target_pairs={{8,16},{12,20},{16,8},{20,12},{9,17},{13,21},{17,9},{21,13},{10,18... | collective-permute-start | bytes 221192 | tf_op jit(solution)/shard_map/ppermute | solution.py:839
  13.8 1.2 %copy-start = (f32[1928,128]{1,0:T(8,128)S(1)}, f32[1928,128]{1,0:T(8,128)}, u32[]{:S(2)}) copy-start(f32[1928,128]{1,0:T(8,128)} %get-tuple-element.22.cells) | copy-start | bytes 2961412
  15.0 0.9 %copy-start.1 = (f32[144,128]{1,0:T(8,128)S(1)}, f32[144,128]{1,0:T(8,128)}, u32[]{:S(2)}) copy-start(f32[144,128]{1,0:T(8,128)} %get-tuple-element.23.up2_msg) | copy-start | bytes 221188
  15.8 0.9 %copy-start.2 = (f32[144,128]{1,0:T(8,128)S(1)}, f32[144,128]{1,0:T(8,128)}, u32[]{:S(2)}) copy-start(f32[144,128]{1,0:T(8,128)} %get-tuple-element.24.down2_msg) | copy-start | bytes 221188
  16.7 0.7 %copy-start.3 = (s32[32,3]{0,1:T(4,128)S(1)}, s32[32,3]{0,1:T(4,128)}, u32[]{:S(2)}) copy-start(s32[32,3]{0,1:T(4,128)} %param.8) | copy-start | bytes 1156
  21.6 6.1 %collective-permute-start.4 = (f32[456,128]{1,0:T(8,128)S(1)}, f32[456,128]{1,0:T(8,128)S(1)}, u32[]{:S(2)}, u32[]{:S(2)}) collective-permute-start(f32[456,128]{1,0:T(8,128)S(1)} %get-tuple-element.33), channel_id=1, source_target_pairs={{0,1},{1,0},{2,3},{3,2},{4,5},{5,4},{6,7},{7,6},{8,9},{9,8},{10,11... | collective-permute-start | bytes 700424 | tf_op jit(solution)/shard_map/ppermute | solution.py:839
  21.7 7.4 %collective-permute-start.5 = (f32[456,128]{1,0:T(8,128)S(1)}, f32[456,128]{1,0:T(8,128)S(1)}, u32[]{:S(2)}, u32[]{:S(2)}) collective-permute-start(f32[456,128]{1,0:T(8,128)S(1)} %get-tuple-element.34), channel_id=1, source_target_pairs={{1,2},{2,1},{5,6},{6,5},{9,10},{10,9},{13,14},{14,13},{17,18},{18,... | collective-permute-start | bytes 700424 | tf_op jit(solution)/shard_map/ppermute | solution.py:839
  24.2 7.7 %collective-permute-start.6 = (f32[304,128]{1,0:T(8,128)}, f32[304,128]{1,0:T(8,128)S(1)}, u32[]{:S(2)}, u32[]{:S(2)}) collective-permute-start(f32[304,128]{1,0:T(8,128)} %get-tuple-element.38), channel_id=1, source_target_pairs={{0,4},{4,0},{8,12},{12,8},{16,20},{20,16},{24,28},{28,24},{1,5},{5... | collective-permute-start | bytes 466952 | tf_op jit(solution)/shard_map/ppermute | solution.py:839
  25.8 8.2 %collective-permute-start.7 = (f32[304,128]{1,0:T(8,128)}, f32[304,128]{1,0:T(8,128)S(1)}, u32[]{:S(2)}, u32[]{:S(2)}) collective-permute-start(f32[304,128]{1,0:T(8,128)} %get-tuple-element.38), channel_id=1, source_target_pairs={{4,8},{8,4},{12,16},{16,12},{20,24},{24,20},{5,9},{9,5},{13,17},{1... | collective-permute-start | bytes 466952 | tf_op jit(solution)/shard_map/ppermute | solution.py:839

commit v6 on v5

--- a/solution.py
+++ b/solution.py
@@ -19,14 +19,17 @@
 SLOT = POPS * PLANE
 OUTWARD = SLOTS * 5 + SLOTS
 LAYERS = 2 * PLANES + OUTWARD
-HALF = POPS * EDGE
+RIM = 11 * EDGE
+REST = POPS * EDGE + 10 * EDGE
+PAIR = 2 * GROUP
 QUADS = PLANES // 4
-TABLE = HALF
-STRIPS = HALF + 8
+TABLE = RIM
+STRIPS = RIM + 8
 FAR = QUADS * GROUP
 EDGE_TABLE = FAR + 3 * GROUP
 EDGE_ROWS = EDGE_TABLE + 24
-NOWHERE = PLANES * PLANE
+NOWHERE = PLANES * GROUP
+ALL_PLANES = PLANES + POPS
 LIMIT = 20 * 1024 * 1024
 WIDE_LIMIT = 127 * 512 * 1024
 
@@ -56,6 +59,12 @@
     + [FLAG0 + s for s in range(SLOTS)]
     for side in (1, -1)
 )
+THIRD = [
+    (pop, source, *((32 + 16 * k, 9) if k < 4 else (16 * (k - 4), 10)))
+    for k, (pop, source) in enumerate(
+        [(p, 32) for p in (4, 8, 9, 16, 18)] + [(p, 80) for p in (3, 7, 10, 15, 17)]
+    )
+]
 OPPOSITE = [0, 2, 1, 4, 3, 6, 5, 8, 7, 10, 9, 12, 11, 14, 13, 16, 15, 18, 17]
 
 
@@ -109,7 +118,7 @@
     other2_hbm,
     up2_hbm,
     down2_hbm,
-    inner_hbm,
+    rest_hbm,
     moves,
     counts,
     pops,
@@ -120,7 +129,7 @@
     down_msg,
     up2_msg,
     down2_msg,
-    inner_msg,
+    rest_msg,
     wide_flags,
     plane_flags,
     site_flags,
@@ -224,17 +233,35 @@
 
     here = lax.axis_index("curve") * cross_size + lax.axis_index("cross")
     leaving = jnp.maximum(moves[0, here], 0)
-    low = lanes_iota() < 64
-    for p in range(POPS):
-        for v in range(2):
-            base = leaving * (POPS * 32) + p * 32 + v * 8
-            first = cells[aligned(base), :]
-            second = cells[aligned(base + EDGE), :]
-            outer = jnp.where(low, first, second)
+    lane = lanes_iota()
+    for v in range(2):
+        halves = [
+            [cells[aligned(leaving * (POPS * 32) + p * 32 + y * EDGE + v * 8), :] for y in (0, 1)]
+            for p in range(POPS)
+        ]
+        outer = [jnp.where(lane < 64, first, second) for first, second in halves]
+        middle = (lane >= 32) & (lane < 96)
+        sets = [
+            jnp.where(middle, pltpu.roll(outer[p + 1], 64, axis=1), outer[p])
+            for p in range(0, POPS - 1, 2)
+        ]
+        sets += [outer[POPS - 1], jnp.zeros_like(outer[0])]
+        for pop, source, target, which in THIRD:
+            moved = pltpu.roll(outer[pop], (target - source) % 128, axis=1)
+            sets[which] = jnp.where(lane // 16 == target // 16, moved, sets[which])
+        for k, value in enumerate(sets):
+            row = k * EDGE + v * 8
+            up_msg[row : row + 8, :] = value
+            down_msg[row : row + 8, :] = value
+        for p, (first, second) in enumerate(halves):
             row = p * EDGE + v * 8
-            up_msg[row : row + 8, :] = outer
-            down_msg[row : row + 8, :] = outer
-            inner_msg[row : row + 8, :] = jnp.where(low, second, first)
+            rest_msg[row : row + 8, :] = jnp.where(lane < 32, second, first)
+        for p in range(0, POPS, 2):
+            value = halves[p][1]
+            if p + 1 < POPS:
+                value = jnp.where(middle, value, pltpu.roll(halves[p + 1][1], 64, axis=1))
+            row = (POPS + p // 2) * EDGE + v * 8
+            rest_msg[row : row + 8, :] = value
     for s in range(SLOTS):
 
         @pl.when(leaving == s)
@@ -246,7 +273,7 @@
                     up2_msg[out : out + POPS, :] = cells[pl.ds(row + 13, POPS, stride=32), :]
                     down2_msg[out : out + POPS, :] = cells[pl.ds(row, POPS, stride=32), :]
 
-    last = [copy(up2_msg, up2_hbm), copy(down2_msg, down2_hbm), copy(inner_msg, inner_hbm)]
+    last = [copy(up2_msg, up2_hbm), copy(down2_msg, down2_hbm), copy(rest_msg, rest_hbm)]
     count = len(started)
     for i, (up, down, mate, other, unit) in enumerate(
         ((up_msg, down_msg, mate_hbm, other_hbm, 1), (up2_msg, down2_msg, mate2_hbm, other2_hbm, 2))
@@ -272,21 +299,17 @@
 
 
 def spread_kernel(
-    curve_size, cross_size, moves, cells, up2_msg, down2_msg, post, outer, own2, landings
+    curve_size, cross_size, moves, cells, up2_msg, down2_msg, outer, own2, landings
 ):
     low = lanes_iota() < 64
     own2[0 : 6 * GROUP, :] = up2_msg[...]
     own2[6 * GROUP :, :] = down2_msg[...]
     for i, slot in enumerate(move_slots(moves, curve_size, cross_size)):
         landings[i : i + 1, :] = jnp.full((1, 128), slot, jnp.int32)
-    post[NOWHERE:, :] = jnp.full((SLOT, 128), jnp.nan, jnp.float32)
     for q in range(PLANES):
         for v in range(2):
             row = q * 32 + v * 8
             first, second = cells[row : row + 8, :], cells[row + EDGE : row + EDGE + 8, :]
-            row = q * PLANE + v * 8
-            post[row : row + 8, :] = first
-            post[row + GROUP : row + GROUP + 8, :] = second
             row = q * GROUP + v * 8
             outer[row : row + 8, :] = jnp.where(low, first, second)
     outer[PLANES * GROUP :, :] = cells[PLANES * 32 :, :]
@@ -308,6 +331,12 @@
         def _():
             low[...] = mate[...]
             high[...] = other[...]
+
+
+def rim_of(msg, p, v):
+    row = p // 2 * EDGE + v * 8
+    value = msg[row : row + 8, :]
+    return pltpu.roll(value, 64, axis=1) if p % 2 else value
 
 
 def sel4(parts, lane):
@@ -379,15 +408,20 @@
                 msg[source : source + count, :],
                 msg[LAYERS + source : LAYERS + source + count, :],
             )
+    lane = lanes_iota()
     for slot, msg in ((from_low, low_msg), (from_high, high_msg)):
 
         @pl.when(slot >= 0)
         def _():
-            for p in range(POPS):
-                for v in range(2):
-                    row = p * EDGE + v * 8
+            for v in range(2):
+                values = [rim_of(msg, p, v) for p in range(POPS)]
+                for pop, target, source, which in THIRD:
+                    row = which * EDGE + v * 8
+                    moved = pltpu.roll(msg[row : row + 8, :], (target - source) % 128, axis=1)
+                    values[pop] = jnp.where(lane // 16 == target // 16, moved, values[pop])
+                for p, value in enumerate(values):
                     base = slot * (POPS * GROUP) + p * GROUP + v * 8
-                    outer[aligned(base), :] = msg[row : row + 8, :]
+                    outer[aligned(base), :] = value
 
     for s in range(SLOTS):
         for slot, msg, row0 in (
@@ -406,7 +440,6 @@
                     )
 
     even = is_even("cross")
-    lane = lanes_iota()
 
     def send(row, north, south):
         near_msg[row : row + 8, :] = jnp.where(even, north, south)
@@ -528,46 +561,57 @@
     return out
 
 
-def fluid_at(post_ref, s, row):
-    return post_ref[aligned((FLAG0 + s) * PLANE + row), :] > 0.0
-
-
-def collide_all(h_ref, post_ref, put, chunks):
+def place(group, start, plane, v):
+    if group == 2:
+        return aligned(start + plane * GROUP + v * 8)
+    return aligned(2 * start + plane * PAIR + group * GROUP + v * 8)
+
+
+def fluid_at(ref, group, s, v):
+    return ref[place(group, s * GROUP, FLAG0, v), :] > 0.0
+
+
+def collide_all(h_ref, flags, posts):
+    for groups in ((0, 1), (2,)):
+        ref = posts[groups[0] // 2]
+        size = len(groups) * GROUP
+
+        @pl.loop(0, SLOTS)
+        def _(s):
+            @pl.loop(0, size // 8, unroll=3)
+            def _(c):
+                base = s * SLOT + groups[0] * GROUP + c * 8
+                is_fluid = flags[groups[0] // 2][aligned((FLAG0 + s) * size + c * 8), :] > 0.0
+                h = [h_ref[aligned(base + p * PLANE), :] for p in range(POPS)]
+                for p, value in enumerate(collided(h, is_fluid)):
+                    row = aligned((s * POPS + p) * size + c * 8)
+                    ref[row, :] = jnp.where(is_fluid, value, jnp.nan)
+
+
+def hide_walls(ref, size):
     @pl.loop(0, SLOTS)
     def _(s):
-        @pl.loop(*chunks, unroll=3)
+        @pl.loop(0, size // 8)
         def _(c):
-            base = s * SLOT + c * 8
-            is_fluid = fluid_at(post_ref, s, c * 8)
-            h = [h_ref[aligned(base + p * PLANE), :] for p in range(POPS)]
-            for p, value in enumerate(collided(h, is_fluid)):
-                put(s, c, p, jnp.where(is_fluid, value, jnp.nan))
-
-
-def hide_walls(post_ref):
-    @pl.loop(0, SLOTS)
-    def _(s):
-        @pl.loop(0, PLANE // 8)
-        def _(c):
-            is_fluid = fluid_at(post_ref, s, c * 8)
+            is_fluid = ref[aligned((FLAG0 + s) * size + c * 8), :] > 0.0
             for p in range(POPS):
-                place = aligned(s * SLOT + p * PLANE + c * 8)
-                post_ref[place, :] = jnp.where(is_fluid, post_ref[place, :], jnp.nan)
-
-
-def stream_all(post_ref, h_ref, table, groups, vregs, finish=None):
+                row = aligned((s * POPS + p) * size + c * 8)
+                ref[row, :] = jnp.where(is_fluid, ref[row, :], jnp.nan)
+
+
+def stream_all(posts, h_ref, flags, table, groups, vregs, finish=None):
     lane = lanes_iota()
     row = rows_iota()
     low = lane < 64
 
     def one_slot(s):
-        own = s * SLOT
+        own = s * (POPS * GROUP)
 
         def shifted(pop, group, j, dy, dz):
             cx = VELOCITY[pop][0]
 
             def rows(start, v):
-                return post_ref[aligned(start + pop * PLANE + group * GROUP + v * 8), :]
+                return posts[group // 2][place(group, start, pop, v), :]
 
             def look(i, j, dx, v):
                 if (dx, dy, dz) == (0, 0, 0):
@@ -640,12 +684,12 @@
                     mask = lane % 16 == (0 if cz > 0 else 15)
                     values = [jnp.where(mask, b, a) for a, b in zip(values, wrapped)]
                 for v, value in enumerate(values[:vregs]):
-                    place = group * GROUP + v * 8
                     if pop:
-                        back = post_ref[aligned(own + OPPOSITE[pop] * PLANE + place), :]
+                        back = posts[group // 2][place(group, own, OPPOSITE[pop], v), :]
                         value = jnp.where(value != value, back, value)
-                    is_fluid = fluid_at(post_ref, s, place)
-                    h_ref[aligned(own + pop * PLANE + place), :] = jnp.where(is_fluid, value, 0.0)
+                    is_fluid = fluid_at(flags[group // 2], group, s, v)
+                    target = aligned(s * SLOT + pop * PLANE + group * GROUP + v * 8)
+                    h_ref[target, :] = jnp.where(is_fluid, value, 0.0)
 
     @pl.loop(0, SLOTS)
     def _(s):
@@ -654,67 +698,68 @@
             finish(s)
 
 
-def widen_kernel(
+def join_kernel(
     landings,
-    own_post,
-    own_outer,
+    cells,
     mate_msg,
     other_msg,
     mate2_msg,
     other2_msg,
     own2,
-    near_msg,
-    far_msg,
+    mate_rest,
+    other_rest,
     post_ref,
     slots,
-    next_outer,
-    h_ref,
     low_msg,
     high_msg,
     low2_msg,
     high2_msg,
-    table,
-    sem,
 ):
     sort_messages(
         mate_msg, other_msg, mate2_msg, other2_msg, low_msg, high_msg, low2_msg, high2_msg
     )
-    even = is_even("cross")
-
-    def received(row):
-        near, far = near_msg[row : row + 8, :], far_msg[row : row + 8, :]
-        return jnp.where(even, far, near), jnp.where(even, near, far)
-
-    for i in range(3):
-        south, north = received(EDGE_TABLE + 8 * i)
-        ref, row = ((low_msg, TABLE), (own_outer, PLANES * GROUP), (high_msg, TABLE))[i]
-        for j, value in enumerate((south, ref[row : row + 8, :], north)):
-            slot = value.astype(jnp.int32)
-            region = 8 * (3 * i + j)
-            slots[region : region + 8, :] = jnp.where(slot == SLOTS, NOWHERE, slot * SLOT)
-    table_copy = pltpu.make_async_copy(slots, table, sem)
-    table_copy.start()
+    for i, (ref, row) in enumerate(((low_msg, TABLE), (cells, PLANES * 32), (high_msg, TABLE))):
+        slots[8 * i : 8 * i + 8, :] = first_rows(ref[row : row + 8, :])
 
     from_low, from_high, low_low, low_me, high_high, high_me = (landings[i, 0] for i in range(6))
-    low = lanes_iota() < 64
-    post_ref[...] = own_post[...]
-    for slot, msg in ((from_low, low_msg), (from_high, high_msg)):
-
-        @pl.when(slot >= 0)
+    lane = lanes_iota()
+    post_ref[PLANES * PAIR :, :] = jnp.full((POPS * PAIR, 128), jnp.nan, jnp.float32)
+    for q in range(PLANES):
+        for y in range(2):
+            start = q * PAIR + y * GROUP
+            post_ref[start : start + EDGE, :] = cells[
+                q * 32 + y * EDGE : q * 32 + (y + 1) * EDGE, :
+            ]
+    even = is_even("curve")
+    odd = jnp.logical_not(even)
+    for slot, msg, wanted, rest in (
+        (from_low, low_msg, odd, mate_rest),
+        (from_low, low_msg, even, other_rest),
+        (from_high, high_msg, even, mate_rest),
+        (from_high, high_msg, odd, other_rest),
+    ):
+
+        @pl.when((slot >= 0) & wanted)
         def _():
             for p in range(POPS):
                 for v in range(2):
+                    rim = rim_of(msg, p, v)
                     row = p * EDGE + v * 8
-                    value = msg[row : row + 8, :]
-                    start = slot * SLOT + p * PLANE + v * 8
-                    post_ref[aligned(start), :] = value
-                    post_ref[aligned(start + GROUP), :] = value
+                    wide = rest[row : row + 8, :]
+                    row = (POPS + p // 2) * EDGE + v * 8
+                    middle = rest[row : row + 8, :]
+                    if p % 2:
+                        middle = pltpu.roll(middle, 64, axis=1)
+                    second = jnp.where(lane < 32, wide, jnp.where(lane < 96, middle, rim))
+                    start = slot * (POPS * PAIR) + p * PAIR + v * 8
+                    post_ref[aligned(start), :] = jnp.where(lane < 32, rim, wide)
+                    post_ref[aligned(start + GROUP), :] = second
 
     for msg, row0, step, first in ((high_msg, 16, 1, 2), (low_msg, 23, -1, 1)):
         for y in range(2):
             for count, planes, row, source in strip_rows(first, row0, step):
                 source += y * LAYERS
-                post_ref[planes(PLANE, row + y * GROUP), :] = msg[source : source + count, :]
+                post_ref[planes(PAIR, row + y * GROUP), :] = msg[source : source + count, :]
     for s in range(SLOTS):
         for slot, msg, row0 in (
             (low_low, low2_msg, 21),
@@ -727,18 +772,55 @@
             def _():
                 for y in range(2):
                     for k in range(3):
-                        row = s * SLOT + y * GROUP + row0 + k
+                        row = s * POPS * PAIR + y * GROUP + row0 + k
                         source = (y * 3 + k) * GROUP
-                        post_ref[pl.ds(row, POPS, stride=PLANE), :] = msg[
-                            source : source + POPS, :
-                        ]
-
+                        post_ref[pl.ds(row, POPS, stride=PAIR), :] = msg[source : source + POPS, :]
+    hide_walls(post_ref, PAIR)
+
+
+def first_rows(slot):
+    slot = slot.astype(jnp.int32)
+    return jnp.where(slot == SLOTS, NOWHERE, slot * (POPS * GROUP))
+
+
+def steps_kernel(
+    own_slots,
+    first_post,
+    near_msg,
+    far_msg,
+    out_hbm,
+    h_ref,
+    post_ref,
+    outer_ref,
+    out,
+    slots,
+    table,
+    sems,
+):
+    even = is_even("cross")
+
+    def received(row):
+        near, far = near_msg[row : row + 8, :], far_msg[row : row + 8, :]
+        return jnp.where(even, far, near), jnp.where(even, near, far)
+
+    for i in range(3):
+        south, north = received(EDGE_TABLE + 8 * i)
+        slots[24 * i : 24 * i + 8, :] = first_rows(south)
+        slots[24 * i + 8 : 24 * i + 16, :] = own_slots[8 * i : 8 * i + 8, :]
+        slots[24 * i + 16 : 24 * i + 24, :] = first_rows(north)
+    table_copy = pltpu.make_async_copy(slots, table, sems.at[SLOTS])
+    table_copy.start()
+
+    nothing = jnp.full((8, 128), jnp.nan, jnp.float32)
+    for row in range(0, POPS * GROUP, 8):
+        outer_ref[NOWHERE + row : NOWHERE + row + 8, :] = nothing
+    for row in range(PLANES * PAIR, ALL_PLANES * PAIR, 8):
+        post_ref[row : row + 8, :] = nothing
     lane = lanes_iota()
     for v in range(3):
 
-        def place(q):
-            row = q * PLANE + 2 * GROUP + v * 8
-            return slice(row, row + 8)
+        def rows(q):
+            return slice(q * GROUP + v * 8, q * GROUP + v * 8 + 8)
 
         for quad in range(QUADS):
             south, north = received(quad * GROUP + v * 8)
@@ -746,62 +828,17 @@
                 value = jnp.where(lane // 32 == (k + 3) % 4, south, north)
                 if k:
                     value = pltpu.roll(value, 128 - 32 * k, axis=1)
-                post_ref[place(4 * quad + k), :] = value
+                outer_ref[rows(4 * quad + k), :] = value
         for part in range(3):
             values = received(FAR + part * GROUP + v * 8)
             for planes, target, value in zip((NORTHWARD, SOUTHWARD), (80, 32), values):
                 for k, q in enumerate(planes[8 * part : 8 * part + 8]):
                     moved = pltpu.roll(value, (target - 16 * k) % 128, axis=1)
-                    post_ref[place(q), :] = jnp.where(
-                        lane // 16 == target // 16, moved, post_ref[place(q), :]
+                    outer_ref[rows(q), :] = jnp.where(
+                        lane // 16 == target // 16, moved, outer_ref[rows(q), :]
                     )
-
-    hide_walls(post_ref)
+    hide_walls(outer_ref, GROUP)
     table_copy.wait()
-    stream_all(post_ref, h_ref, table, (2,), 3)
-
-    def put(s, c, p, value):
-        next_outer[aligned(s * (POPS * GROUP) + p * GROUP + (c - 6) * 8), :] = value
-
-    collide_all(h_ref, post_ref, put, (6, 9))
-
-
-def steps_kernel(
-    landings,
-    table,
-    wide_post,
-    next_outer,
-    mate_inner,
-    other_inner,
-    out_hbm,
-    h_ref,
-    post_ref,
-    out,
-    sems,
-):
-    low = lanes_iota() < 64
-    post_ref[...] = wide_post[...]
-    even = is_even("curve")
-    odd = jnp.logical_not(even)
-    for slot, wanted, inner in (
-        (landings[0, 0], odd, mate_inner),
-        (landings[0, 0], even, other_inner),
-        (landings[1, 0], even, mate_inner),
-        (landings[1, 0], odd, other_inner),
-    ):
-
-        @pl.when((slot >= 0) & wanted)
-        def _():
-            for v in range(2):
-                fluid = [fluid_at(post_ref, slot, y * GROUP + v * 8) for y in range(2)]
-                for p in range(POPS):
-                    row = p * EDGE + v * 8
-                    value = inner[row : row + 8, :]
-                    for y in range(2):
-                        start = aligned(slot * SLOT + p * PLANE + y * GROUP + v * 8)
-                        is_here = low if y else jnp.logical_not(low)
-                        hidden = jnp.where(fluid[y], value, jnp.nan)
-                        post_ref[start, :] = jnp.where(is_here, hidden, post_ref[start, :])
 
     def finish(s):
         for x in range(EDGE):
@@ -814,18 +851,13 @@
                     ]
         pltpu.make_async_copy(out.at[s], out_hbm.at[s], sems.at[s]).start()
 
-    def put(s, c, p, value):
-        post_ref[aligned(s * SLOT + p * PLANE + c * 8), :] = value
-
-    stream_all(post_ref, h_ref, table, (0, 1), 3)
-    collide_all(h_ref, post_ref, put, (0, 6))
-    for q in range(SLOTS * POPS):
-        row = q * PLANE + 2 * GROUP
-        post_ref[row : row + GROUP, :] = next_outer[q * GROUP : (q + 1) * GROUP, :]
-    for _ in range(STEPS - 2):
-        stream_all(post_ref, h_ref, table, (0, 1, 2), 3)
-        collide_all(h_ref, post_ref, put, (0, 9))
-    stream_all(post_ref, h_ref, table, (0, 1), 2, finish)
+    flags = (first_post, outer_ref)
+    posts = flags
+    for _ in range(STEPS - 1):
+        stream_all(posts, h_ref, flags, table, (0, 1, 2), 3)
+        posts = (post_ref, outer_ref)
+        collide_all(h_ref, flags, posts)
+    stream_all(posts, h_ref, flags, table, (0, 1), 2, finish)
     for s in range(SLOTS):
         pltpu.make_async_copy(out.at[s], out_hbm.at[s], sems.at[s]).wait()
 
@@ -870,10 +902,10 @@
         STRIPS + 2 * LAYERS,
         6 * GROUP,
         6 * GROUP,
-        HALF,
+        REST,
     ]
     results = messages[:5] + messages[3:]
-    cells, mate_msg, other_msg, mate2_msg, other2_msg, up2_msg, down2_msg, inner_msg = call(
+    cells, mate_msg, other_msg, mate2_msg, other2_msg, up2_msg, down2_msg, rest_msg = call(
         functools.partial(pack_kernel, sizes[1]),
         "HHHHH",
         "HHHHHHHH",
@@ -896,13 +928,12 @@
     )
     mate_msg, other_msg = swapped((mate_msg, other_msg), "curve")
     mate2_msg, other2_msg = swapped((mate2_msg, other2_msg), "curve", 2)
-    mate_inner, other_inner = swapped((inner_msg, inner_msg), "curve")
-    post, outer, own2, landings = call(
+    mate_rest, other_rest = swapped((rest_msg, rest_msg), "curve")
+    outer, own2, landings = call(
         functools.partial(spread_kernel, *sizes),
         "SVVV",
-        "VVVV",
+        "VVV",
         [
-            rows128(NOWHERE + SLOT),
             rows128(PLANES * GROUP + 8),
             rows128(12 * GROUP),
             jax.ShapeDtypeStruct((8, 128), jnp.int32),
@@ -921,33 +952,28 @@
         [floats(rows) for rows in [PLANES * GROUP] + sorted_rows],
     )
     near_msg, far_msg = swapped((near_msg, far_msg), "cross")
-    post, table, next_outer = call(
-        widen_kernel,
-        "SVVVVVVVVV",
-        "VVV",
-        [
-            rows128(NOWHERE + SLOT),
-            jax.ShapeDtypeStruct((72, 128), jnp.int32),
-            rows128(SLOTS * POPS * GROUP),
-        ],
-        (landings, post, outer, *strips, near_msg, far_msg),
-        [
-            *[floats(rows) for rows in [SLOTS * SLOT] + sorted_rows],
-            pltpu.SMEM((72, 128), jnp.int32),
-            pltpu.SemaphoreType.DMA,
-        ],
+    post, own_slots = call(
+        join_kernel,
+        "SVVVVVVVV",
+        "VV",
+        [rows128(ALL_PLANES * PAIR), jax.ShapeDtypeStruct((24, 128), jnp.int32)],
+        (landings, cells, *strips, mate_rest, other_rest),
+        [floats(rows) for rows in sorted_rows],
     )
     return call(
         steps_kernel,
-        "SSVVVV",
+        "VVVV",
         "H",
         [jax.ShapeDtypeStruct(populations.shape, jnp.float32)],
-        (landings, table, post, next_outer, mate_inner, other_inner),
+        (own_slots, post, near_msg, far_msg),
         [
             floats(SLOTS * SLOT),
-            floats(NOWHERE + SLOT),
+            floats(ALL_PLANES * PAIR),
+            floats(ALL_PLANES * GROUP),
             pltpu.VMEM(populations.shape, jnp.float32),
-            pltpu.SemaphoreType.DMA((SLOTS,)),
+            pltpu.VMEM((72, 128), jnp.int32),
+            pltpu.SMEM((72, 128), jnp.int32),
+            pltpu.SemaphoreType.DMA((SLOTS + 1,)),
         ],
     )[0]
 

time: 40.8 us -> 41.6 us (1.020)
  the two profiles are of different devices: /device:TPU:10 before, /device:TPU:13 now
where the time goes in v6:
time: 41.6 us; the launch traced here: 41.3 us
  starting transfers between devices  16.5 us (40%)
  Pallas kernels  14.9 us (36%)
  waiting for transfers between devices  6.17 us (15%)
  local copies, waits for them, and re-layouts  2.97 us (7%)
  between operations  0.8 us (2%)
    ppermute x8, starting transfers between devices, swapped(): results.append(lax.ppermute(value[which], axis, pairs))  16.5 us
    pallas_call x5, Pallas kernels, call(): pl.pallas_call(kernel, out_shape=outs, in_specs=[spaces[x] for x in in_sp...  14.9 us
    ppermute x8, waiting for transfers between devices, swapped(): results.append(lax.ppermute(value[which], axis, pairs))  6.17 us
    unnamed x10, local copies, waits for them, and re-layouts  2.97 us
  transfers between devices with their start and end apart: 8, of which 2 were waited for; matrix products, arithmetic and copies ran while one was open for 0% of the time, Pallas kernels for 8%

profile of v6, /device:TPU:13, one launch (start us, length us, event | category | flops | bytes accessed | tf_op | source)
XLA Modules:
  0.0 41.3 jit_solution(12303230791861109413)
XLA Ops:
  0.0 0.0 copy-start.4
  0.7 4.1 %shard_map.55 = (f32[1928,128]{1,0:T(8,128)}, f32[460,128]{1,0:T(8,128)}, f32[460,128]{1,0:T(8,128)}, f32[144,128]{1,0:T(8,128)}, f32[144,128]{1,0:T(8,128)}, /*...) custom-call(s32[3,32]{1,0:T(4,128)} %bitcast.1, s32[1]{0:T(128)S(6)} %copy.6.counts_hbm, ...), custom_call_target="tpu_custom_call" | custom-call | tf_op jit(solution)/shard_map/pallas_call | solution.py:885
  4.8 0.3 collective-permute-start
  5.1 4.1 %collective-permute-start.1 = (f32[460,128]{1,0:T(8,128)}, f32[460,128]{1,0:T(8,128)S(1)}, u32[]{:S(2)}, u32[]{:S(2)}) collective-permute-start(f32[460,128]{1,0:T(8,128)} %get-tuple-element.25), channel_id=1, source_target_pairs={{4,8},{8,4},{12,16},{16,12},{20,24},{24,20},{5,9},{9,5},{13,17},{1... | collective-permute-start | bytes 706568 | tf_op jit(solution)/shard_map/ppermute | solution.py:871
  9.2 0.2 collective-permute-start.2
  9.5 3.0 %collective-permute-start.3 = (f32[144,128]{1,0:T(8,128)}, f32[144,128]{1,0:T(8,128)S(1)}, u32[]{:S(2)}, u32[]{:S(2)}) collective-permute-start(f32[144,128]{1,0:T(8,128)} %get-tuple-element.27), channel_id=1, source_target_pairs={{8,16},{12,20},{16,8},{20,12},{9,17},{13,21},{17,9},{21,13},{10,18... | collective-permute-start | bytes 221192 | tf_op jit(solution)/shard_map/ppermute | solution.py:871
  12.5 0.4 %collective-permute-start.4 = (f32[464,128]{1,0:T(8,128)}, f32[464,128]{1,0:T(8,128)S(1)}, u32[]{:S(2)}, u32[]{:S(2)}) collective-permute-start(f32[464,128]{1,0:T(8,128)} %get-tuple-element.29), channel_id=1, source_target_pairs={{0,4},{4,0},{8,12},{12,8},{16,20},{20,16},{24,28},{28,24},{1,5},{5... | collective-permute-start | bytes 712712 | tf_op jit(solution)/shard_map/ppermute | solution.py:871
  13.0 3.2 %collective-permute-done.2.mate2_msg = f32[144,128]{1,0:T(8,128)S(1)} collective-permute-done((f32[144,128]{1,0:T(8,128)}, f32[144,128]{1,0:T(8,128)S(1)}, u32[]{:S(2)}, u32[]{:S(2)}) %collective-permute-start.2) | collective-permute-done | bytes 73760 | tf_op jit(solution)/shard_map/ppermute | solution.py:871
  16.1 3.1 %collective-permute-start.5 = (f32[464,128]{1,0:T(8,128)}, f32[464,128]{1,0:T(8,128)S(1)}, u32[]{:S(2)}, u32[]{:S(2)}) collective-permute-start(f32[464,128]{1,0:T(8,128)} %get-tuple-element.29), channel_id=1, source_target_pairs={{4,8},{8,4},{12,16},{16,12},{20,24},{24,20},{5,9},{9,5},{13,17},{1... | collective-permute-start | bytes 712712 | tf_op jit(solution)/shard_map/ppermute | solution.py:871
  19.3 0.0 copy-done.4
  19.3 0.0 copy-start
  19.3 1.2 %copy-done = f32[1928,128]{1,0:T(8,128)S(1)} copy-done((f32[1928,128]{1,0:T(8,128)S(1)}, f32[1928,128]{1,0:T(8,128)}, u32[]{:S(2)}) %copy-start) | copy-done | bytes 987160
  20.5 0.0 copy-start.2
  20.5 0.9 %copy-done.2 = f32[144,128]{1,0:T(8,128)S(1)} copy-done((f32[144,128]{1,0:T(8,128)S(1)}, f32[144,128]{1,0:T(8,128)}, u32[]{:S(2)}) %copy-start.2) | copy-done | bytes 73752
  21.4 0.0 copy-start.3
  21.4 0.9 %copy-done.3 = f32[144,128]{1,0:T(8,128)S(1)} copy-done((f32[144,128]{1,0:T(8,128)S(1)}, f32[144,128]{1,0:T(8,128)}, u32[]{:S(2)}) %copy-start.3) | copy-done | bytes 73752
  22.2 0.0 copy-start.1
  22.2 0.6 %shard_map.56 = (f32[1448,128]{1,0:T(8,128)S(1)}, f32[288,128]{1,0:T(8,128)S(1)}, s32[8,128]{1,0:T(8,128)S(1)}) custom-call(s32[3,32]{1,0:T(4,128)S(1)} %bitcast.2, f32[1928,128]{1,0:T(8,128)S(1)} %copy-done, f32[144,128]{1,0:T(8,128)S(1)} %copy-done.2, f32[144,128]{1,0:T(8,128)S(1)} %copy-done.3), custom_call_target="tpu_custom_call" | custom-call | tf_op jit(solution)/shard_map/pallas_call | solution.py:885
  22.9 0.0 collective-permute-done.3.other2_msg
  22.9 0.0 collective-permute-done.mate_msg
  22.9 0.0 collective-permute-done.1.other_msg
  22.9 1.2 %shard_map.58 = (f32[456,128]{1,0:T(8,128)S(1)}, f32[456,128]{1,0:T(8,128)S(1)}) custom-call(s32[8,128]{1,0:T(8,128)S(1)} %get-tuple-element.23.landings, f32[1448,128]{1,0:T(8,128)S(1)} %get-tuple-element.32.own_outer, f32[460,128]{1,0:T(8,128)S(1)} %collective-permute-done.mate_msg, f32[460,128]{1,0:T(8,128)S(1)} %collective-permute-done.1.other_msg, ...), custom_call_target="tpu_custom_call" | custom-call | tf_op jit(solution)/shard_map/pallas_call | solution.py:885
  24.1 2.2 %collective-permute-start.6 = (f32[456,128]{1,0:T(8,128)S(1)}, f32[456,128]{1,0:T(8,128)S(1)}, u32[]{:S(2)}, u32[]{:S(2)}) collective-permute-start(f32[456,128]{1,0:T(8,128)S(1)} %get-tuple-element.33), channel_id=1, source_target_pairs={{0,1},{1,0},{2,3},{3,2},{4,5},{5,4},{6,7},{7,6},{8,9},{9,8},{10,11... | collective-permute-start | bytes 700424 | tf_op jit(solution)/shard_map/ppermute | solution.py:871
  26.3 3.0 %collective-permute-start.7 = (f32[456,128]{1,0:T(8,128)S(1)}, f32[456,128]{1,0:T(8,128)S(1)}, u32[]{:S(2)}, u32[]{:S(2)}) collective-permute-start(f32[456,128]{1,0:T(8,128)S(1)} %get-tuple-element.34), channel_id=1, source_target_pairs={{1,2},{2,1},{5,6},{6,5},{9,10},{10,9},{13,14},{14,13},{17,18},{18,... | collective-permute-start | bytes 700424 | tf_op jit(solution)/shard_map/ppermute | solution.py:871
  29.3 0.0 collective-permute-done.4.mate_rest
  29.3 0.0 collective-permute-done.5.other_rest
  29.4 0.0 copy-done.1
  29.4 1.3 %shard_map.57 = (f32[3792,128]{1,0:T(8,128)S(1)}, s32[24,128]{1,0:T(8,128)S(1)}) custom-call(s32[8,128]{1,0:T(8,128)S(1)} %get-tuple-element.23.landings, f32[1928,128]{1,0:T(8,128)S(1)} %copy-done.1, f32[460,128]{1,0:T(8,128)S(1)} %collective-permute-done.mate_msg, f32[460,128]{1,0:T(8,128)S(1)} %collective-permute-done.1.other_msg, ...), custom_call_target="tpu_custom_call" | custom-call | tf_op jit(solution)/shard_map/pallas_call | solution.py:885
  30.7 0.0 collective-permute-done.6.near_msg
  30.7 3.0 %collective-permute-done.7.far_msg = f32[456,128]{1,0:T(8,128)S(1)} collective-permute-done((f32[456,128]{1,0:T(8,128)S(1)}, f32[456,128]{1,0:T(8,128)S(1)}, u32[]{:S(2)}, u32[]{:S(2)}) %collective-permute-start.7) | collective-permute-done | bytes 233504 | tf_op jit(solution)/shard_map/ppermute | solution.py:871
  33.7 7.6 %shard_map.59 = f32[3,19,4096]{2,1,0:T(8,128)} custom-call(s32[24,128]{1,0:T(8,128)S(1)} %get-tuple-element.30.own_slots, f32[3792,128]{1,0:T(8,128)S(1)} %get-tuple-element.31.first_post, f32[456,128]{1,0:T(8,128)S(1)} %collective-permute-done.6.near_msg, f32[456,128]{1,0:T(8,128)S(1)} %collective-permute-done.7.far_msg), custom_call_target="tpu_custom_call" | custom-call | tf_op jit(solution)/shard_map/pallas_call | solution.py:885
Async XLA Ops:
  0.0 19.3 %copy-start.4 = (s32[32,3]{0,1:T(4,128)S(1)}, s32[32,3]{0,1:T(4,128)}, u32[]{:S(2)}) copy-start(s32[32,3]{0,1:T(4,128)} %param.8) | copy-start | bytes 1156
  4.8 18.1 %collective-permute-start = (f32[460,128]{1,0:T(8,128)}, f32[460,128]{1,0:T(8,128)S(1)}, u32[]{:S(2)}, u32[]{:S(2)}) collective-permute-start(f32[460,128]{1,0:T(8,128)} %get-tuple-element.24), channel_id=1, source_target_pairs={{0,4},{4,0},{8,12},{12,8},{16,20},{20,16},{24,28},{28,24},{1,5},{5... | collective-permute-start | bytes 706568 | tf_op jit(solution)/shard_map/ppermute | solution.py:871
  5.1 17.8 %collective-permute-start.1 = (f32[460,128]{1,0:T(8,128)}, f32[460,128]{1,0:T(8,128)S(1)}, u32[]{:S(2)}, u32[]{:S(2)}) collective-permute-start(f32[460,128]{1,0:T(8,128)} %get-tuple-element.25), channel_id=1, source_target_pairs={{4,8},{8,4},{12,16},{16,12},{20,24},{24,20},{5,9},{9,5},{13,17},{1... | collective-permute-start | bytes 706568 | tf_op jit(solution)/shard_map/ppermute | solution.py:871
  9.2 6.9 %collective-permute-start.2 = (f32[144,128]{1,0:T(8,128)}, f32[144,128]{1,0:T(8,128)S(1)}, u32[]{:S(2)}, u32[]{:S(2)}) collective-permute-start(f32[144,128]{1,0:T(8,128)} %get-tuple-element.26), channel_id=1, source_target_pairs={{0,8},{4,12},{8,0},{12,4},{16,24},{20,28},{24,16},{28,20},{1,9},{5... | collective-permute-start | bytes 221192 | tf_op jit(solution)/shard_map/ppermute | solution.py:871
  9.5 13.4 %collective-permute-start.3 = (f32[144,128]{1,0:T(8,128)}, f32[144,128]{1,0:T(8,128)S(1)}, u32[]{:S(2)}, u32[]{:S(2)}) collective-permute-start(f32[144,128]{1,0:T(8,128)} %get-tuple-element.27), channel_id=1, source_target_pairs={{8,16},{12,20},{16,8},{20,12},{9,17},{13,21},{17,9},{21,13},{10,18... | collective-permute-start | bytes 221192 | tf_op jit(solution)/shard_map/ppermute | solution.py:871
  12.5 16.8 %collective-permute-start.4 = (f32[464,128]{1,0:T(8,128)}, f32[464,128]{1,0:T(8,128)S(1)}, u32[]{:S(2)}, u32[]{:S(2)}) collective-permute-start(f32[464,128]{1,0:T(8,128)} %get-tuple-element.29), channel_id=1, source_target_pairs={{0,4},{4,0},{8,12},{12,8},{16,20},{20,16},{24,28},{28,24},{1,5},{5... | collective-permute-start | bytes 712712 | tf_op jit(solution)/shard_map/ppermute | solution.py:871
  16.1 13.2 %collective-permute-start.5 = (f32[464,128]{1,0:T(8,128)}, f32[464,128]{1,0:T(8,128)S(1)}, u32[]{:S(2)}, u32[]{:S(2)}) collective-permute-start(f32[464,128]{1,0:T(8,128)} %get-tuple-element.29), channel_id=1, source_target_pairs={{4,8},{8,4},{12,16},{16,12},{20,24},{24,20},{5,9},{9,5},{13,17},{1... | collective-permute-start | bytes 712712 | tf_op jit(solution)/shard_map/ppermute | solution.py:871
  19.3 1.2 %copy-start = (f32[1928,128]{1,0:T(8,128)S(1)}, f32[1928,128]{1,0:T(8,128)}, u32[]{:S(2)}) copy-start(f32[1928,128]{1,0:T(8,128)} %get-tuple-element.20.cells) | copy-start | bytes 2961412
  20.5 0.9 %copy-start.2 = (f32[144,128]{1,0:T(8,128)S(1)}, f32[144,128]{1,0:T(8,128)}, u32[]{:S(2)}) copy-start(f32[144,128]{1,0:T(8,128)} %get-tuple-element.21.up2_msg) | copy-start | bytes 221188
  21.4 0.9 %copy-start.3 = (f32[144,128]{1,0:T(8,128)S(1)}, f32[144,128]{1,0:T(8,128)}, u32[]{:S(2)}) copy-start(f32[144,128]{1,0:T(8,128)} %get-tuple-element.22.down2_msg) | copy-start | bytes 221188
  22.2 7.1 %copy-start.1 = (f32[1928,128]{1,0:T(8,128)S(1)}, f32[1928,128]{1,0:T(8,128)}, u32[]{:S(2)}) copy-start(f32[1928,128]{1,0:T(8,128)} %get-tuple-element.20.cells) | copy-start | bytes 2961412
  24.1 6.6 %collective-permute-start.6 = (f32[456,128]{1,0:T(8,128)S(1)}, f32[456,128]{1,0:T(8,128)S(1)}, u32[]{:S(2)}, u32[]{:S(2)}) collective-permute-start(f32[456,128]{1,0:T(8,128)S(1)} %get-tuple-element.33), channel_id=1, source_target_pairs={{0,1},{1,0},{2,3},{3,2},{4,5},{5,4},{6,7},{7,6},{8,9},{9,8},{10,11... | collective-permute-start | bytes 700424 | tf_op jit(solution)/shard_map/ppermute | solution.py:871
  26.3 7.4 %collective-permute-start.7 = (f32[456,128]{1,0:T(8,128)S(1)}, f32[456,128]{1,0:T(8,128)S(1)}, u32[]{:S(2)}, u32[]{:S(2)}) collective-permute-start(f32[456,128]{1,0:T(8,128)S(1)} %get-tuple-element.34), channel_id=1, source_target_pairs={{1,2},{2,1},{5,6},{6,5},{9,10},{10,9},{13,14},{14,13},{17,18},{18,... | collective-permute-start | bytes 700424 | tf_op jit(solution)/shard_map/ppermute | solution.py:871

commit v7 on v6

--- a/solution.py
+++ b/solution.py
@@ -17,6 +17,9 @@
 GROUP = 24
 PLANE = 3 * GROUP
 SLOT = POPS * PLANE
+CELLS = PLANES * 32
+LANDINGS = CELLS + 8
+OWN2 = LANDINGS + 8
 OUTWARD = SLOTS * 5 + SLOTS
 LAYERS = 2 * PLANES + OUTWARD
 RIM = 11 * EDGE
@@ -105,6 +108,7 @@
 
 
 def pack_kernel(
+    curve_size,
     cross_size,
     moves_hbm,
     counts_hbm,
@@ -116,8 +120,6 @@
     other_hbm,
     mate2_hbm,
     other2_hbm,
-    up2_hbm,
-    down2_hbm,
     rest_hbm,
     moves,
     counts,
@@ -158,7 +160,7 @@
     named = neighbours[...]
     slot = jnp.where(named >= 0, lax.rem(jnp.maximum(named, 0), SLOTS), SLOTS)
     near[0:SLOTS, 0 : named.shape[1]] = slot.astype(jnp.float32)
-    for ref, row in ((cells, PLANES * 32), (up_msg, TABLE), (down_msg, TABLE)):
+    for ref, row in ((cells, CELLS), (up_msg, TABLE), (down_msg, TABLE)):
         ref[row : row + 8, :] = near[...]
 
     wide_flags[...] = jnp.zeros_like(wide_flags)
@@ -205,11 +207,16 @@
         @pl.loop(0, 4, unroll=2)
         def _(c):
             base = s * (POPS * 32) + c * 8
-            h = [cells[aligned(base + p * 32), :] for p in range(POPS)]
-            for p, value in enumerate(collided(h, True)):
-                cells[aligned(base + p * 32), :] = value
-
-    cells_copy = copy(cells, cells_hbm)
+            view = cells.at[aligned(base, (POPS - 1) * 32 + 8), :]
+            h = [view[p * 32 : p * 32 + 8, :] for p in range(POPS)]
+            for p, value in enumerate(collided(h)):
+                view[p * 32 : p * 32 + 8, :] = value
+
+    for i, slot in enumerate(move_slots(moves, curve_size, cross_size)):
+        value = jnp.full((1, 128), slot, jnp.int32)
+        cells[LANDINGS + i : LANDINGS + i + 1, :] = value.astype(jnp.float32)
+
+    body_copy = copy(cells.at[:OWN2], cells_hbm.at[:OWN2])
 
     for y in range(2):
         for msg, x0, first in ((up_msg, 15, 1), (down_msg, 0, 2)):
@@ -273,7 +280,9 @@
                     up2_msg[out : out + POPS, :] = cells[pl.ds(row + 13, POPS, stride=32), :]
                     down2_msg[out : out + POPS, :] = cells[pl.ds(row, POPS, stride=32), :]
 
-    last = [copy(up2_msg, up2_hbm), copy(down2_msg, down2_hbm), copy(rest_msg, rest_hbm)]
+    cells[OWN2 : OWN2 + 6 * GROUP, :] = up2_msg[...]
+    cells[OWN2 + 6 * GROUP :, :] = down2_msg[...]
+    last = [copy(cells.at[OWN2:], cells_hbm.at[OWN2:]), copy(rest_msg, rest_hbm)]
     count = len(started)
     for i, (up, down, mate, other, unit) in enumerate(
         ((up_msg, down_msg, mate_hbm, other_hbm, 1), (up2_msg, down2_msg, mate2_hbm, other2_hbm, 2))
@@ -293,26 +302,20 @@
 
         last.append(pltpu.make_async_copy(up, mate, first))
         last.append(pltpu.make_async_copy(down, other, second))
-    cells_copy.wait()
+    body_copy.wait()
     for one in last:
         one.wait()
 
 
-def spread_kernel(
-    curve_size, cross_size, moves, cells, up2_msg, down2_msg, outer, own2, landings
-):
+def spread_kernel(cells, outer, landings):
     low = lanes_iota() < 64
-    own2[0 : 6 * GROUP, :] = up2_msg[...]
-    own2[6 * GROUP :, :] = down2_msg[...]
-    for i, slot in enumerate(move_slots(moves, curve_size, cross_size)):
-        landings[i : i + 1, :] = jnp.full((1, 128), slot, jnp.int32)
+    landings[...] = cells[LANDINGS : LANDINGS + 8, :].astype(jnp.int32)
     for q in range(PLANES):
         for v in range(2):
             row = q * 32 + v * 8
             first, second = cells[row : row + 8, :], cells[row + EDGE : row + EDGE + 8, :]
             row = q * GROUP + v * 8
             outer[row : row + 8, :] = jnp.where(low, first, second)
-    outer[PLANES * GROUP :, :] = cells[PLANES * 32 :, :]
 
 
 def sort_messages(mate_msg, other_msg, mate2_msg, other2_msg, low_msg, high_msg, low2, high2):
@@ -375,11 +378,11 @@
 def edge_kernel(
     landings,
     own_outer,
+    cells,
     mate_msg,
     other_msg,
     mate2_msg,
     other2_msg,
-    own2,
     near_msg,
     far_msg,
     outer,
@@ -426,9 +429,9 @@
     for s in range(SLOTS):
         for slot, msg, row0 in (
             (low_low, low2_msg, 21),
-            (low_me, own2, 21),
+            (low_me, cells.at[OWN2:], 21),
             (high_high, high2_msg, 16),
-            (high_me, own2.at[6 * GROUP :], 16),
+            (high_me, cells.at[OWN2 + 6 * GROUP :], 16),
         ):
 
             @pl.when(slot == s)
@@ -463,13 +466,13 @@
                     value = moved if value is None else jnp.where(lane < 16 * k, value, moved)
                 values.append(value)
             send(FAR + part * GROUP + v * 8, *values)
-    tables = (low_msg, TABLE), (own_outer, PLANES * GROUP), (high_msg, TABLE)
+    tables = (low_msg, TABLE), (cells, CELLS), (high_msg, TABLE)
     for i, (ref, row) in enumerate(tables):
         value = ref[row : row + 8, :]
         send(EDGE_TABLE + 8 * i, value, value)
 
 
-def collided(h, is_fluid):
+def collided(h):
     shear = 1.0 / 0.6
     rest = h[0]
     sx, dx = h[1] + h[2], h[1] - h[2]
@@ -493,7 +496,7 @@
     jx = dx * (1.0 / 18.0) + fx * (1.0 / 36.0)
     jy = dy * (1.0 / 18.0) + fy * (1.0 / 36.0)
     jz = dz * (1.0 / 18.0) + fz * (1.0 / 36.0)
-    inverse = 1.0 / jnp.where(is_fluid, rho, 1.0)
+    inverse = 1.0 / rho
     ux, uy, uz = jx * inverse, jy * inverse, jz * inverse
     qxx, qyy, qzz = jx * ux, jy * uy, jz * uz
     total = qxx + qyy + qzz
@@ -561,16 +564,6 @@
     return out
 
 
-def place(group, start, plane, v):
-    if group == 2:
-        return aligned(start + plane * GROUP + v * 8)
-    return aligned(2 * start + plane * PAIR + group * GROUP + v * 8)
-
-
-def fluid_at(ref, group, s, v):
-    return ref[place(group, s * GROUP, FLAG0, v), :] > 0.0
-
-
 def collide_all(h_ref, flags, posts):
     for groups in ((0, 1), (2,)):
         ref = posts[groups[0] // 2]
@@ -580,12 +573,14 @@
         def _(s):
             @pl.loop(0, size // 8, unroll=3)
             def _(c):
-                base = s * SLOT + groups[0] * GROUP + c * 8
                 is_fluid = flags[groups[0] // 2][aligned((FLAG0 + s) * size + c * 8), :] > 0.0
-                h = [h_ref[aligned(base + p * PLANE), :] for p in range(POPS)]
-                for p, value in enumerate(collided(h, is_fluid)):
-                    row = aligned((s * POPS + p) * size + c * 8)
-                    ref[row, :] = jnp.where(is_fluid, value, jnp.nan)
+                start = s * SLOT + groups[0] * GROUP + c * 8
+                h_view = h_ref.at[aligned(start, (POPS - 1) * PLANE + 8), :]
+                start = s * (POPS * size) + c * 8
+                view = ref.at[aligned(start, (POPS - 1) * size + 8), :]
+                h = [h_view[p * PLANE : p * PLANE + 8, :] for p in range(POPS)]
+                for p, value in enumerate(collided(h)):
+                    view[p * size : p * size + 8, :] = jnp.where(is_fluid, value, jnp.nan)
 
 
 def hide_walls(ref, size):
@@ -594,9 +589,11 @@
         @pl.loop(0, size // 8)
         def _(c):
             is_fluid = ref[aligned((FLAG0 + s) * size + c * 8), :] > 0.0
+            start = s * (POPS * size) + c * 8
+            view = ref.at[aligned(start, (POPS - 1) * size + 8), :]
             for p in range(POPS):
-                row = aligned((s * POPS + p) * size + c * 8)
-                ref[row, :] = jnp.where(is_fluid, ref[row, :], jnp.nan)
+                row = p * size
+                view[row : row + 8, :] = jnp.where(is_fluid, view[row : row + 8, :], jnp.nan)
 
 
 def stream_all(posts, h_ref, flags, table, groups, vregs, finish=None):
@@ -605,27 +602,45 @@
     low = lane < 64
 
     def one_slot(s):
-        own = s * (POPS * GROUP)
+        views = {}
+
+        def view(which, key):
+            if (which, key) not in views:
+                start = s * (POPS * GROUP) if key == "own" else table[key[0] * 8 + s, key[1]]
+                start = start if which else 2 * start
+                views[which, key] = posts[which].at[
+                    aligned(start, POPS * (GROUP if which else PAIR)), :
+                ]
+            return views[which, key]
+
+        def load(key, pop, group, v):
+            if group == 2:
+                row = pop * GROUP + v * 8
+            else:
+                row = pop * PAIR + group * GROUP + v * 8
+            return view(group // 2, key)[row : row + 8, :]
+
+        h_view = h_ref.at[aligned(s * SLOT, SLOT), :]
 
         def shifted(pop, group, j, dy, dz):
             cx = VELOCITY[pop][0]
 
-            def rows(start, v):
-                return posts[group // 2][place(group, start, pop, v), :]
+            def rows(key, v):
+                return load(key, pop, group, v)
 
             def look(i, j, dx, v):
                 if (dx, dy, dz) == (0, 0, 0):
-                    return rows(own, v)
+                    return rows("own", v)
                 if j is None:
                     return jnp.where(low, look(i, 1, dx, v), look(i, -1, dx, v))
                 region = (i + 1) * 3 + j + 1
-                return rows(table[region * 8 + s, VELOCITY.index((dx, dy, dz)) - 1], v)
+                return rows((region, VELOCITY.index((dx, dy, dz)) - 1), v)
 
             need_last = vregs == 3
             values = [look(0, j, 0, 0), look(0, j, 0, 1)]
             if need_last:
                 if dy == 0 and dz == 0:
-                    values.append(rows(own, 2))
+                    values.append(rows("own", 2))
                 else:
                     values.append(jnp.where(row < 4, look(1, j, 0, 2), look(-1, j, 0, 2)))
             if cx == 0:
@@ -685,11 +700,14 @@
                     values = [jnp.where(mask, b, a) for a, b in zip(values, wrapped)]
                 for v, value in enumerate(values[:vregs]):
                     if pop:
-                        back = posts[group // 2][place(group, own, OPPOSITE[pop], v), :]
-                        value = jnp.where(value != value, back, value)
-                    is_fluid = fluid_at(flags[group // 2], group, s, v)
-                    target = aligned(s * SLOT + pop * PLANE + group * GROUP + v * 8)
-                    h_ref[target, :] = jnp.where(is_fluid, value, 0.0)
+                        value = jnp.where(value != value, load("own", OPPOSITE[pop], group, v), value)
+                    if finish is not None:
+                        is_fluid = flags[group // 2][
+                            aligned((FLAG0 + s) * PAIR + group * GROUP + v * 8), :
+                        ]
+                        value = jnp.where(is_fluid > 0.0, value, 0.0)
+                    target = pop * PLANE + group * GROUP + v * 8
+                    h_view[target : target + 8, :] = value
 
     @pl.loop(0, SLOTS)
     def _(s):
@@ -705,9 +723,8 @@
     other_msg,
     mate2_msg,
     other2_msg,
-    own2,
     mate_rest,
-    other_rest,
+    passed_rest,
     post_ref,
     slots,
     low_msg,
@@ -718,7 +735,7 @@
     sort_messages(
         mate_msg, other_msg, mate2_msg, other2_msg, low_msg, high_msg, low2_msg, high2_msg
     )
-    for i, (ref, row) in enumerate(((low_msg, TABLE), (cells, PLANES * 32), (high_msg, TABLE))):
+    for i, (ref, row) in enumerate(((low_msg, TABLE), (cells, CELLS), (high_msg, TABLE))):
         slots[8 * i : 8 * i + 8, :] = first_rows(ref[row : row + 8, :])
 
     from_low, from_high, low_low, low_me, high_high, high_me = (landings[i, 0] for i in range(6))
@@ -734,9 +751,9 @@
     odd = jnp.logical_not(even)
     for slot, msg, wanted, rest in (
         (from_low, low_msg, odd, mate_rest),
-        (from_low, low_msg, even, other_rest),
+        (from_low, low_msg, even, passed_rest),
         (from_high, high_msg, even, mate_rest),
-        (from_high, high_msg, odd, other_rest),
+        (from_high, high_msg, odd, passed_rest),
     ):
 
         @pl.when((slot >= 0) & wanted)
@@ -763,9 +780,9 @@
     for s in range(SLOTS):
         for slot, msg, row0 in (
             (low_low, low2_msg, 21),
-            (low_me, own2, 21),
+            (low_me, cells.at[OWN2:], 21),
             (high_high, high2_msg, 16),
-            (high_me, own2.at[6 * GROUP :], 16),
+            (high_me, cells.at[OWN2 + 6 * GROUP :], 16),
         ):
 
             @pl.when(slot == s)
@@ -897,19 +914,18 @@
     moves = migrations.T
     floats = lambda rows: pltpu.VMEM((rows, 128), jnp.float32)
     messages = [
-        PLANES * 32 + 8,
+        OWN2 + 12 * GROUP,
         STRIPS + 2 * LAYERS,
         STRIPS + 2 * LAYERS,
         6 * GROUP,
         6 * GROUP,
         REST,
     ]
-    results = messages[:5] + messages[3:]
-    cells, mate_msg, other_msg, mate2_msg, other2_msg, up2_msg, down2_msg, rest_msg = call(
-        functools.partial(pack_kernel, sizes[1]),
+    cells, mate_msg, other_msg, mate2_msg, other2_msg, rest_msg = call(
+        functools.partial(pack_kernel, *sizes),
         "HHHHH",
-        "HHHHHHHH",
-        [rows128(rows) for rows in results],
+        "HHHHHH",
+        [rows128(rows) for rows in messages],
         (moves, counts, populations, site_flags, neighbours),
         [
             pltpu.SMEM(moves.shape, jnp.int32),
@@ -928,20 +944,21 @@
     )
     mate_msg, other_msg = swapped((mate_msg, other_msg), "curve")
     mate2_msg, other2_msg = swapped((mate2_msg, other2_msg), "curve", 2)
-    mate_rest, other_rest = swapped((rest_msg, rest_msg), "curve")
-    outer, own2, landings = call(
-        functools.partial(spread_kernel, *sizes),
-        "SVVV",
-        "VVV",
-        [
-            rows128(PLANES * GROUP + 8),
-            rows128(12 * GROUP),
-            jax.ShapeDtypeStruct((8, 128), jnp.int32),
-        ],
-        (moves, cells, up2_msg, down2_msg),
+    assert sizes[0] % 2 == 0
+    pairs = [(i, i ^ 1) for i in range(sizes[0])]
+    mate_rest = lax.ppermute(rest_msg, "curve", pairs)
+    pairs = [(i, i - 2 if i % 2 else i + 2) for i in range(sizes[0])]
+    pairs = [pair for pair in pairs if 0 <= pair[1] < sizes[0]]
+    passed_rest = lax.ppermute(mate_rest, "curve", pairs)
+    outer, landings = call(
+        spread_kernel,
+        "V",
+        "VV",
+        [rows128(PLANES * GROUP), jax.ShapeDtypeStruct((8, 128), jnp.int32)],
+        (cells,),
         [],
     )
-    strips = (mate_msg, other_msg, mate2_msg, other2_msg, own2)
+    strips = (cells, mate_msg, other_msg, mate2_msg, other2_msg)
     sorted_rows = [messages[1], messages[1], messages[3], messages[3]]
     near_msg, far_msg = call(
         edge_kernel,
@@ -954,10 +971,10 @@
     near_msg, far_msg = swapped((near_msg, far_msg), "cross")
     post, own_slots = call(
         join_kernel,
-        "SVVVVVVVV",
+        "SVVVVVVV",
         "VV",
         [rows128(ALL_PLANES * PAIR), jax.ShapeDtypeStruct((24, 128), jnp.int32)],
-        (landings, cells, *strips, mate_rest, other_rest),
+        (landings, *strips, mate_rest, passed_rest),
         [floats(rows) for rows in sorted_rows],
     )
     return call(

time: 41.6 us -> 41 us (0.986)
  the two profiles are of different devices: /device:TPU:13 before, /device:TPU:1 now
where the time goes in v7:
time: 41 us; the launch traced here: 40.8 us
  starting transfers between devices  19.1 us (47%)
  Pallas kernels  13.5 us (33%)
  waiting for transfers between devices  6.18 us (15%)
  local copies, waits for them, and re-layouts  1.25 us (3%)
  between operations  0.75 us (2%)
    pallas_call x5, Pallas kernels, call(): pl.pallas_call(kernel, out_shape=outs, in_specs=[spaces[x] for x in in_sp...  13.5 us
    ppermute x6, starting transfers between devices, swapped(): results.append(lax.ppermute(value[which], axis, pairs))  11.7 us
    ppermute x6, waiting for transfers between devices, swapped(): results.append(lax.ppermute(value[which], axis, pairs))  5.74 us
    ppermute x1, starting transfers between devices, per_device(): passed_rest = lax.ppermute(mate_rest, 'curve', pairs)  5.33 us
    ppermute x1, starting transfers between devices, per_device(): mate_rest = lax.ppermute(rest_msg, 'curve', pairs)  2.13 us
    unnamed x2, local copies, waits for them, and re-layouts  1.25 us
  transfers between devices with their start and end apart: 8, of which 3 were waited for; matrix products, arithmetic and copies ran while one was open for 0% of the time, Pallas kernels for 6%

profile of v7, /device:TPU:1, one launch (start us, length us, event | category | flops | bytes accessed | tf_op | source)
XLA Modules:
  0.0 40.8 jit_solution(15398260446298115661)
XLA Ops:
  0.7 4.1 %shard_map.55 = (f32[2224,128]{1,0:T(8,128)}, f32[460,128]{1,0:T(8,128)}, f32[460,128]{1,0:T(8,128)}, f32[144,128]{1,0:T(8,128)}, f32[144,128]{1,0:T(8,128)}, /*index=5*/f32[464,128]{1,0:T(8,128)}) custom-call(s32[3,32]{1,0:T(4,128)} %bitcast.1, s32[1]{0:T(128)S(6)} %copy.6.counts_hbm, f32[3,19,4096]{2,1,0:T(8,128)} %pops_hbm.1, s32[3,5832]{1,0:T(4,128)} %flags_hbm.1, ...), custom_call_target="tpu_custom_call" | custom-call | tf_op jit(solution)/shard_map/pallas_call | solution.py:902
  4.8 2.1 %collective-permute-start.4 = (f32[464,128]{1,0:T(8,128)}, f32[464,128]{1,0:T(8,128)S(1)}, u32[]{:S(2)}, u32[]{:S(2)}) collective-permute-start(f32[464,128]{1,0:T(8,128)} %get-tuple-element.23), channel_id=1, source_target_pairs={{0,4},{4,0},{8,12},{12,8},{16,20},{20,16},{24,28},{28,24},{1,5},{5... | collective-permute-start | bytes 712712 | tf_op jit(solution)/shard_map/ppermute | solution.py:949
  6.9 0.1 collective-permute-start
  7.0 0.7 %collective-permute-start.1 = (f32[460,128]{1,0:T(8,128)}, f32[460,128]{1,0:T(8,128)S(1)}, u32[]{:S(2)}, u32[]{:S(2)}) collective-permute-start(f32[460,128]{1,0:T(8,128)} %get-tuple-element.20), channel_id=1, source_target_pairs={{4,8},{8,4},{12,16},{16,12},{20,24},{24,20},{5,9},{9,5},{13,17},{1... | collective-permute-start | bytes 706568 | tf_op jit(solution)/shard_map/ppermute | solution.py:888
  7.7 3.9 %collective-permute-start.2 = (f32[144,128]{1,0:T(8,128)}, f32[144,128]{1,0:T(8,128)S(1)}, u32[]{:S(2)}, u32[]{:S(2)}) collective-permute-start(f32[144,128]{1,0:T(8,128)} %get-tuple-element.21), channel_id=1, source_target_pairs={{0,8},{4,12},{8,0},{12,4},{16,24},{20,28},{24,16},{28,20},{1,9},{5... | collective-permute-start | bytes 221192 | tf_op jit(solution)/shard_map/ppermute | solution.py:888
  11.5 0.7 %collective-permute-start.3 = (f32[144,128]{1,0:T(8,128)}, f32[144,128]{1,0:T(8,128)S(1)}, u32[]{:S(2)}, u32[]{:S(2)}) collective-permute-start(f32[144,128]{1,0:T(8,128)} %get-tuple-element.22), channel_id=1, source_target_pairs={{8,16},{12,20},{16,8},{20,12},{9,17},{13,21},{17,9},{21,13},{10,18... | collective-permute-start | bytes 221192 | tf_op jit(solution)/shard_map/ppermute | solution.py:888
  12.2 0.4 %collective-permute-done.4.mate_rest = f32[464,128]{1,0:T(8,128)S(1)} collective-permute-done((f32[464,128]{1,0:T(8,128)}, f32[464,128]{1,0:T(8,128)S(1)}, u32[]{:S(2)}, u32[]{:S(2)}) %collective-permute-start.4) | collective-permute-done | bytes 237600 | tf_op jit(solution)/shard_map/ppermute | solution.py:949
  12.6 5.3 %collective-permute-start.5 = (f32[464,128]{1,0:T(8,128)S(1)}, f32[464,128]{1,0:T(8,128)S(1)}, u32[]{:S(2)}, u32[]{:S(2)}) collective-permute-start(f32[464,128]{1,0:T(8,128)S(1)} %collective-permute-done.4.mate_rest), channel_id=1, source_target_pairs={{0,8},{8,16},{12,4},{16,24},{20,12},{28,20},{1,9},{9,17},{13,5},{1... | collective-permute-start | bytes 712712 | tf_op jit(solution)/shard_map/ppermute | solution.py:952
  18.0 0.0 copy-start
  18.0 1.2 %copy-done = f32[2224,128]{1,0:T(8,128)S(1)} copy-done((f32[2224,128]{1,0:T(8,128)S(1)}, f32[2224,128]{1,0:T(8,128)}, u32[]{:S(2)}) %copy-start) | copy-done | bytes 1138712
  19.2 0.1 shard_map.56
  19.3 0.0 collective-permute-done.2.mate2_msg
  19.3 0.0 collective-permute-done.3.other2_msg
  19.3 2.6 %collective-permute-done.mate_msg = f32[460,128]{1,0:T(8,128)S(1)} collective-permute-done((f32[460,128]{1,0:T(8,128)}, f32[460,128]{1,0:T(8,128)S(1)}, u32[]{:S(2)}, u32[]{:S(2)}) %collective-permute-start) | collective-permute-done | bytes 235552 | tf_op jit(solution)/shard_map/ppermute | solution.py:888
  21.9 0.0 collective-permute-done.1.other_msg
  21.9 1.1 %shard_map.58 = (f32[456,128]{1,0:T(8,128)S(1)}, f32[456,128]{1,0:T(8,128)S(1)}) custom-call(s32[8,128]{1,0:T(8,128)S(1)} %get-tuple-element.18.landings, f32[1440,128]{1,0:T(8,128)S(1)} %get-tuple-element.26.own_outer, f32[2224,128]{1,0:T(8,128)S(1)} %copy-done, f32[460,128]{1,0:T(8,128)S(1)} %collective-permute-done.mate_msg, ...), custom_call_target="tpu_custom_call" | custom-call | tf_op jit(solution)/shard_map/pallas_call | solution.py:902
  23.0 3.5 %collective-permute-start.6 = (f32[456,128]{1,0:T(8,128)S(1)}, f32[456,128]{1,0:T(8,128)S(1)}, u32[]{:S(2)}, u32[]{:S(2)}) collective-permute-start(f32[456,128]{1,0:T(8,128)S(1)} %get-tuple-element.27), channel_id=1, source_target_pairs={{0,1},{1,0},{2,3},{3,2},{4,5},{5,4},{6,7},{7,6},{8,9},{9,8},{10,11... | collective-permute-start | bytes 700424 | tf_op jit(solution)/shard_map/ppermute | solution.py:888
  26.4 2.9 %collective-permute-start.7 = (f32[456,128]{1,0:T(8,128)S(1)}, f32[456,128]{1,0:T(8,128)S(1)}, u32[]{:S(2)}, u32[]{:S(2)}) collective-permute-start(f32[456,128]{1,0:T(8,128)S(1)} %get-tuple-element.28), channel_id=1, source_target_pairs={{1,2},{2,1},{5,6},{6,5},{9,10},{10,9},{13,14},{14,13},{17,18},{18,... | collective-permute-start | bytes 700424 | tf_op jit(solution)/shard_map/ppermute | solution.py:888
  29.4 0.0 collective-permute-done.5.passed_rest
  29.4 1.2 %shard_map.57 = (f32[3792,128]{1,0:T(8,128)S(1)}, s32[24,128]{1,0:T(8,128)S(1)}) custom-call(s32[8,128]{1,0:T(8,128)S(1)} %get-tuple-element.18.landings, f32[2224,128]{1,0:T(8,128)S(1)} %copy-done, f32[460,128]{1,0:T(8,128)S(1)} %collective-permute-done.mate_msg, f32[460,128]{1,0:T(8,128)S(1)} %collective-permute-done.1.other_msg, ...), custom_call_target="tpu_custom_call" | custom-call | tf_op jit(solution)/shard_map/pallas_call | solution.py:902
  30.6 0.0 collective-permute-done.6.near_msg
  30.6 3.2 %collective-permute-done.7.far_msg = f32[456,128]{1,0:T(8,128)S(1)} collective-permute-done((f32[456,128]{1,0:T(8,128)S(1)}, f32[456,128]{1,0:T(8,128)S(1)}, u32[]{:S(2)}, u32[]{:S(2)}) %collective-permute-start.7) | collective-permute-done | bytes 233504 | tf_op jit(solution)/shard_map/ppermute | solution.py:888
  33.8 6.9 %shard_map.59 = f32[3,19,4096]{2,1,0:T(8,128)} custom-call(s32[24,128]{1,0:T(8,128)S(1)} %get-tuple-element.24.own_slots, f32[3792,128]{1,0:T(8,128)S(1)} %get-tuple-element.25.first_post, f32[456,128]{1,0:T(8,128)S(1)} %collective-permute-done.6.near_msg, f32[456,128]{1,0:T(8,128)S(1)} %collective-permute-done.7.far_msg), custom_call_target="tpu_custom_call" | custom-call | tf_op jit(solution)/shard_map/pallas_call | solution.py:902
Async XLA Ops:
  4.8 7.8 %collective-permute-start.4 = (f32[464,128]{1,0:T(8,128)}, f32[464,128]{1,0:T(8,128)S(1)}, u32[]{:S(2)}, u32[]{:S(2)}) collective-permute-start(f32[464,128]{1,0:T(8,128)} %get-tuple-element.23), channel_id=1, source_target_pairs={{0,4},{4,0},{8,12},{12,8},{16,20},{20,16},{24,28},{28,24},{1,5},{5... | collective-permute-start | bytes 712712 | tf_op jit(solution)/shard_map/ppermute | solution.py:949
  6.9 14.9 %collective-permute-start = (f32[460,128]{1,0:T(8,128)}, f32[460,128]{1,0:T(8,128)S(1)}, u32[]{:S(2)}, u32[]{:S(2)}) collective-permute-start(f32[460,128]{1,0:T(8,128)} %get-tuple-element.19), channel_id=1, source_target_pairs={{0,4},{4,0},{8,12},{12,8},{16,20},{20,16},{24,28},{28,24},{1,5},{5... | collective-permute-start | bytes 706568 | tf_op jit(solution)/shard_map/ppermute | solution.py:888
  7.0 14.9 %collective-permute-start.1 = (f32[460,128]{1,0:T(8,128)}, f32[460,128]{1,0:T(8,128)S(1)}, u32[]{:S(2)}, u32[]{:S(2)}) collective-permute-start(f32[460,128]{1,0:T(8,128)} %get-tuple-element.20), channel_id=1, source_target_pairs={{4,8},{8,4},{12,16},{16,12},{20,24},{24,20},{5,9},{9,5},{13,17},{1... | collective-permute-start | bytes 706568 | tf_op jit(solution)/shard_map/ppermute | solution.py:888
  7.7 11.6 %collective-permute-start.2 = (f32[144,128]{1,0:T(8,128)}, f32[144,128]{1,0:T(8,128)S(1)}, u32[]{:S(2)}, u32[]{:S(2)}) collective-permute-start(f32[144,128]{1,0:T(8,128)} %get-tuple-element.21), channel_id=1, source_target_pairs={{0,8},{4,12},{8,0},{12,4},{16,24},{20,28},{24,16},{28,20},{1,9},{5... | collective-permute-start | bytes 221192 | tf_op jit(solution)/shard_map/ppermute | solution.py:888
  11.5 7.8 %collective-permute-start.3 = (f32[144,128]{1,0:T(8,128)}, f32[144,128]{1,0:T(8,128)S(1)}, u32[]{:S(2)}, u32[]{:S(2)}) collective-permute-start(f32[144,128]{1,0:T(8,128)} %get-tuple-element.22), channel_id=1, source_target_pairs={{8,16},{12,20},{16,8},{20,12},{9,17},{13,21},{17,9},{21,13},{10,18... | collective-permute-start | bytes 221192 | tf_op jit(solution)/shard_map/ppermute | solution.py:888
  12.6 16.8 %collective-permute-start.5 = (f32[464,128]{1,0:T(8,128)S(1)}, f32[464,128]{1,0:T(8,128)S(1)}, u32[]{:S(2)}, u32[]{:S(2)}) collective-permute-start(f32[464,128]{1,0:T(8,128)S(1)} %collective-permute-done.4.mate_rest), channel_id=1, source_target_pairs={{0,8},{8,16},{12,4},{16,24},{20,12},{28,20},{1,9},{9,17},{13,5},{1... | collective-permute-start | bytes 712712 | tf_op jit(solution)/shard_map/ppermute | solution.py:952
  18.0 1.3 %copy-start = (f32[2224,128]{1,0:T(8,128)S(1)}, f32[2224,128]{1,0:T(8,128)}, u32[]{:S(2)}) copy-start(f32[2224,128]{1,0:T(8,128)} %get-tuple-element.17.cells) | copy-start | bytes 3416068
  23.0 7.6 %collective-permute-start.6 = (f32[456,128]{1,0:T(8,128)S(1)}, f32[456,128]{1,0:T(8,128)S(1)}, u32[]{:S(2)}, u32[]{:S(2)}) collective-permute-start(f32[456,128]{1,0:T(8,128)S(1)} %get-tuple-element.27), channel_id=1, source_target_pairs={{0,1},{1,0},{2,3},{3,2},{4,5},{5,4},{6,7},{7,6},{8,9},{9,8},{10,11... | collective-permute-start | bytes 700424 | tf_op jit(solution)/shard_map/ppermute | solution.py:888
  26.4 7.4 %collective-permute-start.7 = (f32[456,128]{1,0:T(8,128)S(1)}, f32[456,128]{1,0:T(8,128)S(1)}, u32[]{:S(2)}, u32[]{:S(2)}) collective-permute-start(f32[456,128]{1,0:T(8,128)S(1)} %get-tuple-element.28), channel_id=1, source_target_pairs={{1,2},{2,1},{5,6},{6,5},{9,10},{10,9},{13,14},{14,13},{17,18},{18,... | collective-permute-start | bytes 700424 | tf_op jit(solution)/shard_map/ppermute | solution.py:888

commit v8 on v7

--- a/solution.py
+++ b/solution.py
@@ -1,4 +1,5 @@
 import functools
+import itertools
 
 import jax
 import jax.numpy as jnp
@@ -31,6 +32,7 @@
 FAR = QUADS * GROUP
 EDGE_TABLE = FAR + 3 * GROUP
 EDGE_ROWS = EDGE_TABLE + 24
+CUT = EDGE_ROWS // 16 * 8
 NOWHERE = PLANES * GROUP
 ALL_PLANES = PLANES + POPS
 LIMIT = 20 * 1024 * 1024
@@ -307,9 +309,8 @@
         one.wait()
 
 
-def spread_kernel(cells, outer, landings):
+def spread_kernel(cells, outer):
     low = lanes_iota() < 64
-    landings[...] = cells[LANDINGS : LANDINGS + 8, :].astype(jnp.int32)
     for q in range(PLANES):
         for v in range(2):
             row = q * 32 + v * 8
@@ -334,6 +335,10 @@
         def _():
             low[...] = mate[...]
             high[...] = other[...]
+
+
+def landed_slots(cells):
+    return [jnp.max(cells[LANDINGS + i : LANDINGS + i + 1, :]) for i in range(6)]
 
 
 def rim_of(msg, p, v):
@@ -376,7 +381,6 @@
 
 
 def edge_kernel(
-    landings,
     own_outer,
     cells,
     mate_msg,
@@ -385,6 +389,7 @@
     other2_msg,
     near_msg,
     far_msg,
+    far2_msg,
     outer,
     low_msg,
     high_msg,
@@ -394,7 +399,7 @@
     sort_messages(
         mate_msg, other_msg, mate2_msg, other2_msg, low_msg, high_msg, low2_msg, high2_msg
     )
-    from_low, from_high, low_low, low_me, high_high, high_me = (landings[i, 0] for i in range(6))
+    from_low, from_high, low_low, low_me, high_high, high_me = landed_slots(cells)
     low = lanes_iota() < 64
     for q in range(PLANES):
         for v in range(2):
@@ -412,9 +417,11 @@
                 msg[LAYERS + source : LAYERS + source + count, :],
             )
     lane = lanes_iota()
-    for slot, msg in ((from_low, low_msg), (from_high, high_msg)):
-
-        @pl.when(slot >= 0)
+    for s, (slot, msg) in itertools.product(
+        range(SLOTS), ((from_low, low_msg), (from_high, high_msg))
+    ):
+
+        @pl.when(slot == s)
         def _():
             for v in range(2):
                 values = [rim_of(msg, p, v) for p in range(POPS)]
@@ -423,8 +430,8 @@
                     moved = pltpu.roll(msg[row : row + 8, :], (target - source) % 128, axis=1)
                     values[pop] = jnp.where(lane // 16 == target // 16, moved, values[pop])
                 for p, value in enumerate(values):
-                    base = slot * (POPS * GROUP) + p * GROUP + v * 8
-                    outer[aligned(base), :] = value
+                    row = (s * POPS + p) * GROUP + v * 8
+                    outer[row : row + 8, :] = value
 
     for s in range(SLOTS):
         for slot, msg, row0 in (
@@ -446,7 +453,8 @@
 
     def send(row, north, south):
         near_msg[row : row + 8, :] = jnp.where(even, north, south)
-        far_msg[row : row + 8, :] = jnp.where(even, south, north)
+        ref, row = (far_msg, row) if row < CUT else (far2_msg, row - CUT)
+        ref[row : row + 8, :] = jnp.where(even, south, north)
 
     for v in range(3):
 
@@ -717,7 +725,6 @@
 
 
 def join_kernel(
-    landings,
     cells,
     mate_msg,
     other_msg,
@@ -738,7 +745,7 @@
     for i, (ref, row) in enumerate(((low_msg, TABLE), (cells, CELLS), (high_msg, TABLE))):
         slots[8 * i : 8 * i + 8, :] = first_rows(ref[row : row + 8, :])
 
-    from_low, from_high, low_low, low_me, high_high, high_me = (landings[i, 0] for i in range(6))
+    from_low, from_high, low_low, low_me, high_high, high_me = landed_slots(cells)
     lane = lanes_iota()
     post_ref[PLANES * PAIR :, :] = jnp.full((POPS * PAIR, 128), jnp.nan, jnp.float32)
     for q in range(PLANES):
@@ -749,14 +756,17 @@
             ]
     even = is_even("curve")
     odd = jnp.logical_not(even)
-    for slot, msg, wanted, rest in (
-        (from_low, low_msg, odd, mate_rest),
-        (from_low, low_msg, even, passed_rest),
-        (from_high, high_msg, even, mate_rest),
-        (from_high, high_msg, odd, passed_rest),
+    for s, (slot, msg, wanted, rest) in itertools.product(
+        range(SLOTS),
+        (
+            (from_low, low_msg, odd, mate_rest),
+            (from_low, low_msg, even, passed_rest),
+            (from_high, high_msg, even, mate_rest),
+            (from_high, high_msg, odd, passed_rest),
+        ),
     ):
 
-        @pl.when((slot >= 0) & wanted)
+        @pl.when((slot == s) & wanted)
         def _():
             for p in range(POPS):
                 for v in range(2):
@@ -768,9 +778,9 @@
                     if p % 2:
                         middle = pltpu.roll(middle, 64, axis=1)
                     second = jnp.where(lane < 32, wide, jnp.where(lane < 96, middle, rim))
-                    start = slot * (POPS * PAIR) + p * PAIR + v * 8
-                    post_ref[aligned(start), :] = jnp.where(lane < 32, rim, wide)
-                    post_ref[aligned(start + GROUP), :] = second
+                    row = (s * POPS + p) * PAIR + v * 8
+                    post_ref[row : row + 8, :] = jnp.where(lane < 32, rim, wide)
+                    post_ref[row + GROUP : row + GROUP + 8, :] = second
 
     for msg, row0, step, first in ((high_msg, 16, 1, 2), (low_msg, 23, -1, 1)):
         for y in range(2):
@@ -805,6 +815,7 @@
     first_post,
     near_msg,
     far_msg,
+    far2_msg,
     out_hbm,
     h_ref,
     post_ref,
@@ -817,7 +828,9 @@
     even = is_even("cross")
 
     def received(row):
-        near, far = near_msg[row : row + 8, :], far_msg[row : row + 8, :]
+        near = near_msg[row : row + 8, :]
+        ref, row = (far_msg, row) if row < CUT else (far2_msg, row - CUT)
+        far = ref[row : row + 8, :]
         return jnp.where(even, far, near), jnp.where(even, near, far)
 
     for i in range(3):
@@ -883,6 +896,8 @@
     count = lax.axis_size(axis)
     results = []
     for which in (0, 1):
+        if value[which] is None:
+            continue
         sides = [unit if i // unit % 2 == which else -unit for i in range(count)]
         pairs = [(i, i + side) for i, side in enumerate(sides) if 0 <= i + side < count]
         results.append(lax.ppermute(value[which], axis, pairs))
@@ -950,39 +965,33 @@
     pairs = [(i, i - 2 if i % 2 else i + 2) for i in range(sizes[0])]
     pairs = [pair for pair in pairs if 0 <= pair[1] < sizes[0]]
     passed_rest = lax.ppermute(mate_rest, "curve", pairs)
-    outer, landings = call(
-        spread_kernel,
-        "V",
-        "VV",
-        [rows128(PLANES * GROUP), jax.ShapeDtypeStruct((8, 128), jnp.int32)],
-        (cells,),
-        [],
-    )
+    (outer,) = call(spread_kernel, "V", "V", [rows128(PLANES * GROUP)], (cells,), [])
     strips = (cells, mate_msg, other_msg, mate2_msg, other2_msg)
     sorted_rows = [messages[1], messages[1], messages[3], messages[3]]
-    near_msg, far_msg = call(
+    near_msg, far_msg, far2_msg = call(
         edge_kernel,
-        "SVVVVVV",
-        "VV",
-        [rows128(EDGE_ROWS), rows128(EDGE_ROWS)],
-        (landings, outer, *strips),
+        "VVVVVV",
+        "VVV",
+        [rows128(EDGE_ROWS), rows128(CUT), rows128(EDGE_ROWS - CUT)],
+        (outer, *strips),
         [floats(rows) for rows in [PLANES * GROUP] + sorted_rows],
     )
     near_msg, far_msg = swapped((near_msg, far_msg), "cross")
+    (far2_msg,) = swapped((None, far2_msg), "cross")
     post, own_slots = call(
         join_kernel,
-        "SVVVVVVV",
+        "VVVVVVV",
         "VV",
         [rows128(ALL_PLANES * PAIR), jax.ShapeDtypeStruct((24, 128), jnp.int32)],
-        (landings, *strips, mate_rest, passed_rest),
+        (*strips, mate_rest, passed_rest),
         [floats(rows) for rows in sorted_rows],
     )
     return call(
         steps_kernel,
-        "VVVV",
+        "VVVVV",
         "H",
         [jax.ShapeDtypeStruct(populations.shape, jnp.float32)],
-        (own_slots, post, near_msg, far_msg),
+        (own_slots, post, near_msg, far_msg, far2_msg),
         [
             floats(SLOTS * SLOT),
             floats(ALL_PLANES * PAIR),

time: 41 us -> 42.2 us (1.029)
  starting transfers between devices: 19.1 us -> 21.6 us
  Pallas kernels: 13.5 us -> 12.5 us
    ppermute x6 -> x7, starting transfers between devices: 11.7 us -> 14.1 us  [swapped(): results.append(lax.ppermute(value[which], axis, pairs))]
    pallas_call x5, Pallas kernels: 13.5 us -> 12.5 us  [call(): pl.pallas_call(kernel, out_shape=outs, in_specs=[spaces[x] for x in in_sp...]
    ppermute x6 -> x7, waiting for transfers between devices: 5.74 us -> 5.42 us  [swapped(): results.append(lax.ppermute(value[which], axis, pairs))]
  transfers between devices with their start and end apart: 8 -> 9, of which waited for: 3 -> 3; matrix products, arithmetic and copies ran while one was open for 0% -> 0% of each run, Pallas kernels for 6% -> 4%
where the time goes in v8:
time: 42.2 us; the launch traced here: 42 us
  starting transfers between devices  21.6 us (51%)
  Pallas kernels  12.5 us (30%)
  waiting for transfers between devices  5.86 us (14%)
  local copies, waits for them, and re-layouts  1.25 us (3%)
  between operations  0.75 us (2%)
    ppermute x7, starting transfers between devices, swapped(): results.append(lax.ppermute(value[which], axis, pairs))  14.1 us
    pallas_call x5, Pallas kernels, call(): pl.pallas_call(kernel, out_shape=outs, in_specs=[spaces[x] for x in in_sp...  12.5 us
    ppermute x7, waiting for transfers between devices, swapped(): results.append(lax.ppermute(value[which], axis, pairs))  5.42 us
    ppermute x1, starting transfers between devices, per_device(): passed_rest = lax.ppermute(mate_rest, 'curve', pairs)  5.33 us
    ppermute x1, starting transfers between devices, per_device(): mate_rest = lax.ppermute(rest_msg, 'curve', pairs)  2.13 us
    unnamed x2, local copies, waits for them, and re-layouts  1.25 us
  transfers between devices with their start and end apart: 9, of which 3 were waited for; matrix products, arithmetic and copies ran while one was open for 0% of the time, Pallas kernels for 4%

profile of v8, /device:TPU:1, one launch (start us, length us, event | category | flops | bytes accessed | tf_op | source)
XLA Modules:
  0.0 42.0 jit_solution(8356692279537977630)
XLA Ops:
  0.7 4.1 %shard_map.55 = (f32[2224,128]{1,0:T(8,128)}, f32[460,128]{1,0:T(8,128)}, f32[460,128]{1,0:T(8,128)}, f32[144,128]{1,0:T(8,128)}, f32[144,128]{1,0:T(8,128)}, /*index=5*/f32[464,128]{1,0:T(8,128)}) custom-call(s32[3,32]{1,0:T(4,128)} %bitcast.1, s32[1]{0:T(128)S(6)} %copy.6.counts_hbm, f32[3,19,4096]{2,1,0:T(8,128)} %pops_hbm.1, s32[3,5832]{1,0:T(4,128)} %flags_hbm.1, ...), custom_call_target="tpu_custom_call" | custom-call | tf_op jit(solution)/shard_map/pallas_call | solution.py:917
  4.8 2.1 %collective-permute-start.4 = (f32[464,128]{1,0:T(8,128)}, f32[464,128]{1,0:T(8,128)S(1)}, u32[]{:S(2)}, u32[]{:S(2)}) collective-permute-start(f32[464,128]{1,0:T(8,128)} %get-tuple-element.21), channel_id=1, source_target_pairs={{0,4},{4,0},{8,12},{12,8},{16,20},{20,16},{24,28},{28,24},{1,5},{5... | collective-permute-start | bytes 712712 | tf_op jit(solution)/shard_map/ppermute | solution.py:964
  6.9 0.1 collective-permute-start
  7.0 0.7 %collective-permute-start.1 = (f32[460,128]{1,0:T(8,128)}, f32[460,128]{1,0:T(8,128)S(1)}, u32[]{:S(2)}, u32[]{:S(2)}) collective-permute-start(f32[460,128]{1,0:T(8,128)} %get-tuple-element.18), channel_id=1, source_target_pairs={{4,8},{8,4},{12,16},{16,12},{20,24},{24,20},{5,9},{9,5},{13,17},{1... | collective-permute-start | bytes 706568 | tf_op jit(solution)/shard_map/ppermute | solution.py:903
  7.7 3.9 %collective-permute-start.2 = (f32[144,128]{1,0:T(8,128)}, f32[144,128]{1,0:T(8,128)S(1)}, u32[]{:S(2)}, u32[]{:S(2)}) collective-permute-start(f32[144,128]{1,0:T(8,128)} %get-tuple-element.19), channel_id=1, source_target_pairs={{0,8},{4,12},{8,0},{12,4},{16,24},{20,28},{24,16},{28,20},{1,9},{5... | collective-permute-start | bytes 221192 | tf_op jit(solution)/shard_map/ppermute | solution.py:903
  11.5 0.7 %collective-permute-start.3 = (f32[144,128]{1,0:T(8,128)}, f32[144,128]{1,0:T(8,128)S(1)}, u32[]{:S(2)}, u32[]{:S(2)}) collective-permute-start(f32[144,128]{1,0:T(8,128)} %get-tuple-element.20), channel_id=1, source_target_pairs={{8,16},{12,20},{16,8},{20,12},{9,17},{13,21},{17,9},{21,13},{10,18... | collective-permute-start | bytes 221192 | tf_op jit(solution)/shard_map/ppermute | solution.py:903
  12.2 0.4 %collective-permute-done.4.mate_rest = f32[464,128]{1,0:T(8,128)S(1)} collective-permute-done((f32[464,128]{1,0:T(8,128)}, f32[464,128]{1,0:T(8,128)S(1)}, u32[]{:S(2)}, u32[]{:S(2)}) %collective-permute-start.4) | collective-permute-done | bytes 237600 | tf_op jit(solution)/shard_map/ppermute | solution.py:964
  12.6 5.3 %collective-permute-start.5 = (f32[464,128]{1,0:T(8,128)S(1)}, f32[464,128]{1,0:T(8,128)S(1)}, u32[]{:S(2)}, u32[]{:S(2)}) collective-permute-start(f32[464,128]{1,0:T(8,128)S(1)} %collective-permute-done.4.mate_rest), channel_id=1, source_target_pairs={{0,8},{8,16},{12,4},{16,24},{20,12},{28,20},{1,9},{9,17},{13,5},{1... | collective-permute-start | bytes 712712 | tf_op jit(solution)/shard_map/ppermute | solution.py:967
  18.0 0.0 copy-start
  18.0 1.2 %copy-done = f32[2224,128]{1,0:T(8,128)S(1)} copy-done((f32[2224,128]{1,0:T(8,128)S(1)}, f32[2224,128]{1,0:T(8,128)}, u32[]{:S(2)}) %copy-start) | copy-done | bytes 1138712
  19.2 0.1 shard_map.57.own_outer
  19.3 0.0 collective-permute-done.2.mate2_msg
  19.3 0.0 collective-permute-done.3.other2_msg
  19.3 2.6 %collective-permute-done.mate_msg = f32[460,128]{1,0:T(8,128)S(1)} collective-permute-done((f32[460,128]{1,0:T(8,128)}, f32[460,128]{1,0:T(8,128)S(1)}, u32[]{:S(2)}, u32[]{:S(2)}) %collective-permute-start) | collective-permute-done | bytes 235552 | tf_op jit(solution)/shard_map/ppermute | solution.py:903
  21.9 0.0 collective-permute-done.1.other_msg
  21.9 0.7 %shard_map.58 = (f32[456,128]{1,0:T(8,128)S(1)}, f32[224,128]{1,0:T(8,128)S(1)}, f32[232,128]{1,0:T(8,128)S(1)}) custom-call(f32[1440,128]{1,0:T(8,128)S(1)} %shard_map.57.own_outer, f32[2224,128]{1,0:T(8,128)S(1)} %copy-done, f32[460,128]{1,0:T(8,128)S(1)} %collective-permute-done.mate_msg, f32[460,128]{1,0:T(8,128)S(1)} %collective-permute-done.1.other_msg, ...), custom_call_target="tpu_custom_call" | custom-call | tf_op jit(solution)/shard_map/pallas_call | solution.py:917
  22.5 3.3 %collective-permute-start.6 = (f32[456,128]{1,0:T(8,128)S(1)}, f32[456,128]{1,0:T(8,128)S(1)}, u32[]{:S(2)}, u32[]{:S(2)}) collective-permute-start(f32[456,128]{1,0:T(8,128)S(1)} %get-tuple-element.24), channel_id=1, source_target_pairs={{0,1},{1,0},{2,3},{3,2},{4,5},{5,4},{6,7},{7,6},{8,9},{9,8},{10,11... | collective-permute-start | bytes 700424 | tf_op jit(solution)/shard_map/ppermute | solution.py:903
  25.8 3.1 %collective-permute-start.8 = (f32[232,128]{1,0:T(8,128)S(1)}, f32[232,128]{1,0:T(8,128)S(1)}, u32[]{:S(2)}, u32[]{:S(2)}) collective-permute-start(f32[232,128]{1,0:T(8,128)S(1)} %get-tuple-element.26), channel_id=1, source_target_pairs={{1,2},{2,1},{5,6},{6,5},{9,10},{10,9},{13,14},{14,13},{17,18},{18,... | collective-permute-start | bytes 356360 | tf_op jit(solution)/shard_map/ppermute | solution.py:903
  28.9 2.4 %collective-permute-start.7 = (f32[224,128]{1,0:T(8,128)S(1)}, f32[224,128]{1,0:T(8,128)S(1)}, u32[]{:S(2)}, u32[]{:S(2)}) collective-permute-start(f32[224,128]{1,0:T(8,128)S(1)} %get-tuple-element.25), channel_id=1, source_target_pairs={{1,2},{2,1},{5,6},{6,5},{9,10},{10,9},{13,14},{14,13},{17,18},{18,... | collective-permute-start | bytes 344072 | tf_op jit(solution)/shard_map/ppermute | solution.py:903
  31.4 0.0 collective-permute-done.5.passed_rest
  31.4 0.8 %shard_map.56 = (f32[3792,128]{1,0:T(8,128)S(1)}, s32[24,128]{1,0:T(8,128)S(1)}) custom-call(f32[2224,128]{1,0:T(8,128)S(1)} %copy-done, f32[460,128]{1,0:T(8,128)S(1)} %collective-permute-done.mate_msg, f32[460,128]{1,0:T(8,128)S(1)} %collective-permute-done.1.other_msg, f32[144,128]{1,0:T(8,128)S(1)} %collective-permute-done.2.mate2_msg, ...), custom_call_target="tpu_custom_call" | custom-call | tf_op jit(solution)/shard_map/pallas_call | solution.py:917
  32.2 2.9 %collective-permute-done.7.far_msg = f32[224,128]{1,0:T(8,128)S(1)} collective-permute-done((f32[224,128]{1,0:T(8,128)S(1)}, f32[224,128]{1,0:T(8,128)S(1)}, u32[]{:S(2)}, u32[]{:S(2)}) %collective-permute-start.7) | collective-permute-done | bytes 114720 | tf_op jit(solution)/shard_map/ppermute | solution.py:903
  35.1 0.0 collective-permute-done.8.far2_msg
  35.1 0.0 collective-permute-done.6.near_msg
  35.1 6.9 %shard_map.59 = f32[3,19,4096]{2,1,0:T(8,128)} custom-call(s32[24,128]{1,0:T(8,128)S(1)} %get-tuple-element.22.own_slots, f32[3792,128]{1,0:T(8,128)S(1)} %get-tuple-element.23.first_post, f32[456,128]{1,0:T(8,128)S(1)} %collective-permute-done.6.near_msg, f32[224,128]{1,0:T(8,128)S(1)} %collective-permute-done.7.far_msg, ...), custom_call_target="tpu_custom_call" | custom-call | tf_op jit(solution)/shard_map/pallas_call | solution.py:917
Async XLA Ops:
  4.8 7.8 %collective-permute-start.4 = (f32[464,128]{1,0:T(8,128)}, f32[464,128]{1,0:T(8,128)S(1)}, u32[]{:S(2)}, u32[]{:S(2)}) collective-permute-start(f32[464,128]{1,0:T(8,128)} %get-tuple-element.21), channel_id=1, source_target_pairs={{0,4},{4,0},{8,12},{12,8},{16,20},{20,16},{24,28},{28,24},{1,5},{5... | collective-permute-start | bytes 712712 | tf_op jit(solution)/shard_map/ppermute | solution.py:964
  6.9 14.9 %collective-permute-start = (f32[460,128]{1,0:T(8,128)}, f32[460,128]{1,0:T(8,128)S(1)}, u32[]{:S(2)}, u32[]{:S(2)}) collective-permute-start(f32[460,128]{1,0:T(8,128)} %get-tuple-element.17), channel_id=1, source_target_pairs={{0,4},{4,0},{8,12},{12,8},{16,20},{20,16},{24,28},{28,24},{1,5},{5... | collective-permute-start | bytes 706568 | tf_op jit(solution)/shard_map/ppermute | solution.py:903
  7.0 14.9 %collective-permute-start.1 = (f32[460,128]{1,0:T(8,128)}, f32[460,128]{1,0:T(8,128)S(1)}, u32[]{:S(2)}, u32[]{:S(2)}) collective-permute-start(f32[460,128]{1,0:T(8,128)} %get-tuple-element.18), channel_id=1, source_target_pairs={{4,8},{8,4},{12,16},{16,12},{20,24},{24,20},{5,9},{9,5},{13,17},{1... | collective-permute-start | bytes 706568 | tf_op jit(solution)/shard_map/ppermute | solution.py:903
  7.7 11.6 %collective-permute-start.2 = (f32[144,128]{1,0:T(8,128)}, f32[144,128]{1,0:T(8,128)S(1)}, u32[]{:S(2)}, u32[]{:S(2)}) collective-permute-start(f32[144,128]{1,0:T(8,128)} %get-tuple-element.19), channel_id=1, source_target_pairs={{0,8},{4,12},{8,0},{12,4},{16,24},{20,28},{24,16},{28,20},{1,9},{5... | collective-permute-start | bytes 221192 | tf_op jit(solution)/shard_map/ppermute | solution.py:903
  11.5 7.8 %collective-permute-start.3 = (f32[144,128]{1,0:T(8,128)}, f32[144,128]{1,0:T(8,128)S(1)}, u32[]{:S(2)}, u32[]{:S(2)}) collective-permute-start(f32[144,128]{1,0:T(8,128)} %get-tuple-element.20), channel_id=1, source_target_pairs={{8,16},{12,20},{16,8},{20,12},{9,17},{13,21},{17,9},{21,13},{10,18... | collective-permute-start | bytes 221192 | tf_op jit(solution)/shard_map/ppermute | solution.py:903
  12.6 18.8 %collective-permute-start.5 = (f32[464,128]{1,0:T(8,128)S(1)}, f32[464,128]{1,0:T(8,128)S(1)}, u32[]{:S(2)}, u32[]{:S(2)}) collective-permute-start(f32[464,128]{1,0:T(8,128)S(1)} %collective-permute-done.4.mate_rest), channel_id=1, source_target_pairs={{0,8},{8,16},{12,4},{16,24},{20,12},{28,20},{1,9},{9,17},{13,5},{1... | collective-permute-start | bytes 712712 | tf_op jit(solution)/shard_map/ppermute | solution.py:967
  18.0 1.3 %copy-start = (f32[2224,128]{1,0:T(8,128)S(1)}, f32[2224,128]{1,0:T(8,128)}, u32[]{:S(2)}) copy-start(f32[2224,128]{1,0:T(8,128)} %get-tuple-element.16.cells) | copy-start | bytes 3416068
  22.5 12.5 %collective-permute-start.6 = (f32[456,128]{1,0:T(8,128)S(1)}, f32[456,128]{1,0:T(8,128)S(1)}, u32[]{:S(2)}, u32[]{:S(2)}) collective-permute-start(f32[456,128]{1,0:T(8,128)S(1)} %get-tuple-element.24), channel_id=1, source_target_pairs={{0,1},{1,0},{2,3},{3,2},{4,5},{5,4},{6,7},{7,6},{8,9},{9,8},{10,11... | collective-permute-start | bytes 700424 | tf_op jit(solution)/shard_map/ppermute | solution.py:903
  25.8 9.2 %collective-permute-start.8 = (f32[232,128]{1,0:T(8,128)S(1)}, f32[232,128]{1,0:T(8,128)S(1)}, u32[]{:S(2)}, u32[]{:S(2)}) collective-permute-start(f32[232,128]{1,0:T(8,128)S(1)} %get-tuple-element.26), channel_id=1, source_target_pairs={{1,2},{2,1},{5,6},{6,5},{9,10},{10,9},{13,14},{14,13},{17,18},{18,... | collective-permute-start | bytes 356360 | tf_op jit(solution)/shard_map/ppermute | solution.py:903
  28.9 6.1 %collective-permute-start.7 = (f32[224,128]{1,0:T(8,128)S(1)}, f32[224,128]{1,0:T(8,128)S(1)}, u32[]{:S(2)}, u32[]{:S(2)}) collective-permute-start(f32[224,128]{1,0:T(8,128)S(1)} %get-tuple-element.25), channel_id=1, source_target_pairs={{1,2},{2,1},{5,6},{6,5},{9,10},{10,9},{13,14},{14,13},{17,18},{18,... | collective-permute-start | bytes 344072 | tf_op jit(solution)/shard_map/ppermute | solution.py:903

commit v9 on v8

--- a/solution.py
+++ b/solution.py
@@ -32,7 +32,6 @@
 FAR = QUADS * GROUP
 EDGE_TABLE = FAR + 3 * GROUP
 EDGE_ROWS = EDGE_TABLE + 24
-CUT = EDGE_ROWS // 16 * 8
 NOWHERE = PLANES * GROUP
 ALL_PLANES = PLANES + POPS
 LIMIT = 20 * 1024 * 1024
@@ -389,7 +388,6 @@
     other2_msg,
     near_msg,
     far_msg,
-    far2_msg,
     outer,
     low_msg,
     high_msg,
@@ -453,8 +451,7 @@
 
     def send(row, north, south):
         near_msg[row : row + 8, :] = jnp.where(even, north, south)
-        ref, row = (far_msg, row) if row < CUT else (far2_msg, row - CUT)
-        ref[row : row + 8, :] = jnp.where(even, south, north)
+        far_msg[row : row + 8, :] = jnp.where(even, south, north)
 
     for v in range(3):
 
@@ -815,7 +812,6 @@
     first_post,
     near_msg,
     far_msg,
-    far2_msg,
     out_hbm,
     h_ref,
     post_ref,
@@ -828,9 +824,7 @@
     even = is_even("cross")
 
     def received(row):
-        near = near_msg[row : row + 8, :]
-        ref, row = (far_msg, row) if row < CUT else (far2_msg, row - CUT)
-        far = ref[row : row + 8, :]
+        near, far = near_msg[row : row + 8, :], far_msg[row : row + 8, :]
         return jnp.where(even, far, near), jnp.where(even, near, far)
 
     for i in range(3):
@@ -896,10 +890,8 @@
     count = lax.axis_size(axis)
     results = []
     for which in (0, 1):
-        if value[which] is None:
-            continue
-        sides = [unit if i // unit % 2 == which else -unit for i in range(count)]
-        pairs = [(i, i + side) for i, side in enumerate(sides) if 0 <= i + side < count]
+        others = [i + (unit if i // unit % 2 == which else -unit) for i in range(count)]
+        pairs = [(i, j if 0 <= j < count else i) for i, j in enumerate(others)]
         results.append(lax.ppermute(value[which], axis, pairs))
     return results
 
@@ -962,22 +954,20 @@
     assert sizes[0] % 2 == 0
     pairs = [(i, i ^ 1) for i in range(sizes[0])]
     mate_rest = lax.ppermute(rest_msg, "curve", pairs)
-    pairs = [(i, i - 2 if i % 2 else i + 2) for i in range(sizes[0])]
-    pairs = [pair for pair in pairs if 0 <= pair[1] < sizes[0]]
+    pairs = [(i, (i - 2 if i % 2 else i + 2) % sizes[0]) for i in range(sizes[0])]
     passed_rest = lax.ppermute(mate_rest, "curve", pairs)
     (outer,) = call(spread_kernel, "V", "V", [rows128(PLANES * GROUP)], (cells,), [])
     strips = (cells, mate_msg, other_msg, mate2_msg, other2_msg)
     sorted_rows = [messages[1], messages[1], messages[3], messages[3]]
-    near_msg, far_msg, far2_msg = call(
+    near_msg, far_msg = call(
         edge_kernel,
         "VVVVVV",
-        "VVV",
-        [rows128(EDGE_ROWS), rows128(CUT), rows128(EDGE_ROWS - CUT)],
+        "VV",
+        [rows128(EDGE_ROWS), rows128(EDGE_ROWS)],
         (outer, *strips),
         [floats(rows) for rows in [PLANES * GROUP] + sorted_rows],
     )
     near_msg, far_msg = swapped((near_msg, far_msg), "cross")
-    (far2_msg,) = swapped((None, far2_msg), "cross")
     post, own_slots = call(
         join_kernel,
         "VVVVVVV",
@@ -988,10 +978,10 @@
     )
     return call(
         steps_kernel,
-        "VVVVV",
+        "VVVV",
         "H",
         [jax.ShapeDtypeStruct(populations.shape, jnp.float32)],
-        (own_slots, post, near_msg, far_msg, far2_msg),
+        (own_slots, post, near_msg, far_msg),
         [
             floats(SLOTS * SLOT),
             floats(ALL_PLANES * PAIR),

time: 42.2 us -> 38.8 us (0.919)
  the two profiles are of different devices: /device:TPU:1 before, /device:TPU:13 now
where the time goes in v9:
time: 38.8 us; the launch traced here: 38.6 us
  Pallas kernels  12.6 us (32%)
  starting transfers between devices  12.6 us (32%)
  waiting for transfers between devices  11.4 us (29%)
  local copies, waits for them, and re-layouts  1.25 us (3%)
  between operations  0.75 us (2%)
    pallas_call x5, Pallas kernels, call(): pl.pallas_call(kernel, out_shape=outs, in_specs=[spaces[x] for x in in_sp...  12.6 us
    ppermute x6, starting transfers between devices, swapped(): results.append(lax.ppermute(value[which], axis, pairs))  12.3 us
    ppermute x6, waiting for transfers between devices, swapped(): results.append(lax.ppermute(value[which], axis, pairs))  11.4 us
    unnamed x2, local copies, waits for them, and re-layouts  1.25 us
  transfers between devices with their start and end apart: 8, of which 3 were waited for; matrix products, arithmetic and copies ran while one was open for 0% of the time, Pallas kernels for 4%

profile of v9, /device:TPU:13, one launch (start us, length us, event | category | flops | bytes accessed | tf_op | source)
XLA Modules:
  0.0 38.6 jit_solution(13145886583002988792)
XLA Ops:
  0.7 4.1 %shard_map.55 = (f32[2224,128]{1,0:T(8,128)}, f32[460,128]{1,0:T(8,128)}, f32[460,128]{1,0:T(8,128)}, f32[144,128]{1,0:T(8,128)}, f32[144,128]{1,0:T(8,128)}, /*index=5*/f32[464,128]{1,0:T(8,128)}) custom-call(s32[3,32]{1,0:T(4,128)} %bitcast.1, s32[1]{0:T(128)S(6)} %copy.6.counts_hbm, f32[3,19,4096]{2,1,0:T(8,128)} %pops_hbm.1, s32[3,5832]{1,0:T(4,128)} %flags_hbm.1, ...), custom_call_target="tpu_custom_call" | custom-call | tf_op jit(solution)/shard_map/pallas_call | solution.py:909
  4.8 0.3 collective-permute-start.4
  5.1 1.2 %collective-permute-start = (f32[460,128]{1,0:T(8,128)}, f32[460,128]{1,0:T(8,128)S(1)}, u32[]{:S(2)}, u32[]{:S(2)}) collective-permute-start(f32[460,128]{1,0:T(8,128)} %get-tuple-element.16), channel_id=1, source_target_pairs={{0,4},{4,0},{8,12},{12,8},{16,20},{20,16},{24,28},{28,24},{1,5},{5... | collective-permute-start | bytes 706568 | tf_op jit(solution)/shard_map/ppermute | solution.py:895
  6.3 3.1 %collective-permute-start.1 = (f32[460,128]{1,0:T(8,128)}, f32[460,128]{1,0:T(8,128)S(1)}, u32[]{:S(2)}, u32[]{:S(2)}) collective-permute-start(f32[460,128]{1,0:T(8,128)} %get-tuple-element.17), channel_id=1, source_target_pairs={{0,0},{4,8},{8,4},{12,16},{16,12},{20,24},{24,20},{28,28},{1,1},{5... | collective-permute-start | bytes 706568 | tf_op jit(solution)/shard_map/ppermute | solution.py:895
  9.5 0.2 collective-permute-start.2
  9.7 3.0 %collective-permute-start.3 = (f32[144,128]{1,0:T(8,128)}, f32[144,128]{1,0:T(8,128)S(1)}, u32[]{:S(2)}, u32[]{:S(2)}) collective-permute-start(f32[144,128]{1,0:T(8,128)} %get-tuple-element.19), channel_id=1, source_target_pairs={{0,0},{4,4},{8,16},{12,20},{16,8},{20,12},{24,24},{28,28},{1,1},{5... | collective-permute-start | bytes 221192 | tf_op jit(solution)/shard_map/ppermute | solution.py:895
  12.7 0.0 collective-permute-done.4.mate_rest
  12.8 0.1 collective-permute-start.5
  12.8 0.0 copy-start
  12.8 1.2 %copy-done = f32[2224,128]{1,0:T(8,128)S(1)} copy-done((f32[2224,128]{1,0:T(8,128)S(1)}, f32[2224,128]{1,0:T(8,128)}, u32[]{:S(2)}) %copy-start) | copy-done | bytes 1138712
  14.1 0.1 shard_map.57.own_outer
  14.1 1.9 %collective-permute-done.2.mate2_msg = f32[144,128]{1,0:T(8,128)S(1)} collective-permute-done((f32[144,128]{1,0:T(8,128)}, f32[144,128]{1,0:T(8,128)S(1)}, u32[]{:S(2)}, u32[]{:S(2)}) %collective-permute-start.2) | collective-permute-done | bytes 73760 | tf_op jit(solution)/shard_map/ppermute | solution.py:895
  16.1 0.0 collective-permute-done.3.other2_msg
  16.1 5.8 %collective-permute-done.mate_msg = f32[460,128]{1,0:T(8,128)S(1)} collective-permute-done((f32[460,128]{1,0:T(8,128)}, f32[460,128]{1,0:T(8,128)S(1)}, u32[]{:S(2)}, u32[]{:S(2)}) %collective-permute-start) | collective-permute-done | bytes 235552 | tf_op jit(solution)/shard_map/ppermute | solution.py:895
  21.9 0.0 collective-permute-done.1.other_msg
  21.9 0.7 %shard_map.58 = (f32[456,128]{1,0:T(8,128)S(1)}, f32[456,128]{1,0:T(8,128)S(1)}) custom-call(f32[1440,128]{1,0:T(8,128)S(1)} %shard_map.57.own_outer, f32[2224,128]{1,0:T(8,128)S(1)} %copy-done, f32[460,128]{1,0:T(8,128)S(1)} %collective-permute-done.mate_msg, f32[460,128]{1,0:T(8,128)S(1)} %collective-permute-done.1.other_msg, ...), custom_call_target="tpu_custom_call" | custom-call | tf_op jit(solution)/shard_map/pallas_call | solution.py:909
  22.5 1.7 %collective-permute-start.6 = (f32[456,128]{1,0:T(8,128)S(1)}, f32[456,128]{1,0:T(8,128)S(1)}, u32[]{:S(2)}, u32[]{:S(2)}) collective-permute-start(f32[456,128]{1,0:T(8,128)S(1)} %get-tuple-element.23), channel_id=1, source_target_pairs={{0,1},{1,0},{2,3},{3,2},{4,5},{5,4},{6,7},{7,6},{8,9},{9,8},{10,11... | collective-permute-start | bytes 700424 | tf_op jit(solution)/shard_map/ppermute | solution.py:895
  24.3 2.9 %collective-permute-start.7 = (f32[456,128]{1,0:T(8,128)S(1)}, f32[456,128]{1,0:T(8,128)S(1)}, u32[]{:S(2)}, u32[]{:S(2)}) collective-permute-start(f32[456,128]{1,0:T(8,128)S(1)} %get-tuple-element.24), channel_id=1, source_target_pairs={{0,0},{1,2},{2,1},{3,3},{4,4},{5,6},{6,5},{7,7},{8,8},{9,10},{10,9... | collective-permute-start | bytes 700424 | tf_op jit(solution)/shard_map/ppermute | solution.py:895
  27.2 0.0 collective-permute-done.5.passed_rest
  27.2 0.8 %shard_map.56 = (f32[3792,128]{1,0:T(8,128)S(1)}, s32[24,128]{1,0:T(8,128)S(1)}) custom-call(f32[2224,128]{1,0:T(8,128)S(1)} %copy-done, f32[460,128]{1,0:T(8,128)S(1)} %collective-permute-done.mate_msg, f32[460,128]{1,0:T(8,128)S(1)} %collective-permute-done.1.other_msg, f32[144,128]{1,0:T(8,128)S(1)} %collective-permute-done.2.mate2_msg, ...), custom_call_target="tpu_custom_call" | custom-call | tf_op jit(solution)/shard_map/pallas_call | solution.py:909
  28.0 0.0 collective-permute-done.6.near_msg
  28.0 3.6 %collective-permute-done.7.far_msg = f32[456,128]{1,0:T(8,128)S(1)} collective-permute-done((f32[456,128]{1,0:T(8,128)S(1)}, f32[456,128]{1,0:T(8,128)S(1)}, u32[]{:S(2)}, u32[]{:S(2)}) %collective-permute-start.7) | collective-permute-done | bytes 233504 | tf_op jit(solution)/shard_map/ppermute | solution.py:895
  31.6 6.9 %shard_map.59 = f32[3,19,4096]{2,1,0:T(8,128)} custom-call(s32[24,128]{1,0:T(8,128)S(1)} %get-tuple-element.21.own_slots, f32[3792,128]{1,0:T(8,128)S(1)} %get-tuple-element.22.first_post, f32[456,128]{1,0:T(8,128)S(1)} %collective-permute-done.6.near_msg, f32[456,128]{1,0:T(8,128)S(1)} %collective-permute-done.7.far_msg), custom_call_target="tpu_custom_call" | custom-call | tf_op jit(solution)/shard_map/pallas_call | solution.py:909
Async XLA Ops:
  4.8 8.0 %collective-permute-start.4 = (f32[464,128]{1,0:T(8,128)}, f32[464,128]{1,0:T(8,128)S(1)}, u32[]{:S(2)}, u32[]{:S(2)}) collective-permute-start(f32[464,128]{1,0:T(8,128)} %get-tuple-element.20), channel_id=1, source_target_pairs={{0,4},{4,0},{8,12},{12,8},{16,20},{20,16},{24,28},{28,24},{1,5},{5... | collective-permute-start | bytes 712712 | tf_op jit(solution)/shard_map/ppermute | solution.py:956
  5.1 16.8 %collective-permute-start = (f32[460,128]{1,0:T(8,128)}, f32[460,128]{1,0:T(8,128)S(1)}, u32[]{:S(2)}, u32[]{:S(2)}) collective-permute-start(f32[460,128]{1,0:T(8,128)} %get-tuple-element.16), channel_id=1, source_target_pairs={{0,4},{4,0},{8,12},{12,8},{16,20},{20,16},{24,28},{28,24},{1,5},{5... | collective-permute-start | bytes 706568 | tf_op jit(solution)/shard_map/ppermute | solution.py:895
  6.3 15.6 %collective-permute-start.1 = (f32[460,128]{1,0:T(8,128)}, f32[460,128]{1,0:T(8,128)S(1)}, u32[]{:S(2)}, u32[]{:S(2)}) collective-permute-start(f32[460,128]{1,0:T(8,128)} %get-tuple-element.17), channel_id=1, source_target_pairs={{0,0},{4,8},{8,4},{12,16},{16,12},{20,24},{24,20},{28,28},{1,1},{5... | collective-permute-start | bytes 706568 | tf_op jit(solution)/shard_map/ppermute | solution.py:895
  9.5 6.6 %collective-permute-start.2 = (f32[144,128]{1,0:T(8,128)}, f32[144,128]{1,0:T(8,128)S(1)}, u32[]{:S(2)}, u32[]{:S(2)}) collective-permute-start(f32[144,128]{1,0:T(8,128)} %get-tuple-element.18), channel_id=1, source_target_pairs={{0,8},{4,12},{8,0},{12,4},{16,24},{20,28},{24,16},{28,20},{1,9},{5... | collective-permute-start | bytes 221192 | tf_op jit(solution)/shard_map/ppermute | solution.py:895
  9.7 6.4 %collective-permute-start.3 = (f32[144,128]{1,0:T(8,128)}, f32[144,128]{1,0:T(8,128)S(1)}, u32[]{:S(2)}, u32[]{:S(2)}) collective-permute-start(f32[144,128]{1,0:T(8,128)} %get-tuple-element.19), channel_id=1, source_target_pairs={{0,0},{4,4},{8,16},{12,20},{16,8},{20,12},{24,24},{28,28},{1,1},{5... | collective-permute-start | bytes 221192 | tf_op jit(solution)/shard_map/ppermute | solution.py:895
  12.8 14.4 %collective-permute-start.5 = (f32[464,128]{1,0:T(8,128)S(1)}, f32[464,128]{1,0:T(8,128)S(1)}, u32[]{:S(2)}, u32[]{:S(2)}) collective-permute-start(f32[464,128]{1,0:T(8,128)S(1)} %collective-permute-done.4.mate_rest), channel_id=1, source_target_pairs={{0,8},{4,28},{8,16},{12,4},{16,24},{20,12},{24,0},{28,20},{1,9},{5... | collective-permute-start | bytes 712712 | tf_op jit(solution)/shard_map/ppermute | solution.py:958
  12.8 1.3 %copy-start = (f32[2224,128]{1,0:T(8,128)S(1)}, f32[2224,128]{1,0:T(8,128)}, u32[]{:S(2)}) copy-start(f32[2224,128]{1,0:T(8,128)} %get-tuple-element.15.cells) | copy-start | bytes 3416068
  22.5 5.4 %collective-permute-start.6 = (f32[456,128]{1,0:T(8,128)S(1)}, f32[456,128]{1,0:T(8,128)S(1)}, u32[]{:S(2)}, u32[]{:S(2)}) collective-permute-start(f32[456,128]{1,0:T(8,128)S(1)} %get-tuple-element.23), channel_id=1, source_target_pairs={{0,1},{1,0},{2,3},{3,2},{4,5},{5,4},{6,7},{7,6},{8,9},{9,8},{10,11... | collective-permute-start | bytes 700424 | tf_op jit(solution)/shard_map/ppermute | solution.py:895
  24.3 7.4 %collective-permute-start.7 = (f32[456,128]{1,0:T(8,128)S(1)}, f32[456,128]{1,0:T(8,128)S(1)}, u32[]{:S(2)}, u32[]{:S(2)}) collective-permute-start(f32[456,128]{1,0:T(8,128)S(1)} %get-tuple-element.24), channel_id=1, source_target_pairs={{0,0},{1,2},{2,1},{3,3},{4,4},{5,6},{6,5},{7,7},{8,8},{9,10},{10,9... | collective-permute-start | bytes 700424 | tf_op jit(solution)/shard_map/ppermute | solution.py:895

commit v10 on v9

--- a/solution.py
+++ b/solution.py
@@ -32,6 +32,7 @@
 FAR = QUADS * GROUP
 EDGE_TABLE = FAR + 3 * GROUP
 EDGE_ROWS = EDGE_TABLE + 24
+NEAR_ROWS, FAR_ROWS = EDGE_ROWS + 16, EDGE_ROWS + 24
 NOWHERE = PLANES * GROUP
 ALL_PLANES = PLANES + POPS
 LIMIT = 20 * 1024 * 1024
@@ -900,7 +901,7 @@
     return jax.ShapeDtypeStruct((count, 128), jnp.float32)
 
 
-def call(kernel, in_spaces, out_spaces, outs, ins, scratch, limit=LIMIT):
+def call(kernel, in_spaces, out_spaces, outs, ins, scratch, limit=LIMIT, cost=None):
     spaces = {
         "S": pl.BlockSpec(memory_space=pltpu.SMEM),
         "V": pl.BlockSpec(memory_space=pltpu.VMEM),
@@ -913,6 +914,7 @@
         out_specs=[spaces[x] for x in out_spaces],
         scratch_shapes=scratch,
         compiler_params=pltpu.CompilerParams(vmem_limit_bytes=limit),
+        cost_estimate=cost,
     )(*ins)
 
 
@@ -963,9 +965,10 @@
         edge_kernel,
         "VVVVVV",
         "VV",
-        [rows128(EDGE_ROWS), rows128(EDGE_ROWS)],
+        [rows128(NEAR_ROWS), rows128(FAR_ROWS)],
         (outer, *strips),
         [floats(rows) for rows in [PLANES * GROUP] + sorted_rows],
+        cost=pl.CostEstimate(flops=10**10, bytes_accessed=0, transcendentals=0),
     )
     near_msg, far_msg = swapped((near_msg, far_msg), "cross")
     post, own_slots = call(

time: 38.8 us -> 41.8 us (1.077)
  the two profiles are of different devices: /device:TPU:13 before, /device:TPU:0 now
where the time goes in v10:
time: 41.8 us; the launch traced here: 41.5 us
  starting transfers between devices  17.1 us (41%)
  Pallas kernels  12.3 us (29%)
  waiting for transfers between devices  10.2 us (24%)
  local copies, waits for them, and re-layouts  1.26 us (3%)
  between operations  0.71 us (2%)
    pallas_call x5, Pallas kernels, call(): pl.pallas_call(kernel, out_shape=outs, in_specs=[spaces[x] for x in in_sp...  12.3 us
    ppermute x6, starting transfers between devices, swapped(): results.append(lax.ppermute(value[which], axis, pairs))  11.7 us
    ppermute x1, waiting for transfers between devices, per_device(): passed_rest = lax.ppermute(mate_rest, 'curve', pairs)  7.98 us
    ppermute x1, starting transfers between devices, per_device(): mate_rest = lax.ppermute(rest_msg, 'curve', pairs)  3.03 us
    ppermute x1, starting transfers between devices, per_device(): passed_rest = lax.ppermute(mate_rest, 'curve', pairs)  2.34 us
    ppermute x6, waiting for transfers between devices, swapped(): results.append(lax.ppermute(value[which], axis, pairs))  2.18 us
    unnamed x2, local copies, waits for them, and re-layouts  1.26 us
  transfers between devices with their start and end apart: 8, of which 3 were waited for; matrix products, arithmetic and copies ran while one was open for 0% of the time, Pallas kernels for 3%

profile of v10, /device:TPU:0, one launch (start us, length us, event | category | flops | bytes accessed | tf_op | source)
XLA Modules:
  0.0 41.5 jit_solution(16170277597712338252)
XLA Ops:
  0.7 4.1 %shard_map.55 = (f32[2224,128]{1,0:T(8,128)}, f32[460,128]{1,0:T(8,128)}, f32[460,128]{1,0:T(8,128)}, f32[144,128]{1,0:T(8,128)}, f32[144,128]{1,0:T(8,128)}, /*index=5*/f32[464,128]{1,0:T(8,128)}) custom-call(s32[3,32]{1,0:T(4,128)} %bitcast.1, s32[1]{0:T(128)S(6)} %copy.6.counts_hbm, f32[3,19,4096]{2,1,0:T(8,128)} %pops_hbm.1, s32[3,5832]{1,0:T(4,128)} %flags_hbm.1, ...), custom_call_target="tpu_custom_call" | custom-call | tf_op jit(solution)/shard_map/pallas_call | solution.py:910
  4.8 3.0 %collective-permute-start = (f32[460,128]{1,0:T(8,128)}, f32[460,128]{1,0:T(8,128)S(1)}, u32[]{:S(2)}, u32[]{:S(2)}) collective-permute-start(f32[460,128]{1,0:T(8,128)} %get-tuple-element.16), channel_id=1, source_target_pairs={{0,4},{4,0},{8,12},{12,8},{16,20},{20,16},{24,28},{28,24},{1,5},{5... | collective-permute-start | bytes 706568 | tf_op jit(solution)/shard_map/ppermute | solution.py:896
  7.8 1.6 %collective-permute-start.1 = (f32[460,128]{1,0:T(8,128)}, f32[460,128]{1,0:T(8,128)S(1)}, u32[]{:S(2)}, u32[]{:S(2)}) collective-permute-start(f32[460,128]{1,0:T(8,128)} %get-tuple-element.17), channel_id=1, source_target_pairs={{0,0},{4,8},{8,4},{12,16},{16,12},{20,24},{24,20},{28,28},{1,1},{5... | collective-permute-start | bytes 706568 | tf_op jit(solution)/shard_map/ppermute | solution.py:896
  9.4 2.0 %collective-permute-start.2 = (f32[144,128]{1,0:T(8,128)}, f32[144,128]{1,0:T(8,128)S(1)}, u32[]{:S(2)}, u32[]{:S(2)}) collective-permute-start(f32[144,128]{1,0:T(8,128)} %get-tuple-element.18), channel_id=1, source_target_pairs={{0,8},{4,12},{8,0},{12,4},{16,24},{20,28},{24,16},{28,20},{1,9},{5... | collective-permute-start | bytes 221192 | tf_op jit(solution)/shard_map/ppermute | solution.py:896
  11.4 1.5 %collective-permute-start.3 = (f32[144,128]{1,0:T(8,128)}, f32[144,128]{1,0:T(8,128)S(1)}, u32[]{:S(2)}, u32[]{:S(2)}) collective-permute-start(f32[144,128]{1,0:T(8,128)} %get-tuple-element.19), channel_id=1, source_target_pairs={{0,0},{4,4},{8,16},{12,20},{16,8},{20,12},{24,24},{28,28},{1,1},{5... | collective-permute-start | bytes 221192 | tf_op jit(solution)/shard_map/ppermute | solution.py:896
  12.9 3.0 %collective-permute-start.4 = (f32[464,128]{1,0:T(8,128)}, f32[464,128]{1,0:T(8,128)S(1)}, u32[]{:S(2)}, u32[]{:S(2)}) collective-permute-start(f32[464,128]{1,0:T(8,128)} %get-tuple-element.20), channel_id=1, source_target_pairs={{0,4},{4,0},{8,12},{12,8},{16,20},{20,16},{24,28},{28,24},{1,5},{5... | collective-permute-start | bytes 712712 | tf_op jit(solution)/shard_map/ppermute | solution.py:958
  15.9 0.0 copy-start
  15.9 1.3 %copy-done = f32[2224,128]{1,0:T(8,128)S(1)} copy-done((f32[2224,128]{1,0:T(8,128)S(1)}, f32[2224,128]{1,0:T(8,128)}, u32[]{:S(2)}) %copy-start) | copy-done | bytes 1138712
  17.2 0.1 shard_map.57.own_outer
  17.2 1.4 %collective-permute-done.2.mate2_msg = f32[144,128]{1,0:T(8,128)S(1)} collective-permute-done((f32[144,128]{1,0:T(8,128)}, f32[144,128]{1,0:T(8,128)S(1)}, u32[]{:S(2)}, u32[]{:S(2)}) %collective-permute-start.2) | collective-permute-done | bytes 73760 | tf_op jit(solution)/shard_map/ppermute | solution.py:896
  18.6 0.0 collective-permute-done.3.other2_msg
  18.6 0.8 %collective-permute-done.mate_msg = f32[460,128]{1,0:T(8,128)S(1)} collective-permute-done((f32[460,128]{1,0:T(8,128)}, f32[460,128]{1,0:T(8,128)S(1)}, u32[]{:S(2)}, u32[]{:S(2)}) %collective-permute-start) | collective-permute-done | bytes 235552 | tf_op jit(solution)/shard_map/ppermute | solution.py:896
  19.4 0.0 collective-permute-done.1.other_msg
  19.4 0.6 %shard_map.58 = (f32[472,128]{1,0:T(8,128)S(1)}, f32[480,128]{1,0:T(8,128)S(1)}) custom-call(f32[1440,128]{1,0:T(8,128)S(1)} %shard_map.57.own_outer, f32[2224,128]{1,0:T(8,128)S(1)} %copy-done, f32[460,128]{1,0:T(8,128)S(1)} %collective-permute-done.mate_msg, f32[460,128]{1,0:T(8,128)S(1)} %collective-permute-done.1.other_msg, ...), custom_call_target="tpu_custom_call" | custom-call | flops 10000000000 | tf_op jit(solution)/shard_map/pallas_call | solution.py:910
  20.0 0.7 %collective-permute-start.7 = (f32[480,128]{1,0:T(8,128)S(1)}, f32[480,128]{1,0:T(8,128)S(1)}, u32[]{:S(2)}, u32[]{:S(2)}) collective-permute-start(f32[480,128]{1,0:T(8,128)S(1)} %get-tuple-element.24), channel_id=1, source_target_pairs={{0,0},{1,2},{2,1},{3,3},{4,4},{5,6},{6,5},{7,7},{8,8},{9,10},{10,9... | collective-permute-start | bytes 737288 | tf_op jit(solution)/shard_map/ppermute | solution.py:896
  20.7 2.9 %collective-permute-start.6 = (f32[472,128]{1,0:T(8,128)S(1)}, f32[472,128]{1,0:T(8,128)S(1)}, u32[]{:S(2)}, u32[]{:S(2)}) collective-permute-start(f32[472,128]{1,0:T(8,128)S(1)} %get-tuple-element.23), channel_id=1, source_target_pairs={{0,1},{1,0},{2,3},{3,2},{4,5},{5,4},{6,7},{7,6},{8,9},{9,8},{10,11... | collective-permute-start | bytes 725000 | tf_op jit(solution)/shard_map/ppermute | solution.py:896
  23.6 0.0 collective-permute-done.4.mate_rest
  23.6 2.3 %collective-permute-start.5 = (f32[464,128]{1,0:T(8,128)S(1)}, f32[464,128]{1,0:T(8,128)S(1)}, u32[]{:S(2)}, u32[]{:S(2)}) collective-permute-start(f32[464,128]{1,0:T(8,128)S(1)} %collective-permute-done.4.mate_rest), channel_id=1, source_target_pairs={{0,8},{4,28},{8,16},{12,4},{16,24},{20,12},{24,0},{28,20},{1,9},{5... | collective-permute-start | bytes 712712 | tf_op jit(solution)/shard_map/ppermute | solution.py:960
  25.9 8.0 %collective-permute-done.5.passed_rest = f32[464,128]{1,0:T(8,128)S(1)} collective-permute-done((f32[464,128]{1,0:T(8,128)S(1)}, f32[464,128]{1,0:T(8,128)S(1)}, u32[]{:S(2)}, u32[]{:S(2)}) %collective-permute-start.5) | collective-permute-done | bytes 237600 | tf_op jit(solution)/shard_map/ppermute | solution.py:960
  33.9 0.7 %shard_map.56 = (f32[3792,128]{1,0:T(8,128)S(1)}, s32[24,128]{1,0:T(8,128)S(1)}) custom-call(f32[2224,128]{1,0:T(8,128)S(1)} %copy-done, f32[460,128]{1,0:T(8,128)S(1)} %collective-permute-done.mate_msg, f32[460,128]{1,0:T(8,128)S(1)} %collective-permute-done.1.other_msg, f32[144,128]{1,0:T(8,128)S(1)} %collective-permute-done.2.mate2_msg, ...), custom_call_target="tpu_custom_call" | custom-call | tf_op jit(solution)/shard_map/pallas_call | solution.py:910
  34.6 0.0 collective-permute-done.6.near_msg
  34.6 0.0 collective-permute-done.7.far_msg
  34.6 6.9 %shard_map.59 = f32[3,19,4096]{2,1,0:T(8,128)} custom-call(s32[24,128]{1,0:T(8,128)S(1)} %get-tuple-element.21.own_slots, f32[3792,128]{1,0:T(8,128)S(1)} %get-tuple-element.22.first_post, f32[472,128]{1,0:T(8,128)S(1)} %collective-permute-done.6.near_msg, f32[480,128]{1,0:T(8,128)S(1)} %collective-permute-done.7.far_msg), custom_call_target="tpu_custom_call" | custom-call | tf_op jit(solution)/shard_map/pallas_call | solution.py:910
Async XLA Ops:
  4.8 14.6 %collective-permute-start = (f32[460,128]{1,0:T(8,128)}, f32[460,128]{1,0:T(8,128)S(1)}, u32[]{:S(2)}, u32[]{:S(2)}) collective-permute-start(f32[460,128]{1,0:T(8,128)} %get-tuple-element.16), channel_id=1, source_target_pairs={{0,4},{4,0},{8,12},{12,8},{16,20},{20,16},{24,28},{28,24},{1,5},{5... | collective-permute-start | bytes 706568 | tf_op jit(solution)/shard_map/ppermute | solution.py:896
  7.8 11.6 %collective-permute-start.1 = (f32[460,128]{1,0:T(8,128)}, f32[460,128]{1,0:T(8,128)S(1)}, u32[]{:S(2)}, u32[]{:S(2)}) collective-permute-start(f32[460,128]{1,0:T(8,128)} %get-tuple-element.17), channel_id=1, source_target_pairs={{0,0},{4,8},{8,4},{12,16},{16,12},{20,24},{24,20},{28,28},{1,1},{5... | collective-permute-start | bytes 706568 | tf_op jit(solution)/shard_map/ppermute | solution.py:896
  9.4 9.2 %collective-permute-start.2 = (f32[144,128]{1,0:T(8,128)}, f32[144,128]{1,0:T(8,128)S(1)}, u32[]{:S(2)}, u32[]{:S(2)}) collective-permute-start(f32[144,128]{1,0:T(8,128)} %get-tuple-element.18), channel_id=1, source_target_pairs={{0,8},{4,12},{8,0},{12,4},{16,24},{20,28},{24,16},{28,20},{1,9},{5... | collective-permute-start | bytes 221192 | tf_op jit(solution)/shard_map/ppermute | solution.py:896
  11.4 7.2 %collective-permute-start.3 = (f32[144,128]{1,0:T(8,128)}, f32[144,128]{1,0:T(8,128)S(1)}, u32[]{:S(2)}, u32[]{:S(2)}) collective-permute-start(f32[144,128]{1,0:T(8,128)} %get-tuple-element.19), channel_id=1, source_target_pairs={{0,0},{4,4},{8,16},{12,20},{16,8},{20,12},{24,24},{28,28},{1,1},{5... | collective-permute-start | bytes 221192 | tf_op jit(solution)/shard_map/ppermute | solution.py:896
  12.9 10.7 %collective-permute-start.4 = (f32[464,128]{1,0:T(8,128)}, f32[464,128]{1,0:T(8,128)S(1)}, u32[]{:S(2)}, u32[]{:S(2)}) collective-permute-start(f32[464,128]{1,0:T(8,128)} %get-tuple-element.20), channel_id=1, source_target_pairs={{0,4},{4,0},{8,12},{12,8},{16,20},{20,16},{24,28},{28,24},{1,5},{5... | collective-permute-start | bytes 712712 | tf_op jit(solution)/shard_map/ppermute | solution.py:958
  15.9 1.3 %copy-start = (f32[2224,128]{1,0:T(8,128)S(1)}, f32[2224,128]{1,0:T(8,128)}, u32[]{:S(2)}) copy-start(f32[2224,128]{1,0:T(8,128)} %get-tuple-element.15.cells) | copy-start | bytes 3416068
  20.0 14.6 %collective-permute-start.7 = (f32[480,128]{1,0:T(8,128)S(1)}, f32[480,128]{1,0:T(8,128)S(1)}, u32[]{:S(2)}, u32[]{:S(2)}) collective-permute-start(f32[480,128]{1,0:T(8,128)S(1)} %get-tuple-element.24), channel_id=1, source_target_pairs={{0,0},{1,2},{2,1},{3,3},{4,4},{5,6},{6,5},{7,7},{8,8},{9,10},{10,9... | collective-permute-start | bytes 737288 | tf_op jit(solution)/shard_map/ppermute | solution.py:896
  20.7 13.9 %collective-permute-start.6 = (f32[472,128]{1,0:T(8,128)S(1)}, f32[472,128]{1,0:T(8,128)S(1)}, u32[]{:S(2)}, u32[]{:S(2)}) collective-permute-start(f32[472,128]{1,0:T(8,128)S(1)} %get-tuple-element.23), channel_id=1, source_target_pairs={{0,1},{1,0},{2,3},{3,2},{4,5},{5,4},{6,7},{7,6},{8,9},{9,8},{10,11... | collective-permute-start | bytes 725000 | tf_op jit(solution)/shard_map/ppermute | solution.py:896
  23.6 10.3 %collective-permute-start.5 = (f32[464,128]{1,0:T(8,128)S(1)}, f32[464,128]{1,0:T(8,128)S(1)}, u32[]{:S(2)}, u32[]{:S(2)}) collective-permute-start(f32[464,128]{1,0:T(8,128)S(1)} %collective-permute-done.4.mate_rest), channel_id=1, source_target_pairs={{0,8},{4,28},{8,16},{12,4},{16,24},{20,12},{24,0},{28,20},{1,9},{5... | collective-permute-start | bytes 712712 | tf_op jit(solution)/shard_map/ppermute | solution.py:960

commit v11 on v10

--- a/solution.py
+++ b/solution.py
@@ -570,8 +570,8 @@
     return out
 
 
-def collide_all(h_ref, flags, posts):
-    for groups in ((0, 1), (2,)):
+def collide_all(h_ref, flags, posts, parts=((0, 1), (2,))):
+    for groups in parts:
         ref = posts[groups[0] // 2]
         size = len(groups) * GROUP
 
@@ -728,8 +728,6 @@
     other_msg,
     mate2_msg,
     other2_msg,
-    mate_rest,
-    passed_rest,
     post_ref,
     slots,
     low_msg,
@@ -744,7 +742,6 @@
         slots[8 * i : 8 * i + 8, :] = first_rows(ref[row : row + 8, :])
 
     from_low, from_high, low_low, low_me, high_high, high_me = landed_slots(cells)
-    lane = lanes_iota()
     post_ref[PLANES * PAIR :, :] = jnp.full((POPS * PAIR, 128), jnp.nan, jnp.float32)
     for q in range(PLANES):
         for y in range(2):
@@ -752,33 +749,18 @@
             post_ref[start : start + EDGE, :] = cells[
                 q * 32 + y * EDGE : q * 32 + (y + 1) * EDGE, :
             ]
-    even = is_even("curve")
-    odd = jnp.logical_not(even)
-    for s, (slot, msg, wanted, rest) in itertools.product(
-        range(SLOTS),
-        (
-            (from_low, low_msg, odd, mate_rest),
-            (from_low, low_msg, even, passed_rest),
-            (from_high, high_msg, even, mate_rest),
-            (from_high, high_msg, odd, passed_rest),
-        ),
+    for s, (slot, msg) in itertools.product(
+        range(SLOTS), ((from_low, low_msg), (from_high, high_msg))
     ):
 
-        @pl.when((slot == s) & wanted)
+        @pl.when(slot == s)
         def _():
             for p in range(POPS):
                 for v in range(2):
                     rim = rim_of(msg, p, v)
-                    row = p * EDGE + v * 8
-                    wide = rest[row : row + 8, :]
-                    row = (POPS + p // 2) * EDGE + v * 8
-                    middle = rest[row : row + 8, :]
-                    if p % 2:
-                        middle = pltpu.roll(middle, 64, axis=1)
-                    second = jnp.where(lane < 32, wide, jnp.where(lane < 96, middle, rim))
                     row = (s * POPS + p) * PAIR + v * 8
-                    post_ref[row : row + 8, :] = jnp.where(lane < 32, rim, wide)
-                    post_ref[row + GROUP : row + GROUP + 8, :] = second
+                    post_ref[row : row + 8, :] = rim
+                    post_ref[row + GROUP : row + GROUP + 8, :] = rim
 
     for msg, row0, step, first in ((high_msg, 16, 1, 2), (low_msg, 23, -1, 1)):
         for y in range(2):
@@ -808,19 +790,8 @@
     return jnp.where(slot == SLOTS, NOWHERE, slot * (POPS * GROUP))
 
 
-def steps_kernel(
-    own_slots,
-    first_post,
-    near_msg,
-    far_msg,
-    out_hbm,
-    h_ref,
-    post_ref,
-    outer_ref,
-    out,
-    slots,
-    table,
-    sems,
+def outer_kernel(
+    own_slots, first_post, near_msg, far_msg, slots, outer_ref, next_ref, h_ref, table, sem
 ):
     even = is_even("cross")
 
@@ -833,14 +804,13 @@
         slots[24 * i : 24 * i + 8, :] = first_rows(south)
         slots[24 * i + 8 : 24 * i + 16, :] = own_slots[8 * i : 8 * i + 8, :]
         slots[24 * i + 16 : 24 * i + 24, :] = first_rows(north)
-    table_copy = pltpu.make_async_copy(slots, table, sems.at[SLOTS])
+    table_copy = pltpu.make_async_copy(slots, table, sem)
     table_copy.start()
 
     nothing = jnp.full((8, 128), jnp.nan, jnp.float32)
     for row in range(0, POPS * GROUP, 8):
         outer_ref[NOWHERE + row : NOWHERE + row + 8, :] = nothing
-    for row in range(PLANES * PAIR, ALL_PLANES * PAIR, 8):
-        post_ref[row : row + 8, :] = nothing
+        next_ref[NOWHERE + row : NOWHERE + row + 8, :] = nothing
     lane = lanes_iota()
     for v in range(3):
 
@@ -862,8 +832,73 @@
                     outer_ref[rows(q), :] = jnp.where(
                         lane // 16 == target // 16, moved, outer_ref[rows(q), :]
                     )
+    for row in range(FLAG0 * GROUP, NOWHERE, 8):
+        next_ref[row : row + 8, :] = outer_ref[row : row + 8, :]
     hide_walls(outer_ref, GROUP)
     table_copy.wait()
+    flags = (first_post, outer_ref)
+    stream_all(flags, h_ref, flags, table, (2,), 3)
+    collide_all(h_ref, flags, (None, next_ref), ((2,),))
+
+
+def steps_kernel(
+    slots,
+    first_post,
+    first_outer,
+    next_outer,
+    cells,
+    mate_msg,
+    other_msg,
+    mate_rest,
+    passed_rest,
+    out_hbm,
+    h_ref,
+    post_ref,
+    outer_ref,
+    out,
+    table,
+    sems,
+):
+    table_copy = pltpu.make_async_copy(slots, table, sems.at[SLOTS])
+    table_copy.start()
+    post_ref[...] = first_post[...]
+    nothing = jnp.full((8, 128), jnp.nan, jnp.float32)
+    for row in range(0, POPS * GROUP, 8):
+        outer_ref[NOWHERE + row : NOWHERE + row + 8, :] = nothing
+
+    from_low, from_high = landed_slots(cells)[:2]
+    lane = lanes_iota()
+    even = is_even("curve")
+    odd = jnp.logical_not(even)
+    for s, (slot, wanted, msg, rest) in itertools.product(
+        range(SLOTS),
+        (
+            (from_low, odd, mate_msg, mate_rest),
+            (from_low, even, other_msg, passed_rest),
+            (from_high, even, mate_msg, mate_rest),
+            (from_high, odd, other_msg, passed_rest),
+        ),
+    ):
+
+        @pl.when((slot == s) & wanted)
+        def _():
+            for v in range(2):
+                starts = [(FLAG0 + s) * PAIR + y * GROUP + v * 8 for y in range(2)]
+                fluid = [first_post[row : row + 8, :] > 0.0 for row in starts]
+                for p in range(POPS):
+                    rim = rim_of(msg, p, v)
+                    row = p * EDGE + v * 8
+                    wide = rest[row : row + 8, :]
+                    row = (POPS + p // 2) * EDGE + v * 8
+                    middle = rest[row : row + 8, :]
+                    if p % 2:
+                        middle = pltpu.roll(middle, 64, axis=1)
+                    first = jnp.where(lane < 32, rim, wide)
+                    second = jnp.where(lane < 32, wide, jnp.where(lane < 96, middle, rim))
+                    row = (s * POPS + p) * PAIR + v * 8
+                    post_ref[row : row + 8, :] = jnp.where(fluid[0], first, jnp.nan)
+                    row += GROUP
+                    post_ref[row : row + 8, :] = jnp.where(fluid[1], second, jnp.nan)
 
     def finish(s):
         for x in range(EDGE):
@@ -876,9 +911,12 @@
                     ]
         pltpu.make_async_copy(out.at[s], out_hbm.at[s], sems.at[s]).start()
 
-    flags = (first_post, outer_ref)
-    posts = flags
-    for _ in range(STEPS - 1):
+    table_copy.wait()
+    flags = (first_post, first_outer)
+    stream_all((post_ref, first_outer), h_ref, flags, table, (0, 1), 3)
+    collide_all(h_ref, flags, (post_ref, None), ((0, 1),))
+    posts = (post_ref, next_outer)
+    for _ in range(STEPS - 2):
         stream_all(posts, h_ref, flags, table, (0, 1, 2), 3)
         posts = (post_ref, outer_ref)
         collide_all(h_ref, flags, posts)
@@ -956,7 +994,8 @@
     assert sizes[0] % 2 == 0
     pairs = [(i, i ^ 1) for i in range(sizes[0])]
     mate_rest = lax.ppermute(rest_msg, "curve", pairs)
-    pairs = [(i, (i - 2 if i % 2 else i + 2) % sizes[0]) for i in range(sizes[0])]
+    last = sizes[0] - 1
+    pairs = [(i, max(i - 2, 0) if i % 2 else min(i + 2, last)) for i in range(sizes[0])]
     passed_rest = lax.ppermute(mate_rest, "curve", pairs)
     (outer,) = call(spread_kernel, "V", "V", [rows128(PLANES * GROUP)], (cells,), [])
     strips = (cells, mate_msg, other_msg, mate2_msg, other2_msg)
@@ -973,24 +1012,36 @@
     near_msg, far_msg = swapped((near_msg, far_msg), "cross")
     post, own_slots = call(
         join_kernel,
-        "VVVVVVV",
+        "VVVVV",
         "VV",
         [rows128(ALL_PLANES * PAIR), jax.ShapeDtypeStruct((24, 128), jnp.int32)],
-        (*strips, mate_rest, passed_rest),
+        strips,
         [floats(rows) for rows in sorted_rows],
     )
+    slots, outer_post, next_outer = call(
+        outer_kernel,
+        "VVVV",
+        "VVV",
+        [
+            jax.ShapeDtypeStruct((72, 128), jnp.int32),
+            rows128(ALL_PLANES * GROUP),
+            rows128(ALL_PLANES * GROUP),
+        ],
+        (own_slots, post, near_msg, far_msg),
+        [floats(SLOTS * SLOT), pltpu.SMEM((72, 128), jnp.int32), pltpu.SemaphoreType.DMA],
+    )
+    arriving = (cells, mate_msg, other_msg, mate_rest, passed_rest)
     return call(
         steps_kernel,
-        "VVVV",
+        "VVVVVVVVV",
         "H",
         [jax.ShapeDtypeStruct(populations.shape, jnp.float32)],
-        (own_slots, post, near_msg, far_msg),
+        (slots, post, outer_post, next_outer, *arriving),
         [
             floats(SLOTS * SLOT),
             floats(ALL_PLANES * PAIR),
             floats(ALL_PLANES * GROUP),
             pltpu.VMEM(populations.shape, jnp.float32),
-            pltpu.VMEM((72, 128), jnp.int32),
             pltpu.SMEM((72, 128), jnp.int32),
             pltpu.SemaphoreType.DMA((SLOTS + 1,)),
         ],

time: 41.8 us -> 38.4 us (0.919)
  waiting for transfers between devices: 10.2 us -> 5.45 us
  Pallas kernels: 12.3 us -> 13.7 us
    ppermute x1, waiting for transfers between devices: 7.98 us -> 3.28 us  [per_device(): passed_rest = lax.ppermute(mate_rest, 'curve', pairs)]
    pallas_call x5 -> x6, Pallas kernels: 12.3 us -> 13.7 us  [call(): pl.pallas_call(kernel, out_shape=outs, in_specs=[spaces[x] for x in in_sp...]
    unnamed x2 -> x4, local copies, waits for them, and re-layouts: 1.26 us -> 1.26 us
  transfers between devices with their start and end apart: 8 -> 8, of which waited for: 3 -> 3; matrix products, arithmetic and copies ran while one was open for 0% -> 0% of each run, Pallas kernels for 3% -> 9%
where the time goes in v11:
time: 38.4 us; the launch traced here: 38.1 us
  starting transfers between devices  17 us (44%)
  Pallas kernels  13.7 us (36%)
  waiting for transfers between devices  5.45 us (14%)
  local copies, waits for them, and re-layouts  1.26 us (3%)
  between operations  0.72 us (2%)
    pallas_call x6, Pallas kernels, call(): pl.pallas_call(kernel, out_shape=outs, in_specs=[spaces[x] for x in in_sp...  13.7 us
    ppermute x6, starting transfers between devices, swapped(): results.append(lax.ppermute(value[which], axis, pairs))  11.7 us
    ppermute x1, waiting for transfers between devices, per_device(): passed_rest = lax.ppermute(mate_rest, 'curve', pairs)  3.28 us
    ppermute x1, starting transfers between devices, per_device(): mate_rest = lax.ppermute(rest_msg, 'curve', pairs)  3.03 us
    ppermute x1, starting transfers between devices, per_device(): passed_rest = lax.ppermute(mate_rest, 'curve', pairs)  2.25 us
    ppermute x6, waiting for transfers between devices, swapped(): results.append(lax.ppermute(value[which], axis, pairs))  2.18 us
    unnamed x4, local copies, waits for them, and re-layouts  1.26 us
  transfers between devices with their start and end apart: 8, of which 3 were waited for; matrix products, arithmetic and copies ran while one was open for 0% of the time, Pallas kernels for 9%

profile of v11, /device:TPU:0, one launch (start us, length us, event | category | flops | bytes accessed | tf_op | source)
XLA Modules:
  0.0 38.1 jit_solution(2343427445471675903)
XLA Ops:
  0.7 4.1 %shard_map.55 = (f32[2224,128]{1,0:T(8,128)}, f32[460,128]{1,0:T(8,128)}, f32[460,128]{1,0:T(8,128)}, f32[144,128]{1,0:T(8,128)}, f32[144,128]{1,0:T(8,128)}, /*index=5*/f32[464,128]{1,0:T(8,128)}) custom-call(s32[3,32]{1,0:T(4,128)} %bitcast.1, s32[1]{0:T(128)S(6)} %copy.6.counts_hbm, f32[3,19,4096]{2,1,0:T(8,128)} %pops_hbm.1, s32[3,5832]{1,0:T(4,128)} %flags_hbm.1, ...), custom_call_target="tpu_custom_call" | custom-call | tf_op jit(solution)/shard_map/pallas_call | solution.py:948
  4.8 3.0 %collective-permute-start = (f32[460,128]{1,0:T(8,128)}, f32[460,128]{1,0:T(8,128)S(1)}, u32[]{:S(2)}, u32[]{:S(2)}) collective-permute-start(f32[460,128]{1,0:T(8,128)} %get-tuple-element.19), channel_id=1, source_target_pairs={{0,4},{4,0},{8,12},{12,8},{16,20},{20,16},{24,28},{28,24},{1,5},{5... | collective-permute-start | bytes 706568 | tf_op jit(solution)/shard_map/ppermute | solution.py:934
  7.8 1.6 %collective-permute-start.1 = (f32[460,128]{1,0:T(8,128)}, f32[460,128]{1,0:T(8,128)S(1)}, u32[]{:S(2)}, u32[]{:S(2)}) collective-permute-start(f32[460,128]{1,0:T(8,128)} %get-tuple-element.20), channel_id=1, source_target_pairs={{0,0},{4,8},{8,4},{12,16},{16,12},{20,24},{24,20},{28,28},{1,1},{5... | collective-permute-start | bytes 706568 | tf_op jit(solution)/shard_map/ppermute | solution.py:934
  9.4 2.0 %collective-permute-start.2 = (f32[144,128]{1,0:T(8,128)}, f32[144,128]{1,0:T(8,128)S(1)}, u32[]{:S(2)}, u32[]{:S(2)}) collective-permute-start(f32[144,128]{1,0:T(8,128)} %get-tuple-element.21), channel_id=1, source_target_pairs={{0,8},{4,12},{8,0},{12,4},{16,24},{20,28},{24,16},{28,20},{1,9},{5... | collective-permute-start | bytes 221192 | tf_op jit(solution)/shard_map/ppermute | solution.py:934
  11.4 1.5 %collective-permute-start.3 = (f32[144,128]{1,0:T(8,128)}, f32[144,128]{1,0:T(8,128)S(1)}, u32[]{:S(2)}, u32[]{:S(2)}) collective-permute-start(f32[144,128]{1,0:T(8,128)} %get-tuple-element.22), channel_id=1, source_target_pairs={{0,0},{4,4},{8,16},{12,20},{16,8},{20,12},{24,24},{28,28},{1,1},{5... | collective-permute-start | bytes 221192 | tf_op jit(solution)/shard_map/ppermute | solution.py:934
  12.9 3.0 %collective-permute-start.6 = (f32[464,128]{1,0:T(8,128)}, f32[464,128]{1,0:T(8,128)S(1)}, u32[]{:S(2)}, u32[]{:S(2)}) collective-permute-start(f32[464,128]{1,0:T(8,128)} %get-tuple-element.30), channel_id=1, source_target_pairs={{0,4},{4,0},{8,12},{12,8},{16,20},{20,16},{24,28},{28,24},{1,5},{5... | collective-permute-start | bytes 712712 | tf_op jit(solution)/shard_map/ppermute | solution.py:996
  16.0 0.0 copy-start
  16.0 1.3 %copy-done = f32[2224,128]{1,0:T(8,128)S(1)} copy-done((f32[2224,128]{1,0:T(8,128)S(1)}, f32[2224,128]{1,0:T(8,128)}, u32[]{:S(2)}) %copy-start) | copy-done | bytes 1138712
  17.2 0.1 shard_map.57.own_outer
  17.3 1.4 %collective-permute-done.2.mate2_msg = f32[144,128]{1,0:T(8,128)S(1)} collective-permute-done((f32[144,128]{1,0:T(8,128)}, f32[144,128]{1,0:T(8,128)S(1)}, u32[]{:S(2)}, u32[]{:S(2)}) %collective-permute-start.2) | collective-permute-done | bytes 73760 | tf_op jit(solution)/shard_map/ppermute | solution.py:934
  18.6 0.0 collective-permute-done.3.other2_msg
  18.6 0.8 %collective-permute-done.mate_msg = f32[460,128]{1,0:T(8,128)S(1)} collective-permute-done((f32[460,128]{1,0:T(8,128)}, f32[460,128]{1,0:T(8,128)S(1)}, u32[]{:S(2)}, u32[]{:S(2)}) %collective-permute-start) | collective-permute-done | bytes 235552 | tf_op jit(solution)/shard_map/ppermute | solution.py:934
  19.4 0.0 collective-permute-done.1.other_msg
  19.4 0.6 %shard_map.58 = (f32[472,128]{1,0:T(8,128)S(1)}, f32[480,128]{1,0:T(8,128)S(1)}) custom-call(f32[1440,128]{1,0:T(8,128)S(1)} %shard_map.57.own_outer, f32[2224,128]{1,0:T(8,128)S(1)} %copy-done, f32[460,128]{1,0:T(8,128)S(1)} %collective-permute-done.mate_msg, f32[460,128]{1,0:T(8,128)S(1)} %collective-permute-done.1.other_msg, ...), custom_call_target="tpu_custom_call" | custom-call | flops 10000000000 | tf_op jit(solution)/shard_map/pallas_call | solution.py:948
  20.0 0.7 %collective-permute-start.5 = (f32[480,128]{1,0:T(8,128)S(1)}, f32[480,128]{1,0:T(8,128)S(1)}, u32[]{:S(2)}, u32[]{:S(2)}) collective-permute-start(f32[480,128]{1,0:T(8,128)S(1)} %get-tuple-element.26), channel_id=1, source_target_pairs={{0,0},{1,2},{2,1},{3,3},{4,4},{5,6},{6,5},{7,7},{8,8},{9,10},{10,9... | collective-permute-start | bytes 737288 | tf_op jit(solution)/shard_map/ppermute | solution.py:934
  20.7 2.9 %collective-permute-start.4 = (f32[472,128]{1,0:T(8,128)S(1)}, f32[472,128]{1,0:T(8,128)S(1)}, u32[]{:S(2)}, u32[]{:S(2)}) collective-permute-start(f32[472,128]{1,0:T(8,128)S(1)} %get-tuple-element.25), channel_id=1, source_target_pairs={{0,1},{1,0},{2,3},{3,2},{4,5},{5,4},{6,7},{7,6},{8,9},{9,8},{10,11... | collective-permute-start | bytes 725000 | tf_op jit(solution)/shard_map/ppermute | solution.py:934
  23.6 0.0 collective-permute-done.6.mate_rest
  23.6 2.2 %collective-permute-start.7 = (f32[464,128]{1,0:T(8,128)S(1)}, f32[464,128]{1,0:T(8,128)S(1)}, u32[]{:S(2)}, u32[]{:S(2)}) collective-permute-start(f32[464,128]{1,0:T(8,128)S(1)} %collective-permute-done.6.mate_rest), channel_id=1, source_target_pairs={{0,8},{4,0},{8,16},{12,4},{16,24},{20,12},{24,28},{28,20},{1,9},{5... | collective-permute-start | bytes 712712 | tf_op jit(solution)/shard_map/ppermute | solution.py:999
  25.9 0.6 %shard_map.56 = (f32[3792,128]{1,0:T(8,128)S(1)}, s32[24,128]{1,0:T(8,128)S(1)}) custom-call(f32[2224,128]{1,0:T(8,128)S(1)} %copy-done, f32[460,128]{1,0:T(8,128)S(1)} %collective-permute-done.mate_msg, f32[460,128]{1,0:T(8,128)S(1)} %collective-permute-done.1.other_msg, f32[144,128]{1,0:T(8,128)S(1)} %collective-permute-done.2.mate2_msg, ...), custom_call_target="tpu_custom_call" | custom-call | tf_op jit(solution)/shard_map/pallas_call | solution.py:948
  26.5 0.0 collective-permute-done.4.near_msg
  26.5 0.0 collective-permute-done.5.far_msg
  26.5 0.0 copy-start.1
  26.5 2.3 %shard_map.59 = (s32[72,128]{1,0:T(8,128)S(1)}, f32[1896,128]{1,0:T(8,128)S(1)}, f32[1896,128]{1,0:T(8,128)S(1)}) custom-call(s32[24,128]{1,0:T(8,128)S(1)} %get-tuple-element.23.own_slots, f32[3792,128]{1,0:T(8,128)S(1)} %get-tuple-element.24.first_post, f32[472,128]{1,0:T(8,128)S(1)} %collective-permute-done.4.near_msg, ...), custom_call_target="tpu_custom_call" | custom-call | tf_op jit(solution)/shard_map/pallas_call | solution.py:948
  28.8 3.3 %collective-permute-done.7.passed_rest = f32[464,128]{1,0:T(8,128)S(1)} collective-permute-done((f32[464,128]{1,0:T(8,128)S(1)}, f32[464,128]{1,0:T(8,128)S(1)}, u32[]{:S(2)}, u32[]{:S(2)}) %collective-permute-start.7) | collective-permute-done | bytes 237600 | tf_op jit(solution)/shard_map/ppermute | solution.py:999
  32.1 0.0 copy-done.1
  32.1 6.0 %shard_map.60 = f32[3,19,4096]{2,1,0:T(8,128)} custom-call(s32[72,128]{1,0:T(8,128)S(1)} %get-tuple-element.27.slots, f32[3792,128]{1,0:T(8,128)S(1)} %get-tuple-element.24.first_post, f32[1896,128]{1,0:T(8,128)S(1)} %get-tuple-element.28.first_outer, f32[1896,128]{1,0:T(8,128)S(1)} %get-tuple-element.29.next_outer, f32[2224,128]{1,0:T(8,128)S(1)} %copy-done.1, ...), custom_call_target="tpu_custom_call" | custom-call | tf_op jit(solution)/shard_map/pallas_call | solution.py:948
Async XLA Ops:
  4.8 14.6 %collective-permute-start = (f32[460,128]{1,0:T(8,128)}, f32[460,128]{1,0:T(8,128)S(1)}, u32[]{:S(2)}, u32[]{:S(2)}) collective-permute-start(f32[460,128]{1,0:T(8,128)} %get-tuple-element.19), channel_id=1, source_target_pairs={{0,4},{4,0},{8,12},{12,8},{16,20},{20,16},{24,28},{28,24},{1,5},{5... | collective-permute-start | bytes 706568 | tf_op jit(solution)/shard_map/ppermute | solution.py:934
  7.8 11.6 %collective-permute-start.1 = (f32[460,128]{1,0:T(8,128)}, f32[460,128]{1,0:T(8,128)S(1)}, u32[]{:S(2)}, u32[]{:S(2)}) collective-permute-start(f32[460,128]{1,0:T(8,128)} %get-tuple-element.20), channel_id=1, source_target_pairs={{0,0},{4,8},{8,4},{12,16},{16,12},{20,24},{24,20},{28,28},{1,1},{5... | collective-permute-start | bytes 706568 | tf_op jit(solution)/shard_map/ppermute | solution.py:934
  9.4 9.2 %collective-permute-start.2 = (f32[144,128]{1,0:T(8,128)}, f32[144,128]{1,0:T(8,128)S(1)}, u32[]{:S(2)}, u32[]{:S(2)}) collective-permute-start(f32[144,128]{1,0:T(8,128)} %get-tuple-element.21), channel_id=1, source_target_pairs={{0,8},{4,12},{8,0},{12,4},{16,24},{20,28},{24,16},{28,20},{1,9},{5... | collective-permute-start | bytes 221192 | tf_op jit(solution)/shard_map/ppermute | solution.py:934
  11.4 7.2 %collective-permute-start.3 = (f32[144,128]{1,0:T(8,128)}, f32[144,128]{1,0:T(8,128)S(1)}, u32[]{:S(2)}, u32[]{:S(2)}) collective-permute-start(f32[144,128]{1,0:T(8,128)} %get-tuple-element.22), channel_id=1, source_target_pairs={{0,0},{4,4},{8,16},{12,20},{16,8},{20,12},{24,24},{28,28},{1,1},{5... | collective-permute-start | bytes 221192 | tf_op jit(solution)/shard_map/ppermute | solution.py:934
  12.9 10.7 %collective-permute-start.6 = (f32[464,128]{1,0:T(8,128)}, f32[464,128]{1,0:T(8,128)S(1)}, u32[]{:S(2)}, u32[]{:S(2)}) collective-permute-start(f32[464,128]{1,0:T(8,128)} %get-tuple-element.30), channel_id=1, source_target_pairs={{0,4},{4,0},{8,12},{12,8},{16,20},{20,16},{24,28},{28,24},{1,5},{5... | collective-permute-start | bytes 712712 | tf_op jit(solution)/shard_map/ppermute | solution.py:996
  16.0 1.3 %copy-start = (f32[2224,128]{1,0:T(8,128)S(1)}, f32[2224,128]{1,0:T(8,128)}, u32[]{:S(2)}) copy-start(f32[2224,128]{1,0:T(8,128)} %get-tuple-element.18.cells) | copy-start | bytes 3416068
  20.0 6.5 %collective-permute-start.5 = (f32[480,128]{1,0:T(8,128)S(1)}, f32[480,128]{1,0:T(8,128)S(1)}, u32[]{:S(2)}, u32[]{:S(2)}) collective-permute-start(f32[480,128]{1,0:T(8,128)S(1)} %get-tuple-element.26), channel_id=1, source_target_pairs={{0,0},{1,2},{2,1},{3,3},{4,4},{5,6},{6,5},{7,7},{8,8},{9,10},{10,9... | collective-permute-start | bytes 737288 | tf_op jit(solution)/shard_map/ppermute | solution.py:934
  20.7 5.8 %collective-permute-start.4 = (f32[472,128]{1,0:T(8,128)S(1)}, f32[472,128]{1,0:T(8,128)S(1)}, u32[]{:S(2)}, u32[]{:S(2)}) collective-permute-start(f32[472,128]{1,0:T(8,128)S(1)} %get-tuple-element.25), channel_id=1, source_target_pairs={{0,1},{1,0},{2,3},{3,2},{4,5},{5,4},{6,7},{7,6},{8,9},{9,8},{10,11... | collective-permute-start | bytes 725000 | tf_op jit(solution)/shard_map/ppermute | solution.py:934
  23.6 8.5 %collective-permute-start.7 = (f32[464,128]{1,0:T(8,128)S(1)}, f32[464,128]{1,0:T(8,128)S(1)}, u32[]{:S(2)}, u32[]{:S(2)}) collective-permute-start(f32[464,128]{1,0:T(8,128)S(1)} %collective-permute-done.6.mate_rest), channel_id=1, source_target_pairs={{0,8},{4,0},{8,16},{12,4},{16,24},{20,12},{24,28},{28,20},{1,9},{5... | collective-permute-start | bytes 712712 | tf_op jit(solution)/shard_map/ppermute | solution.py:999
  26.5 5.6 %copy-start.1 = (f32[2224,128]{1,0:T(8,128)S(1)}, f32[2224,128]{1,0:T(8,128)}, u32[]{:S(2)}) copy-start(f32[2224,128]{1,0:T(8,128)} %get-tuple-element.18.cells) | copy-start | bytes 3416068

commit v12 on v11

--- a/solution.py
+++ b/solution.py
@@ -25,6 +25,7 @@
 LAYERS = 2 * PLANES + OUTWARD
 RIM = 11 * EDGE
 REST = POPS * EDGE + 10 * EDGE
+HALF = REST // 2
 PAIR = 2 * GROUP
 QUADS = PLANES // 4
 TABLE = RIM
@@ -123,6 +124,7 @@
     mate2_hbm,
     other2_hbm,
     rest_hbm,
+    rest2_hbm,
     moves,
     counts,
     pops,
@@ -285,6 +287,7 @@
     cells[OWN2 : OWN2 + 6 * GROUP, :] = up2_msg[...]
     cells[OWN2 + 6 * GROUP :, :] = down2_msg[...]
     last = [copy(cells.at[OWN2:], cells_hbm.at[OWN2:]), copy(rest_msg, rest_hbm)]
+    last.append(copy(rest_msg.at[HALF:], rest2_hbm))
     count = len(started)
     for i, (up, down, mate, other, unit) in enumerate(
         ((up_msg, down_msg, mate_hbm, other_hbm, 1), (up2_msg, down2_msg, mate2_hbm, other2_hbm, 2))
@@ -387,6 +390,7 @@
     other_msg,
     mate2_msg,
     other2_msg,
+    along_z,
     near_msg,
     far_msg,
     outer,
@@ -851,6 +855,7 @@
     other_msg,
     mate_rest,
     passed_rest,
+    passed2_rest,
     out_hbm,
     h_ref,
     post_ref,
@@ -866,17 +871,24 @@
     for row in range(0, POPS * GROUP, 8):
         outer_ref[NOWHERE + row : NOWHERE + row + 8, :] = nothing
 
+    def rest(row, is_mate):
+        if is_mate:
+            return mate_rest[row : row + 8, :]
+        if row < HALF:
+            return passed_rest[row : row + 8, :]
+        return passed2_rest[row - HALF : row - HALF + 8, :]
+
     from_low, from_high = landed_slots(cells)[:2]
     lane = lanes_iota()
     even = is_even("curve")
     odd = jnp.logical_not(even)
-    for s, (slot, wanted, msg, rest) in itertools.product(
+    for s, (slot, wanted, msg, is_mate) in itertools.product(
         range(SLOTS),
         (
-            (from_low, odd, mate_msg, mate_rest),
-            (from_low, even, other_msg, passed_rest),
-            (from_high, even, mate_msg, mate_rest),
-            (from_high, odd, other_msg, passed_rest),
+            (from_low, odd, mate_msg, True),
+            (from_low, even, other_msg, False),
+            (from_high, even, mate_msg, True),
+            (from_high, odd, other_msg, False),
         ),
     ):
 
@@ -888,9 +900,9 @@
                 for p in range(POPS):
                     rim = rim_of(msg, p, v)
                     row = p * EDGE + v * 8
-                    wide = rest[row : row + 8, :]
+                    wide = rest(row, is_mate)
                     row = (POPS + p // 2) * EDGE + v * 8
-                    middle = rest[row : row + 8, :]
+                    middle = rest(row, is_mate)
                     if p % 2:
                         middle = pltpu.roll(middle, 64, axis=1)
                     first = jnp.where(lane < 32, rim, wide)
@@ -968,11 +980,11 @@
         6 * GROUP,
         REST,
     ]
-    cells, mate_msg, other_msg, mate2_msg, other2_msg, rest_msg = call(
+    cells, mate_msg, other_msg, mate2_msg, other2_msg, rest_msg, rest2_msg = call(
         functools.partial(pack_kernel, *sizes),
         "HHHHH",
-        "HHHHHH",
-        [rows128(rows) for rows in messages],
+        "HHHHHHH",
+        [rows128(rows) for rows in (*messages, REST - HALF)],
         (moves, counts, populations, site_flags, neighbours),
         [
             pltpu.SMEM(moves.shape, jnp.int32),
@@ -985,7 +997,7 @@
             pltpu.VMEM((128, 384), jnp.bfloat16),
             floats(256),
             floats(8),
-            pltpu.SemaphoreType.DMA((4 + SLOTS + 8,)),
+            pltpu.SemaphoreType.DMA((4 + SLOTS + 9,)),
         ],
         WIDE_LIMIT,
     )
@@ -996,16 +1008,19 @@
     mate_rest = lax.ppermute(rest_msg, "curve", pairs)
     last = sizes[0] - 1
     pairs = [(i, max(i - 2, 0) if i % 2 else min(i + 2, last)) for i in range(sizes[0])]
-    passed_rest = lax.ppermute(mate_rest, "curve", pairs)
+    passed_rest = lax.ppermute(mate_rest[:HALF], "curve", pairs)
+    back = [(target, source) for source, target in pairs]
+    along_z = lax.ppermute(rest2_msg, "curve", back)
+    passed2_rest = lax.ppermute(along_z, "curve", [(i, i ^ 1) for i in range(last + 1)])
     (outer,) = call(spread_kernel, "V", "V", [rows128(PLANES * GROUP)], (cells,), [])
     strips = (cells, mate_msg, other_msg, mate2_msg, other2_msg)
     sorted_rows = [messages[1], messages[1], messages[3], messages[3]]
     near_msg, far_msg = call(
         edge_kernel,
-        "VVVVVV",
+        "VVVVVVV",
         "VV",
         [rows128(NEAR_ROWS), rows128(FAR_ROWS)],
-        (outer, *strips),
+        (outer, *strips, along_z),
         [floats(rows) for rows in [PLANES * GROUP] + sorted_rows],
         cost=pl.CostEstimate(flops=10**10, bytes_accessed=0, transcendentals=0),
     )
@@ -1030,10 +1045,10 @@
         (own_slots, post, near_msg, far_msg),
         [floats(SLOTS * SLOT), pltpu.SMEM((72, 128), jnp.int32), pltpu.SemaphoreType.DMA],
     )
-    arriving = (cells, mate_msg, other_msg, mate_rest, passed_rest)
+    arriving = (cells, mate_msg, other_msg, mate_rest, passed_rest, passed2_rest)
     return call(
         steps_kernel,
-        "VVVVVVVVV",
+        "VVVVVVVVVV",
         "H",
         [jax.ShapeDtypeStruct(populations.shape, jnp.float32)],
         (slots, post, outer_post, next_outer, *arriving),

time: 38.4 us -> 40.3 us (1.049)
  waiting for transfers between devices: 5.45 us -> 7.66 us
  starting transfers between devices: 17 us -> 16.5 us
    ppermute x1 -> x3, starting transfers between devices: 2.25 us -> 5.99 us  [the longest x1 3.41 us: per_device(): along_z = lax.ppermute(rest2_msg, 'curve', back)]
    ppermute x6, waiting for transfers between devices: 2.18 us -> 5.52 us  [swapped(): results.append(lax.ppermute(value[which], axis, pairs))]
    ppermute x1, starting transfers between devices: 3.03 us -> 0.82 us  [per_device(): mate_rest = lax.ppermute(rest_msg, 'curve', pairs)]
    ppermute x6, starting transfers between devices: 11.7 us -> 9.65 us  [swapped(): results.append(lax.ppermute(value[which], axis, pairs))]
    ppermute x1 -> x3, waiting for transfers between devices: 3.28 us -> 1.87 us  [the longest x1 1.67 us: per_device(): passed_rest = lax.ppermute(mate_rest[:HALF], 'curve', pairs)]
    unnamed x4 -> x6, local copies, waits for them, and re-layouts: 1.26 us -> 1.27 us
  transfers between devices with their start and end apart: 8 -> 10, of which waited for: 3 -> 4; matrix products, arithmetic and copies ran while one was open for 0% -> 0% of each run, Pallas kernels for 9% -> 9%
where the time goes in v12:
time: 40.3 us; the launch traced here: 40 us
  starting transfers between devices  16.5 us (41%)
  Pallas kernels  13.9 us (34%)
  waiting for transfers between devices  7.66 us (19%)
  local copies, waits for them, and re-layouts  1.27 us (3%)
  between operations  0.74 us (2%)
    pallas_call x6, Pallas kernels, call(): pl.pallas_call(kernel, out_shape=outs, in_specs=[spaces[x] for x in in_sp...  13.9 us
    ppermute x6, starting transfers between devices, swapped(): results.append(lax.ppermute(value[which], axis, pairs))  9.65 us
    ppermute x6, waiting for transfers between devices, swapped(): results.append(lax.ppermute(value[which], axis, pairs))  5.52 us
    ppermute x1, starting transfers between devices, per_device(): along_z = lax.ppermute(rest2_msg, 'curve', back)  3.41 us
    ppermute x1, waiting for transfers between devices, per_device(): passed_rest = lax.ppermute(mate_rest[:HALF], 'curve', pairs)  1.67 us
    ppermute x1, starting transfers between devices, per_device(): lax.ppermute(along_z, 'curve', [(i, i ^ 1) for i in range(last + 1)])  1.39 us
    unnamed x6, local copies, waits for them, and re-layouts  1.27 us
    ppermute x1, starting transfers between devices, per_device(): passed_rest = lax.ppermute(mate_rest[:HALF], 'curve', pairs)  1.19 us
  transfers between devices with their start and end apart: 10, of which 4 were waited for; matrix products, arithmetic and copies ran while one was open for 0% of the time, Pallas kernels for 9%

profile of v12, /device:TPU:0, one launch (start us, length us, event | category | flops | bytes accessed | tf_op | source)
XLA Modules:
  0.0 40.0 jit_solution(5738408115582772868)
XLA Ops:
  0.7 4.2 %shard_map.55 = (f32[2224,128]{1,0:T(8,128)}, f32[460,128]{1,0:T(8,128)}, f32[460,128]{1,0:T(8,128)}, f32[144,128]{1,0:T(8,128)}, f32[144,128]{1,0:T(8,128)}, /*index=5*/f32[464,128]{1,0:T(8,128)}, f32[232,128]{1,0:T(8,128)}) custom-call(s32[3,32]{1,0:T(4,128)} %bitcast.1, s32[1]{0:T(128)S(6)} %copy.6.counts_hbm, f32[3,19,4096]{2,1,0:T(8,128)} %pops_hbm.1, ...), custom_call_target="tpu_custom_call" | custom-call | tf_op jit(solution)/shard_map/pallas_call | solution.py:960
  4.8 3.0 %collective-permute-start = (f32[460,128]{1,0:T(8,128)}, f32[460,128]{1,0:T(8,128)S(1)}, u32[]{:S(2)}, u32[]{:S(2)}) collective-permute-start(f32[460,128]{1,0:T(8,128)} %get-tuple-element.20), channel_id=1, source_target_pairs={{0,4},{4,0},{8,12},{12,8},{16,20},{20,16},{24,28},{28,24},{1,5},{5... | collective-permute-start | bytes 706568 | tf_op jit(solution)/shard_map/ppermute | solution.py:946
  7.9 1.6 %collective-permute-start.1 = (f32[460,128]{1,0:T(8,128)}, f32[460,128]{1,0:T(8,128)S(1)}, u32[]{:S(2)}, u32[]{:S(2)}) collective-permute-start(f32[460,128]{1,0:T(8,128)} %get-tuple-element.21), channel_id=1, source_target_pairs={{0,0},{4,8},{8,4},{12,16},{16,12},{20,24},{24,20},{28,28},{1,1},{5... | collective-permute-start | bytes 706568 | tf_op jit(solution)/shard_map/ppermute | solution.py:946
  9.5 3.4 %collective-permute-start.4 = (f32[232,128]{1,0:T(8,128)}, f32[232,128]{1,0:T(8,128)S(1)}, u32[]{:S(2)}, u32[]{:S(2)}) collective-permute-start(f32[232,128]{1,0:T(8,128)} %get-tuple-element.26), channel_id=1, source_target_pairs={{8,0},{0,4},{16,8},{4,12},{24,16},{12,20},{28,24},{20,28},{9,1},{1... | collective-permute-start | bytes 356360 | tf_op jit(solution)/shard_map/ppermute | solution.py:1013
  12.9 0.0 collective-permute-start.2
  12.9 1.5 %collective-permute-start.3 = (f32[144,128]{1,0:T(8,128)}, f32[144,128]{1,0:T(8,128)S(1)}, u32[]{:S(2)}, u32[]{:S(2)}) collective-permute-start(f32[144,128]{1,0:T(8,128)} %get-tuple-element.23), channel_id=1, source_target_pairs={{0,0},{4,4},{8,16},{12,20},{16,8},{20,12},{24,24},{28,28},{1,1},{5... | collective-permute-start | bytes 221192 | tf_op jit(solution)/shard_map/ppermute | solution.py:946
  14.4 0.0 copy-start
  14.4 1.3 %copy-done = f32[2224,128]{1,0:T(8,128)S(1)} copy-done((f32[2224,128]{1,0:T(8,128)S(1)}, f32[2224,128]{1,0:T(8,128)}, u32[]{:S(2)}) %copy-start) | copy-done | bytes 1138712
  15.7 0.0 copy-start.2
  15.7 0.1 shard_map.57.own_outer
  15.7 5.5 %collective-permute-done.2.mate2_msg = f32[144,128]{1,0:T(8,128)S(1)} collective-permute-done((f32[144,128]{1,0:T(8,128)}, f32[144,128]{1,0:T(8,128)S(1)}, u32[]{:S(2)}, u32[]{:S(2)}) %collective-permute-start.2) | collective-permute-done | bytes 73760 | tf_op jit(solution)/shard_map/ppermute | solution.py:946
  21.2 0.0 copy-done.2
  21.2 0.8 %collective-permute-start.7 = (f32[464,128]{1,0:T(8,128)S(1)}, f32[464,128]{1,0:T(8,128)S(1)}, u32[]{:S(2)}, u32[]{:S(2)}) collective-permute-start(f32[464,128]{1,0:T(8,128)S(1)} %copy-done.2), channel_id=1, source_target_pairs={{0,4},{4,0},{8,12},{12,8},{16,20},{20,16},{24,28},{28,24},{1,5},{5... | collective-permute-start | bytes 712712 | tf_op jit(solution)/shard_map/ppermute | solution.py:1008
  22.0 0.0 collective-permute-done.3.other2_msg
  22.0 0.0 collective-permute-done.4.along_z
  22.0 0.0 collective-permute-done.mate_msg
  22.1 0.0 collective-permute-done.1.other_msg
  22.1 0.7 %shard_map.58 = (f32[472,128]{1,0:T(8,128)S(1)}, f32[480,128]{1,0:T(8,128)S(1)}) custom-call(f32[1440,128]{1,0:T(8,128)S(1)} %shard_map.57.own_outer, f32[2224,128]{1,0:T(8,128)S(1)} %copy-done, f32[460,128]{1,0:T(8,128)S(1)} %collective-permute-done.mate_msg, f32[460,128]{1,0:T(8,128)S(1)} %collective-permute-done.1.other_msg, ...), custom_call_target="tpu_custom_call" | custom-call | flops 10000000000 | tf_op jit(solution)/shard_map/pallas_call | solution.py:960
  22.7 0.7 %collective-permute-start.6 = (f32[480,128]{1,0:T(8,128)S(1)}, f32[480,128]{1,0:T(8,128)S(1)}, u32[]{:S(2)}, u32[]{:S(2)}) collective-permute-start(f32[480,128]{1,0:T(8,128)S(1)} %get-tuple-element.28), channel_id=1, source_target_pairs={{0,0},{1,2},{2,1},{3,3},{4,4},{5,6},{6,5},{7,7},{8,8},{9,10},{10,9... | collective-permute-start | bytes 737288 | tf_op jit(solution)/shard_map/ppermute | solution.py:946
  23.4 2.8 %collective-permute-start.5 = (f32[472,128]{1,0:T(8,128)S(1)}, f32[472,128]{1,0:T(8,128)S(1)}, u32[]{:S(2)}, u32[]{:S(2)}) collective-permute-start(f32[472,128]{1,0:T(8,128)S(1)} %get-tuple-element.27), channel_id=1, source_target_pairs={{0,1},{1,0},{2,3},{3,2},{4,5},{5,4},{6,7},{7,6},{8,9},{9,8},{10,11... | collective-permute-start | bytes 725000 | tf_op jit(solution)/shard_map/ppermute | solution.py:946
  26.2 1.4 %collective-permute-start.9 = (f32[232,128]{1,0:T(8,128)S(1)}, f32[232,128]{1,0:T(8,128)S(1)}, u32[]{:S(2)}, u32[]{:S(2)}) collective-permute-start(f32[232,128]{1,0:T(8,128)S(1)} %collective-permute-done.4.along_z), channel_id=1, source_target_pairs={{0,4},{4,0},{8,12},{12,8},{16,20},{20,16},{24,28},{28,24},{1,5},{5... | collective-permute-start | bytes 356360 | tf_op jit(solution)/shard_map/ppermute | solution.py:1014
  27.6 0.3 collective-permute-done.7.mate_rest
  27.9 1.2 %collective-permute-start.8 = (f32[232,128]{1,0:T(8,128)S(1)}, f32[232,128]{1,0:T(8,128)S(1)}, u32[]{:S(2)}, u32[]{:S(2)}) collective-permute-start(f32[232,128]{1,0:T(8,128)S(1)} %slice.4), channel_id=1, source_target_pairs={{0,8},{4,0},{8,16},{12,4},{16,24},{20,12},{24,28},{28,20},{1,9},{5... | collective-permute-start | bytes 356360 | tf_op jit(solution)/shard_map/ppermute | solution.py:1011
  29.1 0.7 %shard_map.56 = (f32[3792,128]{1,0:T(8,128)S(1)}, s32[24,128]{1,0:T(8,128)S(1)}) custom-call(f32[2224,128]{1,0:T(8,128)S(1)} %copy-done, f32[460,128]{1,0:T(8,128)S(1)} %collective-permute-done.mate_msg, f32[460,128]{1,0:T(8,128)S(1)} %collective-permute-done.1.other_msg, f32[144,128]{1,0:T(8,128)S(1)} %collective-permute-done.2.mate2_msg, ...), custom_call_target="tpu_custom_call" | custom-call | tf_op jit(solution)/shard_map/pallas_call | solution.py:960
  29.8 0.0 collective-permute-done.5.near_msg
  29.8 0.0 collective-permute-done.6.far_msg
  29.9 0.0 copy-start.1
  29.9 2.3 %shard_map.59 = (s32[72,128]{1,0:T(8,128)S(1)}, f32[1896,128]{1,0:T(8,128)S(1)}, f32[1896,128]{1,0:T(8,128)S(1)}) custom-call(s32[24,128]{1,0:T(8,128)S(1)} %get-tuple-element.24.own_slots, f32[3792,128]{1,0:T(8,128)S(1)} %get-tuple-element.25.first_post, f32[472,128]{1,0:T(8,128)S(1)} %collective-permute-done.5.near_msg, ...), custom_call_target="tpu_custom_call" | custom-call | tf_op jit(solution)/shard_map/pallas_call | solution.py:960
  32.1 0.2 collective-permute-done.9.passed2_rest
  32.3 1.7 %collective-permute-done.8.passed_rest = f32[232,128]{1,0:T(8,128)S(1)} collective-permute-done((f32[232,128]{1,0:T(8,128)S(1)}, f32[232,128]{1,0:T(8,128)S(1)}, u32[]{:S(2)}, u32[]{:S(2)}) %collective-permute-start.8) | collective-permute-done | bytes 118816 | tf_op jit(solution)/shard_map/ppermute | solution.py:1011
  34.0 0.0 copy-done.1
  34.0 6.0 %shard_map.60 = f32[3,19,4096]{2,1,0:T(8,128)} custom-call(s32[72,128]{1,0:T(8,128)S(1)} %get-tuple-element.29.slots, f32[3792,128]{1,0:T(8,128)S(1)} %get-tuple-element.25.first_post, f32[1896,128]{1,0:T(8,128)S(1)} %get-tuple-element.30.first_outer, f32[1896,128]{1,0:T(8,128)S(1)} %get-tuple-element.31.next_outer, f32[2224,128]{1,0:T(8,128)S(1)} %copy-done.1, ...), custom_call_target="tpu_custom_call" | custom-call | tf_op jit(solution)/shard_map/pallas_call | solution.py:960
  (1 shorter events, 0.0 us)
Async XLA Ops:
  4.8 17.2 %collective-permute-start = (f32[460,128]{1,0:T(8,128)}, f32[460,128]{1,0:T(8,128)S(1)}, u32[]{:S(2)}, u32[]{:S(2)}) collective-permute-start(f32[460,128]{1,0:T(8,128)} %get-tuple-element.20), channel_id=1, source_target_pairs={{0,4},{4,0},{8,12},{12,8},{16,20},{20,16},{24,28},{28,24},{1,5},{5... | collective-permute-start | bytes 706568 | tf_op jit(solution)/shard_map/ppermute | solution.py:946
  7.9 14.2 %collective-permute-start.1 = (f32[460,128]{1,0:T(8,128)}, f32[460,128]{1,0:T(8,128)S(1)}, u32[]{:S(2)}, u32[]{:S(2)}) collective-permute-start(f32[460,128]{1,0:T(8,128)} %get-tuple-element.21), channel_id=1, source_target_pairs={{0,0},{4,8},{8,4},{12,16},{16,12},{20,24},{24,20},{28,28},{1,1},{5... | collective-permute-start | bytes 706568 | tf_op jit(solution)/shard_map/ppermute | solution.py:946
  9.5 12.6 %collective-permute-start.4 = (f32[232,128]{1,0:T(8,128)}, f32[232,128]{1,0:T(8,128)S(1)}, u32[]{:S(2)}, u32[]{:S(2)}) collective-permute-start(f32[232,128]{1,0:T(8,128)} %get-tuple-element.26), channel_id=1, source_target_pairs={{8,0},{0,4},{16,8},{4,12},{24,16},{12,20},{28,24},{20,28},{9,1},{1... | collective-permute-start | bytes 356360 | tf_op jit(solution)/shard_map/ppermute | solution.py:1013
  12.9 8.3 %collective-permute-start.2 = (f32[144,128]{1,0:T(8,128)}, f32[144,128]{1,0:T(8,128)S(1)}, u32[]{:S(2)}, u32[]{:S(2)}) collective-permute-start(f32[144,128]{1,0:T(8,128)} %get-tuple-element.22), channel_id=1, source_target_pairs={{0,8},{4,12},{8,0},{12,4},{16,24},{20,28},{24,16},{28,20},{1,9},{5... | collective-permute-start | bytes 221192 | tf_op jit(solution)/shard_map/ppermute | solution.py:946
  12.9 9.2 %collective-permute-start.3 = (f32[144,128]{1,0:T(8,128)}, f32[144,128]{1,0:T(8,128)S(1)}, u32[]{:S(2)}, u32[]{:S(2)}) collective-permute-start(f32[144,128]{1,0:T(8,128)} %get-tuple-element.23), channel_id=1, source_target_pairs={{0,0},{4,4},{8,16},{12,20},{16,8},{20,12},{24,24},{28,28},{1,1},{5... | collective-permute-start | bytes 221192 | tf_op jit(solution)/shard_map/ppermute | solution.py:946
  14.4 1.3 %copy-start = (f32[2224,128]{1,0:T(8,128)S(1)}, f32[2224,128]{1,0:T(8,128)}, u32[]{:S(2)}) copy-start(f32[2224,128]{1,0:T(8,128)} %get-tuple-element.19.cells) | copy-start | bytes 3416068
  15.7 5.6 %copy-start.2 = (f32[464,128]{1,0:T(8,128)S(1)}, f32[464,128]{1,0:T(8,128)}, u32[]{:S(2)}) copy-start(f32[464,128]{1,0:T(8,128)} %get-tuple-element.32) | copy-start | bytes 712708
  21.2 6.7 %collective-permute-start.7 = (f32[464,128]{1,0:T(8,128)S(1)}, f32[464,128]{1,0:T(8,128)S(1)}, u32[]{:S(2)}, u32[]{:S(2)}) collective-permute-start(f32[464,128]{1,0:T(8,128)S(1)} %copy-done.2), channel_id=1, source_target_pairs={{0,4},{4,0},{8,12},{12,8},{16,20},{20,16},{24,28},{28,24},{1,5},{5... | collective-permute-start | bytes 712712 | tf_op jit(solution)/shard_map/ppermute | solution.py:1008
  22.7 7.1 %collective-permute-start.6 = (f32[480,128]{1,0:T(8,128)S(1)}, f32[480,128]{1,0:T(8,128)S(1)}, u32[]{:S(2)}, u32[]{:S(2)}) collective-permute-start(f32[480,128]{1,0:T(8,128)S(1)} %get-tuple-element.28), channel_id=1, source_target_pairs={{0,0},{1,2},{2,1},{3,3},{4,4},{5,6},{6,5},{7,7},{8,8},{9,10},{10,9... | collective-permute-start | bytes 737288 | tf_op jit(solution)/shard_map/ppermute | solution.py:946
  23.4 6.4 %collective-permute-start.5 = (f32[472,128]{1,0:T(8,128)S(1)}, f32[472,128]{1,0:T(8,128)S(1)}, u32[]{:S(2)}, u32[]{:S(2)}) collective-permute-start(f32[472,128]{1,0:T(8,128)S(1)} %get-tuple-element.27), channel_id=1, source_target_pairs={{0,1},{1,0},{2,3},{3,2},{4,5},{5,4},{6,7},{7,6},{8,9},{9,8},{10,11... | collective-permute-start | bytes 725000 | tf_op jit(solution)/shard_map/ppermute | solution.py:946
  26.2 6.1 %collective-permute-start.9 = (f32[232,128]{1,0:T(8,128)S(1)}, f32[232,128]{1,0:T(8,128)S(1)}, u32[]{:S(2)}, u32[]{:S(2)}) collective-permute-start(f32[232,128]{1,0:T(8,128)S(1)} %collective-permute-done.4.along_z), channel_id=1, source_target_pairs={{0,4},{4,0},{8,12},{12,8},{16,20},{20,16},{24,28},{28,24},{1,5},{5... | collective-permute-start | bytes 356360 | tf_op jit(solution)/shard_map/ppermute | solution.py:1014
  27.9 6.1 %collective-permute-start.8 = (f32[232,128]{1,0:T(8,128)S(1)}, f32[232,128]{1,0:T(8,128)S(1)}, u32[]{:S(2)}, u32[]{:S(2)}) collective-permute-start(f32[232,128]{1,0:T(8,128)S(1)} %slice.4), channel_id=1, source_target_pairs={{0,8},{4,0},{8,16},{12,4},{16,24},{20,12},{24,28},{28,20},{1,9},{5... | collective-permute-start | bytes 356360 | tf_op jit(solution)/shard_map/ppermute | solution.py:1011
  29.9 4.2 %copy-start.1 = (f32[2224,128]{1,0:T(8,128)S(1)}, f32[2224,128]{1,0:T(8,128)}, u32[]{:S(2)}) copy-start(f32[2224,128]{1,0:T(8,128)} %get-tuple-element.19.cells) | copy-start | bytes 3416068

commit v13 on v12

--- a/solution.py
+++ b/solution.py
@@ -18,14 +18,15 @@
 GROUP = 24
 PLANE = 3 * GROUP
 SLOT = POPS * PLANE
-CELLS = PLANES * 32
+CELL = 40
+CELLS = PLANES * CELL
 LANDINGS = CELLS + 8
 OWN2 = LANDINGS + 8
 OUTWARD = SLOTS * 5 + SLOTS
 LAYERS = 2 * PLANES + OUTWARD
 RIM = 11 * EDGE
 REST = POPS * EDGE + 10 * EDGE
-HALF = REST // 2
+HALF = REST - 136
 PAIR = 2 * GROUP
 QUADS = PLANES // 4
 TABLE = RIM
@@ -192,7 +193,7 @@
         for y in range(2):
             piece = site_flags[pl.ds(128 * y + s, EDGE, stride=8), :]
             is_fluid = (piece == 1.0) & live
-            row = (FLAG0 + s) * 32 + y * EDGE
+            row = (FLAG0 + s) * CELL + y * EDGE
             cells[row : row + EDGE, :] = jnp.where(is_fluid, 1.0, 0.0)
 
     for s in range(SLOTS):
@@ -201,8 +202,8 @@
             for y in range(2):
                 tile = 2 * x + y
                 for p, size in ((0, 8), (8, 8), (16, 3)):
-                    row = (s * POPS + p) * 32 + y * EDGE + x
-                    cells[pl.ds(row, size, stride=32), :] = pops[
+                    row = (s * POPS + p) * CELL + y * EDGE + x
+                    cells[pl.ds(row, size, stride=CELL), :] = pops[
                         s, p : p + size, 128 * tile : 128 * tile + 128
                     ]
 
@@ -210,11 +211,11 @@
     def _(s):
         @pl.loop(0, 4, unroll=2)
         def _(c):
-            base = s * (POPS * 32) + c * 8
-            view = cells.at[aligned(base, (POPS - 1) * 32 + 8), :]
-            h = [view[p * 32 : p * 32 + 8, :] for p in range(POPS)]
+            base = s * (POPS * CELL) + c * 8
+            view = cells.at[aligned(base, (POPS - 1) * CELL + 8), :]
+            h = [view[p * CELL : p * CELL + 8, :] for p in range(POPS)]
             for p, value in enumerate(collided(h)):
-                view[p * 32 : p * 32 + 8, :] = value
+                view[p * CELL : p * CELL + 8, :] = value
 
     for i, slot in enumerate(move_slots(moves, curve_size, cross_size)):
         value = jnp.full((1, 128), slot, jnp.int32)
@@ -228,18 +229,18 @@
             for k in range(2):
                 out = STRIPS + y * LAYERS + k * PLANES
                 msg[out : out + PLANES, :] = cells[
-                    pl.ds(y * EDGE + x0 + step * k, PLANES, stride=32), :
+                    pl.ds(y * EDGE + x0 + step * k, PLANES, stride=CELL), :
                 ]
             row = y * EDGE + x0 + 2 * step
             out = STRIPS + y * LAYERS + 2 * PLANES
             for s in range(SLOTS):
-                base = s * POPS * 32 + row
-                msg[out + 5 * s : out + 5 * s + 1, :] = cells[pl.ds(base + first * 32, 1), :]
+                base = s * POPS * CELL + row
+                msg[out + 5 * s : out + 5 * s + 1, :] = cells[pl.ds(base + first * CELL, 1), :]
                 msg[out + 5 * s + 1 : out + 5 * s + 5, :] = cells[
-                    pl.ds(base + (first + 6) * 32, 4, stride=64), :
+                    pl.ds(base + (first + 6) * CELL, 4, stride=2 * CELL), :
                 ]
             msg[out + 5 * SLOTS : out + OUTWARD, :] = cells[
-                pl.ds(FLAG0 * 32 + row, SLOTS, stride=32), :
+                pl.ds(FLAG0 * CELL + row, SLOTS, stride=CELL), :
             ]
 
     here = lax.axis_index("curve") * cross_size + lax.axis_index("cross")
@@ -247,7 +248,7 @@
     lane = lanes_iota()
     for v in range(2):
         halves = [
-            [cells[aligned(leaving * (POPS * 32) + p * 32 + y * EDGE + v * 8), :] for y in (0, 1)]
+            [cells[aligned(leaving * (POPS * CELL) + p * CELL + y * EDGE + v * 8), :] for y in (0, 1)]
             for p in range(POPS)
         ]
         outer = [jnp.where(lane < 64, first, second) for first, second in halves]
@@ -280,9 +281,9 @@
             for y in range(2):
                 for k in range(3):
                     out = (y * 3 + k) * GROUP
-                    row = s * POPS * 32 + y * EDGE + k
-                    up2_msg[out : out + POPS, :] = cells[pl.ds(row + 13, POPS, stride=32), :]
-                    down2_msg[out : out + POPS, :] = cells[pl.ds(row, POPS, stride=32), :]
+                    row = s * POPS * CELL + y * EDGE + k
+                    up2_msg[out : out + POPS, :] = cells[pl.ds(row + 13, POPS, stride=CELL), :]
+                    down2_msg[out : out + POPS, :] = cells[pl.ds(row, POPS, stride=CELL), :]
 
     cells[OWN2 : OWN2 + 6 * GROUP, :] = up2_msg[...]
     cells[OWN2 + 6 * GROUP :, :] = down2_msg[...]
@@ -316,7 +317,7 @@
     low = lanes_iota() < 64
     for q in range(PLANES):
         for v in range(2):
-            row = q * 32 + v * 8
+            row = q * CELL + v * 8
             first, second = cells[row : row + 8, :], cells[row + EDGE : row + EDGE + 8, :]
             row = q * GROUP + v * 8
             outer[row : row + 8, :] = jnp.where(low, first, second)
@@ -751,7 +752,7 @@
         for y in range(2):
             start = q * PAIR + y * GROUP
             post_ref[start : start + EDGE, :] = cells[
-                q * 32 + y * EDGE : q * 32 + (y + 1) * EDGE, :
+                q * CELL + y * EDGE : q * CELL + (y + 1) * EDGE, :
             ]
     for s, (slot, msg) in itertools.product(
         range(SLOTS), ((from_low, low_msg), (from_high, high_msg))

time: 40.3 us -> 39.9 us (0.990)
  starting transfers between devices: 16.5 us -> 18.9 us
  waiting for transfers between devices: 7.66 us -> 5.53 us
  Pallas kernels: 13.9 us -> 13.1 us
    ppermute x6, waiting for transfers between devices: 5.52 us -> 0.02 us  [swapped(): results.append(lax.ppermute(value[which], axis, pairs))]
    ppermute x1, waiting for transfers between devices: 0.01 us -> 2.78 us  [per_device(): along_z = lax.ppermute(rest2_msg, 'curve', back)]
    ppermute x6, starting transfers between devices: 9.65 us -> 11.8 us  [swapped(): results.append(lax.ppermute(value[which], axis, pairs))]
    ppermute x1, waiting for transfers between devices: 0.2 us -> 2.12 us  [per_device(): lax.ppermute(along_z, 'curve', [(i, i ^ 1) for i in range(last + 1)])]
    ppermute x1, waiting for transfers between devices: 1.67 us -> 0.01 us  [per_device(): passed_rest = lax.ppermute(mate_rest[:HALF], 'curve', pairs)]
    ppermute x1, starting transfers between devices: 0.82 us -> 2.02 us  [per_device(): mate_rest = lax.ppermute(rest_msg, 'curve', pairs)]
    pallas_call x6, Pallas kernels: 13.9 us -> 13.1 us  [call(): pl.pallas_call(kernel, out_shape=outs, in_specs=[spaces[x] for x in in_sp...]
    ppermute x1, starting transfers between devices: 1.39 us -> 0.91 us  [per_device(): lax.ppermute(along_z, 'curve', [(i, i ^ 1) for i in range(last + 1)])]
  transfers between devices with their start and end apart: 10 -> 10, of which waited for: 4 -> 3; matrix products, arithmetic and copies ran while one was open for 0% -> 0% of each run, Pallas kernels for 9% -> 9%
where the time goes in v13:
time: 39.9 us; the launch traced here: 39.7 us
  starting transfers between devices  18.9 us (47%)
  Pallas kernels  13.1 us (33%)
  waiting for transfers between devices  5.53 us (14%)
  local copies, waits for them, and re-layouts  1.36 us (3%)
  between operations  0.74 us (2%)
    pallas_call x6, Pallas kernels, call(): pl.pallas_call(kernel, out_shape=outs, in_specs=[spaces[x] for x in in_sp...  13.1 us
    ppermute x6, starting transfers between devices, swapped(): results.append(lax.ppermute(value[which], axis, pairs))  11.8 us
    ppermute x1, starting transfers between devices, per_device(): along_z = lax.ppermute(rest2_msg, 'curve', back)  3.03 us
    ppermute x1, waiting for transfers between devices, per_device(): along_z = lax.ppermute(rest2_msg, 'curve', back)  2.78 us
    ppermute x1, waiting for transfers between devices, per_device(): lax.ppermute(along_z, 'curve', [(i, i ^ 1) for i in range(last + 1)])  2.12 us
    ppermute x1, starting transfers between devices, per_device(): mate_rest = lax.ppermute(rest_msg, 'curve', pairs)  2.02 us
    unnamed x6, local copies, waits for them, and re-layouts  1.35 us
    ppermute x1, starting transfers between devices, per_device(): passed_rest = lax.ppermute(mate_rest[:HALF], 'curve', pairs)  1.17 us
  transfers between devices with their start and end apart: 10, of which 3 were waited for; matrix products, arithmetic and copies ran while one was open for 0% of the time, Pallas kernels for 9%

profile of v13, /device:TPU:0, one launch (start us, length us, event | category | flops | bytes accessed | tf_op | source)
XLA Modules:
  0.0 39.7 jit_solution(2082966470613852632)
XLA Ops:
  0.7 3.6 %shard_map.55 = (f32[2704,128]{1,0:T(8,128)}, f32[460,128]{1,0:T(8,128)}, f32[460,128]{1,0:T(8,128)}, f32[144,128]{1,0:T(8,128)}, f32[144,128]{1,0:T(8,128)}, /*index=5*/f32[464,128]{1,0:T(8,128)}, f32[136,128]{1,0:T(8,128)}) custom-call(s32[3,32]{1,0:T(4,128)} %bitcast.1, s32[1]{0:T(128)S(6)} %copy.6.counts_hbm, f32[3,19,4096]{2,1,0:T(8,128)} %pops_hbm.1, ...), custom_call_target="tpu_custom_call" | custom-call | tf_op jit(solution)/shard_map/pallas_call | solution.py:961
  4.3 3.0 %collective-permute-start = (f32[460,128]{1,0:T(8,128)}, f32[460,128]{1,0:T(8,128)S(1)}, u32[]{:S(2)}, u32[]{:S(2)}) collective-permute-start(f32[460,128]{1,0:T(8,128)} %get-tuple-element.20), channel_id=1, source_target_pairs={{0,4},{4,0},{8,12},{12,8},{16,20},{20,16},{24,28},{28,24},{1,5},{5... | collective-permute-start | bytes 706568 | tf_op jit(solution)/shard_map/ppermute | solution.py:947
  7.3 1.6 %collective-permute-start.1 = (f32[460,128]{1,0:T(8,128)}, f32[460,128]{1,0:T(8,128)S(1)}, u32[]{:S(2)}, u32[]{:S(2)}) collective-permute-start(f32[460,128]{1,0:T(8,128)} %get-tuple-element.21), channel_id=1, source_target_pairs={{0,0},{4,8},{8,4},{12,16},{16,12},{20,24},{24,20},{28,28},{1,1},{5... | collective-permute-start | bytes 706568 | tf_op jit(solution)/shard_map/ppermute | solution.py:947
  8.9 2.0 %collective-permute-start.2 = (f32[144,128]{1,0:T(8,128)}, f32[144,128]{1,0:T(8,128)S(1)}, u32[]{:S(2)}, u32[]{:S(2)}) collective-permute-start(f32[144,128]{1,0:T(8,128)} %get-tuple-element.22), channel_id=1, source_target_pairs={{0,8},{4,12},{8,0},{12,4},{16,24},{20,28},{24,16},{28,20},{1,9},{5... | collective-permute-start | bytes 221192 | tf_op jit(solution)/shard_map/ppermute | solution.py:947
  10.8 1.5 %collective-permute-start.3 = (f32[144,128]{1,0:T(8,128)}, f32[144,128]{1,0:T(8,128)S(1)}, u32[]{:S(2)}, u32[]{:S(2)}) collective-permute-start(f32[144,128]{1,0:T(8,128)} %get-tuple-element.23), channel_id=1, source_target_pairs={{0,0},{4,4},{8,16},{12,20},{16,8},{20,12},{24,24},{28,28},{1,1},{5... | collective-permute-start | bytes 221192 | tf_op jit(solution)/shard_map/ppermute | solution.py:947
  12.4 3.0 %collective-permute-start.4 = (f32[136,128]{1,0:T(8,128)}, f32[136,128]{1,0:T(8,128)S(1)}, u32[]{:S(2)}, u32[]{:S(2)}) collective-permute-start(f32[136,128]{1,0:T(8,128)} %get-tuple-element.26), channel_id=1, source_target_pairs={{8,0},{0,4},{16,8},{4,12},{24,16},{12,20},{28,24},{20,28},{9,1},{1... | collective-permute-start | bytes 208904 | tf_op jit(solution)/shard_map/ppermute | solution.py:1014
  15.4 0.0 copy-start
  15.4 1.3 %copy-done = f32[2704,128]{1,0:T(8,128)S(1)} copy-done((f32[2704,128]{1,0:T(8,128)S(1)}, f32[2704,128]{1,0:T(8,128)}, u32[]{:S(2)}) %copy-start) | copy-done | bytes 1384472
  16.7 0.0 copy-start.2
  16.7 0.1 shard_map.57.own_outer
  16.8 2.8 %collective-permute-done.4.along_z = f32[136,128]{1,0:T(8,128)S(1)} collective-permute-done((f32[136,128]{1,0:T(8,128)}, f32[136,128]{1,0:T(8,128)S(1)}, u32[]{:S(2)}, u32[]{:S(2)}) %collective-permute-start.4) | collective-permute-done | bytes 69664 | tf_op jit(solution)/shard_map/ppermute | solution.py:1014
  19.6 0.0 copy-done.2
  19.6 2.0 %collective-permute-start.7 = (f32[464,128]{1,0:T(8,128)S(1)}, f32[464,128]{1,0:T(8,128)S(1)}, u32[]{:S(2)}, u32[]{:S(2)}) collective-permute-start(f32[464,128]{1,0:T(8,128)S(1)} %copy-done.2), channel_id=1, source_target_pairs={{0,4},{4,0},{8,12},{12,8},{16,20},{20,16},{24,28},{28,24},{1,5},{5... | collective-permute-start | bytes 712712 | tf_op jit(solution)/shard_map/ppermute | solution.py:1009
  21.6 0.0 collective-permute-done.2.mate2_msg
  21.6 0.0 collective-permute-done.3.other2_msg
  21.6 0.0 collective-permute-done.mate_msg
  21.6 0.0 collective-permute-done.1.other_msg
  21.6 0.6 %shard_map.58 = (f32[472,128]{1,0:T(8,128)S(1)}, f32[480,128]{1,0:T(8,128)S(1)}) custom-call(f32[1440,128]{1,0:T(8,128)S(1)} %shard_map.57.own_outer, f32[2704,128]{1,0:T(8,128)S(1)} %copy-done, f32[460,128]{1,0:T(8,128)S(1)} %collective-permute-done.mate_msg, f32[460,128]{1,0:T(8,128)S(1)} %collective-permute-done.1.other_msg, ...), custom_call_target="tpu_custom_call" | custom-call | flops 10000000000 | tf_op jit(solution)/shard_map/pallas_call | solution.py:961
  22.2 0.7 %collective-permute-start.6 = (f32[480,128]{1,0:T(8,128)S(1)}, f32[480,128]{1,0:T(8,128)S(1)}, u32[]{:S(2)}, u32[]{:S(2)}) collective-permute-start(f32[480,128]{1,0:T(8,128)S(1)} %get-tuple-element.28), channel_id=1, source_target_pairs={{0,0},{1,2},{2,1},{3,3},{4,4},{5,6},{6,5},{7,7},{8,8},{9,10},{10,9... | collective-permute-start | bytes 737288 | tf_op jit(solution)/shard_map/ppermute | solution.py:947
  22.9 3.0 %collective-permute-start.5 = (f32[472,128]{1,0:T(8,128)S(1)}, f32[472,128]{1,0:T(8,128)S(1)}, u32[]{:S(2)}, u32[]{:S(2)}) collective-permute-start(f32[472,128]{1,0:T(8,128)S(1)} %get-tuple-element.27), channel_id=1, source_target_pairs={{0,1},{1,0},{2,3},{3,2},{4,5},{5,4},{6,7},{7,6},{8,9},{9,8},{10,11... | collective-permute-start | bytes 725000 | tf_op jit(solution)/shard_map/ppermute | solution.py:947
  25.9 0.6 %collective-permute-done.7.mate_rest = f32[464,128]{1,0:T(8,128)S(1)} collective-permute-done((f32[464,128]{1,0:T(8,128)S(1)}, f32[464,128]{1,0:T(8,128)S(1)}, u32[]{:S(2)}, u32[]{:S(2)}) %collective-permute-start.7) | collective-permute-done | bytes 237600 | tf_op jit(solution)/shard_map/ppermute | solution.py:1009
  26.5 1.2 %collective-permute-start.8 = (f32[328,128]{1,0:T(8,128)S(1)}, f32[328,128]{1,0:T(8,128)S(1)}, u32[]{:S(2)}, u32[]{:S(2)}) collective-permute-start(f32[328,128]{1,0:T(8,128)S(1)} %slice.4), channel_id=1, source_target_pairs={{0,8},{4,0},{8,16},{12,4},{16,24},{20,12},{24,28},{28,20},{1,9},{5... | collective-permute-start | bytes 503816 | tf_op jit(solution)/shard_map/ppermute | solution.py:1012
  27.7 0.9 %collective-permute-start.9 = (f32[136,128]{1,0:T(8,128)S(1)}, f32[136,128]{1,0:T(8,128)S(1)}, u32[]{:S(2)}, u32[]{:S(2)}) collective-permute-start(f32[136,128]{1,0:T(8,128)S(1)} %collective-permute-done.4.along_z), channel_id=1, source_target_pairs={{0,4},{4,0},{8,12},{12,8},{16,20},{20,16},{24,28},{28,24},{1,5},{5... | collective-permute-start | bytes 208904 | tf_op jit(solution)/shard_map/ppermute | solution.py:1015
  28.6 0.6 %shard_map.56 = (f32[3792,128]{1,0:T(8,128)S(1)}, s32[24,128]{1,0:T(8,128)S(1)}) custom-call(f32[2704,128]{1,0:T(8,128)S(1)} %copy-done, f32[460,128]{1,0:T(8,128)S(1)} %collective-permute-done.mate_msg, f32[460,128]{1,0:T(8,128)S(1)} %collective-permute-done.1.other_msg, f32[144,128]{1,0:T(8,128)S(1)} %collective-permute-done.2.mate2_msg, ...), custom_call_target="tpu_custom_call" | custom-call | tf_op jit(solution)/shard_map/pallas_call | solution.py:961
  29.2 0.0 copy-start.1
  29.3 0.0 collective-permute-done.5.near_msg
  29.3 0.0 collective-permute-done.6.far_msg
  29.3 2.3 %shard_map.59 = (s32[72,128]{1,0:T(8,128)S(1)}, f32[1896,128]{1,0:T(8,128)S(1)}, f32[1896,128]{1,0:T(8,128)S(1)}) custom-call(s32[24,128]{1,0:T(8,128)S(1)} %get-tuple-element.24.own_slots, f32[3792,128]{1,0:T(8,128)S(1)} %get-tuple-element.25.first_post, f32[472,128]{1,0:T(8,128)S(1)} %collective-permute-done.5.near_msg, ...), custom_call_target="tpu_custom_call" | custom-call | tf_op jit(solution)/shard_map/pallas_call | solution.py:961
  31.5 2.1 %collective-permute-done.9.passed2_rest = f32[136,128]{1,0:T(8,128)S(1)} collective-permute-done((f32[136,128]{1,0:T(8,128)S(1)}, f32[136,128]{1,0:T(8,128)S(1)}, u32[]{:S(2)}, u32[]{:S(2)}) %collective-permute-start.9) | collective-permute-done | bytes 69664 | tf_op jit(solution)/shard_map/ppermute | solution.py:1015
  33.7 0.0 collective-permute-done.8.passed_rest
  33.7 0.0 copy-done.1
  33.7 6.0 %shard_map.60 = f32[3,19,4096]{2,1,0:T(8,128)} custom-call(s32[72,128]{1,0:T(8,128)S(1)} %get-tuple-element.29.slots, f32[3792,128]{1,0:T(8,128)S(1)} %get-tuple-element.25.first_post, f32[1896,128]{1,0:T(8,128)S(1)} %get-tuple-element.30.first_outer, f32[1896,128]{1,0:T(8,128)S(1)} %get-tuple-element.31.next_outer, f32[2704,128]{1,0:T(8,128)S(1)} %copy-done.1, ...), custom_call_target="tpu_custom_call" | custom-call | tf_op jit(solution)/shard_map/pallas_call | solution.py:961
  (1 shorter events, 0.0 us)
Async XLA Ops:
  4.3 17.4 %collective-permute-start = (f32[460,128]{1,0:T(8,128)}, f32[460,128]{1,0:T(8,128)S(1)}, u32[]{:S(2)}, u32[]{:S(2)}) collective-permute-start(f32[460,128]{1,0:T(8,128)} %get-tuple-element.20), channel_id=1, source_target_pairs={{0,4},{4,0},{8,12},{12,8},{16,20},{20,16},{24,28},{28,24},{1,5},{5... | collective-permute-start | bytes 706568 | tf_op jit(solution)/shard_map/ppermute | solution.py:947
  7.3 14.3 %collective-permute-start.1 = (f32[460,128]{1,0:T(8,128)}, f32[460,128]{1,0:T(8,128)S(1)}, u32[]{:S(2)}, u32[]{:S(2)}) collective-permute-start(f32[460,128]{1,0:T(8,128)} %get-tuple-element.21), channel_id=1, source_target_pairs={{0,0},{4,8},{8,4},{12,16},{16,12},{20,24},{24,20},{28,28},{1,1},{5... | collective-permute-start | bytes 706568 | tf_op jit(solution)/shard_map/ppermute | solution.py:947
  8.9 12.7 %collective-permute-start.2 = (f32[144,128]{1,0:T(8,128)}, f32[144,128]{1,0:T(8,128)S(1)}, u32[]{:S(2)}, u32[]{:S(2)}) collective-permute-start(f32[144,128]{1,0:T(8,128)} %get-tuple-element.22), channel_id=1, source_target_pairs={{0,8},{4,12},{8,0},{12,4},{16,24},{20,28},{24,16},{28,20},{1,9},{5... | collective-permute-start | bytes 221192 | tf_op jit(solution)/shard_map/ppermute | solution.py:947
  10.8 10.8 %collective-permute-start.3 = (f32[144,128]{1,0:T(8,128)}, f32[144,128]{1,0:T(8,128)S(1)}, u32[]{:S(2)}, u32[]{:S(2)}) collective-permute-start(f32[144,128]{1,0:T(8,128)} %get-tuple-element.23), channel_id=1, source_target_pairs={{0,0},{4,4},{8,16},{12,20},{16,8},{20,12},{24,24},{28,28},{1,1},{5... | collective-permute-start | bytes 221192 | tf_op jit(solution)/shard_map/ppermute | solution.py:947
  12.4 7.2 %collective-permute-start.4 = (f32[136,128]{1,0:T(8,128)}, f32[136,128]{1,0:T(8,128)S(1)}, u32[]{:S(2)}, u32[]{:S(2)}) collective-permute-start(f32[136,128]{1,0:T(8,128)} %get-tuple-element.26), channel_id=1, source_target_pairs={{8,0},{0,4},{16,8},{4,12},{24,16},{12,20},{28,24},{20,28},{9,1},{1... | collective-permute-start | bytes 208904 | tf_op jit(solution)/shard_map/ppermute | solution.py:1014
  15.4 1.3 %copy-start = (f32[2704,128]{1,0:T(8,128)S(1)}, f32[2704,128]{1,0:T(8,128)}, u32[]{:S(2)}) copy-start(f32[2704,128]{1,0:T(8,128)} %get-tuple-element.19.cells) | copy-start | bytes 4153348
  16.7 2.8 %copy-start.2 = (f32[464,128]{1,0:T(8,128)S(1)}, f32[464,128]{1,0:T(8,128)}, u32[]{:S(2)}) copy-start(f32[464,128]{1,0:T(8,128)} %get-tuple-element.32) | copy-start | bytes 712708
  19.6 6.9 %collective-permute-start.7 = (f32[464,128]{1,0:T(8,128)S(1)}, f32[464,128]{1,0:T(8,128)S(1)}, u32[]{:S(2)}, u32[]{:S(2)}) collective-permute-start(f32[464,128]{1,0:T(8,128)S(1)} %copy-done.2), channel_id=1, source_target_pairs={{0,4},{4,0},{8,12},{12,8},{16,20},{20,16},{24,28},{28,24},{1,5},{5... | collective-permute-start | bytes 712712 | tf_op jit(solution)/shard_map/ppermute | solution.py:1009
  22.2 7.0 %collective-permute-start.6 = (f32[480,128]{1,0:T(8,128)S(1)}, f32[480,128]{1,0:T(8,128)S(1)}, u32[]{:S(2)}, u32[]{:S(2)}) collective-permute-start(f32[480,128]{1,0:T(8,128)S(1)} %get-tuple-element.28), channel_id=1, source_target_pairs={{0,0},{1,2},{2,1},{3,3},{4,4},{5,6},{6,5},{7,7},{8,8},{9,10},{10,9... | collective-permute-start | bytes 737288 | tf_op jit(solution)/shard_map/ppermute | solution.py:947
  22.9 6.4 %collective-permute-start.5 = (f32[472,128]{1,0:T(8,128)S(1)}, f32[472,128]{1,0:T(8,128)S(1)}, u32[]{:S(2)}, u32[]{:S(2)}) collective-permute-start(f32[472,128]{1,0:T(8,128)S(1)} %get-tuple-element.27), channel_id=1, source_target_pairs={{0,1},{1,0},{2,3},{3,2},{4,5},{5,4},{6,7},{7,6},{8,9},{9,8},{10,11... | collective-permute-start | bytes 725000 | tf_op jit(solution)/shard_map/ppermute | solution.py:947
  26.5 7.2 %collective-permute-start.8 = (f32[328,128]{1,0:T(8,128)S(1)}, f32[328,128]{1,0:T(8,128)S(1)}, u32[]{:S(2)}, u32[]{:S(2)}) collective-permute-start(f32[328,128]{1,0:T(8,128)S(1)} %slice.4), channel_id=1, source_target_pairs={{0,8},{4,0},{8,16},{12,4},{16,24},{20,12},{24,28},{28,20},{1,9},{5... | collective-permute-start | bytes 503816 | tf_op jit(solution)/shard_map/ppermute | solution.py:1012
  27.7 6.0 %collective-permute-start.9 = (f32[136,128]{1,0:T(8,128)S(1)}, f32[136,128]{1,0:T(8,128)S(1)}, u32[]{:S(2)}, u32[]{:S(2)}) collective-permute-start(f32[136,128]{1,0:T(8,128)S(1)} %collective-permute-done.4.along_z), channel_id=1, source_target_pairs={{0,4},{4,0},{8,12},{12,8},{16,20},{20,16},{24,28},{28,24},{1,5},{5... | collective-permute-start | bytes 208904 | tf_op jit(solution)/shard_map/ppermute | solution.py:1015
  29.2 4.4 %copy-start.1 = (f32[2704,128]{1,0:T(8,128)S(1)}, f32[2704,128]{1,0:T(8,128)}, u32[]{:S(2)}) copy-start(f32[2704,128]{1,0:T(8,128)} %get-tuple-element.19.cells) | copy-start | bytes 4153348

commit v14 on v11

--- a/solution.py
+++ b/solution.py
@@ -18,7 +18,8 @@
 GROUP = 24
 PLANE = 3 * GROUP
 SLOT = POPS * PLANE
-CELLS = PLANES * 32
+CELL = 40
+CELLS = PLANES * CELL
 LANDINGS = CELLS + 8
 OWN2 = LANDINGS + 8
 OUTWARD = SLOTS * 5 + SLOTS
@@ -190,7 +191,7 @@
         for y in range(2):
             piece = site_flags[pl.ds(128 * y + s, EDGE, stride=8), :]
             is_fluid = (piece == 1.0) & live
-            row = (FLAG0 + s) * 32 + y * EDGE
+            row = (FLAG0 + s) * CELL + y * EDGE
             cells[row : row + EDGE, :] = jnp.where(is_fluid, 1.0, 0.0)
 
     for s in range(SLOTS):
@@ -199,8 +200,8 @@
             for y in range(2):
                 tile = 2 * x + y
                 for p, size in ((0, 8), (8, 8), (16, 3)):
-                    row = (s * POPS + p) * 32 + y * EDGE + x
-                    cells[pl.ds(row, size, stride=32), :] = pops[
+                    row = (s * POPS + p) * CELL + y * EDGE + x
+                    cells[pl.ds(row, size, stride=CELL), :] = pops[
                         s, p : p + size, 128 * tile : 128 * tile + 128
                     ]
 
@@ -208,11 +209,11 @@
     def _(s):
         @pl.loop(0, 4, unroll=2)
         def _(c):
-            base = s * (POPS * 32) + c * 8
-            view = cells.at[aligned(base, (POPS - 1) * 32 + 8), :]
-            h = [view[p * 32 : p * 32 + 8, :] for p in range(POPS)]
+            base = s * (POPS * CELL) + c * 8
+            view = cells.at[aligned(base, (POPS - 1) * CELL + 8), :]
+            h = [view[p * CELL : p * CELL + 8, :] for p in range(POPS)]
             for p, value in enumerate(collided(h)):
-                view[p * 32 : p * 32 + 8, :] = value
+                view[p * CELL : p * CELL + 8, :] = value
 
     for i, slot in enumerate(move_slots(moves, curve_size, cross_size)):
         value = jnp.full((1, 128), slot, jnp.int32)
@@ -226,18 +227,18 @@
             for k in range(2):
                 out = STRIPS + y * LAYERS + k * PLANES
                 msg[out : out + PLANES, :] = cells[
-                    pl.ds(y * EDGE + x0 + step * k, PLANES, stride=32), :
+                    pl.ds(y * EDGE + x0 + step * k, PLANES, stride=CELL), :
                 ]
             row = y * EDGE + x0 + 2 * step
             out = STRIPS + y * LAYERS + 2 * PLANES
             for s in range(SLOTS):
-                base = s * POPS * 32 + row
-                msg[out + 5 * s : out + 5 * s + 1, :] = cells[pl.ds(base + first * 32, 1), :]
+                base = s * POPS * CELL + row
+                msg[out + 5 * s : out + 5 * s + 1, :] = cells[pl.ds(base + first * CELL, 1), :]
                 msg[out + 5 * s + 1 : out + 5 * s + 5, :] = cells[
-                    pl.ds(base + (first + 6) * 32, 4, stride=64), :
+                    pl.ds(base + (first + 6) * CELL, 4, stride=2 * CELL), :
                 ]
             msg[out + 5 * SLOTS : out + OUTWARD, :] = cells[
-                pl.ds(FLAG0 * 32 + row, SLOTS, stride=32), :
+                pl.ds(FLAG0 * CELL + row, SLOTS, stride=CELL), :
             ]
 
     here = lax.axis_index("curve") * cross_size + lax.axis_index("cross")
@@ -245,7 +246,7 @@
     lane = lanes_iota()
     for v in range(2):
         halves = [
-            [cells[aligned(leaving * (POPS * 32) + p * 32 + y * EDGE + v * 8), :] for y in (0, 1)]
+            [cells[aligned(leaving * (POPS * CELL) + p * CELL + y * EDGE + v * 8), :] for y in (0, 1)]
             for p in range(POPS)
         ]
         outer = [jnp.where(lane < 64, first, second) for first, second in halves]
@@ -278,9 +279,9 @@
             for y in range(2):
                 for k in range(3):
                     out = (y * 3 + k) * GROUP
-                    row = s * POPS * 32 + y * EDGE + k
-                    up2_msg[out : out + POPS, :] = cells[pl.ds(row + 13, POPS, stride=32), :]
-                    down2_msg[out : out + POPS, :] = cells[pl.ds(row, POPS, stride=32), :]
+                    row = s * POPS * CELL + y * EDGE + k
+                    up2_msg[out : out + POPS, :] = cells[pl.ds(row + 13, POPS, stride=CELL), :]
+                    down2_msg[out : out + POPS, :] = cells[pl.ds(row, POPS, stride=CELL), :]
 
     cells[OWN2 : OWN2 + 6 * GROUP, :] = up2_msg[...]
     cells[OWN2 + 6 * GROUP :, :] = down2_msg[...]
@@ -313,7 +314,7 @@
     low = lanes_iota() < 64
     for q in range(PLANES):
         for v in range(2):
-            row = q * 32 + v * 8
+            row = q * CELL + v * 8
             first, second = cells[row : row + 8, :], cells[row + EDGE : row + EDGE + 8, :]
             row = q * GROUP + v * 8
             outer[row : row + 8, :] = jnp.where(low, first, second)
@@ -747,7 +748,7 @@
         for y in range(2):
             start = q * PAIR + y * GROUP
             post_ref[start : start + EDGE, :] = cells[
-                q * 32 + y * EDGE : q * 32 + (y + 1) * EDGE, :
+                q * CELL + y * EDGE : q * CELL + (y + 1) * EDGE, :
             ]
     for s, (slot, msg) in itertools.product(
         range(SLOTS), ((from_low, low_msg), (from_high, high_msg))

time: 38.4 us -> 37.8 us (0.984)
  Pallas kernels: 13.7 us -> 13.1 us
    pallas_call x6, Pallas kernels: 13.7 us -> 13.1 us  [call(): pl.pallas_call(kernel, out_shape=outs, in_specs=[spaces[x] for x in in_sp...]
where the time goes in v14:
time: 37.8 us; the launch traced here: 37.5 us
  starting transfers between devices  16.9 us (45%)
  Pallas kernels  13.1 us (35%)
  waiting for transfers between devices  5.42 us (14%)
  local copies, waits for them, and re-layouts  1.35 us (4%)
  between operations  0.72 us (2%)
    pallas_call x6, Pallas kernels, call(): pl.pallas_call(kernel, out_shape=outs, in_specs=[spaces[x] for x in in_sp...  13.1 us
    ppermute x6, starting transfers between devices, swapped(): results.append(lax.ppermute(value[which], axis, pairs))  11.8 us
    ppermute x1, waiting for transfers between devices, per_device(): passed_rest = lax.ppermute(mate_rest, 'curve', pairs)  3.33 us
    ppermute x1, starting transfers between devices, per_device(): mate_rest = lax.ppermute(rest_msg, 'curve', pairs)  3.03 us
    ppermute x1, starting transfers between devices, per_device(): passed_rest = lax.ppermute(mate_rest, 'curve', pairs)  2.12 us
    ppermute x6, waiting for transfers between devices, swapped(): results.append(lax.ppermute(value[which], axis, pairs))  2.09 us
    unnamed x4, local copies, waits for them, and re-layouts  1.35 us
  transfers between devices with their start and end apart: 8, of which 3 were waited for; matrix products, arithmetic and copies ran while one was open for 0% of the time, Pallas kernels for 9%

profile of v14, /device:TPU:0, one launch (start us, length us, event | category | flops | bytes accessed | tf_op | source)
XLA Modules:
  0.0 37.5 jit_solution(13026288646541385332)
XLA Ops:
  0.7 3.5 %shard_map.55 = (f32[2704,128]{1,0:T(8,128)}, f32[460,128]{1,0:T(8,128)}, f32[460,128]{1,0:T(8,128)}, f32[144,128]{1,0:T(8,128)}, f32[144,128]{1,0:T(8,128)}, /*index=5*/f32[464,128]{1,0:T(8,128)}) custom-call(s32[3,32]{1,0:T(4,128)} %bitcast.1, s32[1]{0:T(128)S(6)} %copy.6.counts_hbm, f32[3,19,4096]{2,1,0:T(8,128)} %pops_hbm.1, s32[3,5832]{1,0:T(4,128)} %flags_hbm.1, ...), custom_call_target="tpu_custom_call" | custom-call | tf_op jit(solution)/shard_map/pallas_call | solution.py:949
  4.2 3.0 %collective-permute-start = (f32[460,128]{1,0:T(8,128)}, f32[460,128]{1,0:T(8,128)S(1)}, u32[]{:S(2)}, u32[]{:S(2)}) collective-permute-start(f32[460,128]{1,0:T(8,128)} %get-tuple-element.19), channel_id=1, source_target_pairs={{0,4},{4,0},{8,12},{12,8},{16,20},{20,16},{24,28},{28,24},{1,5},{5... | collective-permute-start | bytes 706568 | tf_op jit(solution)/shard_map/ppermute | solution.py:935
  7.2 1.6 %collective-permute-start.1 = (f32[460,128]{1,0:T(8,128)}, f32[460,128]{1,0:T(8,128)S(1)}, u32[]{:S(2)}, u32[]{:S(2)}) collective-permute-start(f32[460,128]{1,0:T(8,128)} %get-tuple-element.20), channel_id=1, source_target_pairs={{0,0},{4,8},{8,4},{12,16},{16,12},{20,24},{24,20},{28,28},{1,1},{5... | collective-permute-start | bytes 706568 | tf_op jit(solution)/shard_map/ppermute | solution.py:935
  8.8 2.0 %collective-permute-start.2 = (f32[144,128]{1,0:T(8,128)}, f32[144,128]{1,0:T(8,128)S(1)}, u32[]{:S(2)}, u32[]{:S(2)}) collective-permute-start(f32[144,128]{1,0:T(8,128)} %get-tuple-element.21), channel_id=1, source_target_pairs={{0,8},{4,12},{8,0},{12,4},{16,24},{20,28},{24,16},{28,20},{1,9},{5... | collective-permute-start | bytes 221192 | tf_op jit(solution)/shard_map/ppermute | solution.py:935
  10.8 1.5 %collective-permute-start.3 = (f32[144,128]{1,0:T(8,128)}, f32[144,128]{1,0:T(8,128)S(1)}, u32[]{:S(2)}, u32[]{:S(2)}) collective-permute-start(f32[144,128]{1,0:T(8,128)} %get-tuple-element.22), channel_id=1, source_target_pairs={{0,0},{4,4},{8,16},{12,20},{16,8},{20,12},{24,24},{28,28},{1,1},{5... | collective-permute-start | bytes 221192 | tf_op jit(solution)/shard_map/ppermute | solution.py:935
  12.3 3.0 %collective-permute-start.6 = (f32[464,128]{1,0:T(8,128)}, f32[464,128]{1,0:T(8,128)S(1)}, u32[]{:S(2)}, u32[]{:S(2)}) collective-permute-start(f32[464,128]{1,0:T(8,128)} %get-tuple-element.30), channel_id=1, source_target_pairs={{0,4},{4,0},{8,12},{12,8},{16,20},{20,16},{24,28},{28,24},{1,5},{5... | collective-permute-start | bytes 712712 | tf_op jit(solution)/shard_map/ppermute | solution.py:997
  15.4 0.0 copy-start
  15.4 1.3 %copy-done = f32[2704,128]{1,0:T(8,128)S(1)} copy-done((f32[2704,128]{1,0:T(8,128)S(1)}, f32[2704,128]{1,0:T(8,128)}, u32[]{:S(2)}) %copy-start) | copy-done | bytes 1384472
  16.7 0.1 shard_map.57.own_outer
  16.8 1.3 %collective-permute-done.2.mate2_msg = f32[144,128]{1,0:T(8,128)S(1)} collective-permute-done((f32[144,128]{1,0:T(8,128)}, f32[144,128]{1,0:T(8,128)S(1)}, u32[]{:S(2)}, u32[]{:S(2)}) %collective-permute-start.2) | collective-permute-done | bytes 73760 | tf_op jit(solution)/shard_map/ppermute | solution.py:935
  18.0 0.0 collective-permute-done.3.other2_msg
  18.0 0.8 %collective-permute-done.mate_msg = f32[460,128]{1,0:T(8,128)S(1)} collective-permute-done((f32[460,128]{1,0:T(8,128)}, f32[460,128]{1,0:T(8,128)S(1)}, u32[]{:S(2)}, u32[]{:S(2)}) %collective-permute-start) | collective-permute-done | bytes 235552 | tf_op jit(solution)/shard_map/ppermute | solution.py:935
  18.8 0.0 collective-permute-done.1.other_msg
  18.8 0.6 %shard_map.58 = (f32[472,128]{1,0:T(8,128)S(1)}, f32[480,128]{1,0:T(8,128)S(1)}) custom-call(f32[1440,128]{1,0:T(8,128)S(1)} %shard_map.57.own_outer, f32[2704,128]{1,0:T(8,128)S(1)} %copy-done, f32[460,128]{1,0:T(8,128)S(1)} %collective-permute-done.mate_msg, f32[460,128]{1,0:T(8,128)S(1)} %collective-permute-done.1.other_msg, ...), custom_call_target="tpu_custom_call" | custom-call | flops 10000000000 | tf_op jit(solution)/shard_map/pallas_call | solution.py:949
  19.4 0.7 %collective-permute-start.5 = (f32[480,128]{1,0:T(8,128)S(1)}, f32[480,128]{1,0:T(8,128)S(1)}, u32[]{:S(2)}, u32[]{:S(2)}) collective-permute-start(f32[480,128]{1,0:T(8,128)S(1)} %get-tuple-element.26), channel_id=1, source_target_pairs={{0,0},{1,2},{2,1},{3,3},{4,4},{5,6},{6,5},{7,7},{8,8},{9,10},{10,9... | collective-permute-start | bytes 737288 | tf_op jit(solution)/shard_map/ppermute | solution.py:935
  20.1 3.0 %collective-permute-start.4 = (f32[472,128]{1,0:T(8,128)S(1)}, f32[472,128]{1,0:T(8,128)S(1)}, u32[]{:S(2)}, u32[]{:S(2)}) collective-permute-start(f32[472,128]{1,0:T(8,128)S(1)} %get-tuple-element.25), channel_id=1, source_target_pairs={{0,1},{1,0},{2,3},{3,2},{4,5},{5,4},{6,7},{7,6},{8,9},{9,8},{10,11... | collective-permute-start | bytes 725000 | tf_op jit(solution)/shard_map/ppermute | solution.py:935
  23.1 0.0 collective-permute-done.6.mate_rest
  23.1 2.1 %collective-permute-start.7 = (f32[464,128]{1,0:T(8,128)S(1)}, f32[464,128]{1,0:T(8,128)S(1)}, u32[]{:S(2)}, u32[]{:S(2)}) collective-permute-start(f32[464,128]{1,0:T(8,128)S(1)} %collective-permute-done.6.mate_rest), channel_id=1, source_target_pairs={{0,8},{4,0},{8,16},{12,4},{16,24},{20,12},{24,28},{28,20},{1,9},{5... | collective-permute-start | bytes 712712 | tf_op jit(solution)/shard_map/ppermute | solution.py:1000
  25.2 0.6 %shard_map.56 = (f32[3792,128]{1,0:T(8,128)S(1)}, s32[24,128]{1,0:T(8,128)S(1)}) custom-call(f32[2704,128]{1,0:T(8,128)S(1)} %copy-done, f32[460,128]{1,0:T(8,128)S(1)} %collective-permute-done.mate_msg, f32[460,128]{1,0:T(8,128)S(1)} %collective-permute-done.1.other_msg, f32[144,128]{1,0:T(8,128)S(1)} %collective-permute-done.2.mate2_msg, ...), custom_call_target="tpu_custom_call" | custom-call | tf_op jit(solution)/shard_map/pallas_call | solution.py:949
  25.9 0.0 copy-start.1
  25.9 0.0 collective-permute-done.4.near_msg
  25.9 0.0 collective-permute-done.5.far_msg
  25.9 2.3 %shard_map.59 = (s32[72,128]{1,0:T(8,128)S(1)}, f32[1896,128]{1,0:T(8,128)S(1)}, f32[1896,128]{1,0:T(8,128)S(1)}) custom-call(s32[24,128]{1,0:T(8,128)S(1)} %get-tuple-element.23.own_slots, f32[3792,128]{1,0:T(8,128)S(1)} %get-tuple-element.24.first_post, f32[472,128]{1,0:T(8,128)S(1)} %collective-permute-done.4.near_msg, ...), custom_call_target="tpu_custom_call" | custom-call | tf_op jit(solution)/shard_map/pallas_call | solution.py:949
  28.2 3.3 %collective-permute-done.7.passed_rest = f32[464,128]{1,0:T(8,128)S(1)} collective-permute-done((f32[464,128]{1,0:T(8,128)S(1)}, f32[464,128]{1,0:T(8,128)S(1)}, u32[]{:S(2)}, u32[]{:S(2)}) %collective-permute-start.7) | collective-permute-done | bytes 237600 | tf_op jit(solution)/shard_map/ppermute | solution.py:1000
  31.5 0.0 copy-done.1
  31.5 6.0 %shard_map.60 = f32[3,19,4096]{2,1,0:T(8,128)} custom-call(s32[72,128]{1,0:T(8,128)S(1)} %get-tuple-element.27.slots, f32[3792,128]{1,0:T(8,128)S(1)} %get-tuple-element.24.first_post, f32[1896,128]{1,0:T(8,128)S(1)} %get-tuple-element.28.first_outer, f32[1896,128]{1,0:T(8,128)S(1)} %get-tuple-element.29.next_outer, f32[2704,128]{1,0:T(8,128)S(1)} %copy-done.1, ...), custom_call_target="tpu_custom_call" | custom-call | tf_op jit(solution)/shard_map/pallas_call | solution.py:949
Async XLA Ops:
  4.2 14.6 %collective-permute-start = (f32[460,128]{1,0:T(8,128)}, f32[460,128]{1,0:T(8,128)S(1)}, u32[]{:S(2)}, u32[]{:S(2)}) collective-permute-start(f32[460,128]{1,0:T(8,128)} %get-tuple-element.19), channel_id=1, source_target_pairs={{0,4},{4,0},{8,12},{12,8},{16,20},{20,16},{24,28},{28,24},{1,5},{5... | collective-permute-start | bytes 706568 | tf_op jit(solution)/shard_map/ppermute | solution.py:935
  7.2 11.6 %collective-permute-start.1 = (f32[460,128]{1,0:T(8,128)}, f32[460,128]{1,0:T(8,128)S(1)}, u32[]{:S(2)}, u32[]{:S(2)}) collective-permute-start(f32[460,128]{1,0:T(8,128)} %get-tuple-element.20), channel_id=1, source_target_pairs={{0,0},{4,8},{8,4},{12,16},{16,12},{20,24},{24,20},{28,28},{1,1},{5... | collective-permute-start | bytes 706568 | tf_op jit(solution)/shard_map/ppermute | solution.py:935
  8.8 9.2 %collective-permute-start.2 = (f32[144,128]{1,0:T(8,128)}, f32[144,128]{1,0:T(8,128)S(1)}, u32[]{:S(2)}, u32[]{:S(2)}) collective-permute-start(f32[144,128]{1,0:T(8,128)} %get-tuple-element.21), channel_id=1, source_target_pairs={{0,8},{4,12},{8,0},{12,4},{16,24},{20,28},{24,16},{28,20},{1,9},{5... | collective-permute-start | bytes 221192 | tf_op jit(solution)/shard_map/ppermute | solution.py:935
  10.8 7.2 %collective-permute-start.3 = (f32[144,128]{1,0:T(8,128)}, f32[144,128]{1,0:T(8,128)S(1)}, u32[]{:S(2)}, u32[]{:S(2)}) collective-permute-start(f32[144,128]{1,0:T(8,128)} %get-tuple-element.22), channel_id=1, source_target_pairs={{0,0},{4,4},{8,16},{12,20},{16,8},{20,12},{24,24},{28,28},{1,1},{5... | collective-permute-start | bytes 221192 | tf_op jit(solution)/shard_map/ppermute | solution.py:935
  12.3 10.8 %collective-permute-start.6 = (f32[464,128]{1,0:T(8,128)}, f32[464,128]{1,0:T(8,128)S(1)}, u32[]{:S(2)}, u32[]{:S(2)}) collective-permute-start(f32[464,128]{1,0:T(8,128)} %get-tuple-element.30), channel_id=1, source_target_pairs={{0,4},{4,0},{8,12},{12,8},{16,20},{20,16},{24,28},{28,24},{1,5},{5... | collective-permute-start | bytes 712712 | tf_op jit(solution)/shard_map/ppermute | solution.py:997
  15.4 1.3 %copy-start = (f32[2704,128]{1,0:T(8,128)S(1)}, f32[2704,128]{1,0:T(8,128)}, u32[]{:S(2)}) copy-start(f32[2704,128]{1,0:T(8,128)} %get-tuple-element.18.cells) | copy-start | bytes 4153348
  19.4 6.5 %collective-permute-start.5 = (f32[480,128]{1,0:T(8,128)S(1)}, f32[480,128]{1,0:T(8,128)S(1)}, u32[]{:S(2)}, u32[]{:S(2)}) collective-permute-start(f32[480,128]{1,0:T(8,128)S(1)} %get-tuple-element.26), channel_id=1, source_target_pairs={{0,0},{1,2},{2,1},{3,3},{4,4},{5,6},{6,5},{7,7},{8,8},{9,10},{10,9... | collective-permute-start | bytes 737288 | tf_op jit(solution)/shard_map/ppermute | solution.py:935
  20.1 5.8 %collective-permute-start.4 = (f32[472,128]{1,0:T(8,128)S(1)}, f32[472,128]{1,0:T(8,128)S(1)}, u32[]{:S(2)}, u32[]{:S(2)}) collective-permute-start(f32[472,128]{1,0:T(8,128)S(1)} %get-tuple-element.25), channel_id=1, source_target_pairs={{0,1},{1,0},{2,3},{3,2},{4,5},{5,4},{6,7},{7,6},{8,9},{9,8},{10,11... | collective-permute-start | bytes 725000 | tf_op jit(solution)/shard_map/ppermute | solution.py:935
  23.1 8.4 %collective-permute-start.7 = (f32[464,128]{1,0:T(8,128)S(1)}, f32[464,128]{1,0:T(8,128)S(1)}, u32[]{:S(2)}, u32[]{:S(2)}) collective-permute-start(f32[464,128]{1,0:T(8,128)S(1)} %collective-permute-done.6.mate_rest), channel_id=1, source_target_pairs={{0,8},{4,0},{8,16},{12,4},{16,24},{20,12},{24,28},{28,20},{1,9},{5... | collective-permute-start | bytes 712712 | tf_op jit(solution)/shard_map/ppermute | solution.py:1000
  25.9 5.6 %copy-start.1 = (f32[2704,128]{1,0:T(8,128)S(1)}, f32[2704,128]{1,0:T(8,128)}, u32[]{:S(2)}) copy-start(f32[2704,128]{1,0:T(8,128)} %get-tuple-element.18.cells) | copy-start | bytes 4153348

commit v15 on v13

--- a/solution.py
+++ b/solution.py
@@ -26,7 +26,9 @@
 LAYERS = 2 * PLANES + OUTWARD
 RIM = 11 * EDGE
 REST = POPS * EDGE + 10 * EDGE
-HALF = REST - 136
+ALONG_Z = 128
+HALF = REST - ALONG_Z
+SECOND = 6 * GROUP + ALONG_Z
 PAIR = 2 * GROUP
 QUADS = PLANES // 4
 TABLE = RIM
@@ -125,7 +127,6 @@
     mate2_hbm,
     other2_hbm,
     rest_hbm,
-    rest2_hbm,
     moves,
     counts,
     pops,
@@ -285,10 +286,11 @@
                     up2_msg[out : out + POPS, :] = cells[pl.ds(row + 13, POPS, stride=CELL), :]
                     down2_msg[out : out + POPS, :] = cells[pl.ds(row, POPS, stride=CELL), :]
 
-    cells[OWN2 : OWN2 + 6 * GROUP, :] = up2_msg[...]
-    cells[OWN2 + 6 * GROUP :, :] = down2_msg[...]
+    cells[OWN2 : OWN2 + 6 * GROUP, :] = up2_msg[: 6 * GROUP, :]
+    cells[OWN2 + 6 * GROUP :, :] = down2_msg[: 6 * GROUP, :]
+    for msg in (up2_msg, down2_msg):
+        msg[6 * GROUP :, :] = rest_msg[HALF:, :]
     last = [copy(cells.at[OWN2:], cells_hbm.at[OWN2:]), copy(rest_msg, rest_hbm)]
-    last.append(copy(rest_msg.at[HALF:], rest2_hbm))
     count = len(started)
     for i, (up, down, mate, other, unit) in enumerate(
         ((up_msg, down_msg, mate_hbm, other_hbm, 1), (up2_msg, down2_msg, mate2_hbm, other2_hbm, 2))
@@ -391,9 +393,9 @@
     other_msg,
     mate2_msg,
     other2_msg,
-    along_z,
     near_msg,
     far_msg,
+    turn_msg,
     outer,
     low_msg,
     high_msg,
@@ -452,6 +454,12 @@
                         msg[k * GROUP : k * GROUP + POPS, :],
                         msg[(3 + k) * GROUP : (3 + k) * GROUP + POPS, :],
                     )
+
+    from_above = is_even("curve")
+    for row in range(0, ALONG_Z, 8):
+        tail = slice(6 * GROUP + row, 6 * GROUP + row + 8)
+        value = jnp.where(from_above, high2_msg[tail, :], low2_msg[tail, :])
+        turn_msg[row : row + 8, :] = value
 
     even = is_even("cross")
 
@@ -977,15 +985,15 @@
         OWN2 + 12 * GROUP,
         STRIPS + 2 * LAYERS,
         STRIPS + 2 * LAYERS,
-        6 * GROUP,
-        6 * GROUP,
+        SECOND,
+        SECOND,
         REST,
     ]
-    cells, mate_msg, other_msg, mate2_msg, other2_msg, rest_msg, rest2_msg = call(
+    cells, mate_msg, other_msg, mate2_msg, other2_msg, rest_msg = call(
         functools.partial(pack_kernel, *sizes),
         "HHHHH",
-        "HHHHHHH",
-        [rows128(rows) for rows in (*messages, REST - HALF)],
+        "HHHHHH",
+        [rows128(rows) for rows in messages],
         (moves, counts, populations, site_flags, neighbours),
         [
             pltpu.SMEM(moves.shape, jnp.int32),
@@ -998,7 +1006,7 @@
             pltpu.VMEM((128, 384), jnp.bfloat16),
             floats(256),
             floats(8),
-            pltpu.SemaphoreType.DMA((4 + SLOTS + 9,)),
+            pltpu.SemaphoreType.DMA((4 + SLOTS + 8,)),
         ],
         WIDE_LIMIT,
     )
@@ -1010,22 +1018,21 @@
     last = sizes[0] - 1
     pairs = [(i, max(i - 2, 0) if i % 2 else min(i + 2, last)) for i in range(sizes[0])]
     passed_rest = lax.ppermute(mate_rest[:HALF], "curve", pairs)
-    back = [(target, source) for source, target in pairs]
-    along_z = lax.ppermute(rest2_msg, "curve", back)
-    passed2_rest = lax.ppermute(along_z, "curve", [(i, i ^ 1) for i in range(last + 1)])
     (outer,) = call(spread_kernel, "V", "V", [rows128(PLANES * GROUP)], (cells,), [])
     strips = (cells, mate_msg, other_msg, mate2_msg, other2_msg)
     sorted_rows = [messages[1], messages[1], messages[3], messages[3]]
-    near_msg, far_msg = call(
+    near_msg, far_msg, turn_msg = call(
         edge_kernel,
-        "VVVVVVV",
-        "VV",
-        [rows128(NEAR_ROWS), rows128(FAR_ROWS)],
-        (outer, *strips, along_z),
+        "VVVVVV",
+        "VVV",
+        [rows128(NEAR_ROWS), rows128(FAR_ROWS), rows128(ALONG_Z)],
+        (outer, *strips),
         [floats(rows) for rows in [PLANES * GROUP] + sorted_rows],
         cost=pl.CostEstimate(flops=10**10, bytes_accessed=0, transcendentals=0),
     )
     near_msg, far_msg = swapped((near_msg, far_msg), "cross")
+    pairs = [(i, i ^ 1) for i in range(sizes[0])]
+    passed2_rest = lax.ppermute(turn_msg, "curve", pairs)
     post, own_slots = call(
         join_kernel,
         "VVVVV",

time: 39.9 us -> 37.9 us (0.950)
  starting transfers between devices: 18.9 us -> 16.9 us
    ppermute x2 -> x1, starting transfers between devices: 3.94 us -> 0.47 us  [per_device(): passed2_rest = lax.ppermute(turn_msg, 'curve', pairs)]
    ppermute x6, waiting for transfers between devices: 0.02 us -> 2.68 us  [swapped(): results.append(lax.ppermute(value[which], axis, pairs))]
    ppermute x2 -> x1, waiting for transfers between devices: 4.9 us -> 2.73 us  [per_device(): passed2_rest = lax.ppermute(turn_msg, 'curve', pairs)]
    ppermute x1, starting transfers between devices: 2.02 us -> 3.03 us  [per_device(): mate_rest = lax.ppermute(rest_msg, 'curve', pairs)]
    ppermute x1, waiting for transfers between devices: 0.61 us -> 0.01 us  [per_device(): mate_rest = lax.ppermute(rest_msg, 'curve', pairs)]
    ppermute x1, starting transfers between devices: 1.17 us -> 1.61 us  [per_device(): passed_rest = lax.ppermute(mate_rest[:HALF], 'curve', pairs)]
    unnamed x6 -> x4, local copies, waits for them, and re-layouts: 1.35 us -> 1.35 us
  transfers between devices with their start and end apart: 10 -> 9, of which waited for: 3 -> 2; matrix products, arithmetic and copies ran while one was open for 0% -> 0% of each run, Pallas kernels for 9% -> 9%
where the time goes in v15:
time: 37.9 us; the launch traced here: 37.6 us
  starting transfers between devices  16.9 us (45%)
  Pallas kernels  13.2 us (35%)
  waiting for transfers between devices  5.42 us (14%)
  local copies, waits for them, and re-layouts  1.36 us (4%)
  between operations  0.73 us (2%)
    pallas_call x6, Pallas kernels, call(): pl.pallas_call(kernel, out_shape=outs, in_specs=[spaces[x] for x in in_sp...  13.2 us
    ppermute x6, starting transfers between devices, swapped(): results.append(lax.ppermute(value[which], axis, pairs))  11.8 us
    ppermute x1, starting transfers between devices, per_device(): mate_rest = lax.ppermute(rest_msg, 'curve', pairs)  3.03 us
    ppermute x1, waiting for transfers between devices, per_device(): passed2_rest = lax.ppermute(turn_msg, 'curve', pairs)  2.73 us
    ppermute x6, waiting for transfers between devices, swapped(): results.append(lax.ppermute(value[which], axis, pairs))  2.68 us
    ppermute x1, starting transfers between devices, per_device(): passed_rest = lax.ppermute(mate_rest[:HALF], 'curve', pairs)  1.61 us
    unnamed x4, local copies, waits for them, and re-layouts  1.35 us
  transfers between devices with their start and end apart: 9, of which 2 were waited for; matrix products, arithmetic and copies ran while one was open for 0% of the time, Pallas kernels for 9%

profile of v15, /device:TPU:0, one launch (start us, length us, event | category | flops | bytes accessed | tf_op | source)
XLA Modules:
  0.0 37.6 jit_solution(4425949968309001747)
XLA Ops:
  0.7 3.6 %shard_map.55 = (f32[2704,128]{1,0:T(8,128)}, f32[460,128]{1,0:T(8,128)}, f32[460,128]{1,0:T(8,128)}, f32[272,128]{1,0:T(8,128)}, f32[272,128]{1,0:T(8,128)}, /*index=5*/f32[464,128]{1,0:T(8,128)}) custom-call(s32[3,32]{1,0:T(4,128)} %bitcast.1, s32[1]{0:T(128)S(6)} %copy.6.counts_hbm, f32[3,19,4096]{2,1,0:T(8,128)} %pops_hbm.1, s32[3,5832]{1,0:T(4,128)} %flags_hbm.1, ...), custom_call_target="tpu_custom_call" | custom-call | tf_op jit(solution)/shard_map/pallas_call | solution.py:969
  4.3 3.0 %collective-permute-start = (f32[460,128]{1,0:T(8,128)}, f32[460,128]{1,0:T(8,128)S(1)}, u32[]{:S(2)}, u32[]{:S(2)}) collective-permute-start(f32[460,128]{1,0:T(8,128)} %get-tuple-element.20), channel_id=1, source_target_pairs={{0,4},{4,0},{8,12},{12,8},{16,20},{20,16},{24,28},{28,24},{1,5},{5... | collective-permute-start | bytes 706568 | tf_op jit(solution)/shard_map/ppermute | solution.py:955
  7.3 1.6 %collective-permute-start.1 = (f32[460,128]{1,0:T(8,128)}, f32[460,128]{1,0:T(8,128)S(1)}, u32[]{:S(2)}, u32[]{:S(2)}) collective-permute-start(f32[460,128]{1,0:T(8,128)} %get-tuple-element.21), channel_id=1, source_target_pairs={{0,0},{4,8},{8,4},{12,16},{16,12},{20,24},{24,20},{28,28},{1,1},{5... | collective-permute-start | bytes 706568 | tf_op jit(solution)/shard_map/ppermute | solution.py:955
  8.9 2.0 %collective-permute-start.2 = (f32[272,128]{1,0:T(8,128)}, f32[272,128]{1,0:T(8,128)S(1)}, u32[]{:S(2)}, u32[]{:S(2)}) collective-permute-start(f32[272,128]{1,0:T(8,128)} %get-tuple-element.22), channel_id=1, source_target_pairs={{0,8},{4,12},{8,0},{12,4},{16,24},{20,28},{24,16},{28,20},{1,9},{5... | collective-permute-start | bytes 417800 | tf_op jit(solution)/shard_map/ppermute | solution.py:955
  10.9 1.6 %collective-permute-start.3 = (f32[272,128]{1,0:T(8,128)}, f32[272,128]{1,0:T(8,128)S(1)}, u32[]{:S(2)}, u32[]{:S(2)}) collective-permute-start(f32[272,128]{1,0:T(8,128)} %get-tuple-element.23), channel_id=1, source_target_pairs={{0,0},{4,4},{8,16},{12,20},{16,8},{20,12},{24,24},{28,28},{1,1},{5... | collective-permute-start | bytes 417800 | tf_op jit(solution)/shard_map/ppermute | solution.py:955
  12.4 3.0 %collective-permute-start.6 = (f32[464,128]{1,0:T(8,128)}, f32[464,128]{1,0:T(8,128)S(1)}, u32[]{:S(2)}, u32[]{:S(2)}) collective-permute-start(f32[464,128]{1,0:T(8,128)} %get-tuple-element.31), channel_id=1, source_target_pairs={{0,4},{4,0},{8,12},{12,8},{16,20},{20,16},{24,28},{28,24},{1,5},{5... | collective-permute-start | bytes 712712 | tf_op jit(solution)/shard_map/ppermute | solution.py:1017
  15.4 0.0 copy-start
  15.4 1.3 %copy-done = f32[2704,128]{1,0:T(8,128)S(1)} copy-done((f32[2704,128]{1,0:T(8,128)S(1)}, f32[2704,128]{1,0:T(8,128)}, u32[]{:S(2)}) %copy-start) | copy-done | bytes 1384472
  16.8 0.1 shard_map.57.own_outer
  16.8 2.7 %collective-permute-done.2.mate2_msg = f32[272,128]{1,0:T(8,128)S(1)} collective-permute-done((f32[272,128]{1,0:T(8,128)}, f32[272,128]{1,0:T(8,128)S(1)}, u32[]{:S(2)}, u32[]{:S(2)}) %collective-permute-start.2) | collective-permute-done | bytes 139296 | tf_op jit(solution)/shard_map/ppermute | solution.py:955
  19.5 0.0 collective-permute-done.3.other2_msg
  19.5 0.0 collective-permute-done.mate_msg
  19.5 0.0 collective-permute-done.1.other_msg
  19.5 0.6 %shard_map.58 = (f32[472,128]{1,0:T(8,128)S(1)}, f32[480,128]{1,0:T(8,128)S(1)}, f32[128,128]{1,0:T(8,128)S(1)}) custom-call(f32[1440,128]{1,0:T(8,128)S(1)} %shard_map.57.own_outer, f32[2704,128]{1,0:T(8,128)S(1)} %copy-done, f32[460,128]{1,0:T(8,128)S(1)} %collective-permute-done.mate_msg, f32[460,128]{1,0:T(8,128)S(1)} %collective-permute-done.1.other_msg, ...), custom_call_target="tpu_custom_call" | custom-call | flops 10000000000 | tf_op jit(solution)/shard_map/pallas_call | solution.py:969
  20.1 0.7 %collective-permute-start.5 = (f32[480,128]{1,0:T(8,128)S(1)}, f32[480,128]{1,0:T(8,128)S(1)}, u32[]{:S(2)}, u32[]{:S(2)}) collective-permute-start(f32[480,128]{1,0:T(8,128)S(1)} %get-tuple-element.27), channel_id=1, source_target_pairs={{0,0},{1,2},{2,1},{3,3},{4,4},{5,6},{6,5},{7,7},{8,8},{9,10},{10,9... | collective-permute-start | bytes 737288 | tf_op jit(solution)/shard_map/ppermute | solution.py:955
  20.8 3.0 %collective-permute-start.4 = (f32[472,128]{1,0:T(8,128)S(1)}, f32[472,128]{1,0:T(8,128)S(1)}, u32[]{:S(2)}, u32[]{:S(2)}) collective-permute-start(f32[472,128]{1,0:T(8,128)S(1)} %get-tuple-element.26), channel_id=1, source_target_pairs={{0,1},{1,0},{2,3},{3,2},{4,5},{5,4},{6,7},{7,6},{8,9},{9,8},{10,11... | collective-permute-start | bytes 725000 | tf_op jit(solution)/shard_map/ppermute | solution.py:955
  23.8 0.0 collective-permute-done.6.mate_rest
  23.8 1.6 %collective-permute-start.7 = (f32[336,128]{1,0:T(8,128)S(1)}, f32[336,128]{1,0:T(8,128)S(1)}, u32[]{:S(2)}, u32[]{:S(2)}) collective-permute-start(f32[336,128]{1,0:T(8,128)S(1)} %slice.4), channel_id=1, source_target_pairs={{0,8},{4,0},{8,16},{12,4},{16,24},{20,12},{24,28},{28,20},{1,9},{5... | collective-permute-start | bytes 516104 | tf_op jit(solution)/shard_map/ppermute | solution.py:1020
  25.4 0.5 %collective-permute-start.8 = (f32[128,128]{1,0:T(8,128)S(1)}, f32[128,128]{1,0:T(8,128)S(1)}, u32[]{:S(2)}, u32[]{:S(2)}) collective-permute-start(f32[128,128]{1,0:T(8,128)S(1)} %get-tuple-element.32), channel_id=1, source_target_pairs={{0,4},{4,0},{8,12},{12,8},{16,20},{20,16},{24,28},{28,24},{1,5},{5... | collective-permute-start | bytes 196616 | tf_op jit(solution)/shard_map/ppermute | solution.py:1035
  25.9 0.6 %shard_map.56 = (f32[3792,128]{1,0:T(8,128)S(1)}, s32[24,128]{1,0:T(8,128)S(1)}) custom-call(f32[2704,128]{1,0:T(8,128)S(1)} %copy-done, f32[460,128]{1,0:T(8,128)S(1)} %collective-permute-done.mate_msg, f32[460,128]{1,0:T(8,128)S(1)} %collective-permute-done.1.other_msg, f32[272,128]{1,0:T(8,128)S(1)} %collective-permute-done.2.mate2_msg, ...), custom_call_target="tpu_custom_call" | custom-call | tf_op jit(solution)/shard_map/pallas_call | solution.py:969
  26.5 0.0 copy-start.1
  26.5 0.0 collective-permute-done.4.near_msg
  26.6 0.0 collective-permute-done.5.far_msg
  26.6 2.3 %shard_map.59 = (s32[72,128]{1,0:T(8,128)S(1)}, f32[1896,128]{1,0:T(8,128)S(1)}, f32[1896,128]{1,0:T(8,128)S(1)}) custom-call(s32[24,128]{1,0:T(8,128)S(1)} %get-tuple-element.24.own_slots, f32[3792,128]{1,0:T(8,128)S(1)} %get-tuple-element.25.first_post, f32[472,128]{1,0:T(8,128)S(1)} %collective-permute-done.4.near_msg, ...), custom_call_target="tpu_custom_call" | custom-call | tf_op jit(solution)/shard_map/pallas_call | solution.py:969
  28.8 2.7 %collective-permute-done.8.passed2_rest = f32[128,128]{1,0:T(8,128)S(1)} collective-permute-done((f32[128,128]{1,0:T(8,128)S(1)}, f32[128,128]{1,0:T(8,128)S(1)}, u32[]{:S(2)}, u32[]{:S(2)}) %collective-permute-start.8) | collective-permute-done | bytes 65568 | tf_op jit(solution)/shard_map/ppermute | solution.py:1035
  31.6 0.0 collective-permute-done.7.passed_rest
  31.6 0.0 copy-done.1
  31.6 6.0 %shard_map.60 = f32[3,19,4096]{2,1,0:T(8,128)} custom-call(s32[72,128]{1,0:T(8,128)S(1)} %get-tuple-element.28.slots, f32[3792,128]{1,0:T(8,128)S(1)} %get-tuple-element.25.first_post, f32[1896,128]{1,0:T(8,128)S(1)} %get-tuple-element.29.first_outer, f32[1896,128]{1,0:T(8,128)S(1)} %get-tuple-element.30.next_outer, f32[2704,128]{1,0:T(8,128)S(1)} %copy-done.1, ...), custom_call_target="tpu_custom_call" | custom-call | tf_op jit(solution)/shard_map/pallas_call | solution.py:969
  (1 shorter events, 0.0 us)
Async XLA Ops:
  4.3 15.2 %collective-permute-start = (f32[460,128]{1,0:T(8,128)}, f32[460,128]{1,0:T(8,128)S(1)}, u32[]{:S(2)}, u32[]{:S(2)}) collective-permute-start(f32[460,128]{1,0:T(8,128)} %get-tuple-element.20), channel_id=1, source_target_pairs={{0,4},{4,0},{8,12},{12,8},{16,20},{20,16},{24,28},{28,24},{1,5},{5... | collective-permute-start | bytes 706568 | tf_op jit(solution)/shard_map/ppermute | solution.py:955
  7.3 12.2 %collective-permute-start.1 = (f32[460,128]{1,0:T(8,128)}, f32[460,128]{1,0:T(8,128)S(1)}, u32[]{:S(2)}, u32[]{:S(2)}) collective-permute-start(f32[460,128]{1,0:T(8,128)} %get-tuple-element.21), channel_id=1, source_target_pairs={{0,0},{4,8},{8,4},{12,16},{16,12},{20,24},{24,20},{28,28},{1,1},{5... | collective-permute-start | bytes 706568 | tf_op jit(solution)/shard_map/ppermute | solution.py:955
  8.9 10.6 %collective-permute-start.2 = (f32[272,128]{1,0:T(8,128)}, f32[272,128]{1,0:T(8,128)S(1)}, u32[]{:S(2)}, u32[]{:S(2)}) collective-permute-start(f32[272,128]{1,0:T(8,128)} %get-tuple-element.22), channel_id=1, source_target_pairs={{0,8},{4,12},{8,0},{12,4},{16,24},{20,28},{24,16},{28,20},{1,9},{5... | collective-permute-start | bytes 417800 | tf_op jit(solution)/shard_map/ppermute | solution.py:955
  10.9 8.6 %collective-permute-start.3 = (f32[272,128]{1,0:T(8,128)}, f32[272,128]{1,0:T(8,128)S(1)}, u32[]{:S(2)}, u32[]{:S(2)}) collective-permute-start(f32[272,128]{1,0:T(8,128)} %get-tuple-element.23), channel_id=1, source_target_pairs={{0,0},{4,4},{8,16},{12,20},{16,8},{20,12},{24,24},{28,28},{1,1},{5... | collective-permute-start | bytes 417800 | tf_op jit(solution)/shard_map/ppermute | solution.py:955
  12.4 11.4 %collective-permute-start.6 = (f32[464,128]{1,0:T(8,128)}, f32[464,128]{1,0:T(8,128)S(1)}, u32[]{:S(2)}, u32[]{:S(2)}) collective-permute-start(f32[464,128]{1,0:T(8,128)} %get-tuple-element.31), channel_id=1, source_target_pairs={{0,4},{4,0},{8,12},{12,8},{16,20},{20,16},{24,28},{28,24},{1,5},{5... | collective-permute-start | bytes 712712 | tf_op jit(solution)/shard_map/ppermute | solution.py:1017
  15.4 1.3 %copy-start = (f32[2704,128]{1,0:T(8,128)S(1)}, f32[2704,128]{1,0:T(8,128)}, u32[]{:S(2)}) copy-start(f32[2704,128]{1,0:T(8,128)} %get-tuple-element.19.cells) | copy-start | bytes 4153348
  20.1 6.5 %collective-permute-start.5 = (f32[480,128]{1,0:T(8,128)S(1)}, f32[480,128]{1,0:T(8,128)S(1)}, u32[]{:S(2)}, u32[]{:S(2)}) collective-permute-start(f32[480,128]{1,0:T(8,128)S(1)} %get-tuple-element.27), channel_id=1, source_target_pairs={{0,0},{1,2},{2,1},{3,3},{4,4},{5,6},{6,5},{7,7},{8,8},{9,10},{10,9... | collective-permute-start | bytes 737288 | tf_op jit(solution)/shard_map/ppermute | solution.py:955
  20.8 5.8 %collective-permute-start.4 = (f32[472,128]{1,0:T(8,128)S(1)}, f32[472,128]{1,0:T(8,128)S(1)}, u32[]{:S(2)}, u32[]{:S(2)}) collective-permute-start(f32[472,128]{1,0:T(8,128)S(1)} %get-tuple-element.26), channel_id=1, source_target_pairs={{0,1},{1,0},{2,3},{3,2},{4,5},{5,4},{6,7},{7,6},{8,9},{9,8},{10,11... | collective-permute-start | bytes 725000 | tf_op jit(solution)/shard_map/ppermute | solution.py:955
  23.8 7.8 %collective-permute-start.7 = (f32[336,128]{1,0:T(8,128)S(1)}, f32[336,128]{1,0:T(8,128)S(1)}, u32[]{:S(2)}, u32[]{:S(2)}) collective-permute-start(f32[336,128]{1,0:T(8,128)S(1)} %slice.4), channel_id=1, source_target_pairs={{0,8},{4,0},{8,16},{12,4},{16,24},{20,12},{24,28},{28,20},{1,9},{5... | collective-permute-start | bytes 516104 | tf_op jit(solution)/shard_map/ppermute | solution.py:1020
  25.4 6.2 %collective-permute-start.8 = (f32[128,128]{1,0:T(8,128)S(1)}, f32[128,128]{1,0:T(8,128)S(1)}, u32[]{:S(2)}, u32[]{:S(2)}) collective-permute-start(f32[128,128]{1,0:T(8,128)S(1)} %get-tuple-element.32), channel_id=1, source_target_pairs={{0,4},{4,0},{8,12},{12,8},{16,20},{20,16},{24,28},{28,24},{1,5},{5... | collective-permute-start | bytes 196616 | tf_op jit(solution)/shard_map/ppermute | solution.py:1035
  26.5 5.0 %copy-start.1 = (f32[2704,128]{1,0:T(8,128)S(1)}, f32[2704,128]{1,0:T(8,128)}, u32[]{:S(2)}) copy-start(f32[2704,128]{1,0:T(8,128)} %get-tuple-element.19.cells) | copy-start | bytes 4153348

commit v16 on v15

--- a/solution.py
+++ b/solution.py
@@ -1015,8 +1015,8 @@
     assert sizes[0] % 2 == 0
     pairs = [(i, i ^ 1) for i in range(sizes[0])]
     mate_rest = lax.ppermute(rest_msg, "curve", pairs)
-    last = sizes[0] - 1
-    pairs = [(i, max(i - 2, 0) if i % 2 else min(i + 2, last)) for i in range(sizes[0])]
+    pairs = [(i, i - 2 if i % 2 else i + 2) for i in range(sizes[0])]
+    pairs = [pair for pair in pairs if 0 <= pair[1] < sizes[0]]
     passed_rest = lax.ppermute(mate_rest[:HALF], "curve", pairs)
     (outer,) = call(spread_kernel, "V", "V", [rows128(PLANES * GROUP)], (cells,), [])
     strips = (cells, mate_msg, other_msg, mate2_msg, other2_msg)

time: 37.9 us -> 37.9 us (level)
  waiting for transfers between devices: 5.42 us -> 3.9 us
  starting transfers between devices: 16.9 us -> 18.3 us
    ppermute x1, starting transfers between devices: 1.61 us -> 3.39 us  [per_device(): passed_rest = lax.ppermute(mate_rest[:HALF], 'curve', pairs)]
    ppermute x1, waiting for transfers between devices: 2.73 us -> 1.21 us  [per_device(): passed2_rest = lax.ppermute(turn_msg, 'curve', pairs)]
    ppermute x1, starting transfers between devices: 0.47 us -> 0.07 us  [per_device(): passed2_rest = lax.ppermute(turn_msg, 'curve', pairs)]
  transfers between devices with their start and end apart: 9 -> 9, of which waited for: 2 -> 2; matrix products, arithmetic and copies ran while one was open for 0% -> 0% of each run, Pallas kernels for 9% -> 10%
where the time goes in v16:
time: 37.9 us; the launch traced here: 37.6 us
  starting transfers between devices  18.3 us (48%)
  Pallas kernels  13.3 us (35%)
  waiting for transfers between devices  3.9 us (10%)
  local copies, waits for them, and re-layouts  1.36 us (4%)
  between operations  0.75 us (2%)
    pallas_call x6, Pallas kernels, call(): pl.pallas_call(kernel, out_shape=outs, in_specs=[spaces[x] for x in in_sp...  13.3 us
    ppermute x6, starting transfers between devices, swapped(): results.append(lax.ppermute(value[which], axis, pairs))  11.8 us
    ppermute x1, starting transfers between devices, per_device(): passed_rest = lax.ppermute(mate_rest[:HALF], 'curve', pairs)  3.39 us
    ppermute x1, starting transfers between devices, per_device(): mate_rest = lax.ppermute(rest_msg, 'curve', pairs)  3.03 us
    ppermute x6, waiting for transfers between devices, swapped(): results.append(lax.ppermute(value[which], axis, pairs))  2.68 us
    unnamed x4, local copies, waits for them, and re-layouts  1.35 us
    ppermute x1, waiting for transfers between devices, per_device(): passed2_rest = lax.ppermute(turn_msg, 'curve', pairs)  1.21 us
  transfers between devices with their start and end apart: 9, of which 2 were waited for; matrix products, arithmetic and copies ran while one was open for 0% of the time, Pallas kernels for 10%

profile of v16, /device:TPU:0, one launch (start us, length us, event | category | flops | bytes accessed | tf_op | source)
XLA Modules:
  0.0 37.6 jit_solution(601539736875391489)
XLA Ops:
  0.7 3.6 %shard_map.55 = (f32[2704,128]{1,0:T(8,128)}, f32[460,128]{1,0:T(8,128)}, f32[460,128]{1,0:T(8,128)}, f32[272,128]{1,0:T(8,128)}, f32[272,128]{1,0:T(8,128)}, /*index=5*/f32[464,128]{1,0:T(8,128)}) custom-call(s32[3,32]{1,0:T(4,128)} %bitcast.1, s32[1]{0:T(128)S(6)} %copy.6.counts_hbm, f32[3,19,4096]{2,1,0:T(8,128)} %pops_hbm.1, s32[3,5832]{1,0:T(4,128)} %flags_hbm.1, ...), custom_call_target="tpu_custom_call" | custom-call | tf_op jit(solution)/shard_map/pallas_call | solution.py:969
  4.3 3.0 %collective-permute-start = (f32[460,128]{1,0:T(8,128)}, f32[460,128]{1,0:T(8,128)S(1)}, u32[]{:S(2)}, u32[]{:S(2)}) collective-permute-start(f32[460,128]{1,0:T(8,128)} %get-tuple-element.20), channel_id=1, source_target_pairs={{0,4},{4,0},{8,12},{12,8},{16,20},{20,16},{24,28},{28,24},{1,5},{5... | collective-permute-start | bytes 706568 | tf_op jit(solution)/shard_map/ppermute | solution.py:955
  7.3 1.6 %collective-permute-start.1 = (f32[460,128]{1,0:T(8,128)}, f32[460,128]{1,0:T(8,128)S(1)}, u32[]{:S(2)}, u32[]{:S(2)}) collective-permute-start(f32[460,128]{1,0:T(8,128)} %get-tuple-element.21), channel_id=1, source_target_pairs={{0,0},{4,8},{8,4},{12,16},{16,12},{20,24},{24,20},{28,28},{1,1},{5... | collective-permute-start | bytes 706568 | tf_op jit(solution)/shard_map/ppermute | solution.py:955
  8.9 2.0 %collective-permute-start.2 = (f32[272,128]{1,0:T(8,128)}, f32[272,128]{1,0:T(8,128)S(1)}, u32[]{:S(2)}, u32[]{:S(2)}) collective-permute-start(f32[272,128]{1,0:T(8,128)} %get-tuple-element.22), channel_id=1, source_target_pairs={{0,8},{4,12},{8,0},{12,4},{16,24},{20,28},{24,16},{28,20},{1,9},{5... | collective-permute-start | bytes 417800 | tf_op jit(solution)/shard_map/ppermute | solution.py:955
  10.9 1.6 %collective-permute-start.3 = (f32[272,128]{1,0:T(8,128)}, f32[272,128]{1,0:T(8,128)S(1)}, u32[]{:S(2)}, u32[]{:S(2)}) collective-permute-start(f32[272,128]{1,0:T(8,128)} %get-tuple-element.23), channel_id=1, source_target_pairs={{0,0},{4,4},{8,16},{12,20},{16,8},{20,12},{24,24},{28,28},{1,1},{5... | collective-permute-start | bytes 417800 | tf_op jit(solution)/shard_map/ppermute | solution.py:955
  12.4 3.0 %collective-permute-start.6 = (f32[464,128]{1,0:T(8,128)}, f32[464,128]{1,0:T(8,128)S(1)}, u32[]{:S(2)}, u32[]{:S(2)}) collective-permute-start(f32[464,128]{1,0:T(8,128)} %get-tuple-element.31), channel_id=1, source_target_pairs={{0,4},{4,0},{8,12},{12,8},{16,20},{20,16},{24,28},{28,24},{1,5},{5... | collective-permute-start | bytes 712712 | tf_op jit(solution)/shard_map/ppermute | solution.py:1017
  15.4 0.0 copy-start
  15.4 1.3 %copy-done = f32[2704,128]{1,0:T(8,128)S(1)} copy-done((f32[2704,128]{1,0:T(8,128)S(1)}, f32[2704,128]{1,0:T(8,128)}, u32[]{:S(2)}) %copy-start) | copy-done | bytes 1384472
  16.8 0.1 shard_map.57.own_outer
  16.8 2.7 %collective-permute-done.2.mate2_msg = f32[272,128]{1,0:T(8,128)S(1)} collective-permute-done((f32[272,128]{1,0:T(8,128)}, f32[272,128]{1,0:T(8,128)S(1)}, u32[]{:S(2)}, u32[]{:S(2)}) %collective-permute-start.2) | collective-permute-done | bytes 139296 | tf_op jit(solution)/shard_map/ppermute | solution.py:955
  19.5 0.0 collective-permute-done.3.other2_msg
  19.5 0.0 collective-permute-done.mate_msg
  19.5 0.0 collective-permute-done.1.other_msg
  19.5 0.7 %shard_map.58 = (f32[472,128]{1,0:T(8,128)S(1)}, f32[480,128]{1,0:T(8,128)S(1)}, f32[128,128]{1,0:T(8,128)S(1)}) custom-call(f32[1440,128]{1,0:T(8,128)S(1)} %shard_map.57.own_outer, f32[2704,128]{1,0:T(8,128)S(1)} %copy-done, f32[460,128]{1,0:T(8,128)S(1)} %collective-permute-done.mate_msg, f32[460,128]{1,0:T(8,128)S(1)} %collective-permute-done.1.other_msg, ...), custom_call_target="tpu_custom_call" | custom-call | flops 10000000000 | tf_op jit(solution)/shard_map/pallas_call | solution.py:969
  20.2 0.7 %collective-permute-start.5 = (f32[480,128]{1,0:T(8,128)S(1)}, f32[480,128]{1,0:T(8,128)S(1)}, u32[]{:S(2)}, u32[]{:S(2)}) collective-permute-start(f32[480,128]{1,0:T(8,128)S(1)} %get-tuple-element.27), channel_id=1, source_target_pairs={{0,0},{1,2},{2,1},{3,3},{4,4},{5,6},{6,5},{7,7},{8,8},{9,10},{10,9... | collective-permute-start | bytes 737288 | tf_op jit(solution)/shard_map/ppermute | solution.py:955
  20.9 3.0 %collective-permute-start.4 = (f32[472,128]{1,0:T(8,128)S(1)}, f32[472,128]{1,0:T(8,128)S(1)}, u32[]{:S(2)}, u32[]{:S(2)}) collective-permute-start(f32[472,128]{1,0:T(8,128)S(1)} %get-tuple-element.26), channel_id=1, source_target_pairs={{0,1},{1,0},{2,3},{3,2},{4,5},{5,4},{6,7},{7,6},{8,9},{9,8},{10,11... | collective-permute-start | bytes 725000 | tf_op jit(solution)/shard_map/ppermute | solution.py:955
  23.9 0.0 collective-permute-done.6.mate_rest
  23.9 3.4 %collective-permute-start.7 = (f32[336,128]{1,0:T(8,128)S(1)}, f32[336,128]{1,0:T(8,128)S(1)}, u32[]{:S(2)}, u32[]{:S(2)}) collective-permute-start(f32[336,128]{1,0:T(8,128)S(1)} %slice.4), channel_id=1, source_target_pairs={{0,8},{8,16},{12,4},{16,24},{20,12},{28,20},{1,9},{9,17},{13,5},{1... | collective-permute-start | bytes 516104 | tf_op jit(solution)/shard_map/ppermute | solution.py:1020
  27.3 0.1 collective-permute-start.8
  27.4 0.7 %shard_map.56 = (f32[3792,128]{1,0:T(8,128)S(1)}, s32[24,128]{1,0:T(8,128)S(1)}) custom-call(f32[2704,128]{1,0:T(8,128)S(1)} %copy-done, f32[460,128]{1,0:T(8,128)S(1)} %collective-permute-done.mate_msg, f32[460,128]{1,0:T(8,128)S(1)} %collective-permute-done.1.other_msg, f32[272,128]{1,0:T(8,128)S(1)} %collective-permute-done.2.mate2_msg, ...), custom_call_target="tpu_custom_call" | custom-call | tf_op jit(solution)/shard_map/pallas_call | solution.py:969
  28.1 0.0 copy-start.1
  28.1 0.0 collective-permute-done.4.near_msg
  28.1 0.0 collective-permute-done.5.far_msg
  28.1 2.3 %shard_map.59 = (s32[72,128]{1,0:T(8,128)S(1)}, f32[1896,128]{1,0:T(8,128)S(1)}, f32[1896,128]{1,0:T(8,128)S(1)}) custom-call(s32[24,128]{1,0:T(8,128)S(1)} %get-tuple-element.24.own_slots, f32[3792,128]{1,0:T(8,128)S(1)} %get-tuple-element.25.first_post, f32[472,128]{1,0:T(8,128)S(1)} %collective-permute-done.4.near_msg, ...), custom_call_target="tpu_custom_call" | custom-call | tf_op jit(solution)/shard_map/pallas_call | solution.py:969
  30.4 1.2 %collective-permute-done.8.passed2_rest = f32[128,128]{1,0:T(8,128)S(1)} collective-permute-done((f32[128,128]{1,0:T(8,128)S(1)}, f32[128,128]{1,0:T(8,128)S(1)}, u32[]{:S(2)}, u32[]{:S(2)}) %collective-permute-start.8) | collective-permute-done | bytes 65568 | tf_op jit(solution)/shard_map/ppermute | solution.py:1035
  31.6 0.0 collective-permute-done.7.passed_rest
  31.6 0.0 copy-done.1
  31.6 6.0 %shard_map.60 = f32[3,19,4096]{2,1,0:T(8,128)} custom-call(s32[72,128]{1,0:T(8,128)S(1)} %get-tuple-element.28.slots, f32[3792,128]{1,0:T(8,128)S(1)} %get-tuple-element.25.first_post, f32[1896,128]{1,0:T(8,128)S(1)} %get-tuple-element.29.first_outer, f32[1896,128]{1,0:T(8,128)S(1)} %get-tuple-element.30.next_outer, f32[2704,128]{1,0:T(8,128)S(1)} %copy-done.1, ...), custom_call_target="tpu_custom_call" | custom-call | tf_op jit(solution)/shard_map/pallas_call | solution.py:969
  (1 shorter events, 0.0 us)
Async XLA Ops:
  4.3 15.2 %collective-permute-start = (f32[460,128]{1,0:T(8,128)}, f32[460,128]{1,0:T(8,128)S(1)}, u32[]{:S(2)}, u32[]{:S(2)}) collective-permute-start(f32[460,128]{1,0:T(8,128)} %get-tuple-element.20), channel_id=1, source_target_pairs={{0,4},{4,0},{8,12},{12,8},{16,20},{20,16},{24,28},{28,24},{1,5},{5... | collective-permute-start | bytes 706568 | tf_op jit(solution)/shard_map/ppermute | solution.py:955
  7.3 12.2 %collective-permute-start.1 = (f32[460,128]{1,0:T(8,128)}, f32[460,128]{1,0:T(8,128)S(1)}, u32[]{:S(2)}, u32[]{:S(2)}) collective-permute-start(f32[460,128]{1,0:T(8,128)} %get-tuple-element.21), channel_id=1, source_target_pairs={{0,0},{4,8},{8,4},{12,16},{16,12},{20,24},{24,20},{28,28},{1,1},{5... | collective-permute-start | bytes 706568 | tf_op jit(solution)/shard_map/ppermute | solution.py:955
  8.9 10.6 %collective-permute-start.2 = (f32[272,128]{1,0:T(8,128)}, f32[272,128]{1,0:T(8,128)S(1)}, u32[]{:S(2)}, u32[]{:S(2)}) collective-permute-start(f32[272,128]{1,0:T(8,128)} %get-tuple-element.22), channel_id=1, source_target_pairs={{0,8},{4,12},{8,0},{12,4},{16,24},{20,28},{24,16},{28,20},{1,9},{5... | collective-permute-start | bytes 417800 | tf_op jit(solution)/shard_map/ppermute | solution.py:955
  10.9 8.6 %collective-permute-start.3 = (f32[272,128]{1,0:T(8,128)}, f32[272,128]{1,0:T(8,128)S(1)}, u32[]{:S(2)}, u32[]{:S(2)}) collective-permute-start(f32[272,128]{1,0:T(8,128)} %get-tuple-element.23), channel_id=1, source_target_pairs={{0,0},{4,4},{8,16},{12,20},{16,8},{20,12},{24,24},{28,28},{1,1},{5... | collective-permute-start | bytes 417800 | tf_op jit(solution)/shard_map/ppermute | solution.py:955
  12.4 11.5 %collective-permute-start.6 = (f32[464,128]{1,0:T(8,128)}, f32[464,128]{1,0:T(8,128)S(1)}, u32[]{:S(2)}, u32[]{:S(2)}) collective-permute-start(f32[464,128]{1,0:T(8,128)} %get-tuple-element.31), channel_id=1, source_target_pairs={{0,4},{4,0},{8,12},{12,8},{16,20},{20,16},{24,28},{28,24},{1,5},{5... | collective-permute-start | bytes 712712 | tf_op jit(solution)/shard_map/ppermute | solution.py:1017
  15.4 1.3 %copy-start = (f32[2704,128]{1,0:T(8,128)S(1)}, f32[2704,128]{1,0:T(8,128)}, u32[]{:S(2)}) copy-start(f32[2704,128]{1,0:T(8,128)} %get-tuple-element.19.cells) | copy-start | bytes 4153348
  20.2 7.9 %collective-permute-start.5 = (f32[480,128]{1,0:T(8,128)S(1)}, f32[480,128]{1,0:T(8,128)S(1)}, u32[]{:S(2)}, u32[]{:S(2)}) collective-permute-start(f32[480,128]{1,0:T(8,128)S(1)} %get-tuple-element.27), channel_id=1, source_target_pairs={{0,0},{1,2},{2,1},{3,3},{4,4},{5,6},{6,5},{7,7},{8,8},{9,10},{10,9... | collective-permute-start | bytes 737288 | tf_op jit(solution)/shard_map/ppermute | solution.py:955
  20.9 7.2 %collective-permute-start.4 = (f32[472,128]{1,0:T(8,128)S(1)}, f32[472,128]{1,0:T(8,128)S(1)}, u32[]{:S(2)}, u32[]{:S(2)}) collective-permute-start(f32[472,128]{1,0:T(8,128)S(1)} %get-tuple-element.26), channel_id=1, source_target_pairs={{0,1},{1,0},{2,3},{3,2},{4,5},{5,4},{6,7},{7,6},{8,9},{9,8},{10,11... | collective-permute-start | bytes 725000 | tf_op jit(solution)/shard_map/ppermute | solution.py:955
  23.9 7.7 %collective-permute-start.7 = (f32[336,128]{1,0:T(8,128)S(1)}, f32[336,128]{1,0:T(8,128)S(1)}, u32[]{:S(2)}, u32[]{:S(2)}) collective-permute-start(f32[336,128]{1,0:T(8,128)S(1)} %slice.4), channel_id=1, source_target_pairs={{0,8},{8,16},{12,4},{16,24},{20,12},{28,20},{1,9},{9,17},{13,5},{1... | collective-permute-start | bytes 516104 | tf_op jit(solution)/shard_map/ppermute | solution.py:1020
  27.3 4.3 %collective-permute-start.8 = (f32[128,128]{1,0:T(8,128)S(1)}, f32[128,128]{1,0:T(8,128)S(1)}, u32[]{:S(2)}, u32[]{:S(2)}) collective-permute-start(f32[128,128]{1,0:T(8,128)S(1)} %get-tuple-element.32), channel_id=1, source_target_pairs={{0,4},{4,0},{8,12},{12,8},{16,20},{20,16},{24,28},{28,24},{1,5},{5... | collective-permute-start | bytes 196616 | tf_op jit(solution)/shard_map/ppermute | solution.py:1035
  28.1 3.5 %copy-start.1 = (f32[2704,128]{1,0:T(8,128)S(1)}, f32[2704,128]{1,0:T(8,128)}, u32[]{:S(2)}) copy-start(f32[2704,128]{1,0:T(8,128)} %get-tuple-element.19.cells) | copy-start | bytes 4153348

commit v17 on v15

--- a/solution.py
+++ b/solution.py
@@ -1027,7 +1027,7 @@
         "VVV",
         [rows128(NEAR_ROWS), rows128(FAR_ROWS), rows128(ALONG_Z)],
         (outer, *strips),
-        [floats(rows) for rows in [PLANES * GROUP] + sorted_rows],
+        [floats(rows) for rows in [(PLANES + 8) * GROUP] + sorted_rows],
         cost=pl.CostEstimate(flops=10**10, bytes_accessed=0, transcendentals=0),
     )
     near_msg, far_msg = swapped((near_msg, far_msg), "cross")
@@ -1061,7 +1061,7 @@
         [jax.ShapeDtypeStruct(populations.shape, jnp.float32)],
         (slots, post, outer_post, next_outer, *arriving),
         [
-            floats(SLOTS * SLOT),
+            floats(SLOTS * SLOT + 8 * PLANE),
             floats(ALL_PLANES * PAIR),
             floats(ALL_PLANES * GROUP),
             pltpu.VMEM(populations.shape, jnp.float32),

time: 37.9 us -> 37.9 us (level)
  no operation moved by 1% of the time
where the time goes in v17:
time: 37.9 us; the launch traced here: 37.7 us
  starting transfers between devices  17 us (45%)
  Pallas kernels  13.2 us (35%)
  waiting for transfers between devices  5.41 us (14%)
  local copies, waits for them, and re-layouts  1.36 us (4%)
  between operations  0.73 us (2%)
    pallas_call x6, Pallas kernels, call(): pl.pallas_call(kernel, out_shape=outs, in_specs=[spaces[x] for x in in_sp...  13.2 us
    ppermute x6, starting transfers between devices, swapped(): results.append(lax.ppermute(value[which], axis, pairs))  11.9 us
    ppermute x1, starting transfers between devices, per_device(): mate_rest = lax.ppermute(rest_msg, 'curve', pairs)  3.03 us
    ppermute x1, waiting for transfers between devices, per_device(): passed2_rest = lax.ppermute(turn_msg, 'curve', pairs)  2.72 us
    ppermute x6, waiting for transfers between devices, swapped(): results.append(lax.ppermute(value[which], axis, pairs))  2.68 us
    ppermute x1, starting transfers between devices, per_device(): passed_rest = lax.ppermute(mate_rest[:HALF], 'curve', pairs)  1.6 us
    unnamed x4, local copies, waits for them, and re-layouts  1.35 us
  transfers between devices with their start and end apart: 9, of which 2 were waited for; matrix products, arithmetic and copies ran while one was open for 0% of the time, Pallas kernels for 9%

profile of v17, /device:TPU:0, one launch (start us, length us, event | category | flops | bytes accessed | tf_op | source)
XLA Modules:
  0.0 37.7 jit_solution(5888388937427825103)
XLA Ops:
  0.7 3.6 %shard_map.55 = (f32[2704,128]{1,0:T(8,128)}, f32[460,128]{1,0:T(8,128)}, f32[460,128]{1,0:T(8,128)}, f32[272,128]{1,0:T(8,128)}, f32[272,128]{1,0:T(8,128)}, /*index=5*/f32[464,128]{1,0:T(8,128)}) custom-call(s32[3,32]{1,0:T(4,128)} %bitcast.1, s32[1]{0:T(128)S(6)} %copy.6.counts_hbm, f32[3,19,4096]{2,1,0:T(8,128)} %pops_hbm.1, s32[3,5832]{1,0:T(4,128)} %flags_hbm.1, ...), custom_call_target="tpu_custom_call" | custom-call | tf_op jit(solution)/shard_map/pallas_call | solution.py:969
  4.3 3.0 %collective-permute-start = (f32[460,128]{1,0:T(8,128)}, f32[460,128]{1,0:T(8,128)S(1)}, u32[]{:S(2)}, u32[]{:S(2)}) collective-permute-start(f32[460,128]{1,0:T(8,128)} %get-tuple-element.20), channel_id=1, source_target_pairs={{0,4},{4,0},{8,12},{12,8},{16,20},{20,16},{24,28},{28,24},{1,5},{5... | collective-permute-start | bytes 706568 | tf_op jit(solution)/shard_map/ppermute | solution.py:955
  7.3 1.6 %collective-permute-start.1 = (f32[460,128]{1,0:T(8,128)}, f32[460,128]{1,0:T(8,128)S(1)}, u32[]{:S(2)}, u32[]{:S(2)}) collective-permute-start(f32[460,128]{1,0:T(8,128)} %get-tuple-element.21), channel_id=1, source_target_pairs={{0,0},{4,8},{8,4},{12,16},{16,12},{20,24},{24,20},{28,28},{1,1},{5... | collective-permute-start | bytes 706568 | tf_op jit(solution)/shard_map/ppermute | solution.py:955
  8.9 2.0 %collective-permute-start.2 = (f32[272,128]{1,0:T(8,128)}, f32[272,128]{1,0:T(8,128)S(1)}, u32[]{:S(2)}, u32[]{:S(2)}) collective-permute-start(f32[272,128]{1,0:T(8,128)} %get-tuple-element.22), channel_id=1, source_target_pairs={{0,8},{4,12},{8,0},{12,4},{16,24},{20,28},{24,16},{28,20},{1,9},{5... | collective-permute-start | bytes 417800 | tf_op jit(solution)/shard_map/ppermute | solution.py:955
  10.9 1.6 %collective-permute-start.3 = (f32[272,128]{1,0:T(8,128)}, f32[272,128]{1,0:T(8,128)S(1)}, u32[]{:S(2)}, u32[]{:S(2)}) collective-permute-start(f32[272,128]{1,0:T(8,128)} %get-tuple-element.23), channel_id=1, source_target_pairs={{0,0},{4,4},{8,16},{12,20},{16,8},{20,12},{24,24},{28,28},{1,1},{5... | collective-permute-start | bytes 417800 | tf_op jit(solution)/shard_map/ppermute | solution.py:955
  12.4 3.0 %collective-permute-start.6 = (f32[464,128]{1,0:T(8,128)}, f32[464,128]{1,0:T(8,128)S(1)}, u32[]{:S(2)}, u32[]{:S(2)}) collective-permute-start(f32[464,128]{1,0:T(8,128)} %get-tuple-element.31), channel_id=1, source_target_pairs={{0,4},{4,0},{8,12},{12,8},{16,20},{20,16},{24,28},{28,24},{1,5},{5... | collective-permute-start | bytes 712712 | tf_op jit(solution)/shard_map/ppermute | solution.py:1017
  15.4 0.0 copy-start
  15.4 1.3 %copy-done = f32[2704,128]{1,0:T(8,128)S(1)} copy-done((f32[2704,128]{1,0:T(8,128)S(1)}, f32[2704,128]{1,0:T(8,128)}, u32[]{:S(2)}) %copy-start) | copy-done | bytes 1384472
  16.8 0.1 shard_map.57.own_outer
  16.8 2.7 %collective-permute-done.2.mate2_msg = f32[272,128]{1,0:T(8,128)S(1)} collective-permute-done((f32[272,128]{1,0:T(8,128)}, f32[272,128]{1,0:T(8,128)S(1)}, u32[]{:S(2)}, u32[]{:S(2)}) %collective-permute-start.2) | collective-permute-done | bytes 139296 | tf_op jit(solution)/shard_map/ppermute | solution.py:955
  19.5 0.0 collective-permute-done.3.other2_msg
  19.5 0.0 collective-permute-done.mate_msg
  19.5 0.0 collective-permute-done.1.other_msg
  19.5 0.6 %shard_map.58 = (f32[472,128]{1,0:T(8,128)S(1)}, f32[480,128]{1,0:T(8,128)S(1)}, f32[128,128]{1,0:T(8,128)S(1)}) custom-call(f32[1440,128]{1,0:T(8,128)S(1)} %shard_map.57.own_outer, f32[2704,128]{1,0:T(8,128)S(1)} %copy-done, f32[460,128]{1,0:T(8,128)S(1)} %collective-permute-done.mate_msg, f32[460,128]{1,0:T(8,128)S(1)} %collective-permute-done.1.other_msg, ...), custom_call_target="tpu_custom_call" | custom-call | flops 10000000000 | tf_op jit(solution)/shard_map/pallas_call | solution.py:969
  20.1 0.7 %collective-permute-start.5 = (f32[480,128]{1,0:T(8,128)S(1)}, f32[480,128]{1,0:T(8,128)S(1)}, u32[]{:S(2)}, u32[]{:S(2)}) collective-permute-start(f32[480,128]{1,0:T(8,128)S(1)} %get-tuple-element.27), channel_id=1, source_target_pairs={{0,0},{1,2},{2,1},{3,3},{4,4},{5,6},{6,5},{7,7},{8,8},{9,10},{10,9... | collective-permute-start | bytes 737288 | tf_op jit(solution)/shard_map/ppermute | solution.py:955
  20.8 3.1 %collective-permute-start.4 = (f32[472,128]{1,0:T(8,128)S(1)}, f32[472,128]{1,0:T(8,128)S(1)}, u32[]{:S(2)}, u32[]{:S(2)}) collective-permute-start(f32[472,128]{1,0:T(8,128)S(1)} %get-tuple-element.26), channel_id=1, source_target_pairs={{0,1},{1,0},{2,3},{3,2},{4,5},{5,4},{6,7},{7,6},{8,9},{9,8},{10,11... | collective-permute-start | bytes 725000 | tf_op jit(solution)/shard_map/ppermute | solution.py:955
  23.9 0.0 collective-permute-done.6.mate_rest
  23.9 1.6 %collective-permute-start.7 = (f32[336,128]{1,0:T(8,128)S(1)}, f32[336,128]{1,0:T(8,128)S(1)}, u32[]{:S(2)}, u32[]{:S(2)}) collective-permute-start(f32[336,128]{1,0:T(8,128)S(1)} %slice.4), channel_id=1, source_target_pairs={{0,8},{4,0},{8,16},{12,4},{16,24},{20,12},{24,28},{28,20},{1,9},{5... | collective-permute-start | bytes 516104 | tf_op jit(solution)/shard_map/ppermute | solution.py:1020
  25.5 0.5 %collective-permute-start.8 = (f32[128,128]{1,0:T(8,128)S(1)}, f32[128,128]{1,0:T(8,128)S(1)}, u32[]{:S(2)}, u32[]{:S(2)}) collective-permute-start(f32[128,128]{1,0:T(8,128)S(1)} %get-tuple-element.32), channel_id=1, source_target_pairs={{0,4},{4,0},{8,12},{12,8},{16,20},{20,16},{24,28},{28,24},{1,5},{5... | collective-permute-start | bytes 196616 | tf_op jit(solution)/shard_map/ppermute | solution.py:1035
  26.0 0.6 %shard_map.56 = (f32[3792,128]{1,0:T(8,128)S(1)}, s32[24,128]{1,0:T(8,128)S(1)}) custom-call(f32[2704,128]{1,0:T(8,128)S(1)} %copy-done, f32[460,128]{1,0:T(8,128)S(1)} %collective-permute-done.mate_msg, f32[460,128]{1,0:T(8,128)S(1)} %collective-permute-done.1.other_msg, f32[272,128]{1,0:T(8,128)S(1)} %collective-permute-done.2.mate2_msg, ...), custom_call_target="tpu_custom_call" | custom-call | tf_op jit(solution)/shard_map/pallas_call | solution.py:969
  26.6 0.0 copy-start.1
  26.6 0.0 collective-permute-done.4.near_msg
  26.7 0.0 collective-permute-done.5.far_msg
  26.7 2.3 %shard_map.59 = (s32[72,128]{1,0:T(8,128)S(1)}, f32[1896,128]{1,0:T(8,128)S(1)}, f32[1896,128]{1,0:T(8,128)S(1)}) custom-call(s32[24,128]{1,0:T(8,128)S(1)} %get-tuple-element.24.own_slots, f32[3792,128]{1,0:T(8,128)S(1)} %get-tuple-element.25.first_post, f32[472,128]{1,0:T(8,128)S(1)} %collective-permute-done.4.near_msg, ...), custom_call_target="tpu_custom_call" | custom-call | tf_op jit(solution)/shard_map/pallas_call | solution.py:969
  28.9 2.7 %collective-permute-done.8.passed2_rest = f32[128,128]{1,0:T(8,128)S(1)} collective-permute-done((f32[128,128]{1,0:T(8,128)S(1)}, f32[128,128]{1,0:T(8,128)S(1)}, u32[]{:S(2)}, u32[]{:S(2)}) %collective-permute-start.8) | collective-permute-done | bytes 65568 | tf_op jit(solution)/shard_map/ppermute | solution.py:1035
  31.7 0.0 collective-permute-done.7.passed_rest
  31.7 0.0 copy-done.1
  31.7 6.0 %shard_map.60 = f32[3,19,4096]{2,1,0:T(8,128)} custom-call(s32[72,128]{1,0:T(8,128)S(1)} %get-tuple-element.28.slots, f32[3792,128]{1,0:T(8,128)S(1)} %get-tuple-element.25.first_post, f32[1896,128]{1,0:T(8,128)S(1)} %get-tuple-element.29.first_outer, f32[1896,128]{1,0:T(8,128)S(1)} %get-tuple-element.30.next_outer, f32[2704,128]{1,0:T(8,128)S(1)} %copy-done.1, ...), custom_call_target="tpu_custom_call" | custom-call | tf_op jit(solution)/shard_map/pallas_call | solution.py:969
  (1 shorter events, 0.0 us)
Async XLA Ops:
  4.3 15.2 %collective-permute-start = (f32[460,128]{1,0:T(8,128)}, f32[460,128]{1,0:T(8,128)S(1)}, u32[]{:S(2)}, u32[]{:S(2)}) collective-permute-start(f32[460,128]{1,0:T(8,128)} %get-tuple-element.20), channel_id=1, source_target_pairs={{0,4},{4,0},{8,12},{12,8},{16,20},{20,16},{24,28},{28,24},{1,5},{5... | collective-permute-start | bytes 706568 | tf_op jit(solution)/shard_map/ppermute | solution.py:955
  7.3 12.2 %collective-permute-start.1 = (f32[460,128]{1,0:T(8,128)}, f32[460,128]{1,0:T(8,128)S(1)}, u32[]{:S(2)}, u32[]{:S(2)}) collective-permute-start(f32[460,128]{1,0:T(8,128)} %get-tuple-element.21), channel_id=1, source_target_pairs={{0,0},{4,8},{8,4},{12,16},{16,12},{20,24},{24,20},{28,28},{1,1},{5... | collective-permute-start | bytes 706568 | tf_op jit(solution)/shard_map/ppermute | solution.py:955
  8.9 10.6 %collective-permute-start.2 = (f32[272,128]{1,0:T(8,128)}, f32[272,128]{1,0:T(8,128)S(1)}, u32[]{:S(2)}, u32[]{:S(2)}) collective-permute-start(f32[272,128]{1,0:T(8,128)} %get-tuple-element.22), channel_id=1, source_target_pairs={{0,8},{4,12},{8,0},{12,4},{16,24},{20,28},{24,16},{28,20},{1,9},{5... | collective-permute-start | bytes 417800 | tf_op jit(solution)/shard_map/ppermute | solution.py:955
  10.9 8.6 %collective-permute-start.3 = (f32[272,128]{1,0:T(8,128)}, f32[272,128]{1,0:T(8,128)S(1)}, u32[]{:S(2)}, u32[]{:S(2)}) collective-permute-start(f32[272,128]{1,0:T(8,128)} %get-tuple-element.23), channel_id=1, source_target_pairs={{0,0},{4,4},{8,16},{12,20},{16,8},{20,12},{24,24},{28,28},{1,1},{5... | collective-permute-start | bytes 417800 | tf_op jit(solution)/shard_map/ppermute | solution.py:955
  12.4 11.5 %collective-permute-start.6 = (f32[464,128]{1,0:T(8,128)}, f32[464,128]{1,0:T(8,128)S(1)}, u32[]{:S(2)}, u32[]{:S(2)}) collective-permute-start(f32[464,128]{1,0:T(8,128)} %get-tuple-element.31), channel_id=1, source_target_pairs={{0,4},{4,0},{8,12},{12,8},{16,20},{20,16},{24,28},{28,24},{1,5},{5... | collective-permute-start | bytes 712712 | tf_op jit(solution)/shard_map/ppermute | solution.py:1017
  15.4 1.3 %copy-start = (f32[2704,128]{1,0:T(8,128)S(1)}, f32[2704,128]{1,0:T(8,128)}, u32[]{:S(2)}) copy-start(f32[2704,128]{1,0:T(8,128)} %get-tuple-element.19.cells) | copy-start | bytes 4153348
  20.1 6.5 %collective-permute-start.5 = (f32[480,128]{1,0:T(8,128)S(1)}, f32[480,128]{1,0:T(8,128)S(1)}, u32[]{:S(2)}, u32[]{:S(2)}) collective-permute-start(f32[480,128]{1,0:T(8,128)S(1)} %get-tuple-element.27), channel_id=1, source_target_pairs={{0,0},{1,2},{2,1},{3,3},{4,4},{5,6},{6,5},{7,7},{8,8},{9,10},{10,9... | collective-permute-start | bytes 737288 | tf_op jit(solution)/shard_map/ppermute | solution.py:955
  20.8 5.9 %collective-permute-start.4 = (f32[472,128]{1,0:T(8,128)S(1)}, f32[472,128]{1,0:T(8,128)S(1)}, u32[]{:S(2)}, u32[]{:S(2)}) collective-permute-start(f32[472,128]{1,0:T(8,128)S(1)} %get-tuple-element.26), channel_id=1, source_target_pairs={{0,1},{1,0},{2,3},{3,2},{4,5},{5,4},{6,7},{7,6},{8,9},{9,8},{10,11... | collective-permute-start | bytes 725000 | tf_op jit(solution)/shard_map/ppermute | solution.py:955
  23.9 7.8 %collective-permute-start.7 = (f32[336,128]{1,0:T(8,128)S(1)}, f32[336,128]{1,0:T(8,128)S(1)}, u32[]{:S(2)}, u32[]{:S(2)}) collective-permute-start(f32[336,128]{1,0:T(8,128)S(1)} %slice.4), channel_id=1, source_target_pairs={{0,8},{4,0},{8,16},{12,4},{16,24},{20,12},{24,28},{28,20},{1,9},{5... | collective-permute-start | bytes 516104 | tf_op jit(solution)/shard_map/ppermute | solution.py:1020
  25.5 6.2 %collective-permute-start.8 = (f32[128,128]{1,0:T(8,128)S(1)}, f32[128,128]{1,0:T(8,128)S(1)}, u32[]{:S(2)}, u32[]{:S(2)}) collective-permute-start(f32[128,128]{1,0:T(8,128)S(1)} %get-tuple-element.32), channel_id=1, source_target_pairs={{0,4},{4,0},{8,12},{12,8},{16,20},{20,16},{24,28},{28,24},{1,5},{5... | collective-permute-start | bytes 196616 | tf_op jit(solution)/shard_map/ppermute | solution.py:1035
  26.6 5.0 %copy-start.1 = (f32[2704,128]{1,0:T(8,128)S(1)}, f32[2704,128]{1,0:T(8,128)}, u32[]{:S(2)}) copy-start(f32[2704,128]{1,0:T(8,128)} %get-tuple-element.19.cells) | copy-start | bytes 4153348
